TPU v7x, 32 devices: a whole 2x2x4 slice. The times are simulated.
32 devices in a mesh: groups: 2 (over x), sites: 16 (over z, y, core).
Axes of the slice: x: 2, y: 2, z: 4, core: 2. Of those that a mesh axis runs over, the one named last changes fastest.
Arguments:
- state: float32 [64, 128, 128], P(('groups', 'sites')), parts along dimension 0
- left_tensor: float32 [64, 128, 128], P(('groups', 'sites')), parts along dimension 0
- right_tensor: float32 [64, 128, 128], P(('groups', 'sites')), parts along dimension 0
- onsite: float32 [64, 128, 128], P(('groups', 'sites')), parts along dimension 0, may hold values from -6 to 6
- left_env: float32 [256, 8, 128, 128], P(('groups', 'sites')), parts along dimension 0
- right_env: float32 [256, 8, 128, 128], P(('groups', 'sites')), parts along dimension 0
- mpo_bond: float32 [256, 8], P(('groups', 'sites')), parts along dimension 0
- sectors: int32 [8, 8], P('groups'), parts along dimension 0, may hold values from 0 to 7, each once within a row
- flow: int32 [8, 8], P('groups'), parts along dimension 0, may hold values from 0 to 7, each once within a row
Outputs:
- new_state: float32 [64, 128, 128], P(('groups', 'sites')), parts along dimension 0
- energy: float32 [32], P(('groups', 'sites')), parts along dimension 0
There are 2 independent parts, one for each index of `groups`. A program takes and returns all parts, laid end to end along the dimension named above; each array names one. Nothing has to cross between parts.
Inputs may be any that keep to these rules, and one draw needn't show every extreme that they name: Each row of sectors names every sector once. Each row of flow names every sector once.
All inputs are finite; a program needn't handle non-finite values.
Results may differ from a plain program's by a relative error of at most 0.0003.
Values sent between devices are 32-bit elements; how exact they have to be, the bound alone decides.
No kernel may reach another device: no remote copies, remote signals or barrier semaphores. Data moves between devices by JAX's collectives and lax.ppermute only.
A program may use at most 128 MiB of HBM per device.

v0:
```python
import math

import jax
import jax.numpy as jnp
from jax import lax
from jax.sharding import PartitionSpec as P

GROUP = 4
CHUNKS = (2, 2, 2, 1, 1)

HIGH = lax.Precision.HIGH
HIGHEST = lax.Precision.HIGHEST


def shift(block, distance):
    devices = range(lax.axis_size("sites"))
    route = [(i - distance, i) for i in devices if i - distance in devices]
    return lax.ppermute(block, "sites", route)


def partner(block, mask):
    route = [(i, i ^ mask) for i in range(lax.axis_size("sites"))]
    return lax.ppermute(block, "sites", route)


def group_gather(local, member):
    whole = local
    for bit in range(GROUP.bit_length() - 1):
        other = partner(whole, 1 << bit)
        lower = member >> bit & 1 == 0
        whole = jnp.where(
            lower, jnp.concatenate([whole, other], 0), jnp.concatenate([other, whole], 0)
        )
    return whole


def group_total(value):
    first, second, third = partner(value, 1), partner(value, 2), partner(value, 3)
    return (value + first) + (second + third)


def inverse(row):
    labels = jnp.arange(row.shape[0], dtype=jnp.int32)
    return jnp.sum(jnp.where(row[None, :] == labels[:, None], labels[None, :], 0), axis=1)


def row_of(table, index):
    return lax.dynamic_index_in_dim(table, jnp.clip(index, 0, table.shape[0] - 1), 0, False)


def pick(env, order):
    return jnp.stack(
        [lax.dynamic_index_in_dim(env, order[j], 1, False) for j in range(order.shape[0])], 0
    )


def weighted(env_left, env_right, bond, middle):
    mixed = jnp.einsum("mn,snij->smij", bond, env_right, precision=HIGHEST)
    temp = jnp.einsum("smij,sjl->smil", env_left, middle, precision=HIGH)
    return mixed, jnp.einsum("smil,smlk->sik", temp, mixed, precision=HIGH)


def on_device(
    state, left_tensor, right_tensor, onsite, left_env, right_env, mpo_bond, sectors, flow
):
    position = lax.axis_index("sites")
    partition = position // GROUP
    member = position % GROUP
    first = partition == 0
    last = partition == lax.axis_size("sites") // GROUP - 1
    own, size = state.shape[0], state.shape[1]
    terms, total = left_env.shape[0], left_env.shape[1]
    eye = jnp.eye(size, dtype=jnp.float32)

    here = inverse(row_of(flow, partition))
    joined = row_of(sectors, partition)
    send_left = here
    send_right = here[row_of(sectors, partition - 1)]
    pos_left = inverse(row_of(flow, partition - 1))
    pos_right = inverse(row_of(flow, partition + 1))[joined]

    bond_rows = jnp.pad(mpo_bond, ((0, 0), (0, size - mpo_bond.shape[1])))
    note = lambda tensor: jnp.concatenate([tensor.reshape(own * size, size), bond_rows], 0)
    from_left = shift(note(left_tensor), GROUP)
    from_right = shift(note(right_tensor), -GROUP)

    starts = [sum(CHUNKS[:i]) for i in range(len(CHUNKS))]
    got = []
    for i, (begin, width) in enumerate(zip(starts, CHUNKS)):
        to_right, to_left = send_left[begin : begin + width], send_right[begin : begin + width]
        if i >= 2:
            to_right, _ = lax.optimization_barrier((to_right, got[i - 2][0]))
            to_left, _ = lax.optimization_barrier((to_left, got[i - 2][1]))
        got.append(
            (shift(pick(left_env, to_right), GROUP), shift(pick(right_env, to_left), -GROUP))
        )

    def edge(flag, block):
        tensor = jnp.where(flag, eye, block[: own * size].reshape(own, size, size))
        small = jnp.eye(terms, dtype=jnp.float32)
        return tensor, jnp.where(flag, small, block[own * size :, : mpo_bond.shape[1]])

    tensor_left, bond_left = edge(first, from_left)
    tensor_right, bond_right = edge(last, from_right)
    bond = jnp.einsum("mn,kn->mk", bond_left, bond_right, precision=HIGHEST)
    gathered = group_gather(jnp.stack([state, tensor_left, tensor_right], 1), member)
    vector = gathered[:, 0]
    outer_left = jnp.take(gathered[:, 1], pos_left, axis=0)
    outer_right = jnp.take(gathered[:, 2], pos_right, axis=0)
    diagonal = lax.dynamic_update_slice_in_dim(
        jnp.zeros_like(vector), onsite, member * own, 0
    )

    def inward(block, a, b):
        return jnp.einsum(
            "sil,slm->sim",
            jnp.einsum("sij,sjl->sil", a, block, precision=HIGHEST),
            b,
            precision=HIGHEST,
        )

    norm_sq = jnp.sum(vector * vector)
    first_vec = vector / jnp.sqrt(norm_sq)
    middle = inward(first_vec, outer_left, outer_right)
    back_left, back_right = jnp.swapaxes(outer_left, 1, 2), jnp.swapaxes(outer_right, 1, 2)

    kept, images = [], []
    for i, (begin, width) in enumerate(zip(starts, CHUNKS)):
        at = slice(begin, begin + width)
        own_left = jnp.moveaxis(left_env[:, at], 1, 0)
        use_left = jnp.where(first, own_left, got[i][0])
        use_right = jnp.where(last, pick(right_env, joined[at]), got[i][1])
        mixed, core = weighted(use_left, use_right, bond, middle[at])
        kept.append((use_left, mixed))
        part = inward(core, back_left[at], back_right[at]) + diagonal[at] * first_vec[at]
        images.append(group_total(part))
    image = jnp.concatenate(images, 0)
    alpha1 = jnp.sum(first_vec * image)
    resid = image - alpha1 * first_vec
    beta = jnp.sqrt(jnp.sum(resid * resid) + 1e-06)
    second_vec = resid / beta
    middle = inward(second_vec, outer_left, outer_right)
    share = jnp.sum(diagonal * second_vec * second_vec)
    for (begin, width), (use_left, mixed) in zip(zip(starts, CHUNKS), kept):
        at = slice(begin, begin + width)
        temp = jnp.einsum("smij,sjl->smil", use_left, middle[at], precision=HIGH)
        core = jnp.einsum("smil,smlk->sik", temp, mixed, precision=HIGH)
        share = share + jnp.sum(middle[at] * core)
    alpha2 = group_total(share)

    energy = (alpha1 + alpha2) / 2.0 - jnp.sqrt(((alpha1 - alpha2) / 2.0) ** 2 + beta * beta)
    height = jnp.sqrt(beta * beta + (energy - alpha1) ** 2)
    scale = math.sqrt(total * size * size)
    mine = lambda block: lax.dynamic_slice_in_dim(block, member * own, own, 0)
    new_state = scale * (
        beta / height * mine(first_vec) + (energy - alpha1) / height * mine(second_vec)
    )
    return (new_state, jnp.reshape(energy, (1,)))


def solution(mesh):
    return jax.shard_map(
        on_device,
        mesh=mesh,
        in_specs=(
            P(("groups", "sites"), None, None),
            P(("groups", "sites"), None, None),
            P(("groups", "sites"), None, None),
            P(("groups", "sites"), None, None),
            P(("groups", "sites"), None, None, None),
            P(("groups", "sites"), None, None, None),
            P(("groups", "sites"), None),
            P("groups", None),
            P("groups", None),
        ),
        out_specs=(P(("groups", "sites"), None, None), P(("groups", "sites"))),
        check_vma=False,
    )
```

profile of v0, /device:TPU:0, one launch (start us, length us, event | category | flops | bytes accessed | tf_op | source)
XLA Modules:
  0.0 258.7 jit_solution(5473186746856467019)
XLA Ops:
  8.3 5.0 %collective-permute-start.4 = (f32[2,8,128,128]{3,2,0,1:T(8,128)}, f32[2,8,128,128]{3,2,0,1:T(8,128)S(1)}, u32[]{:S(2)}, u32[]{:S(2)}) collective-permute-start(f32[2,8,128,128]{3,2,0,1:T(8,128)} %pad_maximum_fusion), channel_id=1, source_target_pairs={{0,4},{1,5},{2,6},{3,7},{4,8},{5,9},{6,10},{7,11},{8,12},{9,13},{1... | collective-permute-start | bytes 3145736 | tf_op jit(solution)/shard_map/ppermute | solution.py:18
  13.3 3.6 %collective-permute-start = (f32[264,128]{1,0:T(8,128)S(1)}, f32[264,128]{1,0:T(8,128)S(1)}, u32[]{:S(2)}, u32[]{:S(2)}) collective-permute-start(f32[264,128]{1,0:T(8,128)S(1)} %get-tuple-element.51), channel_id=1, source_target_pairs={{0,4},{1,5},{2,6},{3,7},{4,8},{5,9},{6,10},{7,11},{8,12},{9,13},{1... | collective-permute-start | bytes 405512 | tf_op jit(solution)/shard_map/ppermute | solution.py:18
  28.3 10.4 %collective-permute-done = f32[264,128]{1,0:T(8,128)S(1)} collective-permute-done((f32[264,128]{1,0:T(8,128)S(1)}, f32[264,128]{1,0:T(8,128)S(1)}, u32[]{:S(2)}, u32[]{:S(2)}) %collective-permute-start) | collective-permute-done | bytes 135200 | tf_op jit(solution)/shard_map/ppermute | solution.py:18
  63.2 1.6 collective-permute-start.3
  69.3 1.7 dynamic-slice_bitcast_fusion.9
  75.2 5.4 %collective-permute-start.9 = (f32[2,8,128,128]{3,2,0,1:T(8,128)}, f32[2,8,128,128]{3,2,0,1:T(8,128)}, u32[]{:S(2)}, u32[]{:S(2)}) collective-permute-start(f32[2,8,128,128]{3,2,0,1:T(8,128)} %pad_maximum_fusion.2), channel_id=1, source_target_pairs={{0,4},{1,5},{2,6},{3,7},{4,8},{5,9},{6,10},{7,11},{8,12},{9,13},{1... | collective-permute-start | bytes 3145736 | tf_op jit(solution)/shard_map/ppermute | solution.py:18
  81.7 3.5 %collective-permute-start.14 = (f32[2,8,128,128]{3,2,0,1:T(8,128)}, f32[2,8,128,128]{3,2,0,1:T(8,128)}, u32[]{:S(2)}, u32[]{:S(2)}) collective-permute-start(f32[2,8,128,128]{3,2,0,1:T(8,128)} %pad_maximum_fusion.4), channel_id=1, source_target_pairs={{0,4},{1,5},{2,6},{3,7},{4,8},{5,9},{6,10},{7,11},{8,12},{9,13},{1... | collective-permute-start | bytes 3145736 | tf_op jit(solution)/shard_map/ppermute | solution.py:18
  86.5 1.7 dynamic-slice_bitcast_fusion.5
  91.5 1.5 collective-permute-start.15
  93.0 1.5 maximum_select_fusion
  100.1 2.1 fusion.59
  104.7 20.5 %collective-permute-done.14 = f32[2,8,128,128]{3,2,0,1:T(8,128)} collective-permute-done((f32[2,8,128,128]{3,2,0,1:T(8,128)}, f32[2,8,128,128]{3,2,0,1:T(8,128)}, u32[]{:S(2)}, u32[]{:S(2)}) %collective-permute-start.14) | collective-permute-done | bytes 1048608 | tf_op jit(solution)/shard_map/ppermute | solution.py:18
  127.5 11.1 %collective-permute-done.15 = f32[2,8,128,128]{3,2,1,0:T(8,128)} collective-permute-done((f32[2,8,128,128]{3,2,1,0:T(8,128)}, f32[2,8,128,128]{3,2,1,0:T(8,128)}, u32[]{:S(2)}, u32[]{:S(2)}) %collective-permute-start.15) | collective-permute-done | bytes 1048608 | tf_op jit(solution)/shard_map/ppermute | solution.py:18
  141.3 3.6 %dynamic-slice_bitcast_fusion = (f32[1,8,128,128]{3,2,1,0:T(8,128)}, f32[1,8,128,128]{3,2,1,0:T(8,128)}, f32[1,8,128,128]{3,2,1,0:T(8,128)S(1)}, f32[1,8,128,128...) fusion(f32[8,8,128,128]{3,2,1,0:T(8,128)} %param.16, ...), kind=kLoop, calls=%fused_computation.95 | loop fusion | bytes 8388640 | tf_op jit(solution)/shard_map/stack | solution.py:52
  144.9 1.5 maximum_select_fusion.2
  146.4 1.6 convolution_bitcast_fusion.1
  154.0 1.6 convolution_bitcast_fusion.2
  158.8 1.5 collective-permute-start.7
  161.8 1.9 convolution_bitcast_fusion
  169.5 1.6 collective-permute-start.13
  177.7 5.2 %collective-permute-start.24 = (f32[1,8,128,128]{3,2,1,0:T(8,128)S(1)}, f32[1,8,128,128]{3,2,1,0:T(8,128)S(1)}, u32[]{:S(2)}, u32[]{:S(2)}) collective-permute-start(f32[1,8,128,128]{3,2,1,0:T(8,128)S(1)} %get-tuple-element.29), channel_id=1, source_target_pairs={{0,4},{1,5},{2,6},{3,7},{4,8},{5,9},{6,10},{7,11},{8,12},{9,13},{1... | collective-permute-start | bytes 1572872 | tf_op jit(solution)/shard_map/ppermute | solution.py:18
  183.0 3.9 %collective-permute-start.19 = (f32[1,8,128,128]{3,2,1,0:T(8,128)S(1)}, f32[1,8,128,128]{3,2,1,0:T(8,128)S(1)}, u32[]{:S(2)}, u32[]{:S(2)}) collective-permute-start(f32[1,8,128,128]{3,2,1,0:T(8,128)S(1)} %get-tuple-element.30), channel_id=1, source_target_pairs={{0,4},{1,5},{2,6},{3,7},{4,8},{5,9},{6,10},{7,11},{8,12},{9,13},{1... | collective-permute-start | bytes 1572872 | tf_op jit(solution)/shard_map/ppermute | solution.py:18
  188.0 10.7 %collective-permute-done.25 = f32[1,8,128,128]{3,2,1,0:T(8,128)S(1)} collective-permute-done((f32[1,8,128,128]{3,2,1,0:T(8,128)}, f32[1,8,128,128]{3,2,1,0:T(8,128)S(1)}, u32[]{:S(2)}, u32[]{:S(2)}) %collective-permute-start.25) | collective-permute-done | bytes 524320 | tf_op jit(solution)/shard_map/ppermute | solution.py:18
  200.8 5.0 %collective-permute-done.19 = f32[1,8,128,128]{3,2,1,0:T(8,128)S(1)} collective-permute-done((f32[1,8,128,128]{3,2,1,0:T(8,128)S(1)}, f32[1,8,128,128]{3,2,1,0:T(8,128)S(1)}, u32[]{:S(2)}, u32[]{:S(2)}) %collective-permute-start.19) | collective-permute-done | bytes 524320 | tf_op jit(solution)/shard_map/ppermute | solution.py:18
  205.8 1.6 fusion.45
  213.0 1.8 fusion.74
  219.4 3.3 %collective-permute-done.27 = f32[1,128,128]{2,1,0:T(8,128)S(1)} collective-permute-done((f32[1,128,128]{2,1,0:T(8,128)S(1)}, f32[1,128,128]{2,1,0:T(8,128)S(1)}, u32[]{:S(2)}, u32[]{:S(2)}) %collective-permute-start.27) | collective-permute-done | bytes 65568 | tf_op jit(solution)/shard_map/ppermute | solution.py:23
  225.7 2.7 %fusion.39 = (f32[]{:T(128)}, f32[8,128,128]{2,1,0:T(8,128)S(1)}) fusion(f32[8,128,128]{2,1,0:T(8,128)} %constant_dynamic-update-slice_fusion, f32[]{:T(128)S(6)} %sqrt.13, f32[8,128,128]{2,1,0:T(8,128)} %copy-done.10, f32[8,1,128,128]{3,2,0,1:T(8,128)S(1)} %get-tuple-element.47, f32[]{:T(128)} %fusion.49), kind=kLoop, calls=%fused_computation.72 | loop fusion | flops 786431 | bytes 2097164 | tf_op jit(solution)/shard_map/reduce_sum | solution.py:143
  228.4 1.9 fusion.61
  240.1 1.5 fusion.31
  246.8 2.8 %collective-permute-start.30 = (f32[]{:T(128)}, f32[]{:T(128)}, u32[]{:S(2)}, u32[]{:S(2)}) collective-permute-start(f32[]{:T(128)} %add.271), channel_id=1, source_target_pairs={{0,2},{1,3},{2,0},{3,1},{4,6},{5,7},{6,4},{7,5},{8,10},{9,11},{10,... | collective-permute-start | bytes 20 | tf_op jit(solution)/shard_map/ppermute | solution.py:23
  255.9 1.6 fusion.87
  (197 shorter events, 77.1 us)
Async XLA Ops:
  8.3 56.4 %collective-permute-start.4 = (f32[2,8,128,128]{3,2,0,1:T(8,128)}, f32[2,8,128,128]{3,2,0,1:T(8,128)S(1)}, u32[]{:S(2)}, u32[]{:S(2)}) collective-permute-start(f32[2,8,128,128]{3,2,0,1:T(8,128)} %pad_maximum_fusion), channel_id=1, source_target_pairs={{0,4},{1,5},{2,6},{3,7},{4,8},{5,9},{6,10},{7,11},{8,12},{9,13},{1... | collective-permute-start | bytes 3145736 | tf_op jit(solution)/shard_map/ppermute | solution.py:18
  13.3 25.4 %collective-permute-start = (f32[264,128]{1,0:T(8,128)S(1)}, f32[264,128]{1,0:T(8,128)S(1)}, u32[]{:S(2)}, u32[]{:S(2)}) collective-permute-start(f32[264,128]{1,0:T(8,128)S(1)} %get-tuple-element.51), channel_id=1, source_target_pairs={{0,4},{1,5},{2,6},{3,7},{4,8},{5,9},{6,10},{7,11},{8,12},{9,13},{1... | collective-permute-start | bytes 405512 | tf_op jit(solution)/shard_map/ppermute | solution.py:18
  16.9 21.8 %collective-permute-start.1 = (f32[264,128]{1,0:T(8,128)S(1)}, f32[264,128]{1,0:T(8,128)S(1)}, u32[]{:S(2)}, u32[]{:S(2)}) collective-permute-start(f32[264,128]{1,0:T(8,128)S(1)} %get-tuple-element.52), channel_id=1, source_target_pairs={{4,0},{5,1},{6,2},{7,3},{8,4},{9,5},{10,6},{11,7},{12,8},{13,9},{1... | collective-permute-start | bytes 405512 | tf_op jit(solution)/shard_map/ppermute | solution.py:18
  25.5 42.5 %collective-permute-start.5 = (f32[2,8,128,128]{3,2,1,0:T(8,128)}, f32[2,8,128,128]{3,2,1,0:T(8,128)}, u32[]{:S(2)}, u32[]{:S(2)}) collective-permute-start(f32[2,8,128,128]{3,2,1,0:T(8,128)} %pad_maximum_fusion.1), channel_id=1, source_target_pairs={{4,0},{5,1},{6,2},{7,3},{8,4},{9,5},{10,6},{11,7},{12,8},{13,9},{1... | collective-permute-start | bytes 3145736 | tf_op jit(solution)/shard_map/ppermute | solution.py:18
  38.8 24.2 %collective-permute-start.2 = (f32[2,3,128,128]{3,2,0,1:T(8,128)S(1)}, f32[2,3,128,128]{3,2,0,1:T(8,128)S(1)}, u32[]{:S(2)}, u32[]{:S(2)}) collective-permute-start(f32[2,3,128,128]{3,2,0,1:T(8,128)S(1)} %pad_maximum_fusion.6), channel_id=1, source_target_pairs={{0,1},{1,0},{2,3},{3,2},{4,5},{5,4},{6,7},{7,6},{8,9},{9,8},{10,11... | collective-permute-start | bytes 1179656 | tf_op jit(solution)/shard_map/ppermute | solution.py:23
  63.2 29.9 %collective-permute-start.3 = (f32[4,3,128,128]{3,2,0,1:T(8,128)S(1)}, f32[4,3,128,128]{3,2,0,1:T(8,128)}, u32[]{:S(2)}, u32[]{:S(2)}) collective-permute-start(f32[4,3,128,128]{3,2,0,1:T(8,128)S(1)} %maximum_select_fusion.4), channel_id=1, source_target_pairs={{0,2},{1,3},{2,0},{3,1},{4,6},{5,7},{6,4},{7,5},{8,10},{9,11},{10,... | collective-permute-start | bytes 2359304 | tf_op jit(solution)/shard_map/ppermute | solution.py:23
  75.2 28.2 %collective-permute-start.9 = (f32[2,8,128,128]{3,2,0,1:T(8,128)}, f32[2,8,128,128]{3,2,0,1:T(8,128)}, u32[]{:S(2)}, u32[]{:S(2)}) collective-permute-start(f32[2,8,128,128]{3,2,0,1:T(8,128)} %pad_maximum_fusion.2), channel_id=1, source_target_pairs={{0,4},{1,5},{2,6},{3,7},{4,8},{5,9},{6,10},{7,11},{8,12},{9,13},{1... | collective-permute-start | bytes 3145736 | tf_op jit(solution)/shard_map/ppermute | solution.py:18
  81.7 43.5 %collective-permute-start.14 = (f32[2,8,128,128]{3,2,0,1:T(8,128)}, f32[2,8,128,128]{3,2,0,1:T(8,128)}, u32[]{:S(2)}, u32[]{:S(2)}) collective-permute-start(f32[2,8,128,128]{3,2,0,1:T(8,128)} %pad_maximum_fusion.4), channel_id=1, source_target_pairs={{0,4},{1,5},{2,6},{3,7},{4,8},{5,9},{6,10},{7,11},{8,12},{9,13},{1... | collective-permute-start | bytes 3145736 | tf_op jit(solution)/shard_map/ppermute | solution.py:18
  89.2 37.0 %collective-permute-start.10 = (f32[2,8,128,128]{3,2,1,0:T(8,128)}, f32[2,8,128,128]{3,2,1,0:T(8,128)}, u32[]{:S(2)}, u32[]{:S(2)}) collective-permute-start(f32[2,8,128,128]{3,2,1,0:T(8,128)} %pad_maximum_fusion.3), channel_id=1, source_target_pairs={{4,0},{5,1},{6,2},{7,3},{8,4},{9,5},{10,6},{11,7},{12,8},{13,9},{1... | collective-permute-start | bytes 3145736 | tf_op jit(solution)/shard_map/ppermute | solution.py:18
  91.5 47.1 %collective-permute-start.15 = (f32[2,8,128,128]{3,2,1,0:T(8,128)}, f32[2,8,128,128]{3,2,1,0:T(8,128)}, u32[]{:S(2)}, u32[]{:S(2)}) collective-permute-start(f32[2,8,128,128]{3,2,1,0:T(8,128)} %pad_maximum_fusion.5), channel_id=1, source_target_pairs={{4,0},{5,1},{6,2},{7,3},{8,4},{9,5},{10,6},{11,7},{12,8},{13,9},{1... | collective-permute-start | bytes 3145736 | tf_op jit(solution)/shard_map/ppermute | solution.py:18
  152.0 22.7 %collective-permute-start.11 = (f32[2,128,128]{2,1,0:T(8,128)S(1)}, f32[2,128,128]{2,1,0:T(8,128)}, u32[]{:S(2)}, u32[]{:S(2)}) collective-permute-start(f32[2,128,128]{2,1,0:T(8,128)S(1)} %convolution_add_fusion.1), channel_id=1, source_target_pairs={{0,1},{1,0},{2,3},{3,2},{4,5},{5,4},{6,7},{7,6},{8,9},{9,8},{10,11... | collective-permute-start | bytes 393224 | tf_op jit(solution)/shard_map/ppermute | solution.py:23
  152.1 22.8 %collective-permute-start.12 = (f32[2,128,128]{2,1,0:T(8,128)S(1)}, f32[2,128,128]{2,1,0:T(8,128)}, u32[]{:S(2)}, u32[]{:S(2)}) collective-permute-start(f32[2,128,128]{2,1,0:T(8,128)S(1)} %convolution_add_fusion.1), channel_id=1, source_target_pairs={{0,2},{1,3},{2,0},{3,1},{4,6},{5,7},{6,4},{7,5},{8,10},{9,11},{10,... | collective-permute-start | bytes 393224 | tf_op jit(solution)/shard_map/ppermute | solution.py:23
  158.5 10.9 %collective-permute-start.6 = (f32[2,128,128]{2,1,0:T(8,128)S(1)}, f32[2,128,128]{2,1,0:T(8,128)}, u32[]{:S(2)}, u32[]{:S(2)}) collective-permute-start(f32[2,128,128]{2,1,0:T(8,128)S(1)} %convolution_add_fusion.2), channel_id=1, source_target_pairs={{0,1},{1,0},{2,3},{3,2},{4,5},{5,4},{6,7},{7,6},{8,9},{9,8},{10,11... | collective-permute-start | bytes 393224 | tf_op jit(solution)/shard_map/ppermute | solution.py:23
  158.8 12.3 %collective-permute-start.7 = (f32[2,128,128]{2,1,0:T(8,128)S(1)}, f32[2,128,128]{2,1,0:T(8,128)}, u32[]{:S(2)}, u32[]{:S(2)}) collective-permute-start(f32[2,128,128]{2,1,0:T(8,128)S(1)} %convolution_add_fusion.2), channel_id=1, source_target_pairs={{0,2},{1,3},{2,0},{3,1},{4,6},{5,7},{6,4},{7,5},{8,10},{9,11},{10,... | collective-permute-start | bytes 393224 | tf_op jit(solution)/shard_map/ppermute | solution.py:23
  160.3 12.1 %collective-permute-start.8 = (f32[2,128,128]{2,1,0:T(8,128)S(1)}, f32[2,128,128]{2,1,0:T(8,128)}, u32[]{:S(2)}, u32[]{:S(2)}) collective-permute-start(f32[2,128,128]{2,1,0:T(8,128)S(1)} %convolution_add_fusion.2), channel_id=1, source_target_pairs={{0,3},{1,2},{2,1},{3,0},{4,7},{5,6},{6,5},{7,4},{8,11},{9,10},{10,... | collective-permute-start | bytes 393224 | tf_op jit(solution)/shard_map/ppermute | solution.py:23
  169.5 6.0 %collective-permute-start.13 = (f32[2,128,128]{2,1,0:T(8,128)S(1)}, f32[2,128,128]{2,1,0:T(8,128)S(1)}, u32[]{:S(2)}, u32[]{:S(2)}) collective-permute-start(f32[2,128,128]{2,1,0:T(8,128)S(1)} %convolution_add_fusion.1), channel_id=1, source_target_pairs={{0,3},{1,2},{2,1},{3,0},{4,7},{5,6},{6,5},{7,4},{8,11},{9,10},{10,... | collective-permute-start | bytes 393224 | tf_op jit(solution)/shard_map/ppermute | solution.py:23
  171.1 16.9 %collective-permute-start.20 = (f32[1,8,128,128]{3,2,1,0:T(8,128)}, f32[1,8,128,128]{3,2,1,0:T(8,128)S(1)}, u32[]{:S(2)}, u32[]{:S(2)}) collective-permute-start(f32[1,8,128,128]{3,2,1,0:T(8,128)} %get-tuple-element.22), channel_id=1, source_target_pairs={{4,0},{5,1},{6,2},{7,3},{8,4},{9,5},{10,6},{11,7},{12,8},{13,9},{1... | collective-permute-start | bytes 1572872 | tf_op jit(solution)/shard_map/ppermute | solution.py:18
  172.4 26.2 %collective-permute-start.25 = (f32[1,8,128,128]{3,2,1,0:T(8,128)}, f32[1,8,128,128]{3,2,1,0:T(8,128)S(1)}, u32[]{:S(2)}, u32[]{:S(2)}) collective-permute-start(f32[1,8,128,128]{3,2,1,0:T(8,128)} %get-tuple-element.21), channel_id=1, source_target_pairs={{4,0},{5,1},{6,2},{7,3},{8,4},{9,5},{10,6},{11,7},{12,8},{13,9},{1... | collective-permute-start | bytes 1572872 | tf_op jit(solution)/shard_map/ppermute | solution.py:18
  174.8 2.9 %collective-permute-start.16 = (f32[2,128,128]{2,1,0:T(8,128)S(1)}, f32[2,128,128]{2,1,0:T(8,128)S(1)}, u32[]{:S(2)}, u32[]{:S(2)}) collective-permute-start(f32[2,128,128]{2,1,0:T(8,128)S(1)} %convolution_add_fusion), channel_id=1, source_target_pairs={{0,1},{1,0},{2,3},{3,2},{4,5},{5,4},{6,7},{7,6},{8,9},{9,8},{10,11... | collective-permute-start | bytes 393224 | tf_op jit(solution)/shard_map/ppermute | solution.py:23
  174.9 8.1 %collective-permute-start.17 = (f32[2,128,128]{2,1,0:T(8,128)S(1)}, f32[2,128,128]{2,1,0:T(8,128)S(1)}, u32[]{:S(2)}, u32[]{:S(2)}) collective-permute-start(f32[2,128,128]{2,1,0:T(8,128)S(1)} %convolution_add_fusion), channel_id=1, source_target_pairs={{0,2},{1,3},{2,0},{3,1},{4,6},{5,7},{6,4},{7,5},{8,10},{9,11},{10,... | collective-permute-start | bytes 393224 | tf_op jit(solution)/shard_map/ppermute | solution.py:23
  175.4 11.5 %collective-permute-start.18 = (f32[2,128,128]{2,1,0:T(8,128)S(1)}, f32[2,128,128]{2,1,0:T(8,128)S(1)}, u32[]{:S(2)}, u32[]{:S(2)}) collective-permute-start(f32[2,128,128]{2,1,0:T(8,128)S(1)} %convolution_add_fusion), channel_id=1, source_target_pairs={{0,3},{1,2},{2,1},{3,0},{4,7},{5,6},{6,5},{7,4},{8,11},{9,10},{10,... | collective-permute-start | bytes 393224 | tf_op jit(solution)/shard_map/ppermute | solution.py:23
  177.7 35.2 %collective-permute-start.24 = (f32[1,8,128,128]{3,2,1,0:T(8,128)S(1)}, f32[1,8,128,128]{3,2,1,0:T(8,128)S(1)}, u32[]{:S(2)}, u32[]{:S(2)}) collective-permute-start(f32[1,8,128,128]{3,2,1,0:T(8,128)S(1)} %get-tuple-element.29), channel_id=1, source_target_pairs={{0,4},{1,5},{2,6},{3,7},{4,8},{5,9},{6,10},{7,11},{8,12},{9,13},{1... | collective-permute-start | bytes 1572872 | tf_op jit(solution)/shard_map/ppermute | solution.py:18
  183.0 22.9 %collective-permute-start.19 = (f32[1,8,128,128]{3,2,1,0:T(8,128)S(1)}, f32[1,8,128,128]{3,2,1,0:T(8,128)S(1)}, u32[]{:S(2)}, u32[]{:S(2)}) collective-permute-start(f32[1,8,128,128]{3,2,1,0:T(8,128)S(1)} %get-tuple-element.30), channel_id=1, source_target_pairs={{0,4},{1,5},{2,6},{3,7},{4,8},{5,9},{6,10},{7,11},{8,12},{9,13},{1... | collective-permute-start | bytes 1572872 | tf_op jit(solution)/shard_map/ppermute | solution.py:18
  210.1 8.2 %collective-permute-start.21 = (f32[1,128,128]{2,1,0:T(8,128)S(1)}, f32[1,128,128]{2,1,0:T(8,128)S(1)}, u32[]{:S(2)}, u32[]{:S(2)}) collective-permute-start(f32[1,128,128]{2,1,0:T(8,128)S(1)} %fusion.5), channel_id=1, source_target_pairs={{0,1},{1,0},{2,3},{3,2},{4,5},{5,4},{6,7},{7,6},{8,9},{9,8},{10,11... | collective-permute-start | bytes 196616 | tf_op jit(solution)/shard_map/ppermute | solution.py:23
  210.2 9.2 %collective-permute-start.22 = (f32[1,128,128]{2,1,0:T(8,128)S(1)}, f32[1,128,128]{2,1,0:T(8,128)S(1)}, u32[]{:S(2)}, u32[]{:S(2)}) collective-permute-start(f32[1,128,128]{2,1,0:T(8,128)S(1)} %fusion.5), channel_id=1, source_target_pairs={{0,2},{1,3},{2,0},{3,1},{4,6},{5,7},{6,4},{7,5},{8,10},{9,11},{10,... | collective-permute-start | bytes 196616 | tf_op jit(solution)/shard_map/ppermute | solution.py:23
  210.8 8.6 %collective-permute-start.23 = (f32[1,128,128]{2,1,0:T(8,128)S(1)}, f32[1,128,128]{2,1,0:T(8,128)S(1)}, u32[]{:S(2)}, u32[]{:S(2)}) collective-permute-start(f32[1,128,128]{2,1,0:T(8,128)S(1)} %fusion.5), channel_id=1, source_target_pairs={{0,3},{1,2},{2,1},{3,0},{4,7},{5,6},{6,5},{7,4},{8,11},{9,10},{10,... | collective-permute-start | bytes 196616 | tf_op jit(solution)/shard_map/ppermute | solution.py:23
  217.4 2.0 collective-permute-start.26
  217.8 4.9 %collective-permute-start.27 = (f32[1,128,128]{2,1,0:T(8,128)S(1)}, f32[1,128,128]{2,1,0:T(8,128)S(1)}, u32[]{:S(2)}, u32[]{:S(2)}) collective-permute-start(f32[1,128,128]{2,1,0:T(8,128)S(1)} %fusion.6), channel_id=1, source_target_pairs={{0,2},{1,3},{2,0},{3,1},{4,6},{5,7},{6,4},{7,5},{8,10},{9,11},{10,... | collective-permute-start | bytes 196616 | tf_op jit(solution)/shard_map/ppermute | solution.py:23
  218.4 4.4 %collective-permute-start.28 = (f32[1,128,128]{2,1,0:T(8,128)S(1)}, f32[1,128,128]{2,1,0:T(8,128)S(1)}, u32[]{:S(2)}, u32[]{:S(2)}) collective-permute-start(f32[1,128,128]{2,1,0:T(8,128)S(1)} %fusion.6), channel_id=1, source_target_pairs={{0,3},{1,2},{2,1},{3,0},{4,7},{5,6},{6,5},{7,4},{8,11},{9,10},{10,... | collective-permute-start | bytes 196616 | tf_op jit(solution)/shard_map/ppermute | solution.py:23
  246.8 5.8 %collective-permute-start.30 = (f32[]{:T(128)}, f32[]{:T(128)}, u32[]{:S(2)}, u32[]{:S(2)}) collective-permute-start(f32[]{:T(128)} %add.271), channel_id=1, source_target_pairs={{0,2},{1,3},{2,0},{3,1},{4,6},{5,7},{6,4},{7,5},{8,10},{9,11},{10,... | collective-permute-start | bytes 20 | tf_op jit(solution)/shard_map/ppermute | solution.py:23
  249.6 3.1 %collective-permute-start.31 = (f32[]{:T(128)}, f32[]{:T(128)}, u32[]{:S(2)}, u32[]{:S(2)}) collective-permute-start(f32[]{:T(128)} %add.271), channel_id=1, source_target_pairs={{0,3},{1,2},{2,1},{3,0},{4,7},{5,6},{6,5},{7,4},{8,11},{9,10},{10,... | collective-permute-start | bytes 20 | tf_op jit(solution)/shard_map/ppermute | solution.py:23
  250.9 1.1 collective-permute-start.29
  (31 other events, 333.2 us)
where the time goes:
time: 261 us; the launch traced here: 259 us
  waiting for transfers between devices  63.4 us (24%)
  between operations  56.7 us (22%)
  starting transfers between devices  51.1 us (20%)
  matrix products  41.4 us (16%)
  other arithmetic  25.9 us (10%)
  local copies, waits for them, and re-layouts  20.2 us (8%)
    ppermute x12, waiting for transfers between devices, shift(): return lax.ppermute(block, 'sites', route)  59.8 us
    ppermute x12, starting transfers between devices, shift(): return lax.ppermute(block, 'sites', route)  34.4 us
    ppermute x20, starting transfers between devices, partner(): return lax.ppermute(block, 'sites', route)  16.7 us
    another operation x6, local copies, waits for them, and re-layouts, pick(): jnp.stack([lax.dynamic_index_in_dim(env, order[j], 1, False) for j in ran...  10.9 us
    dot_general x7, matrix products, inward(): jnp.einsum('sil,slm->sim', jnp.einsum('sij,sjl->sil', a, block, precision...  9.1 us
    dot_general x5, matrix products, weighted(): mixed = jnp.einsum('mn,snij->smij', bond, env_right, precision=HIGHEST)  6.87 us
    dot_general x5, matrix products, on_device(): core = jnp.einsum('smil,smlk->sik', temp, mixed, precision=HIGH)  6.57 us
    another operation x6, other arithmetic, pick(): jnp.stack([lax.dynamic_index_in_dim(env, order[j], 1, False) for j in ran...  6.43 us
  transfers between devices with their start and end apart: 32, of which 9 were waited for; matrix products, arithmetic and copies ran while one was open for 20% of the time, Pallas kernels for 0%

commit v1 on v0

v1 whole, which is shorter than its diff:
```python
import functools
import math

import jax
import jax.numpy as jnp
from jax import lax
from jax.experimental import pallas as pl
from jax.experimental.pallas import tpu as pltpu
from jax.sharding import PartitionSpec as P

GROUP = 4
VMEM_LIMIT = 48 * 1024 * 1024

HIGHEST = lax.Precision.HIGHEST


def shift(block, distance):
    devices = range(lax.axis_size("sites"))
    route = [(i - distance, i) for i in devices if i - distance in devices]
    return lax.ppermute(block, "sites", route)


def partner(block, mask):
    route = [(i, i ^ mask) for i in range(lax.axis_size("sites"))]
    return lax.ppermute(block, "sites", route)


def inverse(row):
    labels = jnp.arange(row.shape[0], dtype=jnp.int32)
    return jnp.sum(jnp.where(row[None, :] == labels[:, None], labels[None, :], 0), axis=1)


def row_of(table, index):
    return lax.dynamic_index_in_dim(table, jnp.clip(index, 0, table.shape[0] - 1), 0, False)


def halves(value):
    high = value.astype(jnp.bfloat16)
    return high, (value - high.astype(jnp.float32)).astype(jnp.bfloat16)


def split_left(value):
    return jnp.concatenate(halves(value), axis=1)


def split_right(value):
    high, low = halves(value)
    return jnp.concatenate(
        [
            jnp.concatenate([high, low], axis=1),
            jnp.concatenate([high, jnp.zeros_like(low)], axis=1),
        ],
        axis=0,
    )


def fold(wide):
    half = wide.shape[1] // 2
    return wide[:, :half] + wide[:, half:]


def product(left, right):
    return fold(jnp.dot(split_left(left), split_right(right), preferred_element_type=jnp.float32))


def core_of(env_split, mixed_split, middle_split, terms):
    size = mixed_split.shape[0] // terms
    temp = fold(jnp.dot(env_split, middle_split, preferred_element_type=jnp.float32))
    high, low = halves(temp)
    wide = lambda part: jnp.concatenate(
        [part[m * size : (m + 1) * size] for m in range(terms)], axis=1
    )
    out = jnp.dot(
        jnp.concatenate([wide(high), wide(low)], axis=0),
        mixed_split,
        preferred_element_type=jnp.float32,
    )
    return fold(out[:size]) + out[size:, :size]


def prepare_kernel(own, table, pieces, vec_out, middle_out, left_out, right_out, back_out):
    total, size = vec_out.shape[0], vec_out.shape[1]
    row = lax.broadcasted_iota(jnp.int32, (size, size), 0)
    col = lax.broadcasted_iota(jnp.int32, (size, size), 1)
    eye = (row == col).astype(jnp.float32)
    member = table[2]

    def block(sector, kind):
        return pieces[(sector // own) ^ member, sector % own, kind]

    square = jnp.zeros((size, size), jnp.float32)
    for j in range(total):
        value = block(jnp.int32(j), 0)
        square = square + value * value
    norm = jnp.sqrt(jnp.sum(square))

    def body(j, carry):
        vec = block(j, 0) / norm
        left = jnp.where(table[0] == 1, eye, block(table[3 + j], 1))
        right = jnp.where(table[1] == 1, eye, block(table[3 + total + j], 2))
        vec_out[j] = vec
        left_out[j] = split_left(left)
        right_out[j] = split_right(right)
        back_out[j, 0] = jnp.transpose(left)
        back_out[j, 1] = jnp.transpose(right)
        middle_out[j] = split_right(product(product(left, vec), right))
        return carry

    lax.fori_loop(0, total, body, 0)


def first_kernel(
    own, table, bond, left_got, left_own, right_got, right_own, middle, vec, back, onsite,
    env_out, mixed_out, part_out,
):
    step = pl.program_id(0)
    terms, size = left_got.shape[0], left_got.shape[-1]
    first, last, member = table[0] == 1, table[1] == 1, table[2]

    def store_left(ref):
        for m in range(terms):
            env_out[0, m * size : (m + 1) * size] = split_left(ref[m, 0])

    def store_right(ref):
        for m in range(terms):
            total = bond[m, 0] * ref[0, 0]
            for k in range(1, terms):
                total = total + bond[m, k] * ref[k, 0]
            mixed_out[0, m * size : (m + 1) * size] = split_left(total)

    pl.when(first)(lambda: store_left(left_own))
    pl.when(jnp.logical_not(first))(lambda: store_left(left_got))
    pl.when(last)(lambda: store_right(right_own))
    pl.when(jnp.logical_not(last))(lambda: store_right(right_got))
    core = core_of(env_out[0], mixed_out[0], middle[0], terms)
    part = product(product(back[0, 0], core), back[0, 1])
    mine = (step // own == member).astype(jnp.float32)
    part_out[0] = part + (mine * onsite[0]) * vec[0]


def second_kernel(
    own, table, part0, part1, part2, part3, vec, left, right, onsite, env_hbm, mixed_hbm,
    second_out, share_out, env, mixed, middle, work, sems,
):
    total, size = vec.shape[0], vec.shape[1]
    terms = mixed.shape[1] // size
    member = table[2]

    def copies(j):
        return (
            pltpu.make_async_copy(env_hbm.at[j], env.at[j], sems.at[0, j]),
            pltpu.make_async_copy(mixed_hbm.at[j], mixed.at[j], sems.at[1, j]),
        )

    for j in range(total):
        for copy in copies(j):
            copy.start()

    dot = jnp.zeros((size, size), jnp.float32)
    for j in range(total):
        image = (part0[j] + part1[j]) + (part2[j] + part3[j])
        work[j] = image
        dot = dot + vec[j] * image
    alpha1 = jnp.sum(dot)
    square = jnp.zeros((size, size), jnp.float32)
    for j in range(total):
        resid = work[j] - alpha1 * vec[j]
        work[j] = resid
        square = square + resid * resid
    beta = jnp.sqrt(jnp.full((8, 128), jnp.sum(square) + 1e-06, jnp.float32))
    scale = 1.0 / beta[0:1, :]

    def inward(j, carry):
        value = work[j] * scale
        work[j] = value
        temp = fold(jnp.dot(left[j], split_right(value), preferred_element_type=jnp.float32))
        moved = fold(
            jnp.dot(split_left(temp), right[j], preferred_element_type=jnp.float32)
        )
        middle[j] = moved
        return carry

    lax.fori_loop(0, total, inward, 0)

    def outward(j, carry):
        for copy in copies(j):
            copy.wait()
        value = middle[j]
        core = core_of(env[j], mixed[j], split_right(value), terms)
        return carry + value * core

    share = lax.fori_loop(0, total, outward, jnp.zeros((size, size), jnp.float32))
    for i in range(own):
        mine = work[member * own + i]
        second_out[i] = mine
        share = share + (onsite[i] * mine) * mine
    share_out[0] = jnp.full((8, 128), jnp.sum(share), jnp.float32)
    share_out[1] = jnp.full((8, 128), alpha1, jnp.float32)
    share_out[2] = beta


def final_kernel(own, count, table, share0, share1, share2, share3, vec, second, out, energy_out):
    member = table[2]
    alpha2 = (share0[0] + share1[0]) + (share2[0] + share3[0])
    alpha1, beta = share0[1], share0[2]
    energy = (alpha1 + alpha2) / 2.0 - jnp.sqrt(((alpha1 - alpha2) / 2.0) ** 2 + beta * beta)
    height = jnp.sqrt(beta * beta + (energy - alpha1) ** 2)
    scale = math.sqrt(count)
    weight1 = (scale * (beta / height))[0:1]
    weight2 = (scale * ((energy - alpha1) / height))[0:1]
    for i in range(own):
        out[i] = weight1 * vec[member * own + i] + weight2 * second[i]
    energy_out[...] = energy


def on_device(
    state, left_tensor, right_tensor, onsite, left_env, right_env, mpo_bond, sectors, flow
):
    position = lax.axis_index("sites")
    partition = position // GROUP
    member = position % GROUP
    first = partition == 0
    last = partition == lax.axis_size("sites") // GROUP - 1
    own, size = state.shape[0], state.shape[1]
    terms, total = left_env.shape[0], left_env.shape[1]
    f32, bf16 = jnp.float32, jnp.bfloat16

    bond_rows = jnp.pad(mpo_bond, ((0, 0), (0, size - mpo_bond.shape[1])))
    note = lambda tensor: jnp.concatenate([tensor.reshape(own * size, size), bond_rows], 0)
    from_left = shift(note(left_tensor), GROUP)
    from_right = shift(note(right_tensor), -GROUP)
    left_got = shift(left_env, GROUP)
    right_got = shift(right_env, -GROUP)

    joined = row_of(sectors, partition)
    pos_left = inverse(row_of(flow, partition - 1))
    pos_right = inverse(row_of(flow, partition + 1))[joined]
    as_int = lambda value: jnp.reshape(value.astype(jnp.int32), (1,))
    table = jnp.concatenate(
        [as_int(first), as_int(last), as_int(member), pos_left, pos_right, joined]
    )

    small = jnp.eye(terms, dtype=f32)
    bond_left = jnp.where(first, small, from_left[own * size :, : mpo_bond.shape[1]])
    bond_right = jnp.where(last, small, from_right[own * size :, : mpo_bond.shape[1]])
    bond = jnp.sum(bond_left[:, None, :] * bond_right[None, :, :], axis=2)

    tensors = lambda block: block[: own * size].reshape(own, size, size)
    stacked = jnp.stack([state, tensors(from_left), tensors(from_right)], 1)
    pieces = jnp.stack([stacked] + [partner(stacked, mask) for mask in (1, 2, 3)], 0)

    params = pltpu.CompilerParams(vmem_limit_bytes=VMEM_LIMIT)
    smem = pl.BlockSpec(memory_space=pltpu.SMEM)
    vmem = pl.BlockSpec(memory_space=pltpu.VMEM)
    anywhere = pl.BlockSpec(memory_space=pl.ANY)
    shape = jax.ShapeDtypeStruct

    vec, middle, left, right, back = pl.pallas_call(
        functools.partial(prepare_kernel, own),
        in_specs=[smem, vmem],
        out_specs=[vmem] * 5,
        out_shape=[
            shape((total, size, size), f32),
            shape((total, 2 * size, 2 * size), bf16),
            shape((total, size, 2 * size), bf16),
            shape((total, 2 * size, 2 * size), bf16),
            shape((total, 2, size, size), f32),
        ],
        compiler_params=params,
        name="prepare",
    )(table, pieces)

    env_block = (terms, 1, size, size)
    at_left_got = lambda j, t: (0, jnp.where(t[0] == 1, 0, t[3 + j]), 0, 0)
    at_left_own = lambda j, t: (0, jnp.where(t[0] == 1, j, 0), 0, 0)
    at_right_got = lambda j, t: (0, jnp.where(t[1] == 1, 0, t[3 + total + j]), 0, 0)
    at_right_own = lambda j, t: (0, jnp.where(t[1] == 1, t[3 + 2 * total + j], 0), 0, 0)
    by_sector = lambda *dims: pl.BlockSpec((1, *dims), lambda j, t: (j,) + (0,) * len(dims))
    env, mixed, part = pl.pallas_call(
        functools.partial(first_kernel, own),
        grid_spec=pltpu.PrefetchScalarGridSpec(
            num_scalar_prefetch=1,
            grid=(total,),
            in_specs=[
                smem,
                pl.BlockSpec(env_block, at_left_got),
                pl.BlockSpec(env_block, at_left_own),
                pl.BlockSpec(env_block, at_right_got),
                pl.BlockSpec(env_block, at_right_own),
                by_sector(2 * size, 2 * size),
                by_sector(size, size),
                by_sector(2, size, size),
                pl.BlockSpec((1, size, size), lambda j, t: (j % own, 0, 0)),
            ],
            out_specs=[
                by_sector(terms * size, 2 * size),
                by_sector(terms * size, 2 * size),
                by_sector(size, size),
            ],
        ),
        out_shape=[
            shape((total, terms * size, 2 * size), bf16),
            shape((total, terms * size, 2 * size), bf16),
            shape((total, size, size), f32),
        ],
        compiler_params=params,
        name="first_matvec",
    )(table, bond, left_got, left_env, right_got, right_env, middle, vec, back, onsite)

    parts = [part] + [partner(part, mask) for mask in (1, 2, 3)]
    second, share = pl.pallas_call(
        functools.partial(second_kernel, own),
        in_specs=[smem] + [vmem] * 8 + [anywhere] * 2,
        out_specs=[vmem] * 2,
        out_shape=[shape((own, size, size), f32), shape((3, 8, 128), f32)],
        scratch_shapes=[
            pltpu.VMEM((total, terms * size, 2 * size), bf16),
            pltpu.VMEM((total, terms * size, 2 * size), bf16),
            pltpu.VMEM((total, size, size), f32),
            pltpu.VMEM((total, size, size), f32),
            pltpu.SemaphoreType.DMA((2, total)),
        ],
        compiler_params=params,
        name="second_matvec",
    )(table, *parts, vec, left, right, onsite, env, mixed)

    shares = [share] + [partner(share[:1], mask) for mask in (1, 2, 3)]
    new_state, energy = pl.pallas_call(
        functools.partial(final_kernel, own, total * size * size),
        in_specs=[smem] + [vmem] * 6,
        out_specs=[vmem] * 2,
        out_shape=[shape((own, size, size), f32), shape((8, 128), f32)],
        compiler_params=params,
        name="ritz_update",
    )(table, *shares, vec, second)
    return (new_state, energy[0, :1])


def solution(mesh):
    return jax.shard_map(
        on_device,
        mesh=mesh,
        in_specs=(
            P(("groups", "sites"), None, None),
            P(("groups", "sites"), None, None),
            P(("groups", "sites"), None, None),
            P(("groups", "sites"), None, None),
            P(("groups", "sites"), None, None, None),
            P(("groups", "sites"), None, None, None),
            P(("groups", "sites"), None),
            P("groups", None),
            P("groups", None),
        ),
        out_specs=(P(("groups", "sites"), None, None), P(("groups", "sites"))),
        check_vma=False,
    )
```

time: 261 us -> 179 us (0.69)
  waiting for transfers between devices: 63.4 us -> 126 us
  between operations: 56.7 us -> 0.81 us
  matrix products: 41.4 us -> 0 us
  starting transfers between devices: 51.1 us -> 20.7 us
  Pallas kernels: 0 us -> 26.7 us
  other arithmetic: 25.9 us -> 2.24 us
  local copies, waits for them, and re-layouts: 20.2 us -> 2.71 us
    dot_general x40 -> x0, matrix products: 41.4 us -> none  [the longest x7 9.1 us: inward(): jnp.einsum('sil,slm->sim', jnp.einsum('sij,sjl->sil', a, block, precision...]
    ppermute x20 -> x9, waiting for transfers between devices: 3.59 us -> 40 us  [partner(): return lax.ppermute(block, 'sites', route)]
    pallas_call x0 -> x4, Pallas kernels: none -> 26.7 us  [the longest x1 13.5 us: on_device(): pl.pallas_call(functools.partial(first_kernel, own), grid_spec=pltpu.Pref...]
    ppermute x12 -> x4, waiting for transfers between devices: 59.8 us -> 85.7 us  [shift(): return lax.ppermute(block, 'sites', route)]
    ppermute x12 -> x4, starting transfers between devices: 34.4 us -> 14.1 us  [shift(): return lax.ppermute(block, 'sites', route)]
    another operation x6 -> x0, local copies, waits for them, and re-layouts: 10.9 us -> none  [pick(): jnp.stack([lax.dynamic_index_in_dim(env, order[j], 1, False) for j in ran...]
    ppermute x20 -> x9, starting transfers between devices: 16.7 us -> 6.54 us  [partner(): return lax.ppermute(block, 'sites', route)]
    another operation x8 -> x2, other arithmetic: 7.77 us -> 0.21 us  [on_device(): jnp.stack([stacked] + [partner(stacked, mask) for mask in (1, 2, 3)], 0)]
  transfers between devices with their start and end apart: 32 -> 13, of which waited for: 9 -> 8; matrix products, arithmetic and copies ran while one was open for 20% -> 2% of each run, Pallas kernels for 0% -> 2%
where the time goes in v1:
time: 179 us
  waiting for transfers between devices  126 us (70%)
  Pallas kernels  26.7 us (15%)
  starting transfers between devices  20.7 us (12%)
  local copies, waits for them, and re-layouts  2.71 us (2%)
  other arithmetic  2.24 us (1%)
    ppermute x4, waiting for transfers between devices, shift(): return lax.ppermute(block, 'sites', route)  85.7 us
    ppermute x9, waiting for transfers between devices, partner(): return lax.ppermute(block, 'sites', route)  40 us
    ppermute x4, starting transfers between devices, shift(): return lax.ppermute(block, 'sites', route)  14.1 us
    pallas_call x1, Pallas kernels, on_device(): pl.pallas_call(functools.partial(first_kernel, own), grid_spec=pltpu.Pref...  13.5 us
    pallas_call x1, Pallas kernels, on_device(): pl.pallas_call(functools.partial(second_kernel, own), in_specs=[smem] + [...  8.54 us
    ppermute x9, starting transfers between devices, partner(): return lax.ppermute(block, 'sites', route)  6.54 us
  transfers between devices with their start and end apart: 13, of which 8 were waited for; matrix products, arithmetic and copies ran while one was open for 2% of the time, Pallas kernels for 2%

profile of v1, /device:TPU:0, one launch (start us, length us, event | category | flops | bytes accessed | tf_op | source)
XLA Modules:
  0.0 178.9 jit_solution(5172850873761524937)
XLA Ops:
  0.6 7.0 %collective-permute-start.2 = (f32[8,8,128,128]{3,2,1,0:T(8,128)}, f32[8,8,128,128]{3,2,1,0:T(8,128)}, u32[]{:S(2)}, u32[]{:S(2)}) collective-permute-start(f32[8,8,128,128]{3,2,1,0:T(8,128)} %left_own.1), channel_id=1, source_target_pairs={{0,4},{1,5},{2,6},{3,7},{4,8},{5,9},{6,10},{7,11},{8,12},{9,13},{1... | collective-permute-start | bytes 12582920 | tf_op jit(solution)/shard_map/ppermute | solution.py:20
  7.7 1.3 collective-permute-start.3
  8.9 1.0 fusion
  10.0 4.6 %collective-permute-start = (f32[264,128]{1,0:T(8,128)S(1)}, f32[264,128]{1,0:T(8,128)S(1)}, u32[]{:S(2)}, u32[]{:S(2)}) collective-permute-start(f32[264,128]{1,0:T(8,128)S(1)} %get-tuple-element.28), channel_id=1, source_target_pairs={{0,4},{1,5},{2,6},{3,7},{4,8},{5,9},{6,10},{7,11},{8,12},{9,13},{1... | collective-permute-start | bytes 405512 | tf_op jit(solution)/shard_map/ppermute | solution.py:20
  14.5 1.3 collective-permute-start.1
  15.8 0.7 fusion.4
  16.5 0.8 fusion.3
  17.3 0.1 select_reduce_fusion
  17.4 0.7 fusion.5
  18.1 0.6 gather_fusion
  18.8 0.1 select_reduce_fusion.1
  18.9 79.7 %collective-permute-done = f32[264,128]{1,0:T(8,128)S(1)} collective-permute-done((f32[264,128]{1,0:T(8,128)S(1)}, f32[264,128]{1,0:T(8,128)S(1)}, u32[]{:S(2)}, u32[]{:S(2)}) %collective-permute-start) | collective-permute-done | bytes 135200 | tf_op jit(solution)/shard_map/ppermute | solution.py:20
  98.6 6.0 %collective-permute-done.1 = f32[264,128]{1,0:T(8,128)S(1)} collective-permute-done((f32[264,128]{1,0:T(8,128)S(1)}, f32[264,128]{1,0:T(8,128)S(1)}, u32[]{:S(2)}, u32[]{:S(2)}) %collective-permute-start.1) | collective-permute-done | bytes 135200 | tf_op jit(solution)/shard_map/ppermute | solution.py:20
  104.8 1.6 collective-permute-start.5
  106.4 0.6 collective-permute-start.6
  107.0 0.1 multiply_reduce_fusion.bond
  107.1 9.8 %collective-permute-done.5 = f32[2,3,128,128]{3,2,1,0:T(8,128)S(1)} collective-permute-done((f32[2,3,128,128]{3,2,1,0:T(8,128)S(1)}, f32[2,3,128,128]{3,2,1,0:T(8,128)S(1)}, u32[]{:S(2)}, u32[]{:S(2)}) %collective-permute-start.5) | collective-permute-done | bytes 393248 | tf_op jit(solution)/shard_map/ppermute | solution.py:25
  116.9 5.2 %collective-permute-done.6 = f32[2,3,128,128]{3,2,1,0:T(8,128)S(1)} collective-permute-done((f32[2,3,128,128]{3,2,1,0:T(8,128)S(1)}, f32[2,3,128,128]{3,2,1,0:T(8,128)S(1)}, u32[]{:S(2)}, u32[]{:S(2)}) %collective-permute-start.6) | collective-permute-done | bytes 393248 | tf_op jit(solution)/shard_map/ppermute | solution.py:25
  122.1 0.1 pad_maximum_fusion.pieces
  122.2 3.3 %prepare.1 = (f32[8,128,128]{2,1,0:T(8,128)S(1)}, bf16[8,256,256]{2,1,0:T(8,128)(2,1)S(1)}, bf16[8,128,256]{2,1,0:T(8,128)(2,1)S(1)}, bf16[8,256,256]{2,1,0:T(8,128)(2,1)S(1)}, f32[8,2,128,128]{3,2,1,0:T(8,128)S(1)}) custom-call(s32[27]{0:T(128)S(1)} %concatenate.9.table, f32[4,2,3,128,128]{4,3,2,1,0:T(8,128)S(1)} %pad_maximum_fusion.pieces), custom_call_target="tpu_custom_call" | custom-call | tf_op jit(solution)/shard_map/prepare/pallas_call | solution.py:258
  125.6 13.5 %first_matvec.1 = (bf16[8,1024,256]{2,1,0:T(8,128)(2,1)}, bf16[8,1024,256]{2,1,0:T(8,128)(2,1)}, f32[8,128,128]{2,1,0:T(8,128)S(1)}) custom-call(s32[27]{0:T(128)S(1)} %concatenate.9.table, f32[8,8]{1,0:T(8,128)S(1)} %multiply_reduce_fusion.bond, f32[8,8,128,128]{3,2,1,0:T(8,128)} %collective-permute-done.2.left_got, f32[8,8,128,128]{3,2,1,0:T(8,128)} %left_own.1, ...), custom_call_target="tpu_custom_call" | custom-call | tf_op jit(solution)/shard_map/first_matvec/pallas_call | solution.py:279
  139.2 1.9 %collective-permute-start.9 = (f32[8,128,128]{2,1,0:T(8,128)S(1)}, f32[8,128,128]{2,1,0:T(8,128)S(1)}, u32[]{:S(2)}, u32[]{:S(2)}) collective-permute-start(f32[8,128,128]{2,1,0:T(8,128)S(1)} %get-tuple-element.17.part0), channel_id=1, source_target_pairs={{0,3},{1,2},{2,1},{3,0},{4,7},{5,6},{6,5},{7,4},{8,11},{9,10},{10,... | collective-permute-start | bytes 1572872 | tf_op jit(solution)/shard_map/ppermute | solution.py:25
  141.1 0.5 collective-permute-start.8
  141.6 11.9 %collective-permute-done.9.part3 = f32[8,128,128]{2,1,0:T(8,128)S(1)} collective-permute-done((f32[8,128,128]{2,1,0:T(8,128)S(1)}, f32[8,128,128]{2,1,0:T(8,128)S(1)}, u32[]{:S(2)}, u32[]{:S(2)}) %collective-permute-start.9) | collective-permute-done | bytes 524320 | tf_op jit(solution)/shard_map/ppermute | solution.py:25
  153.4 11.3 %collective-permute-done.8.part2 = f32[8,128,128]{2,1,0:T(8,128)S(1)} collective-permute-done((f32[8,128,128]{2,1,0:T(8,128)S(1)}, f32[8,128,128]{2,1,0:T(8,128)S(1)}, u32[]{:S(2)}, u32[]{:S(2)}) %collective-permute-start.8) | collective-permute-done | bytes 524320 | tf_op jit(solution)/shard_map/ppermute | solution.py:25
  164.8 8.5 %second_matvec.1 = (f32[2,128,128]{2,1,0:T(8,128)S(1)}, f32[3,8,128]{2,1,0:T(8,128)S(1)}) custom-call(s32[27]{0:T(128)S(1)} %concatenate.9.table, f32[8,128,128]{2,1,0:T(8,128)S(1)} %get-tuple-element.17.part0, f32[8,128,128]{2,1,0:T(8,128)S(1)} %collective-permute-done.7.part1, f32[8,128,128]{2,1,0:T(8,128)S(1)} %collective-permute-done.8.part2, ...), custom_call_target="tpu_custom_call" | custom-call | tf_op jit(solution)/shard_map/second_matvec/pallas_call | solution.py:311
  173.4 1.0 collective-permute-start.11
  174.4 0.9 collective-permute-start.10
  175.3 1.2 collective-permute-done.12.share3
  176.4 0.7 collective-permute-done.11.share2
  177.1 1.2 ritz_update.1
  178.3 0.5 slice.25
  (20 shorter events, 0.3 us)
Async XLA Ops:
  0.6 104.1 %copy-start.1 = (f32[2,128,128]{2,1,0:T(8,128)S(1)}, f32[2,128,128]{2,1,0:T(8,128)}, u32[]{:S(2)}) copy-start(f32[2,128,128]{2,1,0:T(8,128)} %param.9) | copy-start | bytes 393220
  0.6 124.9 %collective-permute-start.2 = (f32[8,8,128,128]{3,2,1,0:T(8,128)}, f32[8,8,128,128]{3,2,1,0:T(8,128)}, u32[]{:S(2)}, u32[]{:S(2)}) collective-permute-start(f32[8,8,128,128]{3,2,1,0:T(8,128)} %left_own.1), channel_id=1, source_target_pairs={{0,4},{1,5},{2,6},{3,7},{4,8},{5,9},{6,10},{7,11},{8,12},{9,13},{1... | collective-permute-start | bytes 12582920 | tf_op jit(solution)/shard_map/ppermute | solution.py:20
  7.7 117.9 %collective-permute-start.3 = (f32[8,8,128,128]{3,2,1,0:T(8,128)}, f32[8,8,128,128]{3,2,1,0:T(8,128)}, u32[]{:S(2)}, u32[]{:S(2)}) collective-permute-start(f32[8,8,128,128]{3,2,1,0:T(8,128)} %right_own.1), channel_id=1, source_target_pairs={{4,0},{5,1},{6,2},{7,3},{8,4},{9,5},{10,6},{11,7},{12,8},{13,9},{1... | collective-permute-start | bytes 12582920 | tf_op jit(solution)/shard_map/ppermute | solution.py:20
  10.0 88.7 %collective-permute-start = (f32[264,128]{1,0:T(8,128)S(1)}, f32[264,128]{1,0:T(8,128)S(1)}, u32[]{:S(2)}, u32[]{:S(2)}) collective-permute-start(f32[264,128]{1,0:T(8,128)S(1)} %get-tuple-element.28), channel_id=1, source_target_pairs={{0,4},{1,5},{2,6},{3,7},{4,8},{5,9},{6,10},{7,11},{8,12},{9,13},{1... | collective-permute-start | bytes 405512 | tf_op jit(solution)/shard_map/ppermute | solution.py:20
  14.5 90.2 %collective-permute-start.1 = (f32[264,128]{1,0:T(8,128)S(1)}, f32[264,128]{1,0:T(8,128)S(1)}, u32[]{:S(2)}, u32[]{:S(2)}) collective-permute-start(f32[264,128]{1,0:T(8,128)S(1)} %get-tuple-element.29), channel_id=1, source_target_pairs={{4,0},{5,1},{6,2},{7,3},{8,4},{9,5},{10,6},{11,7},{12,8},{13,9},{1... | collective-permute-start | bytes 405512 | tf_op jit(solution)/shard_map/ppermute | solution.py:20
  104.8 12.1 %collective-permute-start.5 = (f32[2,3,128,128]{3,2,1,0:T(8,128)S(1)}, f32[2,3,128,128]{3,2,1,0:T(8,128)S(1)}, u32[]{:S(2)}, u32[]{:S(2)}) collective-permute-start(f32[2,3,128,128]{3,2,1,0:T(8,128)S(1)} %get-tuple-element.27), channel_id=1, source_target_pairs={{0,2},{1,3},{2,0},{3,1},{4,6},{5,7},{6,4},{7,5},{8,10},{9,11},{10,... | collective-permute-start | bytes 1179656 | tf_op jit(solution)/shard_map/ppermute | solution.py:25
  106.4 10.5 %collective-permute-start.4 = (f32[2,3,128,128]{3,2,1,0:T(8,128)S(1)}, f32[2,3,128,128]{3,2,1,0:T(8,128)S(1)}, u32[]{:S(2)}, u32[]{:S(2)}) collective-permute-start(f32[2,3,128,128]{3,2,1,0:T(8,128)S(1)} %get-tuple-element.27), channel_id=1, source_target_pairs={{0,1},{1,0},{2,3},{3,2},{4,5},{5,4},{6,7},{7,6},{8,9},{9,8},{10,11... | collective-permute-start | bytes 1179656 | tf_op jit(solution)/shard_map/ppermute | solution.py:25
  106.4 15.7 %collective-permute-start.6 = (f32[2,3,128,128]{3,2,1,0:T(8,128)S(1)}, f32[2,3,128,128]{3,2,1,0:T(8,128)S(1)}, u32[]{:S(2)}, u32[]{:S(2)}) collective-permute-start(f32[2,3,128,128]{3,2,1,0:T(8,128)S(1)} %get-tuple-element.27), channel_id=1, source_target_pairs={{0,3},{1,2},{2,1},{3,0},{4,7},{5,6},{6,5},{7,4},{8,11},{9,10},{10,... | collective-permute-start | bytes 1179656 | tf_op jit(solution)/shard_map/ppermute | solution.py:25
  122.2 3.4 %copy-start = (f32[2,128,128]{2,1,0:T(8,128)S(1)}, f32[2,128,128]{2,1,0:T(8,128)}, u32[]{:S(2)}) copy-start(f32[2,128,128]{2,1,0:T(8,128)} %onsite.3) | copy-start | bytes 393220
  139.2 14.3 %collective-permute-start.9 = (f32[8,128,128]{2,1,0:T(8,128)S(1)}, f32[8,128,128]{2,1,0:T(8,128)S(1)}, u32[]{:S(2)}, u32[]{:S(2)}) collective-permute-start(f32[8,128,128]{2,1,0:T(8,128)S(1)} %get-tuple-element.17.part0), channel_id=1, source_target_pairs={{0,3},{1,2},{2,1},{3,0},{4,7},{5,6},{6,5},{7,4},{8,11},{9,10},{10,... | collective-permute-start | bytes 1572872 | tf_op jit(solution)/shard_map/ppermute | solution.py:25
  141.1 23.7 %collective-permute-start.8 = (f32[8,128,128]{2,1,0:T(8,128)S(1)}, f32[8,128,128]{2,1,0:T(8,128)S(1)}, u32[]{:S(2)}, u32[]{:S(2)}) collective-permute-start(f32[8,128,128]{2,1,0:T(8,128)S(1)} %get-tuple-element.17.part0), channel_id=1, source_target_pairs={{0,2},{1,3},{2,0},{3,1},{4,6},{5,7},{6,4},{7,5},{8,10},{9,11},{10,... | collective-permute-start | bytes 1572872 | tf_op jit(solution)/shard_map/ppermute | solution.py:25
  141.6 23.2 %collective-permute-start.7 = (f32[8,128,128]{2,1,0:T(8,128)S(1)}, f32[8,128,128]{2,1,0:T(8,128)S(1)}, u32[]{:S(2)}, u32[]{:S(2)}) collective-permute-start(f32[8,128,128]{2,1,0:T(8,128)S(1)} %get-tuple-element.17.part0), channel_id=1, source_target_pairs={{0,1},{1,0},{2,3},{3,2},{4,5},{5,4},{6,7},{7,6},{8,9},{9,8},{10,11... | collective-permute-start | bytes 1572872 | tf_op jit(solution)/shard_map/ppermute | solution.py:25
  173.3 3.1 %collective-permute-start.12 = (f32[1,8,128]{2,1,0:T(8,128)S(1)}, f32[1,8,128]{2,1,0:T(8,128)S(1)}, u32[]{:S(2)}, u32[]{:S(2)}) collective-permute-start(f32[1,8,128]{2,1,0:T(8,128)S(1)} %slice.24), channel_id=1, source_target_pairs={{0,3},{1,2},{2,1},{3,0},{4,7},{5,6},{6,5},{7,4},{8,11},{9,10},{10,... | collective-permute-start | bytes 12296 | tf_op jit(solution)/shard_map/ppermute | solution.py:25
  173.4 3.7 %collective-permute-start.11 = (f32[1,8,128]{2,1,0:T(8,128)S(1)}, f32[1,8,128]{2,1,0:T(8,128)S(1)}, u32[]{:S(2)}, u32[]{:S(2)}) collective-permute-start(f32[1,8,128]{2,1,0:T(8,128)S(1)} %slice.24), channel_id=1, source_target_pairs={{0,2},{1,3},{2,0},{3,1},{4,6},{5,7},{6,4},{7,5},{8,10},{9,11},{10,... | collective-permute-start | bytes 12296 | tf_op jit(solution)/shard_map/ppermute | solution.py:25
  174.4 2.7 %collective-permute-start.10 = (f32[1,8,128]{2,1,0:T(8,128)S(1)}, f32[1,8,128]{2,1,0:T(8,128)S(1)}, u32[]{:S(2)}, u32[]{:S(2)}) collective-permute-start(f32[1,8,128]{2,1,0:T(8,128)S(1)} %slice.24), channel_id=1, source_target_pairs={{0,1},{1,0},{2,3},{3,2},{4,5},{5,4},{6,7},{7,6},{8,9},{9,8},{10,11... | collective-permute-start | bytes 12296 | tf_op jit(solution)/shard_map/ppermute | solution.py:25

commit v2 on v1

v2 whole, which is shorter than its diff:
```python
import functools
import math

import jax
import jax.numpy as jnp
from jax import lax
from jax.experimental import pallas as pl
from jax.experimental.pallas import tpu as pltpu
from jax.sharding import PartitionSpec as P

GROUP = 4
CHUNKS = (4, 3, 1)
MIB = 1024 * 1024


def shift(block, distance):
    devices = range(lax.axis_size("sites"))
    route = [(i - distance, i) for i in devices if i - distance in devices]
    return lax.ppermute(block, "sites", route)


def partner(block, mask):
    route = [(i, i ^ mask) for i in range(lax.axis_size("sites"))]
    return lax.ppermute(block, "sites", route)


def gather(block):
    across = partner(block, 2)
    beside = partner(jnp.stack([block, across], 0), 1)
    return jnp.stack([block, beside[0], across, beside[1]], 0)


def total_of(block):
    pair = block + partner(block, 1)
    return pair + partner(pair, 2)


def halves(value):
    high = value.astype(jnp.bfloat16)
    return high, (value - high.astype(jnp.float32)).astype(jnp.bfloat16)


def split_left(value):
    return jnp.concatenate(halves(value), axis=1)


def split_right(value):
    high, low = halves(value)
    return jnp.concatenate(
        [
            jnp.concatenate([high, low], axis=1),
            jnp.concatenate([high, jnp.zeros_like(low)], axis=1),
        ],
        axis=0,
    )


def fold(wide):
    half = wide.shape[1] // 2
    return wide[:, :half] + wide[:, half:]


def product(left, right):
    return fold(jnp.dot(split_left(left), split_right(right), preferred_element_type=jnp.float32))


def core_of(env_split, mixed_split, middle_split, terms):
    size = mixed_split.shape[0] // terms
    temp = fold(jnp.dot(env_split, middle_split, preferred_element_type=jnp.float32))
    high, low = halves(temp)
    wide = lambda part: jnp.concatenate(
        [part[m * size : (m + 1) * size] for m in range(terms)], axis=1
    )
    out = jnp.dot(
        jnp.concatenate([wide(high), wide(low)], axis=0),
        mixed_split,
        preferred_element_type=jnp.float32,
    )
    return fold(out[:size]) + out[size:, :size]


def pick(table, left_env, right_env, to_right, to_left, sems, begin, width):
    terms, total, size = left_env.shape[:3]
    first, last = table[0] == 1, table[1] == 1

    def copies(side, env, base, out):
        return [
            pltpu.make_async_copy(
                env.at[:, begin + s if base is None else table[base + begin + s]],
                out.at[pl.ds(s * terms * size, terms * size)].reshape(terms, size, size),
                sems.at[side, begin + s],
            )
            for s in range(width)
        ]

    def start(flag, usual, edge):
        pl.when(jnp.logical_not(flag))(lambda: [copy.start() for copy in usual] and None)
        pl.when(flag)(lambda: [copy.start() for copy in edge] and None)

    right = copies(0, left_env, 3 + 3 * total, to_right)
    left = copies(1, right_env, 3 + 4 * total, to_left)
    start(last, right, copies(0, right_env, 3 + 2 * total, to_right))
    start(first, left, copies(1, left_env, None, to_left))
    return right + left


def open_kernel(
    chunks, parts, place_hbm, sectors_hbm, flow_hbm, bond_hbm, left_tensor, right_tensor,
    left_env, right_env, table, *refs,
):
    outs, refs = refs[: 2 * len(chunks)], refs[2 * len(chunks) :]
    place, sectors, flow, order, bond, small, sems, more, some = refs
    own, size = left_tensor.shape[0], left_tensor.shape[1]
    terms, total = left_env.shape[0], left_env.shape[1]
    width = chunks[0]
    base = width * terms * size
    copies = [
        pltpu.make_async_copy(tensor.at[i], out.at[pl.ds(base + i * size, size)], more.at[side, i])
        for side, (tensor, out) in enumerate(((left_tensor, outs[0]), (right_tensor, outs[1])))
        for i in range(own)
    ]
    inputs = ((place_hbm, place), (sectors_hbm, sectors), (flow_hbm, flow), (bond_hbm, bond))
    loads = [pltpu.make_async_copy(a, b, some.at[i]) for i, (a, b) in enumerate(inputs)]
    for copy in loads + copies:
        copy.start()
    for copy in loads:
        copy.wait()
    partition = place[0] // GROUP
    before = jnp.maximum(partition - 1, 0)
    after = jnp.minimum(partition + 1, parts - 1)
    table[0] = (partition == 0).astype(jnp.int32)
    table[1] = (partition == parts - 1).astype(jnp.int32)
    table[2] = place[0] % GROUP
    for j in range(total):
        order[flow[before, j]] = j
        order[total + flow[partition, j]] = j
        order[2 * total + flow[after, j]] = j
    for j in range(total):
        joined = sectors[partition, j]
        table[3 + j] = order[j]
        table[3 + total + j] = order[2 * total + joined]
        table[3 + 2 * total + j] = joined
        table[3 + 3 * total + j] = order[total + j]
        table[3 + 4 * total + j] = order[total + sectors[before, j]]
    begin = 0
    for c, count in enumerate(chunks):
        copies += pick(
            table, left_env, right_env, outs[2 * c], outs[2 * c + 1], sems, begin, count
        )
        begin += count
    small[...] = jnp.zeros_like(small)
    small[:, : bond.shape[1]] = bond[...]
    for side in range(2):
        copy = pltpu.make_async_copy(
            small, outs[side].at[pl.ds(base + own * size, terms)], more.at[side, own]
        )
        copy.start()
        copies.append(copy)
    for copy in copies:
        copy.wait()


def prepare_kernel(own, table, states, pieces, vec_out, middle_out, left_out, right_out, back_out):
    total, size = vec_out.shape[0], vec_out.shape[1]
    row = lax.broadcasted_iota(jnp.int32, (size, size), 0)
    col = lax.broadcasted_iota(jnp.int32, (size, size), 1)
    eye = (row == col).astype(jnp.float32)
    member = table[2]

    def block(sector, kind):
        return pieces[(sector // own) ^ member, sector % own, kind]

    def state_of(sector):
        return states[(sector // own) ^ member, sector % own]

    square = jnp.zeros((size, size), jnp.float32)
    for j in range(total):
        value = state_of(j)
        square = square + value * value
    norm = jnp.sqrt(jnp.sum(square))

    def body(j, carry):
        vec = state_of(j) / norm
        left = jnp.where(table[0] == 1, eye, block(table[3 + j], 0))
        right = jnp.where(table[1] == 1, eye, block(table[3 + total + j], 1))
        vec_out[j] = vec
        left_out[j] = split_left(left)
        right_out[j] = split_right(right)
        back_out[j, 0] = jnp.transpose(left)
        back_out[j, 1] = jnp.transpose(right)
        middle_out[j] = split_right(product(product(left, vec), right))
        return carry

    lax.fori_loop(0, total, body, 0)


def first_kernel(
    own, begin, table, bond, left_got, left_own, right_got, right_own, middle, vec, back, onsite,
    env_out, mixed_out, part_out,
):
    size = vec.shape[-1]
    terms = bond.shape[0]
    first, last, member = table[0] == 1, table[1] == 1, table[2]
    rows = lambda s, m: slice((s * terms + m) * size, (s * terms + m + 1) * size)

    for s in range(part_out.shape[0]):
        for m in range(terms):
            block = jnp.where(first, left_own[rows(s, m)], left_got[rows(s, m)])
            env_out[s, rows(0, m)] = split_left(block)
        blocks = [jnp.where(last, right_own[rows(s, m)], right_got[rows(s, m)]) for m in range(terms)]
        for m in range(terms):
            total = bond[m, 0] * blocks[0]
            for k in range(1, terms):
                total = total + bond[m, k] * blocks[k]
            mixed_out[s, rows(0, m)] = split_left(total)
        j = begin + s
        core = core_of(env_out[s], mixed_out[s], middle[j], terms)
        part = product(product(back[j, 0], core), back[j, 1])
        mine = (j // own == member).astype(jnp.float32)
        part_out[s] = part + (mine * onsite[j % own]) * vec[j]


def second_kernel(own, early, table, image, part0, part1, part2, part3, *refs):
    vec, left, right, onsite, *refs = refs
    count = len(CHUNKS)
    env_parts, mixed_parts, refs = refs[:count], refs[count : 2 * count], refs[2 * count :]
    second_out, share_out, work, middle = refs
    total, size = vec.shape[0], vec.shape[1]
    terms = mixed_parts[0].shape[1] // size
    member = table[2]
    home = [(c, s) for c, width in enumerate(CHUNKS) for s in range(width)]

    dot = jnp.zeros((size, size), jnp.float32)
    for j in range(total):
        if j < early:
            value = image[j]
        else:
            i = j - early
            value = (part0[i] + part1[i]) + (part2[i] + part3[i])
        work[j] = value
        dot = dot + vec[j] * value
    alpha1 = jnp.sum(dot)
    square = jnp.zeros((size, size), jnp.float32)
    for j in range(total):
        resid = work[j] - alpha1 * vec[j]
        work[j] = resid
        square = square + resid * resid
    beta = jnp.sqrt(jnp.full((8, 128), jnp.sum(square) + 1e-06, jnp.float32))
    scale = 1.0 / beta[0:1, :]

    for j in range(total):
        value = work[j] * scale
        work[j] = value
        temp = fold(jnp.dot(left[j], split_right(value), preferred_element_type=jnp.float32))
        middle[j] = fold(
            jnp.dot(split_left(temp), right[j], preferred_element_type=jnp.float32)
        )

    share = jnp.zeros((size, size), jnp.float32)
    for j, (c, s) in enumerate(home):
        value = middle[j]
        core = core_of(env_parts[c][s], mixed_parts[c][s], split_right(value), terms)
        share = share + value * core
    for i in range(own):
        mine = work[member * own + i]
        second_out[i] = mine
        share = share + (onsite[i] * mine) * mine
    share_out[0] = jnp.full((8, 128), jnp.sum(share), jnp.float32)
    share_out[1] = jnp.full((8, 128), alpha1, jnp.float32)
    share_out[2] = beta


def final_kernel(own, count, table, share0, share1, share2, share3, vec, second, out, energy_out):
    member = table[2]
    alpha2 = (share0[0] + share1[0]) + (share2[0] + share3[0])
    alpha1, beta = share0[1], share0[2]
    energy = (alpha1 + alpha2) / 2.0 - jnp.sqrt(((alpha1 - alpha2) / 2.0) ** 2 + beta * beta)
    height = jnp.sqrt(beta * beta + (energy - alpha1) ** 2)
    scale = math.sqrt(count)
    weight1 = (scale * (beta / height))[0:1]
    weight2 = (scale * ((energy - alpha1) / height))[0:1]
    for i in range(own):
        out[i] = weight1 * vec[member * own + i] + weight2 * second[i]
    energy_out[0] = energy[0, 0]


def on_device(
    state, left_tensor, right_tensor, onsite, left_env, right_env, mpo_bond, sectors, flow
):
    position = lax.axis_index("sites")
    parts = lax.axis_size("sites") // GROUP
    own, size = state.shape[0], state.shape[1]
    terms, total = left_env.shape[0], left_env.shape[1]
    f32, bf16 = jnp.float32, jnp.bfloat16
    begins = [sum(CHUNKS[:c]) for c in range(len(CHUNKS))]
    early = begins[-1]

    smem = pl.BlockSpec(memory_space=pltpu.SMEM)
    vmem = pl.BlockSpec(memory_space=pltpu.VMEM)
    hbm = pl.BlockSpec(memory_space=pltpu.HBM)
    shape = jax.ShapeDtypeStruct
    dma = pltpu.SemaphoreType.DMA
    params = lambda mib: pltpu.CompilerParams(vmem_limit_bytes=mib * MIB)

    small_cost = pl.CostEstimate(flops=1, bytes_accessed=1, transcendentals=0)

    rows = lambda width: width * terms * size
    chunk = lambda c: (rows(CHUNKS[c]) + (own * size + terms if c == 0 else 0), size)
    pair = lambda sent: (shift(sent[0], GROUP), shift(sent[1], -GROUP))
    table, *opened = pl.pallas_call(
        functools.partial(open_kernel, CHUNKS, parts),
        in_specs=[hbm] * 8,
        out_specs=[smem] + [vmem] * (2 * len(CHUNKS)),
        out_shape=[shape((3 + 5 * total,), jnp.int32)]
        + [pltpu.VMEM(chunk(c), f32) for c in range(len(CHUNKS)) for _ in range(2)],
        scratch_shapes=[
            pltpu.SMEM((1,), jnp.int32),
            pltpu.SMEM(sectors.shape, jnp.int32),
            pltpu.SMEM(flow.shape, jnp.int32),
            pltpu.SMEM((3 * total,), jnp.int32),
            pltpu.VMEM(mpo_bond.shape, f32),
            pltpu.VMEM((terms, size), f32),
            dma((2, total)),
            dma((2, own + 1)),
            dma((4,)),
        ],
        cost_estimate=small_cost,
        compiler_params=params(16),
        name="open",
    )(
        *(
            pltpu.with_memory_space_constraint(value, pltpu.HBM)
            for value in (
                jnp.reshape(position, (1,)).astype(jnp.int32), sectors, flow, mpo_bond,
                left_tensor, right_tensor, left_env, right_env,
            )
        )
    )
    sent, got = [], []
    for c in range(len(CHUNKS)):
        buffers = tuple(opened[2 * c : 2 * c + 2])
        sent.append(buffers)
        got.append(pair(buffers))
    states = gather(state)

    from_left, from_right = (block[rows(CHUNKS[0]) :] for block in got[0])
    small = jnp.eye(terms, dtype=f32)
    bond_left = jnp.where(table[0] == 1, small, from_left[own * size :, : mpo_bond.shape[1]])
    bond_right = jnp.where(table[1] == 1, small, from_right[own * size :, : mpo_bond.shape[1]])
    bond = jnp.sum(bond_left[:, None, :] * bond_right[None, :, :], axis=2)
    tensors = lambda block: block[: own * size].reshape(own, size, size)
    pieces = gather(jnp.stack([tensors(from_left), tensors(from_right)], 1))

    vec, middle, left, right, back = pl.pallas_call(
        functools.partial(prepare_kernel, own),
        in_specs=[smem, vmem, vmem],
        out_specs=[vmem] * 5,
        out_shape=[
            shape((total, size, size), f32),
            shape((total, 2 * size, 2 * size), bf16),
            shape((total, size, 2 * size), bf16),
            shape((total, 2 * size, 2 * size), bf16),
            shape((total, 2, size, size), f32),
        ],
        cost_estimate=small_cost,
        compiler_params=params(12),
        name="prepare",
    )(table, states, pieces)

    envs, mixeds, sums = [], [], []
    for c, (begin, width) in enumerate(zip(begins, CHUNKS)):
        if c > 0:
            got[c], _ = lax.optimization_barrier((got[c], sums[c - 1]))
        env, mixed, part = pl.pallas_call(
            functools.partial(first_kernel, own, begin),
            in_specs=[smem, smem] + [vmem] * 8,
            out_specs=[vmem] * 3,
            out_shape=[
                shape((width, rows(1), 2 * size), bf16),
                shape((width, rows(1), 2 * size), bf16),
                shape((width, size, size), f32),
            ],
            cost_estimate=small_cost,
        compiler_params=params(12),
            name=f"first_matvec{c}",
        )(table, bond, got[c][0], sent[c][1], got[c][1], sent[c][0], middle, vec, back, onsite)
        envs.append(env)
        mixeds.append(mixed)
        if c < len(CHUNKS) - 1:
            sums.append(total_of(part))

    image = jnp.concatenate(sums, 0)
    parts = [part] + [partner(part, mask) for mask in (1, 2, 3)]
    second, share = pl.pallas_call(
        functools.partial(second_kernel, own, early),
        in_specs=[smem] + [vmem] * (9 + 2 * len(CHUNKS)),
        out_specs=[vmem] * 2,
        out_shape=[shape((own, size, size), f32), shape((3, 8, 128), f32)],
        scratch_shapes=[
            pltpu.VMEM((total, size, size), f32),
            pltpu.VMEM((total, size, size), f32),
        ],
        cost_estimate=small_cost,
        compiler_params=params(20),
        name="second_matvec",
    )(table, image, *parts, vec, left, right, onsite, *envs, *mixeds)

    shares = [share] + [partner(share[:1], mask) for mask in (1, 2, 3)]
    new_state, energy = pl.pallas_call(
        functools.partial(final_kernel, own, total * size * size),
        in_specs=[smem] + [vmem] * 6,
        out_specs=[vmem, smem],
        out_shape=[shape((own, size, size), f32), shape((1,), f32)],
        cost_estimate=small_cost,
        compiler_params=params(4),
        name="ritz_update",
    )(table, *shares, vec, second)
    return (new_state, energy)


def solution(mesh):
    return jax.shard_map(
        on_device,
        mesh=mesh,
        in_specs=(
            P(("groups", "sites"), None, None),
            P(("groups", "sites"), None, None),
            P(("groups", "sites"), None, None),
            P(("groups", "sites"), None, None),
            P(("groups", "sites"), None, None, None),
            P(("groups", "sites"), None, None, None),
            P(("groups", "sites"), None),
            P("groups", None),
            P("groups", None),
        ),
        out_specs=(P(("groups", "sites"), None, None), P(("groups", "sites"))),
        check_vma=False,
    )
```

time: 179 us -> 128 us (0.72)
  waiting for transfers between devices: 126 us -> 73.2 us
  starting transfers between devices: 20.7 us -> 27.6 us
  Pallas kernels: 26.7 us -> 23.1 us
  local copies, waits for them, and re-layouts: 2.71 us -> 0.67 us
    ppermute x4 -> x6, waiting for transfers between devices: 85.7 us -> 48.2 us  [shift(): return lax.ppermute(block, 'sites', route)]
    ppermute x9 -> x14, waiting for transfers between devices: 40 us -> 24.9 us  [partner(): return lax.ppermute(block, 'sites', route)]
    ppermute x9 -> x14, starting transfers between devices: 6.54 us -> 10.6 us  [partner(): return lax.ppermute(block, 'sites', route)]
    pallas_call x2 -> x5, Pallas kernels: 22.1 us -> 18.5 us  [the longest x3 9.36 us: on_device(): pl.pallas_call(functools.partial(first_kernel, own, begin), in_specs=[sme...]
    ppermute x4 -> x6, starting transfers between devices: 14.1 us -> 17 us  [shift(): return lax.ppermute(block, 'sites', route)]
  transfers between devices with their start and end apart: 13 -> 20, of which waited for: 8 -> 15; matrix products, arithmetic and copies ran while one was open for 2% -> 1% of each run, Pallas kernels for 2% -> 9%
where the time goes in v2:
time: 128 us; the launch traced here: 127 us
  waiting for transfers between devices  73.2 us (57%)
  starting transfers between devices  27.6 us (22%)
  Pallas kernels  23.1 us (18%)
  between operations  2.38 us (2%)
    ppermute x6, waiting for transfers between devices, shift(): return lax.ppermute(block, 'sites', route)  48.2 us
    ppermute x14, waiting for transfers between devices, partner(): return lax.ppermute(block, 'sites', route)  24.9 us
    ppermute x6, starting transfers between devices, shift(): return lax.ppermute(block, 'sites', route)  17 us
    ppermute x14, starting transfers between devices, partner(): return lax.ppermute(block, 'sites', route)  10.6 us
    pallas_call x3, Pallas kernels, on_device(): pl.pallas_call(functools.partial(first_kernel, own, begin), in_specs=[sme...  9.36 us
    pallas_call x1, Pallas kernels, on_device(): pl.pallas_call(functools.partial(open_kernel, CHUNKS, parts), in_specs=[h...  5.28 us
    pallas_call x1, Pallas kernels, on_device(): pl.pallas_call(functools.partial(second_kernel, own, early), in_specs=[sm...  3.91 us
    pallas_call x1, Pallas kernels, on_device(): pl.pallas_call(functools.partial(prepare_kernel, own), in_specs=[smem, vm...  3.33 us
  transfers between devices with their start and end apart: 20, of which 15 were waited for; matrix products, arithmetic and copies ran while one was open for 1% of the time, Pallas kernels for 9%

profile of v2, /device:TPU:0, one launch (start us, length us, event | category | flops | bytes accessed | tf_op | source)
XLA Modules:
  0.0 127.4 jit_solution(1442129232480103857)
XLA Ops:
  0.6 5.3 %open.1 = (s32[43]{0:T(128)S(1)}, f32[4360,128]{1,0:T(8,128)S(1)}, f32[4360,128]{1,0:T(8,128)S(1)}, f32[3072,128]{1,0:T(8,128)S(1)}, f32[3072,128]{1,0:T(8,128)S...) custom-call(s32[1]{0:T(128)} %bitcast.place_hbm, s32[4,8]{1,0:T(4,128)} %sectors_hbm.1, s32[4,8]{1,0:T(4,128)} %flow_hbm.1, ...), custom_call_target="tpu_custom_call" | custom-call | flops 1 | bytes 1 | tf_op jit(solution)/shard_map/open/pallas_call | solution.py:310
  5.9 4.9 %collective-permute-start = (f32[4360,128]{1,0:T(8,128)S(1)}, f32[4360,128]{1,0:T(8,128)S(1)}, u32[]{:S(2)}, u32[]{:S(2)}) collective-permute-start(f32[4360,128]{1,0:T(8,128)S(1)} %get-tuple-element.30.right_own), channel_id=1, source_target_pairs={{0,4},{1,5},{2,6},{3,7},{4,8},{5,9},{6,10},{7,11},{8,12},{9,13},{1... | collective-permute-start | bytes 6696968 | tf_op jit(solution)/shard_map/ppermute | solution.py:19
  10.9 1.3 %collective-permute-start.1 = (f32[4360,128]{1,0:T(8,128)S(1)}, f32[4360,128]{1,0:T(8,128)S(1)}, u32[]{:S(2)}, u32[]{:S(2)}) collective-permute-start(f32[4360,128]{1,0:T(8,128)S(1)} %get-tuple-element.31.left_own), channel_id=1, source_target_pairs={{4,0},{5,1},{6,2},{7,3},{8,4},{9,5},{10,6},{11,7},{12,8},{13,9},{1... | collective-permute-start | bytes 6696968 | tf_op jit(solution)/shard_map/ppermute | solution.py:19
  12.2 1.6 %collective-permute-start.2 = (f32[2,128,128]{2,1,0:T(8,128)S(1)}, f32[2,128,128]{2,1,0:T(8,128)S(1)}, u32[]{:S(2)}, u32[]{:S(2)}) collective-permute-start(f32[2,128,128]{2,1,0:T(8,128)S(1)} %copy-done.1), channel_id=1, source_target_pairs={{0,2},{1,3},{2,0},{3,1},{4,6},{5,7},{6,4},{7,5},{8,10},{9,11},{10,... | collective-permute-start | bytes 393224 | tf_op jit(solution)/shard_map/ppermute | solution.py:24
  13.8 3.4 %collective-permute-done.2 = f32[2,128,128]{2,1,0:T(8,128)S(1)} collective-permute-done((f32[2,128,128]{2,1,0:T(8,128)S(1)}, f32[2,128,128]{2,1,0:T(8,128)S(1)}, u32[]{:S(2)}, u32[]{:S(2)}) %collective-permute-start.2) | collective-permute-done | bytes 131104 | tf_op jit(solution)/shard_map/ppermute | solution.py:24
  17.3 4.6 %collective-permute-start.8 = (f32[3072,128]{1,0:T(8,128)S(1)}, f32[3072,128]{1,0:T(8,128)S(1)}, u32[]{:S(2)}, u32[]{:S(2)}) collective-permute-start(f32[3072,128]{1,0:T(8,128)S(1)} %get-tuple-element.36.right_own), channel_id=1, source_target_pairs={{0,4},{1,5},{2,6},{3,7},{4,8},{5,9},{6,10},{7,11},{8,12},{9,13},{1... | collective-permute-start | bytes 4718600 | tf_op jit(solution)/shard_map/ppermute | solution.py:19
  22.0 1.3 %collective-permute-start.9 = (f32[3072,128]{1,0:T(8,128)S(1)}, f32[3072,128]{1,0:T(8,128)S(1)}, u32[]{:S(2)}, u32[]{:S(2)}) collective-permute-start(f32[3072,128]{1,0:T(8,128)S(1)} %get-tuple-element.37.left_own), channel_id=1, source_target_pairs={{4,0},{5,1},{6,2},{7,3},{8,4},{9,5},{10,6},{11,7},{12,8},{13,9},{1... | collective-permute-start | bytes 4718600 | tf_op jit(solution)/shard_map/ppermute | solution.py:19
  23.3 36.4 %collective-permute-done.left_got = f32[4360,128]{1,0:T(8,128)S(1)} collective-permute-done((f32[4360,128]{1,0:T(8,128)S(1)}, f32[4360,128]{1,0:T(8,128)S(1)}, u32[]{:S(2)}, u32[]{:S(2)}) %collective-permute-start) | collective-permute-done | bytes 2232352 | tf_op jit(solution)/shard_map/ppermute | solution.py:19
  59.7 4.6 %collective-permute-done.1.right_got = f32[4360,128]{1,0:T(8,128)S(1)} collective-permute-done((f32[4360,128]{1,0:T(8,128)S(1)}, f32[4360,128]{1,0:T(8,128)S(1)}, u32[]{:S(2)}, u32[]{:S(2)}) %collective-permute-start.1) | collective-permute-done | bytes 2232352 | tf_op jit(solution)/shard_map/ppermute | solution.py:19
  64.3 1.6 %collective-permute-start.4 = (f32[2,2,128,128]{3,2,1,0:T(8,128)S(1)}, f32[2,2,128,128]{3,2,1,0:T(8,128)S(1)}, u32[]{:S(2)}, u32[]{:S(2)}) collective-permute-start(f32[2,2,128,128]{3,2,1,0:T(8,128)S(1)} %get-tuple-element.59), channel_id=1, source_target_pairs={{0,2},{1,3},{2,0},{3,1},{4,6},{5,7},{6,4},{7,5},{8,10},{9,11},{10,... | collective-permute-start | bytes 786440 | tf_op jit(solution)/shard_map/ppermute | solution.py:24
  67.8 2.9 %collective-permute-done.4 = f32[2,2,128,128]{3,2,1,0:T(8,128)S(1)} collective-permute-done((f32[2,2,128,128]{3,2,1,0:T(8,128)S(1)}, f32[2,2,128,128]{3,2,1,0:T(8,128)S(1)}, u32[]{:S(2)}, u32[]{:S(2)}) %collective-permute-start.4) | collective-permute-done | bytes 262176 | tf_op jit(solution)/shard_map/ppermute | solution.py:24
  70.9 1.8 %collective-permute-done.5 = f32[2,2,2,128,128]{4,3,2,1,0:T(8,128)S(1)} collective-permute-done((f32[2,2,2,128,128]{4,3,2,1,0:T(8,128)S(1)}, f32[2,2,2,128,128]{4,3,2,1,0:T(8,128)S(1)}, u32[]{:S(2)}, u32[]{:S(2)}) %collective-permute-start.5) | collective-permute-done | bytes 524320 | tf_op jit(solution)/shard_map/ppermute | solution.py:24
  72.9 3.3 %prepare.1 = (f32[8,128,128]{2,1,0:T(8,128)S(1)}, bf16[8,256,256]{2,1,0:T(8,128)(2,1)S(1)}, bf16[8,128,256]{2,1,0:T(8,128)(2,1)S(1)}, bf16[8,256,256]{2,1,0:T(8,128)(2,1)S(1)}, f32[8,2,128,128]{3,2,1,0:T(8,128)S(1)}) custom-call(s32[43]{0:T(128)S(1)} %get-tuple-element.29.table, f32[4,2,128,128]{3,2,1,0:T(8,128)S(1)} %pad_maximum_fusion.1.states, ...), custom_call_target="tpu_custom_call" | custom-call | flops 1 | bytes 1 | tf_op jit(solution)/shard_map/prepare/pallas_call | solution.py:354
  76.3 4.3 %first_matvec0.1 = (bf16[4,1024,256]{2,1,0:T(8,128)(2,1)S(1)}, bf16[4,1024,256]{2,1,0:T(8,128)(2,1)S(1)}, f32[4,128,128]{2,1,0:T(8,128)S(1)}) custom-call(s32[43]{0:T(128)S(1)} %get-tuple-element.29.table, f32[8,8]{1,0:T(8,128)S(1)} %multiply_reduce_fusion.bond, f32[4360,128]{1,0:T(8,128)S(1)} %collective-permute-done.left_got, ...), custom_call_target="tpu_custom_call" | custom-call | flops 1 | bytes 1 | tf_op jit(solution)/shard_map/first_matvec0/pallas_call | solution.py:374
  80.8 1.4 %collective-permute-done.6 = f32[4,128,128]{2,1,0:T(8,128)S(1)} collective-permute-done((f32[4,128,128]{2,1,0:T(8,128)S(1)}, f32[4,128,128]{2,1,0:T(8,128)S(1)}, u32[]{:S(2)}, u32[]{:S(2)}) %collective-permute-start.6) | collective-permute-done | bytes 262176 | tf_op jit(solution)/shard_map/ppermute | solution.py:24
  82.2 1.6 %collective-permute-start.7 = (f32[4,128,128]{2,1,0:T(8,128)S(1)}, f32[4,128,128]{2,1,0:T(8,128)S(1)}, u32[]{:S(2)}, u32[]{:S(2)}) collective-permute-start(f32[4,128,128]{2,1,0:T(8,128)S(1)} %add.12), channel_id=1, source_target_pairs={{0,2},{1,3},{2,0},{3,1},{4,6},{5,7},{6,4},{7,5},{8,10},{9,11},{10,... | collective-permute-start | bytes 786440 | tf_op jit(solution)/shard_map/ppermute | solution.py:24
  83.8 3.4 %collective-permute-start.12 = (f32[1024,128]{1,0:T(8,128)S(1)}, f32[1024,128]{1,0:T(8,128)S(1)}, u32[]{:S(2)}, u32[]{:S(2)}) collective-permute-start(f32[1024,128]{1,0:T(8,128)S(1)} %get-tuple-element.41.right_own), channel_id=1, source_target_pairs={{0,4},{1,5},{2,6},{3,7},{4,8},{5,9},{6,10},{7,11},{8,12},{9,13},{1... | collective-permute-start | bytes 1572872 | tf_op jit(solution)/shard_map/ppermute | solution.py:19
  87.2 1.5 %collective-permute-start.13 = (f32[1024,128]{1,0:T(8,128)S(1)}, f32[1024,128]{1,0:T(8,128)S(1)}, u32[]{:S(2)}, u32[]{:S(2)}) collective-permute-start(f32[1024,128]{1,0:T(8,128)S(1)} %get-tuple-element.42.left_own), channel_id=1, source_target_pairs={{4,0},{5,1},{6,2},{7,3},{8,4},{9,5},{10,6},{11,7},{12,8},{13,9},{1... | collective-permute-start | bytes 1572872 | tf_op jit(solution)/shard_map/ppermute | solution.py:19
  88.6 2.0 %collective-permute-done.7 = f32[4,128,128]{2,1,0:T(8,128)S(1)} collective-permute-done((f32[4,128,128]{2,1,0:T(8,128)S(1)}, f32[4,128,128]{2,1,0:T(8,128)S(1)}, u32[]{:S(2)}, u32[]{:S(2)}) %collective-permute-start.7) | collective-permute-done | bytes 262176 | tf_op jit(solution)/shard_map/ppermute | solution.py:24
  90.7 2.7 %collective-permute-done.8.left_got = f32[3072,128]{1,0:T(8,128)S(1)} collective-permute-done((f32[3072,128]{1,0:T(8,128)S(1)}, f32[3072,128]{1,0:T(8,128)S(1)}, u32[]{:S(2)}, u32[]{:S(2)}) %collective-permute-start.8) | collective-permute-done | bytes 1572896 | tf_op jit(solution)/shard_map/ppermute | solution.py:19
  93.4 4.6 %collective-permute-done.9.right_got = f32[3072,128]{1,0:T(8,128)S(1)} collective-permute-done((f32[3072,128]{1,0:T(8,128)S(1)}, f32[3072,128]{1,0:T(8,128)S(1)}, u32[]{:S(2)}, u32[]{:S(2)}) %collective-permute-start.9) | collective-permute-done | bytes 1572896 | tf_op jit(solution)/shard_map/ppermute | solution.py:19
  97.9 3.4 %first_matvec1.1 = (bf16[3,1024,256]{2,1,0:T(8,128)(2,1)S(1)}, bf16[3,1024,256]{2,1,0:T(8,128)(2,1)S(1)}, f32[3,128,128]{2,1,0:T(8,128)S(1)}) custom-call(s32[43]{0:T(128)S(1)} %get-tuple-element.29.table, f32[8,8]{1,0:T(8,128)S(1)} %multiply_reduce_fusion.bond, f32[3072,128]{1,0:T(8,128)S(1)} %collective-permute-done.8.left_got, ...), custom_call_target="tpu_custom_call" | custom-call | flops 1 | bytes 1 | tf_op jit(solution)/shard_map/first_matvec1/pallas_call | solution.py:374
  101.4 1.4 %collective-permute-done.10 = f32[3,128,128]{2,1,0:T(8,128)S(1)} collective-permute-done((f32[3,128,128]{2,1,0:T(8,128)S(1)}, f32[3,128,128]{2,1,0:T(8,128)S(1)}, u32[]{:S(2)}, u32[]{:S(2)}) %collective-permute-start.10) | collective-permute-done | bytes 196640 | tf_op jit(solution)/shard_map/ppermute | solution.py:24
  102.9 1.6 %collective-permute-start.11 = (f32[3,128,128]{2,1,0:T(8,128)S(1)}, f32[3,128,128]{2,1,0:T(8,128)S(1)}, u32[]{:S(2)}, u32[]{:S(2)}) collective-permute-start(f32[3,128,128]{2,1,0:T(8,128)S(1)} %add.14), channel_id=1, source_target_pairs={{0,2},{1,3},{2,0},{3,1},{4,6},{5,7},{6,4},{7,5},{8,10},{9,11},{10,... | collective-permute-start | bytes 589832 | tf_op jit(solution)/shard_map/ppermute | solution.py:24
  104.4 5.4 %collective-permute-done.11 = f32[3,128,128]{2,1,0:T(8,128)S(1)} collective-permute-done((f32[3,128,128]{2,1,0:T(8,128)S(1)}, f32[3,128,128]{2,1,0:T(8,128)S(1)}, u32[]{:S(2)}, u32[]{:S(2)}) %collective-permute-start.11) | collective-permute-done | bytes 196640 | tf_op jit(solution)/shard_map/ppermute | solution.py:24
  109.9 1.7 %first_matvec2.1 = (bf16[1,1024,256]{2,1,0:T(8,128)(2,1)S(1)}, bf16[1,1024,256]{2,1,0:T(8,128)(2,1)S(1)}, f32[1,128,128]{2,1,0:T(8,128)S(1)}) custom-call(s32[43]{0:T(128)S(1)} %get-tuple-element.29.table, f32[8,8]{1,0:T(8,128)S(1)} %multiply_reduce_fusion.bond, f32[1024,128]{1,0:T(8,128)S(1)} %collective-permute-done.12.left_got, ...), custom_call_target="tpu_custom_call" | custom-call | flops 1 | bytes 1 | tf_op jit(solution)/shard_map/first_matvec2/pallas_call | solution.py:374
  111.7 1.6 %collective-permute-start.15 = (f32[1,128,128]{2,1,0:T(8,128)S(1)}, f32[1,128,128]{2,1,0:T(8,128)S(1)}, u32[]{:S(2)}, u32[]{:S(2)}) collective-permute-start(f32[1,128,128]{2,1,0:T(8,128)S(1)} %get-tuple-element.45.part0), channel_id=1, source_target_pairs={{0,2},{1,3},{2,0},{3,1},{4,6},{5,7},{6,4},{7,5},{8,10},{9,11},{10,... | collective-permute-start | bytes 196616 | tf_op jit(solution)/shard_map/ppermute | solution.py:24
  113.6 2.6 %collective-permute-done.15.part2 = f32[1,128,128]{2,1,0:T(8,128)S(1)} collective-permute-done((f32[1,128,128]{2,1,0:T(8,128)S(1)}, f32[1,128,128]{2,1,0:T(8,128)S(1)}, u32[]{:S(2)}, u32[]{:S(2)}) %collective-permute-start.15) | collective-permute-done | bytes 65568 | tf_op jit(solution)/shard_map/ppermute | solution.py:24
  117.3 3.9 %second_matvec.1 = (f32[2,128,128]{2,1,0:T(8,128)S(1)}, f32[3,8,128]{2,1,0:T(8,128)S(1)}) custom-call(s32[43]{0:T(128)S(1)} %get-tuple-element.29.table, f32[7,128,128]{2,1,0:T(8,128)S(1)} %pad_maximum_fusion.3.image, f32[1,128,128]{2,1,0:T(8,128)S(1)} %get-tuple-element.45.part0, f32[1,128,128]{2,1,0:T(8,128)S(1)} %collective-permute-done.14.part1, ...), custom_call_target="tpu_custom_call" | custom-call | flops 1 | bytes 1 | tf_op jit(solution)/shard_map/second_matvec/pallas_call | solution.py:394
  121.5 1.5 %collective-permute-start.18 = (f32[1,8,128]{2,1,0:T(8,128)S(1)}, f32[1,8,128]{2,1,0:T(8,128)S(1)}, u32[]{:S(2)}, u32[]{:S(2)}) collective-permute-start(f32[1,8,128]{2,1,0:T(8,128)S(1)} %slice.51), channel_id=1, source_target_pairs={{0,2},{1,3},{2,0},{3,1},{4,6},{5,7},{6,4},{7,5},{8,10},{9,11},{10,... | collective-permute-start | bytes 12296 | tf_op jit(solution)/shard_map/ppermute | solution.py:24
  123.2 1.9 %collective-permute-done.18.share2 = f32[1,8,128]{2,1,0:T(8,128)S(1)} collective-permute-done((f32[1,8,128]{2,1,0:T(8,128)S(1)}, f32[1,8,128]{2,1,0:T(8,128)S(1)}, u32[]{:S(2)}, u32[]{:S(2)}) %collective-permute-start.18) | collective-permute-done | bytes 4128 | tf_op jit(solution)/shard_map/ppermute | solution.py:24
  126.0 1.3 ritz_update.1
  (38 shorter events, 4.4 us)
Async XLA Ops:
  0.6 11.5 %copy-start.1 = (f32[2,128,128]{2,1,0:T(8,128)S(1)}, f32[2,128,128]{2,1,0:T(8,128)}, u32[]{:S(2)}) copy-start(f32[2,128,128]{2,1,0:T(8,128)} %param.9) | copy-start | bytes 393220
  5.9 53.7 %collective-permute-start = (f32[4360,128]{1,0:T(8,128)S(1)}, f32[4360,128]{1,0:T(8,128)S(1)}, u32[]{:S(2)}, u32[]{:S(2)}) collective-permute-start(f32[4360,128]{1,0:T(8,128)S(1)} %get-tuple-element.30.right_own), channel_id=1, source_target_pairs={{0,4},{1,5},{2,6},{3,7},{4,8},{5,9},{6,10},{7,11},{8,12},{9,13},{1... | collective-permute-start | bytes 6696968 | tf_op jit(solution)/shard_map/ppermute | solution.py:19
  10.9 53.3 %collective-permute-start.1 = (f32[4360,128]{1,0:T(8,128)S(1)}, f32[4360,128]{1,0:T(8,128)S(1)}, u32[]{:S(2)}, u32[]{:S(2)}) collective-permute-start(f32[4360,128]{1,0:T(8,128)S(1)} %get-tuple-element.31.left_own), channel_id=1, source_target_pairs={{4,0},{5,1},{6,2},{7,3},{8,4},{9,5},{10,6},{11,7},{12,8},{13,9},{1... | collective-permute-start | bytes 6696968 | tf_op jit(solution)/shard_map/ppermute | solution.py:19
  12.2 5.0 %collective-permute-start.2 = (f32[2,128,128]{2,1,0:T(8,128)S(1)}, f32[2,128,128]{2,1,0:T(8,128)S(1)}, u32[]{:S(2)}, u32[]{:S(2)}) collective-permute-start(f32[2,128,128]{2,1,0:T(8,128)S(1)} %copy-done.1), channel_id=1, source_target_pairs={{0,2},{1,3},{2,0},{3,1},{4,6},{5,7},{6,4},{7,5},{8,10},{9,11},{10,... | collective-permute-start | bytes 393224 | tf_op jit(solution)/shard_map/ppermute | solution.py:24
  17.2 50.5 %collective-permute-start.3 = (f32[2,2,128,128]{3,2,1,0:T(8,128)S(1)}, f32[2,2,128,128]{3,2,1,0:T(8,128)S(1)}, u32[]{:S(2)}, u32[]{:S(2)}) collective-permute-start(f32[2,2,128,128]{3,2,1,0:T(8,128)S(1)} %pad_maximum_fusion.4), channel_id=1, source_target_pairs={{0,1},{1,0},{2,3},{3,2},{4,5},{5,4},{6,7},{7,6},{8,9},{9,8},{10,11... | collective-permute-start | bytes 786440 | tf_op jit(solution)/shard_map/ppermute | solution.py:24
  17.3 76.0 %collective-permute-start.8 = (f32[3072,128]{1,0:T(8,128)S(1)}, f32[3072,128]{1,0:T(8,128)S(1)}, u32[]{:S(2)}, u32[]{:S(2)}) collective-permute-start(f32[3072,128]{1,0:T(8,128)S(1)} %get-tuple-element.36.right_own), channel_id=1, source_target_pairs={{0,4},{1,5},{2,6},{3,7},{4,8},{5,9},{6,10},{7,11},{8,12},{9,13},{1... | collective-permute-start | bytes 4718600 | tf_op jit(solution)/shard_map/ppermute | solution.py:19
  22.0 76.0 %collective-permute-start.9 = (f32[3072,128]{1,0:T(8,128)S(1)}, f32[3072,128]{1,0:T(8,128)S(1)}, u32[]{:S(2)}, u32[]{:S(2)}) collective-permute-start(f32[3072,128]{1,0:T(8,128)S(1)} %get-tuple-element.37.left_own), channel_id=1, source_target_pairs={{4,0},{5,1},{6,2},{7,3},{8,4},{9,5},{10,6},{11,7},{12,8},{13,9},{1... | collective-permute-start | bytes 4718600 | tf_op jit(solution)/shard_map/ppermute | solution.py:19
  64.3 6.4 %collective-permute-start.4 = (f32[2,2,128,128]{3,2,1,0:T(8,128)S(1)}, f32[2,2,128,128]{3,2,1,0:T(8,128)S(1)}, u32[]{:S(2)}, u32[]{:S(2)}) collective-permute-start(f32[2,2,128,128]{3,2,1,0:T(8,128)S(1)} %get-tuple-element.59), channel_id=1, source_target_pairs={{0,2},{1,3},{2,0},{3,1},{4,6},{5,7},{6,4},{7,5},{8,10},{9,11},{10,... | collective-permute-start | bytes 786440 | tf_op jit(solution)/shard_map/ppermute | solution.py:24
  70.8 2.0 %collective-permute-start.5 = (f32[2,2,2,128,128]{4,3,2,1,0:T(8,128)S(1)}, f32[2,2,2,128,128]{4,3,2,1,0:T(8,128)S(1)}, u32[]{:S(2)}, u32[]{:S(2)}) collective-permute-start(f32[2,2,2,128,128]{4,3,2,1,0:T(8,128)S(1)} %pad_maximum_fusion.2), channel_id=1, source_target_pairs={{0,1},{1,0},{2,3},{3,2},{4,5},{5,4},{6,7},{7,6},{8,9},{9,8},{10,11... | collective-permute-start | bytes 1572872 | tf_op jit(solution)/shard_map/ppermute | solution.py:24
  70.9 5.4 %copy-start = (f32[2,128,128]{2,1,0:T(8,128)S(1)}, f32[2,128,128]{2,1,0:T(8,128)}, u32[]{:S(2)}) copy-start(f32[2,128,128]{2,1,0:T(8,128)} %refs_3_.1) | copy-start | bytes 393220
  80.5 1.6 %collective-permute-start.6 = (f32[4,128,128]{2,1,0:T(8,128)S(1)}, f32[4,128,128]{2,1,0:T(8,128)S(1)}, u32[]{:S(2)}, u32[]{:S(2)}) collective-permute-start(f32[4,128,128]{2,1,0:T(8,128)S(1)} %get-tuple-element.35), channel_id=1, source_target_pairs={{0,1},{1,0},{2,3},{3,2},{4,5},{5,4},{6,7},{7,6},{8,9},{9,8},{10,11... | collective-permute-start | bytes 786440 | tf_op jit(solution)/shard_map/ppermute | solution.py:24
  82.2 8.4 %collective-permute-start.7 = (f32[4,128,128]{2,1,0:T(8,128)S(1)}, f32[4,128,128]{2,1,0:T(8,128)S(1)}, u32[]{:S(2)}, u32[]{:S(2)}) collective-permute-start(f32[4,128,128]{2,1,0:T(8,128)S(1)} %add.12), channel_id=1, source_target_pairs={{0,2},{1,3},{2,0},{3,1},{4,6},{5,7},{6,4},{7,5},{8,10},{9,11},{10,... | collective-permute-start | bytes 786440 | tf_op jit(solution)/shard_map/ppermute | solution.py:24
  83.8 26.1 %collective-permute-start.12 = (f32[1024,128]{1,0:T(8,128)S(1)}, f32[1024,128]{1,0:T(8,128)S(1)}, u32[]{:S(2)}, u32[]{:S(2)}) collective-permute-start(f32[1024,128]{1,0:T(8,128)S(1)} %get-tuple-element.41.right_own), channel_id=1, source_target_pairs={{0,4},{1,5},{2,6},{3,7},{4,8},{5,9},{6,10},{7,11},{8,12},{9,13},{1... | collective-permute-start | bytes 1572872 | tf_op jit(solution)/shard_map/ppermute | solution.py:19
  87.2 22.8 %collective-permute-start.13 = (f32[1024,128]{1,0:T(8,128)S(1)}, f32[1024,128]{1,0:T(8,128)S(1)}, u32[]{:S(2)}, u32[]{:S(2)}) collective-permute-start(f32[1024,128]{1,0:T(8,128)S(1)} %get-tuple-element.42.left_own), channel_id=1, source_target_pairs={{4,0},{5,1},{6,2},{7,3},{8,4},{9,5},{10,6},{11,7},{12,8},{13,9},{1... | collective-permute-start | bytes 1572872 | tf_op jit(solution)/shard_map/ppermute | solution.py:19
  101.3 1.5 %collective-permute-start.10 = (f32[3,128,128]{2,1,0:T(8,128)S(1)}, f32[3,128,128]{2,1,0:T(8,128)S(1)}, u32[]{:S(2)}, u32[]{:S(2)}) collective-permute-start(f32[3,128,128]{2,1,0:T(8,128)S(1)} %get-tuple-element.40), channel_id=1, source_target_pairs={{0,1},{1,0},{2,3},{3,2},{4,5},{5,4},{6,7},{7,6},{8,9},{9,8},{10,11... | collective-permute-start | bytes 589832 | tf_op jit(solution)/shard_map/ppermute | solution.py:24
  102.9 7.0 %collective-permute-start.11 = (f32[3,128,128]{2,1,0:T(8,128)S(1)}, f32[3,128,128]{2,1,0:T(8,128)S(1)}, u32[]{:S(2)}, u32[]{:S(2)}) collective-permute-start(f32[3,128,128]{2,1,0:T(8,128)S(1)} %add.14), channel_id=1, source_target_pairs={{0,2},{1,3},{2,0},{3,1},{4,6},{5,7},{6,4},{7,5},{8,10},{9,11},{10,... | collective-permute-start | bytes 589832 | tf_op jit(solution)/shard_map/ppermute | solution.py:24
  111.6 2.0 %collective-permute-start.14 = (f32[1,128,128]{2,1,0:T(8,128)S(1)}, f32[1,128,128]{2,1,0:T(8,128)S(1)}, u32[]{:S(2)}, u32[]{:S(2)}) collective-permute-start(f32[1,128,128]{2,1,0:T(8,128)S(1)} %get-tuple-element.45.part0), channel_id=1, source_target_pairs={{0,1},{1,0},{2,3},{3,2},{4,5},{5,4},{6,7},{7,6},{8,9},{9,8},{10,11... | collective-permute-start | bytes 196616 | tf_op jit(solution)/shard_map/ppermute | solution.py:24
  111.7 4.5 %collective-permute-start.15 = (f32[1,128,128]{2,1,0:T(8,128)S(1)}, f32[1,128,128]{2,1,0:T(8,128)S(1)}, u32[]{:S(2)}, u32[]{:S(2)}) collective-permute-start(f32[1,128,128]{2,1,0:T(8,128)S(1)} %get-tuple-element.45.part0), channel_id=1, source_target_pairs={{0,2},{1,3},{2,0},{3,1},{4,6},{5,7},{6,4},{7,5},{8,10},{9,11},{10,... | collective-permute-start | bytes 196616 | tf_op jit(solution)/shard_map/ppermute | solution.py:24
  113.3 4.0 %collective-permute-start.16 = (f32[1,128,128]{2,1,0:T(8,128)S(1)}, f32[1,128,128]{2,1,0:T(8,128)S(1)}, u32[]{:S(2)}, u32[]{:S(2)}) collective-permute-start(f32[1,128,128]{2,1,0:T(8,128)S(1)} %get-tuple-element.45.part0), channel_id=1, source_target_pairs={{0,3},{1,2},{2,1},{3,0},{4,7},{5,6},{6,5},{7,4},{8,11},{9,10},{10,... | collective-permute-start | bytes 196616 | tf_op jit(solution)/shard_map/ppermute | solution.py:24
  121.3 1.9 %collective-permute-start.17 = (f32[1,8,128]{2,1,0:T(8,128)S(1)}, f32[1,8,128]{2,1,0:T(8,128)S(1)}, u32[]{:S(2)}, u32[]{:S(2)}) collective-permute-start(f32[1,8,128]{2,1,0:T(8,128)S(1)} %slice.51), channel_id=1, source_target_pairs={{0,1},{1,0},{2,3},{3,2},{4,5},{5,4},{6,7},{7,6},{8,9},{9,8},{10,11... | collective-permute-start | bytes 12296 | tf_op jit(solution)/shard_map/ppermute | solution.py:24
  121.5 3.6 %collective-permute-start.18 = (f32[1,8,128]{2,1,0:T(8,128)S(1)}, f32[1,8,128]{2,1,0:T(8,128)S(1)}, u32[]{:S(2)}, u32[]{:S(2)}) collective-permute-start(f32[1,8,128]{2,1,0:T(8,128)S(1)} %slice.51), channel_id=1, source_target_pairs={{0,2},{1,3},{2,0},{3,1},{4,6},{5,7},{6,4},{7,5},{8,10},{9,11},{10,... | collective-permute-start | bytes 12296 | tf_op jit(solution)/shard_map/ppermute | solution.py:24
  123.0 3.0 %collective-permute-start.19 = (f32[1,8,128]{2,1,0:T(8,128)S(1)}, f32[1,8,128]{2,1,0:T(8,128)S(1)}, u32[]{:S(2)}, u32[]{:S(2)}) collective-permute-start(f32[1,8,128]{2,1,0:T(8,128)S(1)} %slice.51), channel_id=1, source_target_pairs={{0,3},{1,2},{2,1},{3,0},{4,7},{5,6},{6,5},{7,4},{8,11},{9,10},{10,... | collective-permute-start | bytes 12296 | tf_op jit(solution)/shard_map/ppermute | solution.py:24

commit v3 on v2

v3 whole, which is shorter than its diff:
```python
import functools
import math

import jax
import jax.numpy as jnp
from jax import lax
from jax.experimental import pallas as pl
from jax.experimental.pallas import tpu as pltpu
from jax.sharding import PartitionSpec as P

GROUP = 4
CHUNKS = (3, 3, 1, 1)
MIB = 1024 * 1024


def hand_over(block, parity):
    count = lax.axis_size("sites")
    route = [(i, i + (GROUP if i % 2 == parity else -GROUP)) for i in range(count)]
    return lax.ppermute(block, "sites", [(i, j) for i, j in route if 0 <= j < count])


def partner(block, mask):
    route = [(i, i ^ mask) for i in range(lax.axis_size("sites"))]
    return lax.ppermute(block, "sites", route)


def gather(block):
    pieces = [block] + [partner(block, mask) for mask in (1, 2, 3)]
    return jnp.stack(pieces, 0)


def total_of(block):
    pair = block + partner(block, 1)
    return pair + partner(pair, 2)


def halves(value):
    high = value.astype(jnp.bfloat16)
    return high, (value - high.astype(jnp.float32)).astype(jnp.bfloat16)


def split_left(value):
    return jnp.concatenate(halves(value), axis=1)


def split_right(value):
    high, low = halves(value)
    return jnp.concatenate(
        [
            jnp.concatenate([high, low], axis=1),
            jnp.concatenate([high, jnp.zeros_like(low)], axis=1),
        ],
        axis=0,
    )


def fold(wide):
    half = wide.shape[1] // 2
    return wide[:, :half] + wide[:, half:]


def product(left, right):
    return fold(jnp.dot(split_left(left), split_right(right), preferred_element_type=jnp.float32))


def core_of(env_split, mixed_split, middle_split, terms):
    size = mixed_split.shape[0] // terms
    temp = fold(jnp.dot(env_split, middle_split, preferred_element_type=jnp.float32))
    high, low = halves(temp)
    wide = lambda part: jnp.concatenate(
        [part[m * size : (m + 1) * size] for m in range(terms)], axis=1
    )
    out = jnp.dot(
        jnp.concatenate([wide(high), wide(low)], axis=0),
        mixed_split,
        preferred_element_type=jnp.float32,
    )
    return fold(out[:size]) + out[size:, :size]


HEAD = 4


def sector_copy(env, index, out, row, sem):
    terms, _, size, _ = env.shape
    target = out.at[pl.ds(row, terms * size)].reshape(terms, size, size)
    return pltpu.make_async_copy(env.at[:, index], target, sem)


def pick(table, left_env, right_env, outs, sems, begin, chunks):
    terms, total, size = left_env.shape[:3]
    copies = []
    for c, width in enumerate(chunks):
        for side in range(2):
            base = HEAD + (3 + side) * total
            from_left = table[HEAD + 5 * total + side] == 0
            for s in range(width):
                place = (
                    table[base + begin + s], outs[2 * c + side], s * terms * size,
                    sems.at[side, begin + s],
                )
                left, right = sector_copy(left_env, *place), sector_copy(right_env, *place)
                pl.when(from_left)(left.start)
                pl.when(jnp.logical_not(from_left))(right.start)
                copies.append(left)
        begin += width
    return copies


def open_kernel(
    chunks, parts, place_hbm, sectors_hbm, flow_hbm, bond_hbm, left_tensor, right_tensor,
    left_env, right_env, table, *refs,
):
    outs, refs = refs[: 2 * len(chunks)], refs[2 * len(chunks) :]
    place, sectors, flow, order, bond, small, sems, more, some = refs
    own, size = left_tensor.shape[0], left_tensor.shape[1]
    terms, total = left_env.shape[0], left_env.shape[1]
    base = chunks[0] * terms * size
    inputs = ((place_hbm, place), (sectors_hbm, sectors), (flow_hbm, flow), (bond_hbm, bond))
    loads = [pltpu.make_async_copy(a, b, some.at[i]) for i, (a, b) in enumerate(inputs)]
    for copy in loads:
        copy.start()
    for copy in loads:
        copy.wait()
    partition = place[0] // GROUP
    before = jnp.maximum(partition - 1, 0)
    after = jnp.minimum(partition + 1, parts - 1)
    first, last = partition == 0, partition == parts - 1
    swap = place[0] % 2 == 1
    table[0] = first.astype(jnp.int32)
    table[1] = last.astype(jnp.int32)
    table[2] = place[0] % GROUP
    table[3] = swap.astype(jnp.int32)
    for j in range(total):
        order[flow[before, j]] = j
        order[total + flow[partition, j]] = j
        order[2 * total + flow[after, j]] = j
    for j in range(total):
        joined = sectors[partition, j]
        table[HEAD + j] = order[j]
        table[HEAD + total + j] = order[2 * total + joined]
        table[HEAD + 2 * total + j] = joined
        ahead = jnp.where(last, joined, order[total + j])
        behind = jnp.where(first, j, order[total + sectors[before, j]])
        table[HEAD + 3 * total + j] = jnp.where(swap, behind, ahead)
        table[HEAD + 4 * total + j] = jnp.where(swap, ahead, behind)
    ahead, behind = last.astype(jnp.int32), 1 - first.astype(jnp.int32)
    table[HEAD + 5 * total] = jnp.where(swap, behind, ahead)
    table[HEAD + 5 * total + 1] = jnp.where(swap, ahead, behind)
    copies = pick(table, left_env, right_env, outs, sems, 0, chunks)
    small[...] = jnp.zeros_like(small)
    small[:, : bond.shape[1]] = bond[...]
    for side in range(2):
        for i in range(own):
            target = outs[side].at[pl.ds(base + i * size, size)]
            straight = pltpu.make_async_copy(
                (left_tensor, right_tensor)[side].at[i], target, more.at[side, i]
            )
            crossed = pltpu.make_async_copy(
                (right_tensor, left_tensor)[side].at[i], target, more.at[side, i]
            )
            pl.when(jnp.logical_not(swap))(straight.start)
            pl.when(swap)(crossed.start)
            copies.append(straight)
        copy = pltpu.make_async_copy(
            small, outs[side].at[pl.ds(base + own * size, terms)], more.at[side, own]
        )
        copy.start()
        copies.append(copy)
    for copy in copies:
        copy.wait()


def prepare_kernel(
    own, table, states, pieces, vec_out, middle_out, plain_out, left_out, right_out, back_out,
):
    total, size = vec_out.shape[0], vec_out.shape[1]
    row = lax.broadcasted_iota(jnp.int32, (size, size), 0)
    col = lax.broadcasted_iota(jnp.int32, (size, size), 1)
    eye = (row == col).astype(jnp.float32)
    member = table[2]

    def block(sector, kind):
        return pieces[(sector // own) ^ member, sector % own, kind]

    def state_of(sector):
        return states[(sector // own) ^ member, sector % own]

    square = jnp.zeros((size, size), jnp.float32)
    for j in range(total):
        value = state_of(j)
        square = square + value * value
    norm = jnp.sqrt(jnp.sum(square))

    def body(j, carry):
        vec = state_of(j) / norm
        left = jnp.where(table[0] == 1, eye, block(table[HEAD + j], 0))
        right = jnp.where(table[1] == 1, eye, block(table[HEAD + total + j], 1))
        vec_out[j] = vec
        left_out[j] = split_left(left)
        right_out[j] = split_right(right)
        back_out[j, 0] = jnp.transpose(left)
        back_out[j, 1] = jnp.transpose(right)
        middle = product(product(left, vec), right)
        middle_out[j] = split_right(middle)
        plain_out[j] = middle
        return carry

    lax.fori_loop(0, total, body, 0)


def first_kernel(
    own, begin, table, bond, got0, got1, sent0, sent1, middle, vec, back, onsite,
    env_out, mixed_out, part_out,
):
    size = vec.shape[-1]
    terms = bond.shape[0]
    first, last, member, swap = table[0] == 1, table[1] == 1, table[2], table[3] == 1
    rows = lambda s, m: slice((s * terms + m) * size, (s * terms + m + 1) * size)

    def chosen(at, end, sent_a, sent_b, got_a, got_b):
        there = jnp.where(swap, got_b[at], got_a[at])
        return jnp.where(end, jnp.where(swap, sent_b[at], sent_a[at]), there)

    for s in range(part_out.shape[0]):
        for m in range(terms):
            block = chosen(rows(s, m), first, sent1, sent0, got0, got1)
            env_out[s, rows(0, m)] = split_left(block)
        blocks = [chosen(rows(s, m), last, sent0, sent1, got1, got0) for m in range(terms)]
        for m in range(terms):
            total = bond[m, 0] * blocks[0]
            for k in range(1, terms):
                total = total + bond[m, k] * blocks[k]
            mixed_out[s, rows(0, m)] = split_left(total)
        j = begin + s
        core = core_of(env_out[s], mixed_out[s], middle[j], terms)
        part = product(product(back[j, 0], core), back[j, 1])
        mine = (j // own == member).astype(jnp.float32)
        part_out[s] = part + (mine * onsite[j % own]) * vec[j]


def inward(block, left, right):
    temp = fold(jnp.dot(left, split_right(block), preferred_element_type=jnp.float32))
    return fold(jnp.dot(split_left(temp), right, preferred_element_type=jnp.float32))


def early_kernel(
    own, begin, table, image, part, vec, middle, left, right, onsite, env, mixed,
    resid_out, stat_out, moved, cores,
):
    width, size = image.shape[0], image.shape[1]
    terms = mixed.shape[1] // size
    member = table[2]
    zero = jnp.zeros((size, size), jnp.float32)
    tile = lambda value: jnp.full((8, 128), value, jnp.float32)

    along, norm = zero, zero
    for i in range(width):
        along = along + vec[begin + i] * image[i]
        norm = norm + vec[begin + i] * vec[begin + i]
    along, norm = jnp.sum(along), jnp.sum(norm)
    guess = jnp.where(norm > 0, along / jnp.where(norm > 0, norm, 1.0), 0.0)
    left_over, square = zero, zero
    for i in range(width):
        resid = image[i] - guess * vec[begin + i]
        resid_out[i] = resid
        left_over = left_over + resid * vec[begin + i]
        square = square + resid * resid
    square = tile(jnp.sum(square))
    length = jnp.sqrt(square + 1e-06)
    scale = (1.0 / length)[0:1]
    stat_out[0] = tile(guess)
    stat_out[1] = tile(norm)
    stat_out[2] = tile(jnp.sum(left_over))
    stat_out[3] = square
    stat_out[4] = length

    for i in range(width):
        resid = resid_out[i] * scale
        resid_out[i] = resid
        moved[i] = inward(resid, left[begin + i], right[begin + i])
    for i in range(width):
        cores[i] = core_of(env[i], mixed[i], split_right(moved[i]), terms)
    shares = lambda i: jnp.where((begin + i) // own == member, 1.0, 0.0) * onsite[(begin + i) % own]
    both = zero
    for i in range(width):
        resid = resid_out[i]
        both = both + moved[i] * cores[i] + (shares(i) * resid) * resid
    stat_out[5] = tile(jnp.sum(both))
    cross = zero
    for i in range(width):
        resid = resid_out[i]
        cross = cross + middle[begin + i] * cores[i]
        cross = cross + resid * (part[i] + shares(i) * vec[begin + i])
    stat_out[6] = tile(jnp.sum(cross))
    plain = zero
    for i in range(width):
        plain = plain + vec[begin + i] * part[i]
    stat_out[7] = tile(jnp.sum(plain))


def second_kernel(
    own, widths, table, part0, part1, part2, part3, vec, left, right, onsite, env, mixed, *refs
):
    count = len(widths)
    resids, stats = refs[:count], refs[count : 2 * count]
    second_out, share_out, work = refs[2 * count :]
    total, size, late = vec.shape[0], vec.shape[1], part0.shape[0]
    early = total - late
    terms = mixed.shape[1] // size
    member = table[2]
    zero = jnp.zeros((size, size), jnp.float32)
    tile = lambda value: jnp.full((8, 128), value, jnp.float32)

    images = [(part0[i] + part1[i]) + (part2[i] + part3[i]) for i in range(late)]
    along = zero
    for i in range(late):
        along = along + vec[early + i] * images[i]
    alpha1 = tile(jnp.sum(along))
    for stat in stats:
        alpha1 = alpha1 + (stat[0] * stat[1] + stat[2])
    rest = zero
    for i in range(late):
        images[i] = images[i] - alpha1[0:1] * vec[early + i]
        rest = rest + images[i] * images[i]
    square = tile(jnp.sum(rest)) + 1e-06
    for stat in stats:
        away = alpha1 - stat[0]
        square = square + jnp.maximum(
            stat[3] - 2.0 * away * stat[2] + away * (away * stat[1]), 0.0
        )
    beta = jnp.sqrt(square)
    scale = (1.0 / beta)[0:1]
    share = zero
    for i in range(late):
        j = early + i
        value = images[i] * scale
        work[j] = value
        moved = inward(value, left[j], right[j])
        core = core_of(env[i], mixed[i], split_right(moved), terms)
        mine = jnp.where(j // own == member, 1.0, 0.0) * onsite[j % own]
        share = share + moved * core + (mine * value) * value
    begin = 0
    sums = zero[:8]
    for resid, stat, width in zip(resids, stats, widths):
        long, off = stat[4] / beta, (alpha1 - stat[0]) / beta
        sums = sums + long * (long * stat[5]) - off * (long * stat[6]) + off * (off * stat[7])
        for i in range(width):
            work[begin + i] = long[0:1] * resid[i] - off[0:1] * vec[begin + i]
        begin += width
    share_out[0] = tile(jnp.sum(share)) + sums
    share_out[1] = alpha1
    share_out[2] = beta
    for i in range(own):
        second_out[i] = work[member * own + i]


def final_kernel(own, count, table, share0, share1, share2, share3, vec, second, out, energy_out):
    member = table[2]
    alpha2 = (share0[0] + share1[0]) + (share2[0] + share3[0])
    alpha1, beta = share0[1], share0[2]
    energy = (alpha1 + alpha2) / 2.0 - jnp.sqrt(((alpha1 - alpha2) / 2.0) ** 2 + beta * beta)
    height = jnp.sqrt(beta * beta + (energy - alpha1) ** 2)
    scale = math.sqrt(count)
    weight1 = (scale * (beta / height))[0:1]
    weight2 = (scale * ((energy - alpha1) / height))[0:1]
    for i in range(own):
        out[i] = weight1 * vec[member * own + i] + weight2 * second[i]
    energy_out[0] = energy[0, 0]


def on_device(
    state, left_tensor, right_tensor, onsite, left_env, right_env, mpo_bond, sectors, flow
):
    position = lax.axis_index("sites")
    parts = lax.axis_size("sites") // GROUP
    own, size = state.shape[0], state.shape[1]
    terms, total = left_env.shape[0], left_env.shape[1]
    f32, bf16 = jnp.float32, jnp.bfloat16
    begins = [sum(CHUNKS[:c]) for c in range(len(CHUNKS))]

    smem = pl.BlockSpec(memory_space=pltpu.SMEM)
    vmem = pl.BlockSpec(memory_space=pltpu.VMEM)
    hbm = pl.BlockSpec(memory_space=pltpu.HBM)
    shape = jax.ShapeDtypeStruct
    dma = pltpu.SemaphoreType.DMA
    params = lambda mib: pltpu.CompilerParams(vmem_limit_bytes=mib * MIB)

    small_cost = pl.CostEstimate(flops=1, bytes_accessed=1, transcendentals=0)

    rows = lambda width: width * terms * size
    chunk = lambda c: (rows(CHUNKS[c]) + (own * size + terms if c == 0 else 0), size)
    chunks = lambda some: [pltpu.VMEM(chunk(c), f32) for c in some for _ in range(2)]
    in_hbm = lambda *values: [
        pltpu.with_memory_space_constraint(value, pltpu.HBM) for value in values
    ]
    table, *opened = pl.pallas_call(
        functools.partial(open_kernel, CHUNKS, parts),
        in_specs=[hbm] * 8,
        out_specs=[smem] + [vmem] * (2 * len(CHUNKS)),
        out_shape=[shape((HEAD + 5 * total + 2,), jnp.int32)] + chunks(range(len(CHUNKS))),
        scratch_shapes=[
            pltpu.SMEM((1,), jnp.int32),
            pltpu.SMEM(sectors.shape, jnp.int32),
            pltpu.SMEM(flow.shape, jnp.int32),
            pltpu.SMEM((3 * total,), jnp.int32),
            pltpu.VMEM(mpo_bond.shape, f32),
            pltpu.VMEM((terms, size), f32),
            dma((2, total)),
            dma((2, own + 1)),
            dma((4,)),
        ],
        cost_estimate=small_cost,
        compiler_params=params(16),
        name="open",
    )(
        *in_hbm(
            jnp.reshape(position, (1,)).astype(jnp.int32), sectors, flow, mpo_bond,
            left_tensor, right_tensor, left_env, right_env,
        )
    )
    sent = [tuple(opened[2 * c : 2 * c + 2]) for c in range(len(CHUNKS))]
    states = gather(state)
    sent[1], _ = lax.optimization_barrier((sent[1], states))
    got = [tuple(hand_over(block, side) for side, block in enumerate(pair)) for pair in sent]

    tail = [block[rows(CHUNKS[0]) :] for block in got[0]]
    swap = table[3] == 1
    from_left, from_right = jnp.where(swap, tail[1], tail[0]), jnp.where(swap, tail[0], tail[1])
    small = jnp.eye(terms, dtype=f32)
    bond_left = jnp.where(table[0] == 1, small, from_left[own * size :, : mpo_bond.shape[1]])
    bond_right = jnp.where(table[1] == 1, small, from_right[own * size :, : mpo_bond.shape[1]])
    bond = jnp.sum(bond_left[:, None, :] * bond_right[None, :, :], axis=2)
    tensors = lambda block: block[: own * size].reshape(own, size, size)
    pieces = gather(jnp.stack([tensors(from_left), tensors(from_right)], 1))

    vec, middle, plain, left, right, back = pl.pallas_call(
        functools.partial(prepare_kernel, own),
        in_specs=[smem, vmem, vmem],
        out_specs=[vmem] * 6,
        out_shape=[
            shape((total, size, size), f32),
            shape((total, 2 * size, 2 * size), bf16),
            shape((total, size, size), f32),
            shape((total, size, 2 * size), bf16),
            shape((total, 2 * size, 2 * size), bf16),
            shape((total, 2, size, size), f32),
        ],
        cost_estimate=small_cost,
        compiler_params=params(12),
        name="prepare",
    )(table, states, pieces)

    def early(begin, width, image, part, env, mixed, after):
        image, _ = lax.optimization_barrier((image, after))
        return pl.pallas_call(
            functools.partial(early_kernel, own, begin),
            in_specs=[smem] + [vmem] * 9,
            out_specs=[vmem] * 2,
            out_shape=[shape((width, size, size), f32), shape((8, 8, 128), f32)],
            scratch_shapes=[pltpu.VMEM((width, size, size), f32)] * 2,
            cost_estimate=small_cost,
            compiler_params=params(12),
            name="early_second_matvec",
        )(table, image, part, vec, plain, left, right, onsite, env, mixed)

    resids, stats, waits, held = [], [], [], None
    for c, (begin, width) in enumerate(zip(begins, CHUNKS)):
        if c > 0:
            got[c], _ = lax.optimization_barrier((got[c], waits[c - 1]))
        env, mixed, part = pl.pallas_call(
            functools.partial(first_kernel, own, begin),
            in_specs=[smem, smem] + [vmem] * 8,
            out_specs=[vmem] * 3,
            out_shape=[
                shape((width, rows(1), 2 * size), bf16),
                shape((width, rows(1), 2 * size), bf16),
                shape((width, size, size), f32),
            ],
            cost_estimate=small_cost,
        compiler_params=params(12),
            name=f"first_matvec{c}",
        )(table, bond, *got[c], *sent[c], middle, vec, back, onsite)
        if held is not None:
            resid, stat = early(*held, after=part)
            resids.append(resid)
            stats.append(stat)
        if c < len(CHUNKS) - 1:
            image = total_of(part)
            held = (begin, width, image, part, env, mixed)
            waits.append([image] + stats[-1:])

    parts = [part] + [partner(part, mask) for mask in (1, 2, 3)]
    second, share = pl.pallas_call(
        functools.partial(second_kernel, own, CHUNKS[:-1]),
        in_specs=[smem] + [vmem] * (10 + 2 * (len(CHUNKS) - 1)),
        out_specs=[vmem] * 2,
        out_shape=[shape((own, size, size), f32), shape((3, 8, 128), f32)],
        scratch_shapes=[pltpu.VMEM((total, size, size), f32)],
        cost_estimate=small_cost,
        compiler_params=params(12),
        name="second_matvec",
    )(table, *parts, vec, left, right, onsite, env, mixed, *resids, *stats)

    shares = [share] + [partner(share[:1], mask) for mask in (1, 2, 3)]
    new_state, energy = pl.pallas_call(
        functools.partial(final_kernel, own, total * size * size),
        in_specs=[smem] + [vmem] * 6,
        out_specs=[vmem, smem],
        out_shape=[shape((own, size, size), f32), shape((1,), f32)],
        cost_estimate=small_cost,
        compiler_params=params(4),
        name="ritz_update",
    )(table, *shares, vec, second)
    return (new_state, energy)


def solution(mesh):
    return jax.shard_map(
        on_device,
        mesh=mesh,
        in_specs=(
            P(("groups", "sites"), None, None),
            P(("groups", "sites"), None, None),
            P(("groups", "sites"), None, None),
            P(("groups", "sites"), None, None),
            P(("groups", "sites"), None, None, None),
            P(("groups", "sites"), None, None, None),
            P(("groups", "sites"), None),
            P("groups", None),
            P("groups", None),
        ),
        out_specs=(P(("groups", "sites"), None, None), P(("groups", "sites"))),
        check_vma=False,
    )
```

time: 128 us -> 123 us (0.961)
  waiting for transfers between devices: 73.2 us -> 48.8 us
  starting transfers between devices: 27.6 us -> 39.7 us
  Pallas kernels: 23.1 us -> 29.6 us
    ppermute x6 -> x8, waiting for transfers between devices: 48.2 us -> 21.5 us  [hand_over(): lax.ppermute(block, 'sites', [(i, j) for i, j in route if 0 <= j < count])]
    ppermute x6 -> x8, starting transfers between devices: 17 us -> 23.9 us  [hand_over(): lax.ppermute(block, 'sites', [(i, j) for i, j in route if 0 <= j < count])]
    ppermute x14 -> x18, starting transfers between devices: 10.6 us -> 15.8 us  [partner(): return lax.ppermute(block, 'sites', route)]
    pallas_call x1 -> x4, Pallas kernels: 3.91 us -> 8.77 us  [the longest x3 6.87 us: early(): pl.pallas_call(functools.partial(early_kernel, own, begin), in_specs=[sme...]
    ppermute x14 -> x18, waiting for transfers between devices: 24.9 us -> 27.3 us  [partner(): return lax.ppermute(block, 'sites', route)]
    pallas_call x3 -> x4, Pallas kernels: 9.36 us -> 10.9 us  [on_device(): pl.pallas_call(functools.partial(first_kernel, own, begin), in_specs=[sme...]
  transfers between devices with their start and end apart: 20 -> 26, of which waited for: 15 -> 15; matrix products, arithmetic and copies ran while one was open for 1% -> 1% of each run, Pallas kernels for 9% -> 16%
where the time goes in v3:
time: 123 us; the launch traced here: 122 us
  waiting for transfers between devices  48.8 us (40%)
  starting transfers between devices  39.7 us (32%)
  Pallas kernels  29.6 us (24%)
  between operations  3.06 us (2%)
    ppermute x18, waiting for transfers between devices, partner(): return lax.ppermute(block, 'sites', route)  27.3 us
    ppermute x8, starting transfers between devices, hand_over(): lax.ppermute(block, 'sites', [(i, j) for i, j in route if 0 <= j < count])  23.9 us
    ppermute x8, waiting for transfers between devices, hand_over(): lax.ppermute(block, 'sites', [(i, j) for i, j in route if 0 <= j < count])  21.5 us
    ppermute x18, starting transfers between devices, partner(): return lax.ppermute(block, 'sites', route)  15.8 us
    pallas_call x4, Pallas kernels, on_device(): pl.pallas_call(functools.partial(first_kernel, own, begin), in_specs=[sme...  10.9 us
    pallas_call x3, Pallas kernels, early(): pl.pallas_call(functools.partial(early_kernel, own, begin), in_specs=[sme...  6.87 us
    pallas_call x1, Pallas kernels, on_device(): pl.pallas_call(functools.partial(open_kernel, CHUNKS, parts), in_specs=[h...  5.33 us
    pallas_call x1, Pallas kernels, on_device(): pl.pallas_call(functools.partial(prepare_kernel, own), in_specs=[smem, vm...  3.33 us
  transfers between devices with their start and end apart: 26, of which 15 were waited for; matrix products, arithmetic and copies ran while one was open for 1% of the time, Pallas kernels for 16%

profile of v3, /device:TPU:0, one launch (start us, length us, event | category | flops | bytes accessed | tf_op | source)
XLA Modules:
  0.0 122.2 jit_solution(11192237006966391053)
XLA Ops:
  0.6 5.3 %open.1 = (s32[46]{0:T(128)S(1)}, f32[3336,128]{1,0:T(8,128)S(1)}, f32[3336,128]{1,0:T(8,128)S(1)}, f32[3072,128]{1,0:T(8,128)S(1)}, f32[3072,128]{1,0:T(8,128)S...) custom-call(s32[1]{0:T(128)} %bitcast.place_hbm, ...), custom_call_target="tpu_custom_call" | custom-call | flops 1 | bytes 1 | tf_op jit(solution)/shard_map/open/pallas_call | solution.py:397
  6.0 1.3 %collective-permute-start = (f32[3336,128]{1,0:T(8,128)S(1)}, f32[3336,128]{1,0:T(8,128)S(1)}, u32[]{:S(2)}, u32[]{:S(2)}) collective-permute-start(f32[3336,128]{1,0:T(8,128)S(1)} %get-tuple-element.49.sent1), channel_id=1, source_target_pairs={{1,5},{3,7},{4,0},{5,9},{6,2},{7,11},{8,4},{9,13},{10,6},{11,15},{... | collective-permute-start | bytes 5124104 | tf_op jit(solution)/shard_map/ppermute | solution.py:19
  7.3 5.5 %collective-permute-start.1 = (f32[3336,128]{1,0:T(8,128)S(1)}, f32[3336,128]{1,0:T(8,128)S(1)}, u32[]{:S(2)}, u32[]{:S(2)}) collective-permute-start(f32[3336,128]{1,0:T(8,128)S(1)} %get-tuple-element.50.sent0), channel_id=1, source_target_pairs={{0,4},{2,6},{4,8},{5,1},{6,10},{7,3},{8,12},{9,5},{10,14},{11,7},{... | collective-permute-start | bytes 5124104 | tf_op jit(solution)/shard_map/ppermute | solution.py:19
  12.9 2.2 %collective-permute-start.7 = (f32[2,128,128]{2,1,0:T(8,128)S(1)}, f32[2,128,128]{2,1,0:T(8,128)S(1)}, u32[]{:S(2)}, u32[]{:S(2)}) collective-permute-start(f32[2,128,128]{2,1,0:T(8,128)S(1)} %copy-done.1), channel_id=1, source_target_pairs={{0,2},{1,3},{2,0},{3,1},{4,6},{5,7},{6,4},{7,5},{8,10},{9,11},{10,... | collective-permute-start | bytes 393224 | tf_op jit(solution)/shard_map/ppermute | solution.py:24
  15.1 4.3 %collective-permute-done.7 = f32[2,128,128]{2,1,0:T(8,128)S(1)} collective-permute-done((f32[2,128,128]{2,1,0:T(8,128)S(1)}, f32[2,128,128]{2,1,0:T(8,128)S(1)}, u32[]{:S(2)}, u32[]{:S(2)}) %collective-permute-start.7) | collective-permute-done | bytes 131104 | tf_op jit(solution)/shard_map/ppermute | solution.py:24
  19.4 2.3 %collective-permute-done.8 = f32[2,128,128]{2,1,0:T(8,128)S(1)} collective-permute-done((f32[2,128,128]{2,1,0:T(8,128)S(1)}, f32[2,128,128]{2,1,0:T(8,128)S(1)}, u32[]{:S(2)}, u32[]{:S(2)}) %collective-permute-start.8) | collective-permute-done | bytes 131104 | tf_op jit(solution)/shard_map/ppermute | solution.py:24
  23.1 4.6 %collective-permute-start.9 = (f32[3072,128]{1,0:T(8,128)S(1)}, f32[3072,128]{1,0:T(8,128)S(1)}, u32[]{:S(2)}, u32[]{:S(2)}) collective-permute-start(f32[3072,128]{1,0:T(8,128)S(1)} %get-tuple-element.57.sent0), channel_id=1, source_target_pairs={{0,4},{2,6},{4,8},{5,1},{6,10},{7,3},{8,12},{9,5},{10,14},{11,7},{... | collective-permute-start | bytes 4718600 | tf_op jit(solution)/shard_map/ppermute | solution.py:19
  28.9 17.3 %collective-permute-done.got1 = f32[3336,128]{1,0:T(8,128)S(1)} collective-permute-done((f32[3336,128]{1,0:T(8,128)S(1)}, f32[3336,128]{1,0:T(8,128)S(1)}, u32[]{:S(2)}, u32[]{:S(2)}) %collective-permute-start) | collective-permute-done | bytes 1708064 | tf_op jit(solution)/shard_map/ppermute | solution.py:19
  46.2 4.2 %collective-permute-done.1.got0 = f32[3336,128]{1,0:T(8,128)S(1)} collective-permute-done((f32[3336,128]{1,0:T(8,128)S(1)}, f32[3336,128]{1,0:T(8,128)S(1)}, u32[]{:S(2)}, u32[]{:S(2)}) %collective-permute-start.1) | collective-permute-done | bytes 1708064 | tf_op jit(solution)/shard_map/ppermute | solution.py:19
  50.6 1.3 %collective-permute-start.11 = (f32[2,2,128,128]{3,2,1,0:T(8,128)S(1)}, f32[2,2,128,128]{3,2,1,0:T(8,128)S(1)}, u32[]{:S(2)}, u32[]{:S(2)}) collective-permute-start(f32[2,2,128,128]{3,2,1,0:T(8,128)S(1)} %get-tuple-element.97), channel_id=1, source_target_pairs={{0,1},{1,0},{2,3},{3,2},{4,5},{5,4},{6,7},{7,6},{8,9},{9,8},{10,11... | collective-permute-start | bytes 786440 | tf_op jit(solution)/shard_map/ppermute | solution.py:24
  51.9 1.5 %collective-permute-start.12 = (f32[2,2,128,128]{3,2,1,0:T(8,128)S(1)}, f32[2,2,128,128]{3,2,1,0:T(8,128)S(1)}, u32[]{:S(2)}, u32[]{:S(2)}) collective-permute-start(f32[2,2,128,128]{3,2,1,0:T(8,128)S(1)} %get-tuple-element.97), channel_id=1, source_target_pairs={{0,2},{1,3},{2,0},{3,1},{4,6},{5,7},{6,4},{7,5},{8,10},{9,11},{10,... | collective-permute-start | bytes 786440 | tf_op jit(solution)/shard_map/ppermute | solution.py:24
  54.7 6.3 %collective-permute-done.12 = f32[2,2,128,128]{3,2,1,0:T(8,128)S(1)} collective-permute-done((f32[2,2,128,128]{3,2,1,0:T(8,128)S(1)}, f32[2,2,128,128]{3,2,1,0:T(8,128)S(1)}, u32[]{:S(2)}, u32[]{:S(2)}) %collective-permute-start.12) | collective-permute-done | bytes 262176 | tf_op jit(solution)/shard_map/ppermute | solution.py:24
  61.1 3.9 %collective-permute-done.13 = f32[2,2,128,128]{3,2,1,0:T(8,128)S(1)} collective-permute-done((f32[2,2,128,128]{3,2,1,0:T(8,128)S(1)}, f32[2,2,128,128]{3,2,1,0:T(8,128)S(1)}, u32[]{:S(2)}, u32[]{:S(2)}) %collective-permute-start.13) | collective-permute-done | bytes 262176 | tf_op jit(solution)/shard_map/ppermute | solution.py:24
  65.1 3.3 %prepare.1 = (f32[8,128,128]{2,1,0:T(8,128)S(1)}, bf16[8,256,256]{2,1,0:T(8,128)(2,1)S(1)}, f32[8,128,128]{2,1,0:T(8,128)S(1)}, bf16[8,128,256]{2,1,0:T(8,128)(2...) custom-call(s32[46]{0:T(128)S(1)} %get-tuple-element.48.table, ...), custom_call_target="tpu_custom_call" | custom-call | flops 1 | bytes 1 | tf_op jit(solution)/shard_map/prepare/pallas_call | solution.py:437
  68.4 3.8 %first_matvec0.1 = (bf16[3,1024,256]{2,1,0:T(8,128)(2,1)S(1)}, bf16[3,1024,256]{2,1,0:T(8,128)(2,1)S(1)}, f32[3,128,128]{2,1,0:T(8,128)S(1)}) custom-call(s32[46]{0:T(128)S(1)} %get-tuple-element.48.table, f32[8,8]{1,0:T(8,128)S(1)} %multiply_reduce_fusion.bond, f32[3336,128]{1,0:T(8,128)S(1)} %collective-permute-done.1.got0, ...), custom_call_target="tpu_custom_call" | custom-call | flops 1 | bytes 1 | tf_op jit(solution)/shard_map/first_matvec0/pallas_call | solution.py:471
  74.4 1.6 %collective-permute-start.15 = (f32[3,128,128]{2,1,0:T(8,128)S(1)}, f32[3,128,128]{2,1,0:T(8,128)S(1)}, u32[]{:S(2)}, u32[]{:S(2)}) collective-permute-start(f32[3,128,128]{2,1,0:T(8,128)S(1)} %add.18), channel_id=1, source_target_pairs={{0,2},{1,3},{2,0},{3,1},{4,6},{5,7},{6,4},{7,5},{8,10},{9,11},{10,... | collective-permute-start | bytes 589832 | tf_op jit(solution)/shard_map/ppermute | solution.py:24
  76.0 4.2 %collective-permute-start.4 = (f32[1024,128]{1,0:T(8,128)S(1)}, f32[1024,128]{1,0:T(8,128)S(1)}, u32[]{:S(2)}, u32[]{:S(2)}) collective-permute-start(f32[1024,128]{1,0:T(8,128)S(1)} %get-tuple-element.53.sent0), channel_id=1, source_target_pairs={{0,4},{2,6},{4,8},{5,1},{6,10},{7,3},{8,12},{9,5},{10,14},{11,7},{... | collective-permute-start | bytes 1572872 | tf_op jit(solution)/shard_map/ppermute | solution.py:19
  81.7 3.6 %first_matvec1.1 = (bf16[3,1024,256]{2,1,0:T(8,128)(2,1)S(1)}, bf16[3,1024,256]{2,1,0:T(8,128)(2,1)S(1)}, f32[3,128,128]{2,1,0:T(8,128)S(1)}) custom-call(s32[46]{0:T(128)S(1)} %get-tuple-element.48.table, f32[8,8]{1,0:T(8,128)S(1)} %multiply_reduce_fusion.bond, f32[3072,128]{1,0:T(8,128)S(1)} %collective-permute-done.9.got0, ...), custom_call_target="tpu_custom_call" | custom-call | flops 1 | bytes 1 | tf_op jit(solution)/shard_map/first_matvec1/pallas_call | solution.py:471
  86.1 4.2 %collective-permute-start.2 = (f32[1024,128]{1,0:T(8,128)S(1)}, f32[1024,128]{1,0:T(8,128)S(1)}, u32[]{:S(2)}, u32[]{:S(2)}) collective-permute-start(f32[1024,128]{1,0:T(8,128)S(1)} %get-tuple-element.51.sent0), channel_id=1, source_target_pairs={{0,4},{2,6},{4,8},{5,1},{6,10},{7,3},{8,12},{9,5},{10,14},{11,7},{... | collective-permute-start | bytes 1572872 | tf_op jit(solution)/shard_map/ppermute | solution.py:19
  90.3 1.5 %collective-permute-start.3 = (f32[1024,128]{1,0:T(8,128)S(1)}, f32[1024,128]{1,0:T(8,128)S(1)}, u32[]{:S(2)}, u32[]{:S(2)}) collective-permute-start(f32[1024,128]{1,0:T(8,128)S(1)} %get-tuple-element.52.sent1), channel_id=1, source_target_pairs={{1,5},{3,7},{4,0},{5,9},{6,2},{7,11},{8,4},{9,13},{10,6},{11,15},{... | collective-permute-start | bytes 1572872 | tf_op jit(solution)/shard_map/ppermute | solution.py:19
  91.8 1.6 %collective-permute-start.17 = (f32[3,128,128]{2,1,0:T(8,128)S(1)}, f32[3,128,128]{2,1,0:T(8,128)S(1)}, u32[]{:S(2)}, u32[]{:S(2)}) collective-permute-start(f32[3,128,128]{2,1,0:T(8,128)S(1)} %add.20), channel_id=1, source_target_pairs={{0,2},{1,3},{2,0},{3,1},{4,6},{5,7},{6,4},{7,5},{8,10},{9,11},{10,... | collective-permute-start | bytes 589832 | tf_op jit(solution)/shard_map/ppermute | solution.py:24
  93.5 2.5 %early_second_matvec.3 = (f32[3,128,128]{2,1,0:T(8,128)S(1)}, f32[8,8,128]{2,1,0:T(8,128)S(1)}) custom-call(s32[46]{0:T(128)S(1)} %get-tuple-element.48.table, f32[3,128,128]{2,1,0:T(8,128)S(1)} %add.19.image, f32[3,128,128]{2,1,0:T(8,128)S(1)} %get-tuple-element.62.part, f32[8,128,128]{2,1,0:T(8,128)S(1)} %get-tuple-element.60.vec, ...), custom_call_target="tpu_custom_call" | custom-call | flops 1 | bytes 1 | tf_op jit(solution)/shard_map/early_second_matvec/pallas_call | solution.py:456
  96.0 3.1 %collective-permute-done.17 = f32[3,128,128]{2,1,0:T(8,128)S(1)} collective-permute-done((f32[3,128,128]{2,1,0:T(8,128)S(1)}, f32[3,128,128]{2,1,0:T(8,128)S(1)}, u32[]{:S(2)}, u32[]{:S(2)}) %collective-permute-start.17) | collective-permute-done | bytes 196640 | tf_op jit(solution)/shard_map/ppermute | solution.py:24
  99.1 1.8 %first_matvec2.1 = (bf16[1,1024,256]{2,1,0:T(8,128)(2,1)S(1)}, bf16[1,1024,256]{2,1,0:T(8,128)(2,1)S(1)}, f32[1,128,128]{2,1,0:T(8,128)S(1)}) custom-call(s32[46]{0:T(128)S(1)} %get-tuple-element.48.table, f32[8,8]{1,0:T(8,128)S(1)} %multiply_reduce_fusion.bond, f32[1024,128]{1,0:T(8,128)S(1)} %collective-permute-done.4.got0, ...), custom_call_target="tpu_custom_call" | custom-call | flops 1 | bytes 1 | tf_op jit(solution)/shard_map/first_matvec2/pallas_call | solution.py:471
  102.3 1.6 %collective-permute-start.19 = (f32[1,128,128]{2,1,0:T(8,128)S(1)}, f32[1,128,128]{2,1,0:T(8,128)S(1)}, u32[]{:S(2)}, u32[]{:S(2)}) collective-permute-start(f32[1,128,128]{2,1,0:T(8,128)S(1)} %add.22), channel_id=1, source_target_pairs={{0,2},{1,3},{2,0},{3,1},{4,6},{5,7},{6,4},{7,5},{8,10},{9,11},{10,... | collective-permute-start | bytes 196616 | tf_op jit(solution)/shard_map/ppermute | solution.py:24
  103.9 2.5 %early_second_matvec.4 = (f32[3,128,128]{2,1,0:T(8,128)S(1)}, f32[8,8,128]{2,1,0:T(8,128)S(1)}) custom-call(s32[46]{0:T(128)S(1)} %get-tuple-element.48.table, f32[3,128,128]{2,1,0:T(8,128)S(1)} %add.21.image, f32[3,128,128]{2,1,0:T(8,128)S(1)} %get-tuple-element.65.part, f32[8,128,128]{2,1,0:T(8,128)S(1)} %get-tuple-element.60.vec, ...), custom_call_target="tpu_custom_call" | custom-call | flops 1 | bytes 1 | tf_op jit(solution)/shard_map/early_second_matvec/pallas_call | solution.py:456
  106.6 1.8 %first_matvec3.1 = (bf16[1,1024,256]{2,1,0:T(8,128)(2,1)S(1)}, bf16[1,1024,256]{2,1,0:T(8,128)(2,1)S(1)}, f32[1,128,128]{2,1,0:T(8,128)S(1)}) custom-call(s32[46]{0:T(128)S(1)} %get-tuple-element.48.table, f32[8,8]{1,0:T(8,128)S(1)} %multiply_reduce_fusion.bond, f32[1024,128]{1,0:T(8,128)S(1)} %collective-permute-done.2.got0, ...), custom_call_target="tpu_custom_call" | custom-call | flops 1 | bytes 1 | tf_op jit(solution)/shard_map/first_matvec3/pallas_call | solution.py:471
  108.5 1.6 %collective-permute-start.21 = (f32[1,128,128]{2,1,0:T(8,128)S(1)}, f32[1,128,128]{2,1,0:T(8,128)S(1)}, u32[]{:S(2)}, u32[]{:S(2)}) collective-permute-start(f32[1,128,128]{2,1,0:T(8,128)S(1)} %get-tuple-element.82.part0), channel_id=1, source_target_pairs={{0,2},{1,3},{2,0},{3,1},{4,6},{5,7},{6,4},{7,5},{8,10},{9,11},{10,... | collective-permute-start | bytes 196616 | tf_op jit(solution)/shard_map/ppermute | solution.py:24
  110.4 1.9 %early_second_matvec.5 = (f32[1,128,128]{2,1,0:T(8,128)S(1)}, f32[8,8,128]{2,1,0:T(8,128)S(1)}) custom-call(s32[46]{0:T(128)S(1)} %get-tuple-element.48.table, f32[1,128,128]{2,1,0:T(8,128)S(1)} %add.23.image, f32[1,128,128]{2,1,0:T(8,128)S(1)} %get-tuple-element.75.part, f32[8,128,128]{2,1,0:T(8,128)S(1)} %get-tuple-element.60.vec, ...), custom_call_target="tpu_custom_call" | custom-call | flops 1 | bytes 1 | tf_op jit(solution)/shard_map/early_second_matvec/pallas_call | solution.py:456
  114.1 1.9 %second_matvec.1 = (f32[2,128,128]{2,1,0:T(8,128)S(1)}, f32[3,8,128]{2,1,0:T(8,128)S(1)}) custom-call(s32[46]{0:T(128)S(1)} %get-tuple-element.48.table, f32[1,128,128]{2,1,0:T(8,128)S(1)} %get-tuple-element.82.part0, f32[1,128,128]{2,1,0:T(8,128)S(1)} %collective-permute-done.20.part1, f32[1,128,128]{2,1,0:T(8,128)S(1)} %collective-permute-done.21.part2, ...), custom_call_target="tpu_custom_call" | custom-call | flops 1 | bytes 1 | tf_op jit(solution)/shard_map/second_matvec/pallas_call | solution.py:494
  116.3 1.5 %collective-permute-start.24 = (f32[1,8,128]{2,1,0:T(8,128)S(1)}, f32[1,8,128]{2,1,0:T(8,128)S(1)}, u32[]{:S(2)}, u32[]{:S(2)}) collective-permute-start(f32[1,8,128]{2,1,0:T(8,128)S(1)} %slice.41), channel_id=1, source_target_pairs={{0,2},{1,3},{2,0},{3,1},{4,6},{5,7},{6,4},{7,5},{8,10},{9,11},{10,... | collective-permute-start | bytes 12296 | tf_op jit(solution)/shard_map/ppermute | solution.py:24
  118.0 1.9 %collective-permute-done.24.share2 = f32[1,8,128]{2,1,0:T(8,128)S(1)} collective-permute-done((f32[1,8,128]{2,1,0:T(8,128)S(1)}, f32[1,8,128]{2,1,0:T(8,128)S(1)}, u32[]{:S(2)}, u32[]{:S(2)}) %collective-permute-start.24) | collective-permute-done | bytes 4128 | tf_op jit(solution)/shard_map/ppermute | solution.py:24
  (51 shorter events, 13.3 us)
Async XLA Ops:
  0.6 12.2 %copy-start.1 = (f32[2,128,128]{2,1,0:T(8,128)S(1)}, f32[2,128,128]{2,1,0:T(8,128)}, u32[]{:S(2)}) copy-start(f32[2,128,128]{2,1,0:T(8,128)} %param.9) | copy-start | bytes 393220
  6.0 40.2 %collective-permute-start = (f32[3336,128]{1,0:T(8,128)S(1)}, f32[3336,128]{1,0:T(8,128)S(1)}, u32[]{:S(2)}, u32[]{:S(2)}) collective-permute-start(f32[3336,128]{1,0:T(8,128)S(1)} %get-tuple-element.49.sent1), channel_id=1, source_target_pairs={{1,5},{3,7},{4,0},{5,9},{6,2},{7,11},{8,4},{9,13},{10,6},{11,15},{... | collective-permute-start | bytes 5124104 | tf_op jit(solution)/shard_map/ppermute | solution.py:19
  7.3 43.2 %collective-permute-start.1 = (f32[3336,128]{1,0:T(8,128)S(1)}, f32[3336,128]{1,0:T(8,128)S(1)}, u32[]{:S(2)}, u32[]{:S(2)}) collective-permute-start(f32[3336,128]{1,0:T(8,128)S(1)} %get-tuple-element.50.sent0), channel_id=1, source_target_pairs={{0,4},{2,6},{4,8},{5,1},{6,10},{7,3},{8,12},{9,5},{10,14},{11,7},{... | collective-permute-start | bytes 5124104 | tf_op jit(solution)/shard_map/ppermute | solution.py:19
  12.8 2.3 %collective-permute-start.6 = (f32[2,128,128]{2,1,0:T(8,128)S(1)}, f32[2,128,128]{2,1,0:T(8,128)S(1)}, u32[]{:S(2)}, u32[]{:S(2)}) collective-permute-start(f32[2,128,128]{2,1,0:T(8,128)S(1)} %copy-done.1), channel_id=1, source_target_pairs={{0,1},{1,0},{2,3},{3,2},{4,5},{5,4},{6,7},{7,6},{8,9},{9,8},{10,11... | collective-permute-start | bytes 393224 | tf_op jit(solution)/shard_map/ppermute | solution.py:24
  12.9 6.5 %collective-permute-start.7 = (f32[2,128,128]{2,1,0:T(8,128)S(1)}, f32[2,128,128]{2,1,0:T(8,128)S(1)}, u32[]{:S(2)}, u32[]{:S(2)}) collective-permute-start(f32[2,128,128]{2,1,0:T(8,128)S(1)} %copy-done.1), channel_id=1, source_target_pairs={{0,2},{1,3},{2,0},{3,1},{4,6},{5,7},{6,4},{7,5},{8,10},{9,11},{10,... | collective-permute-start | bytes 393224 | tf_op jit(solution)/shard_map/ppermute | solution.py:24
  15.1 6.6 %collective-permute-start.8 = (f32[2,128,128]{2,1,0:T(8,128)S(1)}, f32[2,128,128]{2,1,0:T(8,128)S(1)}, u32[]{:S(2)}, u32[]{:S(2)}) collective-permute-start(f32[2,128,128]{2,1,0:T(8,128)S(1)} %copy-done.1), channel_id=1, source_target_pairs={{0,3},{1,2},{2,1},{3,0},{4,7},{5,6},{6,5},{7,4},{8,11},{9,10},{10,... | collective-permute-start | bytes 393224 | tf_op jit(solution)/shard_map/ppermute | solution.py:24
  21.8 59.9 %collective-permute-start.10 = (f32[3072,128]{1,0:T(8,128)S(1)}, f32[3072,128]{1,0:T(8,128)S(1)}, u32[]{:S(2)}, u32[]{:S(2)}) collective-permute-start(f32[3072,128]{1,0:T(8,128)S(1)} %get-tuple-element.58.sent1), channel_id=1, source_target_pairs={{1,5},{3,7},{4,0},{5,9},{6,2},{7,11},{8,4},{9,13},{10,6},{11,15},{... | collective-permute-start | bytes 4718600 | tf_op jit(solution)/shard_map/ppermute | solution.py:19
  23.1 58.6 %collective-permute-start.9 = (f32[3072,128]{1,0:T(8,128)S(1)}, f32[3072,128]{1,0:T(8,128)S(1)}, u32[]{:S(2)}, u32[]{:S(2)}) collective-permute-start(f32[3072,128]{1,0:T(8,128)S(1)} %get-tuple-element.57.sent0), channel_id=1, source_target_pairs={{0,4},{2,6},{4,8},{5,1},{6,10},{7,3},{8,12},{9,5},{10,14},{11,7},{... | collective-permute-start | bytes 4718600 | tf_op jit(solution)/shard_map/ppermute | solution.py:19
  50.6 4.2 %collective-permute-start.11 = (f32[2,2,128,128]{3,2,1,0:T(8,128)S(1)}, f32[2,2,128,128]{3,2,1,0:T(8,128)S(1)}, u32[]{:S(2)}, u32[]{:S(2)}) collective-permute-start(f32[2,2,128,128]{3,2,1,0:T(8,128)S(1)} %get-tuple-element.97), channel_id=1, source_target_pairs={{0,1},{1,0},{2,3},{3,2},{4,5},{5,4},{6,7},{7,6},{8,9},{9,8},{10,11... | collective-permute-start | bytes 786440 | tf_op jit(solution)/shard_map/ppermute | solution.py:24
  51.9 9.2 %collective-permute-start.12 = (f32[2,2,128,128]{3,2,1,0:T(8,128)S(1)}, f32[2,2,128,128]{3,2,1,0:T(8,128)S(1)}, u32[]{:S(2)}, u32[]{:S(2)}) collective-permute-start(f32[2,2,128,128]{3,2,1,0:T(8,128)S(1)} %get-tuple-element.97), channel_id=1, source_target_pairs={{0,2},{1,3},{2,0},{3,1},{4,6},{5,7},{6,4},{7,5},{8,10},{9,11},{10,... | collective-permute-start | bytes 786440 | tf_op jit(solution)/shard_map/ppermute | solution.py:24
  53.4 11.5 %collective-permute-start.13 = (f32[2,2,128,128]{3,2,1,0:T(8,128)S(1)}, f32[2,2,128,128]{3,2,1,0:T(8,128)S(1)}, u32[]{:S(2)}, u32[]{:S(2)}) collective-permute-start(f32[2,2,128,128]{3,2,1,0:T(8,128)S(1)} %get-tuple-element.97), channel_id=1, source_target_pairs={{0,3},{1,2},{2,1},{3,0},{4,7},{5,6},{6,5},{7,4},{8,11},{9,10},{10,... | collective-permute-start | bytes 786440 | tf_op jit(solution)/shard_map/ppermute | solution.py:24
  64.9 3.5 %copy-start = (f32[2,128,128]{2,1,0:T(8,128)S(1)}, f32[2,128,128]{2,1,0:T(8,128)}, u32[]{:S(2)}) copy-start(f32[2,128,128]{2,1,0:T(8,128)} %onsite.15) | copy-start | bytes 393220
  72.2 2.1 %collective-permute-start.14 = (f32[3,128,128]{2,1,0:T(8,128)S(1)}, f32[3,128,128]{2,1,0:T(8,128)S(1)}, u32[]{:S(2)}, u32[]{:S(2)}) collective-permute-start(f32[3,128,128]{2,1,0:T(8,128)S(1)} %get-tuple-element.62.part), channel_id=1, source_target_pairs={{0,1},{1,0},{2,3},{3,2},{4,5},{5,4},{6,7},{7,6},{8,9},{9,8},{10,11... | collective-permute-start | bytes 589832 | tf_op jit(solution)/shard_map/ppermute | solution.py:24
  74.4 7.2 %collective-permute-start.15 = (f32[3,128,128]{2,1,0:T(8,128)S(1)}, f32[3,128,128]{2,1,0:T(8,128)S(1)}, u32[]{:S(2)}, u32[]{:S(2)}) collective-permute-start(f32[3,128,128]{2,1,0:T(8,128)S(1)} %add.18), channel_id=1, source_target_pairs={{0,2},{1,3},{2,0},{3,1},{4,6},{5,7},{6,4},{7,5},{8,10},{9,11},{10,... | collective-permute-start | bytes 589832 | tf_op jit(solution)/shard_map/ppermute | solution.py:24
  76.0 23.2 %collective-permute-start.4 = (f32[1024,128]{1,0:T(8,128)S(1)}, f32[1024,128]{1,0:T(8,128)S(1)}, u32[]{:S(2)}, u32[]{:S(2)}) collective-permute-start(f32[1024,128]{1,0:T(8,128)S(1)} %get-tuple-element.53.sent0), channel_id=1, source_target_pairs={{0,4},{2,6},{4,8},{5,1},{6,10},{7,3},{8,12},{9,5},{10,14},{11,7},{... | collective-permute-start | bytes 1572872 | tf_op jit(solution)/shard_map/ppermute | solution.py:19
  80.1 19.0 %collective-permute-start.5 = (f32[1024,128]{1,0:T(8,128)S(1)}, f32[1024,128]{1,0:T(8,128)S(1)}, u32[]{:S(2)}, u32[]{:S(2)}) collective-permute-start(f32[1024,128]{1,0:T(8,128)S(1)} %get-tuple-element.54.sent1), channel_id=1, source_target_pairs={{1,5},{3,7},{4,0},{5,9},{6,2},{7,11},{8,4},{9,13},{10,6},{11,15},{... | collective-permute-start | bytes 1572872 | tf_op jit(solution)/shard_map/ppermute | solution.py:19
  85.2 6.6 %collective-permute-start.16 = (f32[3,128,128]{2,1,0:T(8,128)S(1)}, f32[3,128,128]{2,1,0:T(8,128)S(1)}, u32[]{:S(2)}, u32[]{:S(2)}) collective-permute-start(f32[3,128,128]{2,1,0:T(8,128)S(1)} %get-tuple-element.65.part), channel_id=1, source_target_pairs={{0,1},{1,0},{2,3},{3,2},{4,5},{5,4},{6,7},{7,6},{8,9},{9,8},{10,11... | collective-permute-start | bytes 589832 | tf_op jit(solution)/shard_map/ppermute | solution.py:24
  86.1 20.5 %collective-permute-start.2 = (f32[1024,128]{1,0:T(8,128)S(1)}, f32[1024,128]{1,0:T(8,128)S(1)}, u32[]{:S(2)}, u32[]{:S(2)}) collective-permute-start(f32[1024,128]{1,0:T(8,128)S(1)} %get-tuple-element.51.sent0), channel_id=1, source_target_pairs={{0,4},{2,6},{4,8},{5,1},{6,10},{7,3},{8,12},{9,5},{10,14},{11,7},{... | collective-permute-start | bytes 1572872 | tf_op jit(solution)/shard_map/ppermute | solution.py:19
  90.3 16.3 %collective-permute-start.3 = (f32[1024,128]{1,0:T(8,128)S(1)}, f32[1024,128]{1,0:T(8,128)S(1)}, u32[]{:S(2)}, u32[]{:S(2)}) collective-permute-start(f32[1024,128]{1,0:T(8,128)S(1)} %get-tuple-element.52.sent1), channel_id=1, source_target_pairs={{1,5},{3,7},{4,0},{5,9},{6,2},{7,11},{8,4},{9,13},{10,6},{11,15},{... | collective-permute-start | bytes 1572872 | tf_op jit(solution)/shard_map/ppermute | solution.py:19
  91.8 7.2 %collective-permute-start.17 = (f32[3,128,128]{2,1,0:T(8,128)S(1)}, f32[3,128,128]{2,1,0:T(8,128)S(1)}, u32[]{:S(2)}, u32[]{:S(2)}) collective-permute-start(f32[3,128,128]{2,1,0:T(8,128)S(1)} %add.20), channel_id=1, source_target_pairs={{0,2},{1,3},{2,0},{3,1},{4,6},{5,7},{6,4},{7,5},{8,10},{9,11},{10,... | collective-permute-start | bytes 589832 | tf_op jit(solution)/shard_map/ppermute | solution.py:24
  100.9 1.3 %collective-permute-start.18 = (f32[1,128,128]{2,1,0:T(8,128)S(1)}, f32[1,128,128]{2,1,0:T(8,128)S(1)}, u32[]{:S(2)}, u32[]{:S(2)}) collective-permute-start(f32[1,128,128]{2,1,0:T(8,128)S(1)} %get-tuple-element.75.part), channel_id=1, source_target_pairs={{0,1},{1,0},{2,3},{3,2},{4,5},{5,4},{6,7},{7,6},{8,9},{9,8},{10,11... | collective-permute-start | bytes 196616 | tf_op jit(solution)/shard_map/ppermute | solution.py:24
  102.3 4.3 %collective-permute-start.19 = (f32[1,128,128]{2,1,0:T(8,128)S(1)}, f32[1,128,128]{2,1,0:T(8,128)S(1)}, u32[]{:S(2)}, u32[]{:S(2)}) collective-permute-start(f32[1,128,128]{2,1,0:T(8,128)S(1)} %add.22), channel_id=1, source_target_pairs={{0,2},{1,3},{2,0},{3,1},{4,6},{5,7},{6,4},{7,5},{8,10},{9,11},{10,... | collective-permute-start | bytes 196616 | tf_op jit(solution)/shard_map/ppermute | solution.py:24
  108.4 3.8 %collective-permute-start.20 = (f32[1,128,128]{2,1,0:T(8,128)S(1)}, f32[1,128,128]{2,1,0:T(8,128)S(1)}, u32[]{:S(2)}, u32[]{:S(2)}) collective-permute-start(f32[1,128,128]{2,1,0:T(8,128)S(1)} %get-tuple-element.82.part0), channel_id=1, source_target_pairs={{0,1},{1,0},{2,3},{3,2},{4,5},{5,4},{6,7},{7,6},{8,9},{9,8},{10,11... | collective-permute-start | bytes 196616 | tf_op jit(solution)/shard_map/ppermute | solution.py:24
  108.5 4.5 %collective-permute-start.21 = (f32[1,128,128]{2,1,0:T(8,128)S(1)}, f32[1,128,128]{2,1,0:T(8,128)S(1)}, u32[]{:S(2)}, u32[]{:S(2)}) collective-permute-start(f32[1,128,128]{2,1,0:T(8,128)S(1)} %get-tuple-element.82.part0), channel_id=1, source_target_pairs={{0,2},{1,3},{2,0},{3,1},{4,6},{5,7},{6,4},{7,5},{8,10},{9,11},{10,... | collective-permute-start | bytes 196616 | tf_op jit(solution)/shard_map/ppermute | solution.py:24
  110.1 4.0 %collective-permute-start.22 = (f32[1,128,128]{2,1,0:T(8,128)S(1)}, f32[1,128,128]{2,1,0:T(8,128)S(1)}, u32[]{:S(2)}, u32[]{:S(2)}) collective-permute-start(f32[1,128,128]{2,1,0:T(8,128)S(1)} %get-tuple-element.82.part0), channel_id=1, source_target_pairs={{0,3},{1,2},{2,1},{3,0},{4,7},{5,6},{6,5},{7,4},{8,11},{9,10},{10,... | collective-permute-start | bytes 196616 | tf_op jit(solution)/shard_map/ppermute | solution.py:24
  116.0 1.9 %collective-permute-start.23 = (f32[1,8,128]{2,1,0:T(8,128)S(1)}, f32[1,8,128]{2,1,0:T(8,128)S(1)}, u32[]{:S(2)}, u32[]{:S(2)}) collective-permute-start(f32[1,8,128]{2,1,0:T(8,128)S(1)} %slice.41), channel_id=1, source_target_pairs={{0,1},{1,0},{2,3},{3,2},{4,5},{5,4},{6,7},{7,6},{8,9},{9,8},{10,11... | collective-permute-start | bytes 12296 | tf_op jit(solution)/shard_map/ppermute | solution.py:24
  116.3 3.6 %collective-permute-start.24 = (f32[1,8,128]{2,1,0:T(8,128)S(1)}, f32[1,8,128]{2,1,0:T(8,128)S(1)}, u32[]{:S(2)}, u32[]{:S(2)}) collective-permute-start(f32[1,8,128]{2,1,0:T(8,128)S(1)} %slice.41), channel_id=1, source_target_pairs={{0,2},{1,3},{2,0},{3,1},{4,6},{5,7},{6,4},{7,5},{8,10},{9,11},{10,... | collective-permute-start | bytes 12296 | tf_op jit(solution)/shard_map/ppermute | solution.py:24
  117.7 3.0 %collective-permute-start.25 = (f32[1,8,128]{2,1,0:T(8,128)S(1)}, f32[1,8,128]{2,1,0:T(8,128)S(1)}, u32[]{:S(2)}, u32[]{:S(2)}) collective-permute-start(f32[1,8,128]{2,1,0:T(8,128)S(1)} %slice.41), channel_id=1, source_target_pairs={{0,3},{1,2},{2,1},{3,0},{4,7},{5,6},{6,5},{7,4},{8,11},{9,10},{10,... | collective-permute-start | bytes 12296 | tf_op jit(solution)/shard_map/ppermute | solution.py:24

commit v4 on v3

--- a/solution.py
+++ b/solution.py
@@ -171,6 +171,11 @@
         copy.wait()
 
 
+def pick_kernel(begin, chunks, table, left_env, right_env, *refs):
+    for copy in pick(table, left_env, right_env, refs[:-1], refs[-1], begin, chunks):
+        copy.wait()
+
+
 def prepare_kernel(
     own, table, states, pieces, vec_out, middle_out, plain_out, left_out, right_out, back_out,
 ):
@@ -395,10 +400,10 @@
         pltpu.with_memory_space_constraint(value, pltpu.HBM) for value in values
     ]
     table, *opened = pl.pallas_call(
-        functools.partial(open_kernel, CHUNKS, parts),
+        functools.partial(open_kernel, CHUNKS[:1], parts),
         in_specs=[hbm] * 8,
-        out_specs=[smem] + [vmem] * (2 * len(CHUNKS)),
-        out_shape=[shape((HEAD + 5 * total + 2,), jnp.int32)] + chunks(range(len(CHUNKS))),
+        out_specs=[smem] + [vmem] * 2,
+        out_shape=[shape((HEAD + 5 * total + 2,), jnp.int32)] + chunks([0]),
         scratch_shapes=[
             pltpu.SMEM((1,), jnp.int32),
             pltpu.SMEM(sectors.shape, jnp.int32),
@@ -419,6 +424,17 @@
             left_tensor, right_tensor, left_env, right_env,
         )
     )
+    later = range(1, len(CHUNKS))
+    opened += pl.pallas_call(
+        functools.partial(pick_kernel, CHUNKS[0], CHUNKS[1:]),
+        in_specs=[smem] + [hbm] * 2,
+        out_specs=[vmem] * (2 * len(later)),
+        out_shape=chunks(later),
+        scratch_shapes=[dma((2, total))],
+        cost_estimate=small_cost,
+        compiler_params=params(16),
+        name="pick",
+    )(table, *in_hbm(left_env, right_env))
     sent = [tuple(opened[2 * c : 2 * c + 2]) for c in range(len(CHUNKS))]
     states = gather(state)
     sent[1], _ = lax.optimization_barrier((sent[1], states))

time: 123 us -> 121 us (0.984)
  waiting for transfers between devices: 48.8 us -> 45.8 us
  Pallas kernels: 29.6 us -> 31.3 us
    ppermute x18, waiting for transfers between devices: 27.3 us -> 24.2 us  [partner(): return lax.ppermute(block, 'sites', route)]
    pallas_call x1 -> x2, Pallas kernels: 5.33 us -> 6.85 us  [the longest x1 3.62 us: on_device(): pl.pallas_call(functools.partial(open_kernel, CHUNKS[:1], parts), in_spec...]
  transfers between devices with their start and end apart: 26 -> 26, of which waited for: 15 -> 15; matrix products, arithmetic and copies ran while one was open for 1% -> 1% of each run, Pallas kernels for 16% -> 19%
where the time goes in v4:
time: 121 us
  waiting for transfers between devices  45.8 us (38%)
  starting transfers between devices  39.5 us (33%)
  Pallas kernels  31.3 us (26%)
  between operations  3.08 us (3%)
    ppermute x18, waiting for transfers between devices, partner(): return lax.ppermute(block, 'sites', route)  24.2 us
    ppermute x8, starting transfers between devices, hand_over(): lax.ppermute(block, 'sites', [(i, j) for i, j in route if 0 <= j < count])  23.9 us
    ppermute x8, waiting for transfers between devices, hand_over(): lax.ppermute(block, 'sites', [(i, j) for i, j in route if 0 <= j < count])  21.7 us
    ppermute x18, starting transfers between devices, partner(): return lax.ppermute(block, 'sites', route)  15.6 us
    pallas_call x4, Pallas kernels, on_device(): pl.pallas_call(functools.partial(first_kernel, own, begin), in_specs=[sme...  11.1 us
    pallas_call x3, Pallas kernels, early(): pl.pallas_call(functools.partial(early_kernel, own, begin), in_specs=[sme...  6.88 us
    pallas_call x1, Pallas kernels, on_device(): pl.pallas_call(functools.partial(open_kernel, CHUNKS[:1], parts), in_spec...  3.62 us
    pallas_call x1, Pallas kernels, on_device(): pl.pallas_call(functools.partial(prepare_kernel, own), in_specs=[smem, vm...  3.33 us
  transfers between devices with their start and end apart: 26, of which 15 were waited for; matrix products, arithmetic and copies ran while one was open for 1% of the time, Pallas kernels for 19%

profile of v4, /device:TPU:0, one launch (start us, length us, event | category | flops | bytes accessed | tf_op | source)
XLA Modules:
  0.0 120.8 jit_solution(7284069086917666064)
XLA Ops:
  0.6 3.6 %open.1 = (s32[46]{0:T(128)S(1)}, f32[3336,128]{1,0:T(8,128)S(1)}, f32[3336,128]{1,0:T(8,128)S(1)}) custom-call(s32[1]{0:T(128)} %bitcast.place_hbm, s32[4,8]{1,0:T(4,128)} %sectors_hbm.1, s32[4,8]{1,0:T(4,128)} %flow_hbm.1, f32[8,8]{1,0:T(8,128)} %bond_hbm.1, f32[2,128,128]{2,1,0:T(8,128)} %left_tensor.1, f32[2,128,128]{2,1,0:T(8,128)} %right_tensor.1, ...), custom_call_target="tpu_custom_call" | custom-call | flops 1 | bytes 1 | tf_op jit(solution)/shard_map/open/pallas_call | solution.py:402
  5.6 5.7 %collective-permute-start.1 = (f32[3336,128]{1,0:T(8,128)S(1)}, f32[3336,128]{1,0:T(8,128)S(1)}, u32[]{:S(2)}, u32[]{:S(2)}) collective-permute-start(f32[3336,128]{1,0:T(8,128)S(1)} %get-tuple-element.50.sent0), channel_id=1, source_target_pairs={{0,4},{2,6},{4,8},{5,1},{6,10},{7,3},{8,12},{9,5},{10,14},{11,7},{... | collective-permute-start | bytes 5124104 | tf_op jit(solution)/shard_map/ppermute | solution.py:19
  11.3 2.0 %collective-permute-start.7 = (f32[2,128,128]{2,1,0:T(8,128)S(1)}, f32[2,128,128]{2,1,0:T(8,128)S(1)}, u32[]{:S(2)}, u32[]{:S(2)}) collective-permute-start(f32[2,128,128]{2,1,0:T(8,128)S(1)} %copy-done.1), channel_id=1, source_target_pairs={{0,2},{1,3},{2,0},{3,1},{4,6},{5,7},{6,4},{7,5},{8,10},{9,11},{10,... | collective-permute-start | bytes 393224 | tf_op jit(solution)/shard_map/ppermute | solution.py:24
  13.4 3.2 %pick.1 = (f32[3072,128]{1,0:T(8,128)S(1)}, f32[3072,128]{1,0:T(8,128)S(1)}, f32[1024,128]{1,0:T(8,128)S(1)}, f32[1024,128]{1,0:T(8,128)S(1)}, f32[1024,128]{1,0:T(8,128)S(1)}, /*index=5*/f32[1024,128]{1,0:T(8,128)S(1)}) custom-call(s32[46]{0:T(128)S(1)} %get-tuple-element.48.table, f32[8,8,128,128]{3,2,1,0:T(8,128)} %left_env.3, f32[8,8,128,128]{3,2,1,0:T(8,128)} %right_env.3), custom_call_target="tpu_custom_call" | custom-call | flops 1 | bytes 1 | tf_op jit(solution)/shard_map/pick/pallas_call | solution.py:428
  17.8 2.2 %collective-permute-done.8 = f32[2,128,128]{2,1,0:T(8,128)S(1)} collective-permute-done((f32[2,128,128]{2,1,0:T(8,128)S(1)}, f32[2,128,128]{2,1,0:T(8,128)S(1)}, u32[]{:S(2)}, u32[]{:S(2)}) %collective-permute-start.8) | collective-permute-done | bytes 131104 | tf_op jit(solution)/shard_map/ppermute | solution.py:24
  20.0 1.3 %collective-permute-start.10 = (f32[3072,128]{1,0:T(8,128)S(1)}, f32[3072,128]{1,0:T(8,128)S(1)}, u32[]{:S(2)}, u32[]{:S(2)}) collective-permute-start(f32[3072,128]{1,0:T(8,128)S(1)} %get-tuple-element.58.sent1), channel_id=1, source_target_pairs={{1,5},{3,7},{4,0},{5,9},{6,2},{7,11},{8,4},{9,13},{10,6},{11,15},{... | collective-permute-start | bytes 4718600 | tf_op jit(solution)/shard_map/ppermute | solution.py:19
  21.3 4.6 %collective-permute-start.9 = (f32[3072,128]{1,0:T(8,128)S(1)}, f32[3072,128]{1,0:T(8,128)S(1)}, u32[]{:S(2)}, u32[]{:S(2)}) collective-permute-start(f32[3072,128]{1,0:T(8,128)S(1)} %get-tuple-element.57.sent0), channel_id=1, source_target_pairs={{0,4},{2,6},{4,8},{5,1},{6,10},{7,3},{8,12},{9,5},{10,14},{11,7},{... | collective-permute-start | bytes 4718600 | tf_op jit(solution)/shard_map/ppermute | solution.py:19
  27.2 17.4 %collective-permute-done.got1 = f32[3336,128]{1,0:T(8,128)S(1)} collective-permute-done((f32[3336,128]{1,0:T(8,128)S(1)}, f32[3336,128]{1,0:T(8,128)S(1)}, u32[]{:S(2)}, u32[]{:S(2)}) %collective-permute-start) | collective-permute-done | bytes 1708064 | tf_op jit(solution)/shard_map/ppermute | solution.py:19
  44.6 4.3 %collective-permute-done.1.got0 = f32[3336,128]{1,0:T(8,128)S(1)} collective-permute-done((f32[3336,128]{1,0:T(8,128)S(1)}, f32[3336,128]{1,0:T(8,128)S(1)}, u32[]{:S(2)}, u32[]{:S(2)}) %collective-permute-start.1) | collective-permute-done | bytes 1708064 | tf_op jit(solution)/shard_map/ppermute | solution.py:19
  49.0 1.4 %collective-permute-start.11 = (f32[2,2,128,128]{3,2,1,0:T(8,128)S(1)}, f32[2,2,128,128]{3,2,1,0:T(8,128)S(1)}, u32[]{:S(2)}, u32[]{:S(2)}) collective-permute-start(f32[2,2,128,128]{3,2,1,0:T(8,128)S(1)} %get-tuple-element.97), channel_id=1, source_target_pairs={{0,1},{1,0},{2,3},{3,2},{4,5},{5,4},{6,7},{7,6},{8,9},{9,8},{10,11... | collective-permute-start | bytes 786440 | tf_op jit(solution)/shard_map/ppermute | solution.py:24
  50.4 1.5 %collective-permute-start.12 = (f32[2,2,128,128]{3,2,1,0:T(8,128)S(1)}, f32[2,2,128,128]{3,2,1,0:T(8,128)S(1)}, u32[]{:S(2)}, u32[]{:S(2)}) collective-permute-start(f32[2,2,128,128]{3,2,1,0:T(8,128)S(1)} %get-tuple-element.97), channel_id=1, source_target_pairs={{0,2},{1,3},{2,0},{3,1},{4,6},{5,7},{6,4},{7,5},{8,10},{9,11},{10,... | collective-permute-start | bytes 786440 | tf_op jit(solution)/shard_map/ppermute | solution.py:24
  53.2 6.3 %collective-permute-done.12 = f32[2,2,128,128]{3,2,1,0:T(8,128)S(1)} collective-permute-done((f32[2,2,128,128]{3,2,1,0:T(8,128)S(1)}, f32[2,2,128,128]{3,2,1,0:T(8,128)S(1)}, u32[]{:S(2)}, u32[]{:S(2)}) %collective-permute-start.12) | collective-permute-done | bytes 262176 | tf_op jit(solution)/shard_map/ppermute | solution.py:24
  59.5 3.9 %collective-permute-done.13 = f32[2,2,128,128]{3,2,1,0:T(8,128)S(1)} collective-permute-done((f32[2,2,128,128]{3,2,1,0:T(8,128)S(1)}, f32[2,2,128,128]{3,2,1,0:T(8,128)S(1)}, u32[]{:S(2)}, u32[]{:S(2)}) %collective-permute-start.13) | collective-permute-done | bytes 262176 | tf_op jit(solution)/shard_map/ppermute | solution.py:24
  63.5 3.3 %prepare.1 = (f32[8,128,128]{2,1,0:T(8,128)S(1)}, bf16[8,256,256]{2,1,0:T(8,128)(2,1)S(1)}, f32[8,128,128]{2,1,0:T(8,128)S(1)}, bf16[8,128,256]{2,1,0:T(8,128)(2...) custom-call(s32[46]{0:T(128)S(1)} %get-tuple-element.48.table, ...), custom_call_target="tpu_custom_call" | custom-call | flops 1 | bytes 1 | tf_op jit(solution)/shard_map/prepare/pallas_call | solution.py:453
  66.9 3.8 %first_matvec0.1 = (bf16[3,1024,256]{2,1,0:T(8,128)(2,1)S(1)}, bf16[3,1024,256]{2,1,0:T(8,128)(2,1)S(1)}, f32[3,128,128]{2,1,0:T(8,128)S(1)}) custom-call(s32[46]{0:T(128)S(1)} %get-tuple-element.48.table, f32[8,8]{1,0:T(8,128)S(1)} %multiply_reduce_fusion.bond, f32[3336,128]{1,0:T(8,128)S(1)} %collective-permute-done.1.got0, ...), custom_call_target="tpu_custom_call" | custom-call | flops 1 | bytes 1 | tf_op jit(solution)/shard_map/first_matvec0/pallas_call | solution.py:487
  72.8 1.6 %collective-permute-start.15 = (f32[3,128,128]{2,1,0:T(8,128)S(1)}, f32[3,128,128]{2,1,0:T(8,128)S(1)}, u32[]{:S(2)}, u32[]{:S(2)}) collective-permute-start(f32[3,128,128]{2,1,0:T(8,128)S(1)} %add.18), channel_id=1, source_target_pairs={{0,2},{1,3},{2,0},{3,1},{4,6},{5,7},{6,4},{7,5},{8,10},{9,11},{10,... | collective-permute-start | bytes 589832 | tf_op jit(solution)/shard_map/ppermute | solution.py:24
  74.4 4.0 %collective-permute-start.4 = (f32[1024,128]{1,0:T(8,128)S(1)}, f32[1024,128]{1,0:T(8,128)S(1)}, u32[]{:S(2)}, u32[]{:S(2)}) collective-permute-start(f32[1024,128]{1,0:T(8,128)S(1)} %get-tuple-element.53.sent0), channel_id=1, source_target_pairs={{0,4},{2,6},{4,8},{5,1},{6,10},{7,3},{8,12},{9,5},{10,14},{11,7},{... | collective-permute-start | bytes 1572872 | tf_op jit(solution)/shard_map/ppermute | solution.py:19
  80.1 3.7 %first_matvec1.1 = (bf16[3,1024,256]{2,1,0:T(8,128)(2,1)S(1)}, bf16[3,1024,256]{2,1,0:T(8,128)(2,1)S(1)}, f32[3,128,128]{2,1,0:T(8,128)S(1)}) custom-call(s32[46]{0:T(128)S(1)} %get-tuple-element.48.table, f32[8,8]{1,0:T(8,128)S(1)} %multiply_reduce_fusion.bond, f32[3072,128]{1,0:T(8,128)S(1)} %collective-permute-done.9.got0, ...), custom_call_target="tpu_custom_call" | custom-call | flops 1 | bytes 1 | tf_op jit(solution)/shard_map/first_matvec1/pallas_call | solution.py:487
  84.6 4.2 %collective-permute-start.2 = (f32[1024,128]{1,0:T(8,128)S(1)}, f32[1024,128]{1,0:T(8,128)S(1)}, u32[]{:S(2)}, u32[]{:S(2)}) collective-permute-start(f32[1024,128]{1,0:T(8,128)S(1)} %get-tuple-element.51.sent0), channel_id=1, source_target_pairs={{0,4},{2,6},{4,8},{5,1},{6,10},{7,3},{8,12},{9,5},{10,14},{11,7},{... | collective-permute-start | bytes 1572872 | tf_op jit(solution)/shard_map/ppermute | solution.py:19
  88.8 1.5 %collective-permute-start.3 = (f32[1024,128]{1,0:T(8,128)S(1)}, f32[1024,128]{1,0:T(8,128)S(1)}, u32[]{:S(2)}, u32[]{:S(2)}) collective-permute-start(f32[1024,128]{1,0:T(8,128)S(1)} %get-tuple-element.52.sent1), channel_id=1, source_target_pairs={{1,5},{3,7},{4,0},{5,9},{6,2},{7,11},{8,4},{9,13},{10,6},{11,15},{... | collective-permute-start | bytes 1572872 | tf_op jit(solution)/shard_map/ppermute | solution.py:19
  90.4 1.6 %collective-permute-start.17 = (f32[3,128,128]{2,1,0:T(8,128)S(1)}, f32[3,128,128]{2,1,0:T(8,128)S(1)}, u32[]{:S(2)}, u32[]{:S(2)}) collective-permute-start(f32[3,128,128]{2,1,0:T(8,128)S(1)} %add.20), channel_id=1, source_target_pairs={{0,2},{1,3},{2,0},{3,1},{4,6},{5,7},{6,4},{7,5},{8,10},{9,11},{10,... | collective-permute-start | bytes 589832 | tf_op jit(solution)/shard_map/ppermute | solution.py:24
  92.0 2.5 %early_second_matvec.3 = (f32[3,128,128]{2,1,0:T(8,128)S(1)}, f32[8,8,128]{2,1,0:T(8,128)S(1)}) custom-call(s32[46]{0:T(128)S(1)} %get-tuple-element.48.table, f32[3,128,128]{2,1,0:T(8,128)S(1)} %add.19.image, f32[3,128,128]{2,1,0:T(8,128)S(1)} %get-tuple-element.62.part, f32[8,128,128]{2,1,0:T(8,128)S(1)} %get-tuple-element.60.vec, ...), custom_call_target="tpu_custom_call" | custom-call | flops 1 | bytes 1 | tf_op jit(solution)/shard_map/early_second_matvec/pallas_call | solution.py:472
  94.5 3.1 %collective-permute-done.17 = f32[3,128,128]{2,1,0:T(8,128)S(1)} collective-permute-done((f32[3,128,128]{2,1,0:T(8,128)S(1)}, f32[3,128,128]{2,1,0:T(8,128)S(1)}, u32[]{:S(2)}, u32[]{:S(2)}) %collective-permute-start.17) | collective-permute-done | bytes 196640 | tf_op jit(solution)/shard_map/ppermute | solution.py:24
  97.7 1.8 %first_matvec2.1 = (bf16[1,1024,256]{2,1,0:T(8,128)(2,1)S(1)}, bf16[1,1024,256]{2,1,0:T(8,128)(2,1)S(1)}, f32[1,128,128]{2,1,0:T(8,128)S(1)}) custom-call(s32[46]{0:T(128)S(1)} %get-tuple-element.48.table, f32[8,8]{1,0:T(8,128)S(1)} %multiply_reduce_fusion.bond, f32[1024,128]{1,0:T(8,128)S(1)} %collective-permute-done.4.got0, ...), custom_call_target="tpu_custom_call" | custom-call | flops 1 | bytes 1 | tf_op jit(solution)/shard_map/first_matvec2/pallas_call | solution.py:487
  100.8 1.6 %collective-permute-start.19 = (f32[1,128,128]{2,1,0:T(8,128)S(1)}, f32[1,128,128]{2,1,0:T(8,128)S(1)}, u32[]{:S(2)}, u32[]{:S(2)}) collective-permute-start(f32[1,128,128]{2,1,0:T(8,128)S(1)} %add.22), channel_id=1, source_target_pairs={{0,2},{1,3},{2,0},{3,1},{4,6},{5,7},{6,4},{7,5},{8,10},{9,11},{10,... | collective-permute-start | bytes 196616 | tf_op jit(solution)/shard_map/ppermute | solution.py:24
  102.4 2.5 %early_second_matvec.4 = (f32[3,128,128]{2,1,0:T(8,128)S(1)}, f32[8,8,128]{2,1,0:T(8,128)S(1)}) custom-call(s32[46]{0:T(128)S(1)} %get-tuple-element.48.table, f32[3,128,128]{2,1,0:T(8,128)S(1)} %add.21.image, f32[3,128,128]{2,1,0:T(8,128)S(1)} %get-tuple-element.65.part, f32[8,128,128]{2,1,0:T(8,128)S(1)} %get-tuple-element.60.vec, ...), custom_call_target="tpu_custom_call" | custom-call | flops 1 | bytes 1 | tf_op jit(solution)/shard_map/early_second_matvec/pallas_call | solution.py:472
  105.2 1.8 %first_matvec3.1 = (bf16[1,1024,256]{2,1,0:T(8,128)(2,1)S(1)}, bf16[1,1024,256]{2,1,0:T(8,128)(2,1)S(1)}, f32[1,128,128]{2,1,0:T(8,128)S(1)}) custom-call(s32[46]{0:T(128)S(1)} %get-tuple-element.48.table, f32[8,8]{1,0:T(8,128)S(1)} %multiply_reduce_fusion.bond, f32[1024,128]{1,0:T(8,128)S(1)} %collective-permute-done.2.got0, ...), custom_call_target="tpu_custom_call" | custom-call | flops 1 | bytes 1 | tf_op jit(solution)/shard_map/first_matvec3/pallas_call | solution.py:487
  107.1 1.6 %collective-permute-start.21 = (f32[1,128,128]{2,1,0:T(8,128)S(1)}, f32[1,128,128]{2,1,0:T(8,128)S(1)}, u32[]{:S(2)}, u32[]{:S(2)}) collective-permute-start(f32[1,128,128]{2,1,0:T(8,128)S(1)} %get-tuple-element.82.part0), channel_id=1, source_target_pairs={{0,2},{1,3},{2,0},{3,1},{4,6},{5,7},{6,4},{7,5},{8,10},{9,11},{10,... | collective-permute-start | bytes 196616 | tf_op jit(solution)/shard_map/ppermute | solution.py:24
  109.0 1.9 %early_second_matvec.5 = (f32[1,128,128]{2,1,0:T(8,128)S(1)}, f32[8,8,128]{2,1,0:T(8,128)S(1)}) custom-call(s32[46]{0:T(128)S(1)} %get-tuple-element.48.table, f32[1,128,128]{2,1,0:T(8,128)S(1)} %add.23.image, f32[1,128,128]{2,1,0:T(8,128)S(1)} %get-tuple-element.75.part, f32[8,128,128]{2,1,0:T(8,128)S(1)} %get-tuple-element.60.vec, ...), custom_call_target="tpu_custom_call" | custom-call | flops 1 | bytes 1 | tf_op jit(solution)/shard_map/early_second_matvec/pallas_call | solution.py:472
  112.7 1.9 %second_matvec.1 = (f32[2,128,128]{2,1,0:T(8,128)S(1)}, f32[3,8,128]{2,1,0:T(8,128)S(1)}) custom-call(s32[46]{0:T(128)S(1)} %get-tuple-element.48.table, f32[1,128,128]{2,1,0:T(8,128)S(1)} %get-tuple-element.82.part0, f32[1,128,128]{2,1,0:T(8,128)S(1)} %collective-permute-done.20.part1, f32[1,128,128]{2,1,0:T(8,128)S(1)} %collective-permute-done.21.part2, ...), custom_call_target="tpu_custom_call" | custom-call | flops 1 | bytes 1 | tf_op jit(solution)/shard_map/second_matvec/pallas_call | solution.py:510
  114.9 1.5 %collective-permute-start.24 = (f32[1,8,128]{2,1,0:T(8,128)S(1)}, f32[1,8,128]{2,1,0:T(8,128)S(1)}, u32[]{:S(2)}, u32[]{:S(2)}) collective-permute-start(f32[1,8,128]{2,1,0:T(8,128)S(1)} %slice.41), channel_id=1, source_target_pairs={{0,2},{1,3},{2,0},{3,1},{4,6},{5,7},{6,4},{7,5},{8,10},{9,11},{10,... | collective-permute-start | bytes 12296 | tf_op jit(solution)/shard_map/ppermute | solution.py:24
  116.6 1.9 %collective-permute-done.24.share2 = f32[1,8,128]{2,1,0:T(8,128)S(1)} collective-permute-done((f32[1,8,128]{2,1,0:T(8,128)S(1)}, f32[1,8,128]{2,1,0:T(8,128)S(1)}, u32[]{:S(2)}, u32[]{:S(2)}) %collective-permute-start.24) | collective-permute-done | bytes 4128 | tf_op jit(solution)/shard_map/ppermute | solution.py:24
  (52 shorter events, 14.6 us)
Async XLA Ops:
  0.6 10.6 %copy-start.1 = (f32[2,128,128]{2,1,0:T(8,128)S(1)}, f32[2,128,128]{2,1,0:T(8,128)}, u32[]{:S(2)}) copy-start(f32[2,128,128]{2,1,0:T(8,128)} %param.9) | copy-start | bytes 393220
  4.3 40.3 %collective-permute-start = (f32[3336,128]{1,0:T(8,128)S(1)}, f32[3336,128]{1,0:T(8,128)S(1)}, u32[]{:S(2)}, u32[]{:S(2)}) collective-permute-start(f32[3336,128]{1,0:T(8,128)S(1)} %get-tuple-element.49.sent1), channel_id=1, source_target_pairs={{1,5},{3,7},{4,0},{5,9},{6,2},{7,11},{8,4},{9,13},{10,6},{11,15},{... | collective-permute-start | bytes 5124104 | tf_op jit(solution)/shard_map/ppermute | solution.py:19
  5.6 43.3 %collective-permute-start.1 = (f32[3336,128]{1,0:T(8,128)S(1)}, f32[3336,128]{1,0:T(8,128)S(1)}, u32[]{:S(2)}, u32[]{:S(2)}) collective-permute-start(f32[3336,128]{1,0:T(8,128)S(1)} %get-tuple-element.50.sent0), channel_id=1, source_target_pairs={{0,4},{2,6},{4,8},{5,1},{6,10},{7,3},{8,12},{9,5},{10,14},{11,7},{... | collective-permute-start | bytes 5124104 | tf_op jit(solution)/shard_map/ppermute | solution.py:19
  11.3 5.4 %collective-permute-start.6 = (f32[2,128,128]{2,1,0:T(8,128)S(1)}, f32[2,128,128]{2,1,0:T(8,128)S(1)}, u32[]{:S(2)}, u32[]{:S(2)}) collective-permute-start(f32[2,128,128]{2,1,0:T(8,128)S(1)} %copy-done.1), channel_id=1, source_target_pairs={{0,1},{1,0},{2,3},{3,2},{4,5},{5,4},{6,7},{7,6},{8,9},{9,8},{10,11... | collective-permute-start | bytes 393224 | tf_op jit(solution)/shard_map/ppermute | solution.py:24
  11.3 6.4 %collective-permute-start.7 = (f32[2,128,128]{2,1,0:T(8,128)S(1)}, f32[2,128,128]{2,1,0:T(8,128)S(1)}, u32[]{:S(2)}, u32[]{:S(2)}) collective-permute-start(f32[2,128,128]{2,1,0:T(8,128)S(1)} %copy-done.1), channel_id=1, source_target_pairs={{0,2},{1,3},{2,0},{3,1},{4,6},{5,7},{6,4},{7,5},{8,10},{9,11},{10,... | collective-permute-start | bytes 393224 | tf_op jit(solution)/shard_map/ppermute | solution.py:24
  13.4 6.6 %collective-permute-start.8 = (f32[2,128,128]{2,1,0:T(8,128)S(1)}, f32[2,128,128]{2,1,0:T(8,128)S(1)}, u32[]{:S(2)}, u32[]{:S(2)}) collective-permute-start(f32[2,128,128]{2,1,0:T(8,128)S(1)} %copy-done.1), channel_id=1, source_target_pairs={{0,3},{1,2},{2,1},{3,0},{4,7},{5,6},{6,5},{7,4},{8,11},{9,10},{10,... | collective-permute-start | bytes 393224 | tf_op jit(solution)/shard_map/ppermute | solution.py:24
  20.0 60.1 %collective-permute-start.10 = (f32[3072,128]{1,0:T(8,128)S(1)}, f32[3072,128]{1,0:T(8,128)S(1)}, u32[]{:S(2)}, u32[]{:S(2)}) collective-permute-start(f32[3072,128]{1,0:T(8,128)S(1)} %get-tuple-element.58.sent1), channel_id=1, source_target_pairs={{1,5},{3,7},{4,0},{5,9},{6,2},{7,11},{8,4},{9,13},{10,6},{11,15},{... | collective-permute-start | bytes 4718600 | tf_op jit(solution)/shard_map/ppermute | solution.py:19
  21.3 58.9 %collective-permute-start.9 = (f32[3072,128]{1,0:T(8,128)S(1)}, f32[3072,128]{1,0:T(8,128)S(1)}, u32[]{:S(2)}, u32[]{:S(2)}) collective-permute-start(f32[3072,128]{1,0:T(8,128)S(1)} %get-tuple-element.57.sent0), channel_id=1, source_target_pairs={{0,4},{2,6},{4,8},{5,1},{6,10},{7,3},{8,12},{9,5},{10,14},{11,7},{... | collective-permute-start | bytes 4718600 | tf_op jit(solution)/shard_map/ppermute | solution.py:19
  49.0 4.2 %collective-permute-start.11 = (f32[2,2,128,128]{3,2,1,0:T(8,128)S(1)}, f32[2,2,128,128]{3,2,1,0:T(8,128)S(1)}, u32[]{:S(2)}, u32[]{:S(2)}) collective-permute-start(f32[2,2,128,128]{3,2,1,0:T(8,128)S(1)} %get-tuple-element.97), channel_id=1, source_target_pairs={{0,1},{1,0},{2,3},{3,2},{4,5},{5,4},{6,7},{7,6},{8,9},{9,8},{10,11... | collective-permute-start | bytes 786440 | tf_op jit(solution)/shard_map/ppermute | solution.py:24
  50.4 9.2 %collective-permute-start.12 = (f32[2,2,128,128]{3,2,1,0:T(8,128)S(1)}, f32[2,2,128,128]{3,2,1,0:T(8,128)S(1)}, u32[]{:S(2)}, u32[]{:S(2)}) collective-permute-start(f32[2,2,128,128]{3,2,1,0:T(8,128)S(1)} %get-tuple-element.97), channel_id=1, source_target_pairs={{0,2},{1,3},{2,0},{3,1},{4,6},{5,7},{6,4},{7,5},{8,10},{9,11},{10,... | collective-permute-start | bytes 786440 | tf_op jit(solution)/shard_map/ppermute | solution.py:24
  51.9 11.5 %collective-permute-start.13 = (f32[2,2,128,128]{3,2,1,0:T(8,128)S(1)}, f32[2,2,128,128]{3,2,1,0:T(8,128)S(1)}, u32[]{:S(2)}, u32[]{:S(2)}) collective-permute-start(f32[2,2,128,128]{3,2,1,0:T(8,128)S(1)} %get-tuple-element.97), channel_id=1, source_target_pairs={{0,3},{1,2},{2,1},{3,0},{4,7},{5,6},{6,5},{7,4},{8,11},{9,10},{10,... | collective-permute-start | bytes 786440 | tf_op jit(solution)/shard_map/ppermute | solution.py:24
  63.4 3.5 %copy-start = (f32[2,128,128]{2,1,0:T(8,128)S(1)}, f32[2,128,128]{2,1,0:T(8,128)}, u32[]{:S(2)}) copy-start(f32[2,128,128]{2,1,0:T(8,128)} %onsite.15) | copy-start | bytes 393220
  70.7 2.1 %collective-permute-start.14 = (f32[3,128,128]{2,1,0:T(8,128)S(1)}, f32[3,128,128]{2,1,0:T(8,128)S(1)}, u32[]{:S(2)}, u32[]{:S(2)}) collective-permute-start(f32[3,128,128]{2,1,0:T(8,128)S(1)} %get-tuple-element.62.part), channel_id=1, source_target_pairs={{0,1},{1,0},{2,3},{3,2},{4,5},{5,4},{6,7},{7,6},{8,9},{9,8},{10,11... | collective-permute-start | bytes 589832 | tf_op jit(solution)/shard_map/ppermute | solution.py:24
  72.8 7.2 %collective-permute-start.15 = (f32[3,128,128]{2,1,0:T(8,128)S(1)}, f32[3,128,128]{2,1,0:T(8,128)S(1)}, u32[]{:S(2)}, u32[]{:S(2)}) collective-permute-start(f32[3,128,128]{2,1,0:T(8,128)S(1)} %add.18), channel_id=1, source_target_pairs={{0,2},{1,3},{2,0},{3,1},{4,6},{5,7},{6,4},{7,5},{8,10},{9,11},{10,... | collective-permute-start | bytes 589832 | tf_op jit(solution)/shard_map/ppermute | solution.py:24
  74.4 23.2 %collective-permute-start.4 = (f32[1024,128]{1,0:T(8,128)S(1)}, f32[1024,128]{1,0:T(8,128)S(1)}, u32[]{:S(2)}, u32[]{:S(2)}) collective-permute-start(f32[1024,128]{1,0:T(8,128)S(1)} %get-tuple-element.53.sent0), channel_id=1, source_target_pairs={{0,4},{2,6},{4,8},{5,1},{6,10},{7,3},{8,12},{9,5},{10,14},{11,7},{... | collective-permute-start | bytes 1572872 | tf_op jit(solution)/shard_map/ppermute | solution.py:19
  78.4 19.2 %collective-permute-start.5 = (f32[1024,128]{1,0:T(8,128)S(1)}, f32[1024,128]{1,0:T(8,128)S(1)}, u32[]{:S(2)}, u32[]{:S(2)}) collective-permute-start(f32[1024,128]{1,0:T(8,128)S(1)} %get-tuple-element.54.sent1), channel_id=1, source_target_pairs={{1,5},{3,7},{4,0},{5,9},{6,2},{7,11},{8,4},{9,13},{10,6},{11,15},{... | collective-permute-start | bytes 1572872 | tf_op jit(solution)/shard_map/ppermute | solution.py:19
  83.8 6.5 %collective-permute-start.16 = (f32[3,128,128]{2,1,0:T(8,128)S(1)}, f32[3,128,128]{2,1,0:T(8,128)S(1)}, u32[]{:S(2)}, u32[]{:S(2)}) collective-permute-start(f32[3,128,128]{2,1,0:T(8,128)S(1)} %get-tuple-element.65.part), channel_id=1, source_target_pairs={{0,1},{1,0},{2,3},{3,2},{4,5},{5,4},{6,7},{7,6},{8,9},{9,8},{10,11... | collective-permute-start | bytes 589832 | tf_op jit(solution)/shard_map/ppermute | solution.py:24
  84.6 20.6 %collective-permute-start.2 = (f32[1024,128]{1,0:T(8,128)S(1)}, f32[1024,128]{1,0:T(8,128)S(1)}, u32[]{:S(2)}, u32[]{:S(2)}) collective-permute-start(f32[1024,128]{1,0:T(8,128)S(1)} %get-tuple-element.51.sent0), channel_id=1, source_target_pairs={{0,4},{2,6},{4,8},{5,1},{6,10},{7,3},{8,12},{9,5},{10,14},{11,7},{... | collective-permute-start | bytes 1572872 | tf_op jit(solution)/shard_map/ppermute | solution.py:19
  88.8 16.3 %collective-permute-start.3 = (f32[1024,128]{1,0:T(8,128)S(1)}, f32[1024,128]{1,0:T(8,128)S(1)}, u32[]{:S(2)}, u32[]{:S(2)}) collective-permute-start(f32[1024,128]{1,0:T(8,128)S(1)} %get-tuple-element.52.sent1), channel_id=1, source_target_pairs={{1,5},{3,7},{4,0},{5,9},{6,2},{7,11},{8,4},{9,13},{10,6},{11,15},{... | collective-permute-start | bytes 1572872 | tf_op jit(solution)/shard_map/ppermute | solution.py:19
  90.4 7.2 %collective-permute-start.17 = (f32[3,128,128]{2,1,0:T(8,128)S(1)}, f32[3,128,128]{2,1,0:T(8,128)S(1)}, u32[]{:S(2)}, u32[]{:S(2)}) collective-permute-start(f32[3,128,128]{2,1,0:T(8,128)S(1)} %add.20), channel_id=1, source_target_pairs={{0,2},{1,3},{2,0},{3,1},{4,6},{5,7},{6,4},{7,5},{8,10},{9,11},{10,... | collective-permute-start | bytes 589832 | tf_op jit(solution)/shard_map/ppermute | solution.py:24
  99.5 1.3 %collective-permute-start.18 = (f32[1,128,128]{2,1,0:T(8,128)S(1)}, f32[1,128,128]{2,1,0:T(8,128)S(1)}, u32[]{:S(2)}, u32[]{:S(2)}) collective-permute-start(f32[1,128,128]{2,1,0:T(8,128)S(1)} %get-tuple-element.75.part), channel_id=1, source_target_pairs={{0,1},{1,0},{2,3},{3,2},{4,5},{5,4},{6,7},{7,6},{8,9},{9,8},{10,11... | collective-permute-start | bytes 196616 | tf_op jit(solution)/shard_map/ppermute | solution.py:24
  100.8 4.3 %collective-permute-start.19 = (f32[1,128,128]{2,1,0:T(8,128)S(1)}, f32[1,128,128]{2,1,0:T(8,128)S(1)}, u32[]{:S(2)}, u32[]{:S(2)}) collective-permute-start(f32[1,128,128]{2,1,0:T(8,128)S(1)} %add.22), channel_id=1, source_target_pairs={{0,2},{1,3},{2,0},{3,1},{4,6},{5,7},{6,4},{7,5},{8,10},{9,11},{10,... | collective-permute-start | bytes 196616 | tf_op jit(solution)/shard_map/ppermute | solution.py:24
  107.0 3.8 %collective-permute-start.20 = (f32[1,128,128]{2,1,0:T(8,128)S(1)}, f32[1,128,128]{2,1,0:T(8,128)S(1)}, u32[]{:S(2)}, u32[]{:S(2)}) collective-permute-start(f32[1,128,128]{2,1,0:T(8,128)S(1)} %get-tuple-element.82.part0), channel_id=1, source_target_pairs={{0,1},{1,0},{2,3},{3,2},{4,5},{5,4},{6,7},{7,6},{8,9},{9,8},{10,11... | collective-permute-start | bytes 196616 | tf_op jit(solution)/shard_map/ppermute | solution.py:24
  107.1 4.5 %collective-permute-start.21 = (f32[1,128,128]{2,1,0:T(8,128)S(1)}, f32[1,128,128]{2,1,0:T(8,128)S(1)}, u32[]{:S(2)}, u32[]{:S(2)}) collective-permute-start(f32[1,128,128]{2,1,0:T(8,128)S(1)} %get-tuple-element.82.part0), channel_id=1, source_target_pairs={{0,2},{1,3},{2,0},{3,1},{4,6},{5,7},{6,4},{7,5},{8,10},{9,11},{10,... | collective-permute-start | bytes 196616 | tf_op jit(solution)/shard_map/ppermute | solution.py:24
  108.7 4.0 %collective-permute-start.22 = (f32[1,128,128]{2,1,0:T(8,128)S(1)}, f32[1,128,128]{2,1,0:T(8,128)S(1)}, u32[]{:S(2)}, u32[]{:S(2)}) collective-permute-start(f32[1,128,128]{2,1,0:T(8,128)S(1)} %get-tuple-element.82.part0), channel_id=1, source_target_pairs={{0,3},{1,2},{2,1},{3,0},{4,7},{5,6},{6,5},{7,4},{8,11},{9,10},{10,... | collective-permute-start | bytes 196616 | tf_op jit(solution)/shard_map/ppermute | solution.py:24
  114.7 1.9 %collective-permute-start.23 = (f32[1,8,128]{2,1,0:T(8,128)S(1)}, f32[1,8,128]{2,1,0:T(8,128)S(1)}, u32[]{:S(2)}, u32[]{:S(2)}) collective-permute-start(f32[1,8,128]{2,1,0:T(8,128)S(1)} %slice.41), channel_id=1, source_target_pairs={{0,1},{1,0},{2,3},{3,2},{4,5},{5,4},{6,7},{7,6},{8,9},{9,8},{10,11... | collective-permute-start | bytes 12296 | tf_op jit(solution)/shard_map/ppermute | solution.py:24
  114.9 3.6 %collective-permute-start.24 = (f32[1,8,128]{2,1,0:T(8,128)S(1)}, f32[1,8,128]{2,1,0:T(8,128)S(1)}, u32[]{:S(2)}, u32[]{:S(2)}) collective-permute-start(f32[1,8,128]{2,1,0:T(8,128)S(1)} %slice.41), channel_id=1, source_target_pairs={{0,2},{1,3},{2,0},{3,1},{4,6},{5,7},{6,4},{7,5},{8,10},{9,11},{10,... | collective-permute-start | bytes 12296 | tf_op jit(solution)/shard_map/ppermute | solution.py:24
  116.3 3.0 %collective-permute-start.25 = (f32[1,8,128]{2,1,0:T(8,128)S(1)}, f32[1,8,128]{2,1,0:T(8,128)S(1)}, u32[]{:S(2)}, u32[]{:S(2)}) collective-permute-start(f32[1,8,128]{2,1,0:T(8,128)S(1)} %slice.41), channel_id=1, source_target_pairs={{0,3},{1,2},{2,1},{3,0},{4,7},{5,6},{6,5},{7,4},{8,11},{9,10},{10,... | collective-permute-start | bytes 12296 | tf_op jit(solution)/shard_map/ppermute | solution.py:24

commit v5 on v4

--- a/solution.py
+++ b/solution.py
@@ -61,6 +61,11 @@
 
 def product(left, right):
     return fold(jnp.dot(split_left(left), split_right(right), preferred_element_type=jnp.float32))
+
+
+def inward(block, left, right):
+    temp = fold(jnp.dot(left, split_right(block), preferred_element_type=jnp.float32))
+    return fold(jnp.dot(split_left(temp), right, preferred_element_type=jnp.float32))
 
 
 def core_of(env_split, mixed_split, middle_split, terms):
@@ -177,7 +182,8 @@
 
 
 def prepare_kernel(
-    own, table, states, pieces, vec_out, middle_out, plain_out, left_out, right_out, back_out,
+    own, table, states, pieces, onsite, vec_out, middle_out, plain_out, left_out, right_out,
+    back_out, diagonal_out, mine_out,
 ):
     total, size = vec_out.shape[0], vec_out.shape[1]
     row = lax.broadcasted_iota(jnp.int32, (size, size), 0)
@@ -188,44 +194,47 @@
     def block(sector, kind):
         return pieces[(sector // own) ^ member, sector % own, kind]
 
-    def state_of(sector):
-        return states[(sector // own) ^ member, sector % own]
-
     square = jnp.zeros((size, size), jnp.float32)
     for j in range(total):
-        value = state_of(j)
+        value = states[(j // own) ^ member, j % own]
         square = square + value * value
-    norm = jnp.sqrt(jnp.sum(square))
-
-    def body(j, carry):
-        vec = state_of(j) / norm
+    norm = jnp.sqrt(jnp.full((8, size), jnp.sum(square), jnp.float32))[0:1]
+
+    for j in range(total):
+        vec = states[(j // own) ^ member, j % own] / norm
+        vec_out[j] = vec
+        diagonal_out[j] = jnp.where(j // own == member, onsite[j % own], 0.0)
         left = jnp.where(table[0] == 1, eye, block(table[HEAD + j], 0))
         right = jnp.where(table[1] == 1, eye, block(table[HEAD + total + j], 1))
-        vec_out[j] = vec
         left_out[j] = split_left(left)
         right_out[j] = split_right(right)
         back_out[j, 0] = jnp.transpose(left)
         back_out[j, 1] = jnp.transpose(right)
-        middle = product(product(left, vec), right)
+    for i in range(own):
+        mine_out[i] = states[0, i] / norm
+    for j in range(total):
+        middle = inward(vec_out[j], left_out[j], right_out[j])
         middle_out[j] = split_right(middle)
         plain_out[j] = middle
-        return carry
-
-    lax.fori_loop(0, total, body, 0)
 
 
 def first_kernel(
-    own, begin, table, bond, got0, got1, sent0, sent1, middle, vec, back, onsite,
+    begin, flags, bond, got0, got1, sent0, sent1, middle, vec, back, diagonal,
     env_out, mixed_out, part_out,
 ):
     size = vec.shape[-1]
     terms = bond.shape[0]
-    first, last, member, swap = table[0] == 1, table[1] == 1, table[2], table[3] == 1
+    flag = lambda k: jnp.broadcast_to(flags[k, 0:1] != 0, (size, size))
+    first, last, swap = flag(0), flag(1), flag(2)
     rows = lambda s, m: slice((s * terms + m) * size, (s * terms + m + 1) * size)
 
     def chosen(at, end, sent_a, sent_b, got_a, got_b):
         there = jnp.where(swap, got_b[at], got_a[at])
         return jnp.where(end, jnp.where(swap, sent_b[at], sent_a[at]), there)
+
+    def weighted(m, k, block):
+        tiles = block.reshape(size // 8, 8, size)
+        return (tiles * bond[m, k][None]).reshape(size, size)
 
     for s in range(part_out.shape[0]):
         for m in range(terms):
@@ -233,29 +242,22 @@
             env_out[s, rows(0, m)] = split_left(block)
         blocks = [chosen(rows(s, m), last, sent0, sent1, got1, got0) for m in range(terms)]
         for m in range(terms):
-            total = bond[m, 0] * blocks[0]
+            total = weighted(m, 0, blocks[0])
             for k in range(1, terms):
-                total = total + bond[m, k] * blocks[k]
+                total = total + weighted(m, k, blocks[k])
             mixed_out[s, rows(0, m)] = split_left(total)
         j = begin + s
         core = core_of(env_out[s], mixed_out[s], middle[j], terms)
         part = product(product(back[j, 0], core), back[j, 1])
-        mine = (j // own == member).astype(jnp.float32)
-        part_out[s] = part + (mine * onsite[j % own]) * vec[j]
-
-
-def inward(block, left, right):
-    temp = fold(jnp.dot(left, split_right(block), preferred_element_type=jnp.float32))
-    return fold(jnp.dot(split_left(temp), right, preferred_element_type=jnp.float32))
+        part_out[s] = part + diagonal[j] * vec[j]
 
 
 def early_kernel(
-    own, begin, table, image, part, vec, middle, left, right, onsite, env, mixed,
+    begin, image, part, vec, middle, left, right, diagonal, env, mixed,
     resid_out, stat_out, moved, cores,
 ):
     width, size = image.shape[0], image.shape[1]
     terms = mixed.shape[1] // size
-    member = table[2]
     zero = jnp.zeros((size, size), jnp.float32)
     tile = lambda value: jnp.full((8, 128), value, jnp.float32)
 
@@ -286,7 +288,7 @@
         moved[i] = inward(resid, left[begin + i], right[begin + i])
     for i in range(width):
         cores[i] = core_of(env[i], mixed[i], split_right(moved[i]), terms)
-    shares = lambda i: jnp.where((begin + i) // own == member, 1.0, 0.0) * onsite[(begin + i) % own]
+    shares = lambda i: diagonal[begin + i]
     both = zero
     for i in range(width):
         resid = resid_out[i]
@@ -305,7 +307,7 @@
 
 
 def second_kernel(
-    own, widths, table, part0, part1, part2, part3, vec, left, right, onsite, env, mixed, *refs
+    own, widths, flags, part0, part1, part2, part3, vec, left, right, diagonal, env, mixed, *refs
 ):
     count = len(widths)
     resids, stats = refs[:count], refs[count : 2 * count]
@@ -313,7 +315,6 @@
     total, size, late = vec.shape[0], vec.shape[1], part0.shape[0]
     early = total - late
     terms = mixed.shape[1] // size
-    member = table[2]
     zero = jnp.zeros((size, size), jnp.float32)
     tile = lambda value: jnp.full((8, 128), value, jnp.float32)
 
@@ -343,8 +344,7 @@
         work[j] = value
         moved = inward(value, left[j], right[j])
         core = core_of(env[i], mixed[i], split_right(moved), terms)
-        mine = jnp.where(j // own == member, 1.0, 0.0) * onsite[j % own]
-        share = share + moved * core + (mine * value) * value
+        share = share + moved * core + (diagonal[j] * value) * value
     begin = 0
     sums = zero[:8]
     for resid, stat, width in zip(resids, stats, widths):
@@ -357,11 +357,13 @@
     share_out[1] = alpha1
     share_out[2] = beta
     for i in range(own):
-        second_out[i] = work[member * own + i]
-
-
-def final_kernel(own, count, table, share0, share1, share2, share3, vec, second, out, energy_out):
-    member = table[2]
+        mine = work[i]
+        for g in range(1, total // own):
+            mine = jnp.where(flags[3 + g, 0:1] != 0, work[g * own + i], mine)
+        second_out[i] = mine
+
+
+def final_kernel(count, share0, share1, share2, share3, mine, second, out, energy_out):
     alpha2 = (share0[0] + share1[0]) + (share2[0] + share3[0])
     alpha1, beta = share0[1], share0[2]
     energy = (alpha1 + alpha2) / 2.0 - jnp.sqrt(((alpha1 - alpha2) / 2.0) ** 2 + beta * beta)
@@ -369,8 +371,8 @@
     scale = math.sqrt(count)
     weight1 = (scale * (beta / height))[0:1]
     weight2 = (scale * ((energy - alpha1) / height))[0:1]
-    for i in range(own):
-        out[i] = weight1 * vec[member * own + i] + weight2 * second[i]
+    for i in range(out.shape[0]):
+        out[i] = weight1 * mine[i] + weight2 * second[i]
     energy_out[0] = energy[0, 0]
 
 
@@ -447,13 +449,18 @@
     bond_left = jnp.where(table[0] == 1, small, from_left[own * size :, : mpo_bond.shape[1]])
     bond_right = jnp.where(table[1] == 1, small, from_right[own * size :, : mpo_bond.shape[1]])
     bond = jnp.sum(bond_left[:, None, :] * bond_right[None, :, :], axis=2)
+    bond = jnp.broadcast_to(bond[:, :, None, None], (terms, terms, 8, size))
+    flags = jnp.concatenate(
+        [table[0:2], table[3:4], (table[2] == jnp.arange(GROUP)).astype(jnp.int32)]
+    )
+    flags = jnp.broadcast_to(flags[:, None, None], (3 + GROUP, 8, size))
     tensors = lambda block: block[: own * size].reshape(own, size, size)
     pieces = gather(jnp.stack([tensors(from_left), tensors(from_right)], 1))
 
-    vec, middle, plain, left, right, back = pl.pallas_call(
+    vec, middle, plain, left, right, back, diagonal, mine = pl.pallas_call(
         functools.partial(prepare_kernel, own),
-        in_specs=[smem, vmem, vmem],
-        out_specs=[vmem] * 6,
+        in_specs=[smem] + [vmem] * 3,
+        out_specs=[vmem] * 8,
         out_shape=[
             shape((total, size, size), f32),
             shape((total, 2 * size, 2 * size), bf16),
@@ -461,32 +468,34 @@
             shape((total, size, 2 * size), bf16),
             shape((total, 2 * size, 2 * size), bf16),
             shape((total, 2, size, size), f32),
+            shape((total, size, size), f32),
+            shape((own, size, size), f32),
         ],
         cost_estimate=small_cost,
         compiler_params=params(12),
         name="prepare",
-    )(table, states, pieces)
+    )(table, states, pieces, onsite)
 
     def early(begin, width, image, part, env, mixed, after):
         image, _ = lax.optimization_barrier((image, after))
         return pl.pallas_call(
-            functools.partial(early_kernel, own, begin),
-            in_specs=[smem] + [vmem] * 9,
+            functools.partial(early_kernel, begin),
+            in_specs=[vmem] * 9,
             out_specs=[vmem] * 2,
             out_shape=[shape((width, size, size), f32), shape((8, 8, 128), f32)],
             scratch_shapes=[pltpu.VMEM((width, size, size), f32)] * 2,
             cost_estimate=small_cost,
             compiler_params=params(12),
             name="early_second_matvec",
-        )(table, image, part, vec, plain, left, right, onsite, env, mixed)
+        )(image, part, vec, plain, left, right, diagonal, env, mixed)
 
     resids, stats, waits, held = [], [], [], None
     for c, (begin, width) in enumerate(zip(begins, CHUNKS)):
         if c > 0:
             got[c], _ = lax.optimization_barrier((got[c], waits[c - 1]))
         env, mixed, part = pl.pallas_call(
-            functools.partial(first_kernel, own, begin),
-            in_specs=[smem, smem] + [vmem] * 8,
+            functools.partial(first_kernel, begin),
+            in_specs=[vmem] * 10,
             out_specs=[vmem] * 3,
             out_shape=[
                 shape((width, rows(1), 2 * size), bf16),
@@ -496,7 +505,7 @@
             cost_estimate=small_cost,
         compiler_params=params(12),
             name=f"first_matvec{c}",
-        )(table, bond, *got[c], *sent[c], middle, vec, back, onsite)
+        )(flags, bond, *got[c], *sent[c], middle, vec, back, diagonal)
         if held is not None:
             resid, stat = early(*held, after=part)
             resids.append(resid)
@@ -509,25 +518,25 @@
     parts = [part] + [partner(part, mask) for mask in (1, 2, 3)]
     second, share = pl.pallas_call(
         functools.partial(second_kernel, own, CHUNKS[:-1]),
-        in_specs=[smem] + [vmem] * (10 + 2 * (len(CHUNKS) - 1)),
+        in_specs=[vmem] * (11 + 2 * (len(CHUNKS) - 1)),
         out_specs=[vmem] * 2,
         out_shape=[shape((own, size, size), f32), shape((3, 8, 128), f32)],
         scratch_shapes=[pltpu.VMEM((total, size, size), f32)],
         cost_estimate=small_cost,
         compiler_params=params(12),
         name="second_matvec",
-    )(table, *parts, vec, left, right, onsite, env, mixed, *resids, *stats)
+    )(flags, *parts, vec, left, right, diagonal, env, mixed, *resids, *stats)
 
     shares = [share] + [partner(share[:1], mask) for mask in (1, 2, 3)]
     new_state, energy = pl.pallas_call(
-        functools.partial(final_kernel, own, total * size * size),
-        in_specs=[smem] + [vmem] * 6,
+        functools.partial(final_kernel, total * size * size),
+        in_specs=[vmem] * 6,
         out_specs=[vmem, smem],
         out_shape=[shape((own, size, size), f32), shape((1,), f32)],
         cost_estimate=small_cost,
         compiler_params=params(4),
         name="ritz_update",
-    )(table, *shares, vec, second)
+    )(*shares, mine, second)
     return (new_state, energy)
 
 

time: 121 us -> 120 us (level)
  Pallas kernels: 31.3 us -> 24.3 us
  waiting for transfers between devices: 45.8 us -> 48.6 us
  starting transfers between devices: 39.5 us -> 41.1 us
  other arithmetic: 0.39 us -> 1.73 us
    pallas_call x9, Pallas kernels: 22.6 us -> 16.2 us  [the longest x4 8.82 us: on_device(): pl.pallas_call(functools.partial(first_kernel, begin), in_specs=[vmem] *...]
    ppermute x18, waiting for transfers between devices: 24.2 us -> 26.7 us  [partner(): return lax.ppermute(block, 'sites', route)]
    ppermute x18, starting transfers between devices: 15.6 us -> 17.1 us  [partner(): return lax.ppermute(block, 'sites', route)]
  transfers between devices with their start and end apart: 26 -> 26, of which waited for: 15 -> 17; matrix products, arithmetic and copies ran while one was open for 1% -> 2% of each run, Pallas kernels for 19% -> 15%
where the time goes in v5:
time: 120 us
  waiting for transfers between devices  48.6 us (40%)
  starting transfers between devices  41.1 us (34%)
  Pallas kernels  24.3 us (20%)
  between operations  3.08 us (3%)
  other arithmetic  1.73 us (1%)
    ppermute x18, waiting for transfers between devices, partner(): return lax.ppermute(block, 'sites', route)  26.7 us
    ppermute x8, starting transfers between devices, hand_over(): lax.ppermute(block, 'sites', [(i, j) for i, j in route if 0 <= j < count])  23.9 us
    ppermute x8, waiting for transfers between devices, hand_over(): lax.ppermute(block, 'sites', [(i, j) for i, j in route if 0 <= j < count])  22 us
    ppermute x18, starting transfers between devices, partner(): return lax.ppermute(block, 'sites', route)  17.1 us
    pallas_call x4, Pallas kernels, on_device(): pl.pallas_call(functools.partial(first_kernel, begin), in_specs=[vmem] *...  8.82 us
    pallas_call x3, Pallas kernels, early(): pl.pallas_call(functools.partial(early_kernel, begin), in_specs=[vmem] *...  5.27 us
    pallas_call x1, Pallas kernels, on_device(): pl.pallas_call(functools.partial(open_kernel, CHUNKS[:1], parts), in_spec...  3.62 us
    pallas_call x1, Pallas kernels, on_device(): pl.pallas_call(functools.partial(pick_kernel, CHUNKS[0], CHUNKS[1:]), in_...  3.15 us
  transfers between devices with their start and end apart: 26, of which 17 were waited for; matrix products, arithmetic and copies ran while one was open for 2% of the time, Pallas kernels for 15%

profile of v5, /device:TPU:0, one launch (start us, length us, event | category | flops | bytes accessed | tf_op | source)
XLA Modules:
  0.0 119.7 jit_solution(4604194421401699878)
XLA Ops:
  0.6 3.6 %open.1 = (s32[46]{0:T(128)S(1)}, f32[3336,128]{1,0:T(8,128)S(1)}, f32[3336,128]{1,0:T(8,128)S(1)}) custom-call(s32[1]{0:T(128)} %bitcast.place_hbm, s32[4,8]{1,0:T(4,128)} %sectors_hbm.1, s32[4,8]{1,0:T(4,128)} %flow_hbm.1, f32[8,8]{1,0:T(8,128)} %bond_hbm.1, f32[2,128,128]{2,1,0:T(8,128)} %left_tensor.1, f32[2,128,128]{2,1,0:T(8,128)} %right_tensor.1, ...), custom_call_target="tpu_custom_call" | custom-call | flops 1 | bytes 1 | tf_op jit(solution)/shard_map/open/pallas_call | solution.py:404
  4.3 1.3 %collective-permute-start = (f32[3336,128]{1,0:T(8,128)S(1)}, f32[3336,128]{1,0:T(8,128)S(1)}, u32[]{:S(2)}, u32[]{:S(2)}) collective-permute-start(f32[3336,128]{1,0:T(8,128)S(1)} %get-tuple-element.51.sent1), channel_id=1, source_target_pairs={{1,5},{3,7},{4,0},{5,9},{6,2},{7,11},{8,4},{9,13},{10,6},{11,15},{... | collective-permute-start | bytes 5124104 | tf_op jit(solution)/shard_map/ppermute | solution.py:19
  5.6 5.7 %collective-permute-start.1 = (f32[3336,128]{1,0:T(8,128)S(1)}, f32[3336,128]{1,0:T(8,128)S(1)}, u32[]{:S(2)}, u32[]{:S(2)}) collective-permute-start(f32[3336,128]{1,0:T(8,128)S(1)} %get-tuple-element.52.sent0), channel_id=1, source_target_pairs={{0,4},{2,6},{4,8},{5,1},{6,10},{7,3},{8,12},{9,5},{10,14},{11,7},{... | collective-permute-start | bytes 5124104 | tf_op jit(solution)/shard_map/ppermute | solution.py:19
  11.3 2.0 %collective-permute-start.7 = (f32[2,128,128]{2,1,0:T(8,128)S(1)}, f32[2,128,128]{2,1,0:T(8,128)S(1)}, u32[]{:S(2)}, u32[]{:S(2)}) collective-permute-start(f32[2,128,128]{2,1,0:T(8,128)S(1)} %copy-done.1), channel_id=1, source_target_pairs={{0,2},{1,3},{2,0},{3,1},{4,6},{5,7},{6,4},{7,5},{8,10},{9,11},{10,... | collective-permute-start | bytes 393224 | tf_op jit(solution)/shard_map/ppermute | solution.py:24
  13.4 3.1 %pick.1 = (f32[3072,128]{1,0:T(8,128)S(1)}, f32[3072,128]{1,0:T(8,128)S(1)}, f32[1024,128]{1,0:T(8,128)S(1)}, f32[1024,128]{1,0:T(8,128)S(1)}, f32[1024,128]{1,0:T(8,128)S(1)}, /*index=5*/f32[1024,128]{1,0:T(8,128)S(1)}) custom-call(s32[46]{0:T(128)S(1)} %get-tuple-element.50.table, f32[8,8,128,128]{3,2,1,0:T(8,128)} %left_env.3, f32[8,8,128,128]{3,2,1,0:T(8,128)} %right_env.3), custom_call_target="tpu_custom_call" | custom-call | flops 1 | bytes 1 | tf_op jit(solution)/shard_map/pick/pallas_call | solution.py:430
  17.8 2.2 %collective-permute-done.8 = f32[2,128,128]{2,1,0:T(8,128)S(1)} collective-permute-done((f32[2,128,128]{2,1,0:T(8,128)S(1)}, f32[2,128,128]{2,1,0:T(8,128)S(1)}, u32[]{:S(2)}, u32[]{:S(2)}) %collective-permute-start.8) | collective-permute-done | bytes 131104 | tf_op jit(solution)/shard_map/ppermute | solution.py:24
  21.3 4.6 %collective-permute-start.9 = (f32[3072,128]{1,0:T(8,128)S(1)}, f32[3072,128]{1,0:T(8,128)S(1)}, u32[]{:S(2)}, u32[]{:S(2)}) collective-permute-start(f32[3072,128]{1,0:T(8,128)S(1)} %get-tuple-element.59.sent0), channel_id=1, source_target_pairs={{0,4},{2,6},{4,8},{5,1},{6,10},{7,3},{8,12},{9,5},{10,14},{11,7},{... | collective-permute-start | bytes 4718600 | tf_op jit(solution)/shard_map/ppermute | solution.py:19
  29.8 14.8 %collective-permute-done.got1 = f32[3336,128]{1,0:T(8,128)S(1)} collective-permute-done((f32[3336,128]{1,0:T(8,128)S(1)}, f32[3336,128]{1,0:T(8,128)S(1)}, u32[]{:S(2)}, u32[]{:S(2)}) %collective-permute-start) | collective-permute-done | bytes 1708064 | tf_op jit(solution)/shard_map/ppermute | solution.py:19
  44.6 4.3 %collective-permute-done.1.got0 = f32[3336,128]{1,0:T(8,128)S(1)} collective-permute-done((f32[3336,128]{1,0:T(8,128)S(1)}, f32[3336,128]{1,0:T(8,128)S(1)}, u32[]{:S(2)}, u32[]{:S(2)}) %collective-permute-start.1) | collective-permute-done | bytes 1708064 | tf_op jit(solution)/shard_map/ppermute | solution.py:19
  49.0 1.4 %collective-permute-start.11 = (f32[2,2,128,128]{3,2,1,0:T(8,128)S(1)}, f32[2,2,128,128]{3,2,1,0:T(8,128)S(1)}, u32[]{:S(2)}, u32[]{:S(2)}) collective-permute-start(f32[2,2,128,128]{3,2,1,0:T(8,128)S(1)} %get-tuple-element.101), channel_id=1, source_target_pairs={{0,1},{1,0},{2,3},{3,2},{4,5},{5,4},{6,7},{7,6},{8,9},{9,8},{10,11... | collective-permute-start | bytes 786440 | tf_op jit(solution)/shard_map/ppermute | solution.py:24
  50.4 1.5 %collective-permute-start.12 = (f32[2,2,128,128]{3,2,1,0:T(8,128)S(1)}, f32[2,2,128,128]{3,2,1,0:T(8,128)S(1)}, u32[]{:S(2)}, u32[]{:S(2)}) collective-permute-start(f32[2,2,128,128]{3,2,1,0:T(8,128)S(1)} %get-tuple-element.101), channel_id=1, source_target_pairs={{0,2},{1,3},{2,0},{3,1},{4,6},{5,7},{6,4},{7,5},{8,10},{9,11},{10,... | collective-permute-start | bytes 786440 | tf_op jit(solution)/shard_map/ppermute | solution.py:24
  52.0 7.5 %collective-permute-done.12 = f32[2,2,128,128]{3,2,1,0:T(8,128)S(1)} collective-permute-done((f32[2,2,128,128]{3,2,1,0:T(8,128)S(1)}, f32[2,2,128,128]{3,2,1,0:T(8,128)S(1)}, u32[]{:S(2)}, u32[]{:S(2)}) %collective-permute-start.12) | collective-permute-done | bytes 262176 | tf_op jit(solution)/shard_map/ppermute | solution.py:24
  59.5 3.9 %collective-permute-done.13 = f32[2,2,128,128]{3,2,1,0:T(8,128)S(1)} collective-permute-done((f32[2,2,128,128]{3,2,1,0:T(8,128)S(1)}, f32[2,2,128,128]{3,2,1,0:T(8,128)S(1)}, u32[]{:S(2)}, u32[]{:S(2)}) %collective-permute-start.13) | collective-permute-done | bytes 262176 | tf_op jit(solution)/shard_map/ppermute | solution.py:24
  63.5 1.4 %prepare.1 = (f32[8,128,128]{2,1,0:T(8,128)S(1)}, bf16[8,256,256]{2,1,0:T(8,128)(2,1)S(1)}, f32[8,128,128]{2,1,0:T(8,128)S(1)}, bf16[8,128,256]{2,1,0:T(8,128)(2...) custom-call(s32[46]{0:T(128)S(1)} %get-tuple-element.50.table, ...), custom_call_target="tpu_custom_call" | custom-call | flops 1 | bytes 1 | tf_op jit(solution)/shard_map/prepare/pallas_call | solution.py:460
  65.1 3.3 %first_matvec0.1 = (bf16[3,1024,256]{2,1,0:T(8,128)(2,1)S(1)}, bf16[3,1024,256]{2,1,0:T(8,128)(2,1)S(1)}, f32[3,128,128]{2,1,0:T(8,128)S(1)}) custom-call(s32[7,8,128]{2,1,0:T(8,128)S(1)} %broadcast_in_dim.4.flags, f32[8,8,8,128]{3,2,1,0:T(8,128)S(1)} %broadcast_in_dim.5.bond, f32[3336,128]{1,0:T(8,128)S(1)} %collective-permute-done.1.got0, ...), custom_call_target="tpu_custom_call" | custom-call | flops 1 | bytes 1 | tf_op jit(solution)/shard_map/first_matvec0/pallas_call | solution.py:496
  70.5 1.6 %collective-permute-start.15 = (f32[3,128,128]{2,1,0:T(8,128)S(1)}, f32[3,128,128]{2,1,0:T(8,128)S(1)}, u32[]{:S(2)}, u32[]{:S(2)}) collective-permute-start(f32[3,128,128]{2,1,0:T(8,128)S(1)} %add.18), channel_id=1, source_target_pairs={{0,2},{1,3},{2,0},{3,1},{4,6},{5,7},{6,4},{7,5},{8,10},{9,11},{10,... | collective-permute-start | bytes 589832 | tf_op jit(solution)/shard_map/ppermute | solution.py:24
  72.1 4.0 %collective-permute-start.4 = (f32[1024,128]{1,0:T(8,128)S(1)}, f32[1024,128]{1,0:T(8,128)S(1)}, u32[]{:S(2)}, u32[]{:S(2)}) collective-permute-start(f32[1024,128]{1,0:T(8,128)S(1)} %get-tuple-element.55.sent0), channel_id=1, source_target_pairs={{0,4},{2,6},{4,8},{5,1},{6,10},{7,3},{8,12},{9,5},{10,14},{11,7},{... | collective-permute-start | bytes 1572872 | tf_op jit(solution)/shard_map/ppermute | solution.py:19
  78.3 2.4 %collective-permute-done.9.got0 = f32[3072,128]{1,0:T(8,128)S(1)} collective-permute-done((f32[3072,128]{1,0:T(8,128)S(1)}, f32[3072,128]{1,0:T(8,128)S(1)}, u32[]{:S(2)}, u32[]{:S(2)}) %collective-permute-start.9) | collective-permute-done | bytes 1572896 | tf_op jit(solution)/shard_map/ppermute | solution.py:19
  80.7 3.1 %first_matvec1.1 = (bf16[3,1024,256]{2,1,0:T(8,128)(2,1)S(1)}, bf16[3,1024,256]{2,1,0:T(8,128)(2,1)S(1)}, f32[3,128,128]{2,1,0:T(8,128)S(1)}) custom-call(s32[7,8,128]{2,1,0:T(8,128)S(1)} %broadcast_in_dim.4.flags, f32[8,8,8,128]{3,2,1,0:T(8,128)S(1)} %broadcast_in_dim.5.bond, f32[3072,128]{1,0:T(8,128)S(1)} %collective-permute-done.9.got0, ...), custom_call_target="tpu_custom_call" | custom-call | flops 1 | bytes 1 | tf_op jit(solution)/shard_map/first_matvec1/pallas_call | solution.py:496
  84.1 4.3 %collective-permute-start.2 = (f32[1024,128]{1,0:T(8,128)S(1)}, f32[1024,128]{1,0:T(8,128)S(1)}, u32[]{:S(2)}, u32[]{:S(2)}) collective-permute-start(f32[1024,128]{1,0:T(8,128)S(1)} %get-tuple-element.53.sent0), channel_id=1, source_target_pairs={{0,4},{2,6},{4,8},{5,1},{6,10},{7,3},{8,12},{9,5},{10,14},{11,7},{... | collective-permute-start | bytes 1572872 | tf_op jit(solution)/shard_map/ppermute | solution.py:19
  88.4 1.5 %collective-permute-start.3 = (f32[1024,128]{1,0:T(8,128)S(1)}, f32[1024,128]{1,0:T(8,128)S(1)}, u32[]{:S(2)}, u32[]{:S(2)}) collective-permute-start(f32[1024,128]{1,0:T(8,128)S(1)} %get-tuple-element.54.sent1), channel_id=1, source_target_pairs={{1,5},{3,7},{4,0},{5,9},{6,2},{7,11},{8,4},{9,13},{10,6},{11,15},{... | collective-permute-start | bytes 1572872 | tf_op jit(solution)/shard_map/ppermute | solution.py:19
  89.9 2.8 %collective-permute-start.17 = (f32[3,128,128]{2,1,0:T(8,128)S(1)}, f32[3,128,128]{2,1,0:T(8,128)S(1)}, u32[]{:S(2)}, u32[]{:S(2)}) collective-permute-start(f32[3,128,128]{2,1,0:T(8,128)S(1)} %add.20), channel_id=1, source_target_pairs={{0,2},{1,3},{2,0},{3,1},{4,6},{5,7},{6,4},{7,5},{8,10},{9,11},{10,... | collective-permute-start | bytes 589832 | tf_op jit(solution)/shard_map/ppermute | solution.py:24
  92.7 2.0 %early_second_matvec.3 = (f32[3,128,128]{2,1,0:T(8,128)S(1)}, f32[8,8,128]{2,1,0:T(8,128)S(1)}) custom-call(f32[3,128,128]{2,1,0:T(8,128)S(1)} %add.19.image, f32[3,128,128]{2,1,0:T(8,128)S(1)} %get-tuple-element.65.part, f32[8,128,128]{2,1,0:T(8,128)S(1)} %get-tuple-element.62.vec, f32[8,128,128]{2,1,0:T(8,128)S(1)} %get-tuple-element.70.middle, ...), custom_call_target="tpu_custom_call" | custom-call | flops 1 | bytes 1 | tf_op jit(solution)/shard_map/early_second_matvec/pallas_call | solution.py:481
  94.7 3.6 %collective-permute-done.17 = f32[3,128,128]{2,1,0:T(8,128)S(1)} collective-permute-done((f32[3,128,128]{2,1,0:T(8,128)S(1)}, f32[3,128,128]{2,1,0:T(8,128)S(1)}, u32[]{:S(2)}, u32[]{:S(2)}) %collective-permute-start.17) | collective-permute-done | bytes 196640 | tf_op jit(solution)/shard_map/ppermute | solution.py:24
  100.9 2.1 %collective-permute-start.19 = (f32[1,128,128]{2,1,0:T(8,128)S(1)}, f32[1,128,128]{2,1,0:T(8,128)S(1)}, u32[]{:S(2)}, u32[]{:S(2)}) collective-permute-start(f32[1,128,128]{2,1,0:T(8,128)S(1)} %add.22), channel_id=1, source_target_pairs={{0,2},{1,3},{2,0},{3,1},{4,6},{5,7},{6,4},{7,5},{8,10},{9,11},{10,... | collective-permute-start | bytes 196616 | tf_op jit(solution)/shard_map/ppermute | solution.py:24
  103.0 2.0 %early_second_matvec.4 = (f32[3,128,128]{2,1,0:T(8,128)S(1)}, f32[8,8,128]{2,1,0:T(8,128)S(1)}) custom-call(f32[3,128,128]{2,1,0:T(8,128)S(1)} %add.21.image, f32[3,128,128]{2,1,0:T(8,128)S(1)} %get-tuple-element.68.part, f32[8,128,128]{2,1,0:T(8,128)S(1)} %get-tuple-element.62.vec, f32[8,128,128]{2,1,0:T(8,128)S(1)} %get-tuple-element.70.middle, ...), custom_call_target="tpu_custom_call" | custom-call | flops 1 | bytes 1 | tf_op jit(solution)/shard_map/early_second_matvec/pallas_call | solution.py:481
  106.8 1.9 %collective-permute-start.21 = (f32[1,128,128]{2,1,0:T(8,128)S(1)}, f32[1,128,128]{2,1,0:T(8,128)S(1)}, u32[]{:S(2)}, u32[]{:S(2)}) collective-permute-start(f32[1,128,128]{2,1,0:T(8,128)S(1)} %get-tuple-element.85.part0), channel_id=1, source_target_pairs={{0,2},{1,3},{2,0},{3,1},{4,6},{5,7},{6,4},{7,5},{8,10},{9,11},{10,... | collective-permute-start | bytes 196616 | tf_op jit(solution)/shard_map/ppermute | solution.py:24
  108.7 1.3 %early_second_matvec.5 = (f32[1,128,128]{2,1,0:T(8,128)S(1)}, f32[8,8,128]{2,1,0:T(8,128)S(1)}) custom-call(f32[1,128,128]{2,1,0:T(8,128)S(1)} %add.23.image, f32[1,128,128]{2,1,0:T(8,128)S(1)} %get-tuple-element.78.part, f32[8,128,128]{2,1,0:T(8,128)S(1)} %get-tuple-element.62.vec, f32[8,128,128]{2,1,0:T(8,128)S(1)} %get-tuple-element.70.middle, ...), custom_call_target="tpu_custom_call" | custom-call | flops 1 | bytes 1 | tf_op jit(solution)/shard_map/early_second_matvec/pallas_call | solution.py:481
  111.4 1.4 %collective-permute-done.22.part3 = f32[1,128,128]{2,1,0:T(8,128)S(1)} collective-permute-done((f32[1,128,128]{2,1,0:T(8,128)S(1)}, f32[1,128,128]{2,1,0:T(8,128)S(1)}, u32[]{:S(2)}, u32[]{:S(2)}) %collective-permute-start.22) | collective-permute-done | bytes 65568 | tf_op jit(solution)/shard_map/ppermute | solution.py:24
  112.7 1.3 %second_matvec.1 = (f32[2,128,128]{2,1,0:T(8,128)S(1)}, f32[3,8,128]{2,1,0:T(8,128)S(1)}) custom-call(s32[7,8,128]{2,1,0:T(8,128)S(1)} %broadcast_in_dim.4.flags, f32[1,128,128]{2,1,0:T(8,128)S(1)} %get-tuple-element.85.part0, f32[1,128,128]{2,1,0:T(8,128)S(1)} %collective-permute-done.20.part1, f32[1,128,128]{2,1,0:T(8,128)S(1)} %collective-permute-done.21.part2, ...), custom_call_target="tpu_custom_call" | custom-call | flops 1 | bytes 1 | tf_op jit(solution)/shard_map/second_matvec/pallas_call | solution.py:519
  114.3 1.5 %collective-permute-start.24 = (f32[1,8,128]{2,1,0:T(8,128)S(1)}, f32[1,8,128]{2,1,0:T(8,128)S(1)}, u32[]{:S(2)}, u32[]{:S(2)}) collective-permute-start(f32[1,8,128]{2,1,0:T(8,128)S(1)} %slice.50), channel_id=1, source_target_pairs={{0,2},{1,3},{2,0},{3,1},{4,6},{5,7},{6,4},{7,5},{8,10},{9,11},{10,... | collective-permute-start | bytes 12296 | tf_op jit(solution)/shard_map/ppermute | solution.py:24
  116.0 1.9 %collective-permute-done.24.share2 = f32[1,8,128]{2,1,0:T(8,128)S(1)} collective-permute-done((f32[1,8,128]{2,1,0:T(8,128)S(1)}, f32[1,8,128]{2,1,0:T(8,128)S(1)}, u32[]{:S(2)}, u32[]{:S(2)}) %collective-permute-start.24) | collective-permute-done | bytes 4128 | tf_op jit(solution)/shard_map/ppermute | solution.py:24
  (56 shorter events, 17.4 us)
Async XLA Ops:
  0.6 10.6 %copy-start.1 = (f32[2,128,128]{2,1,0:T(8,128)S(1)}, f32[2,128,128]{2,1,0:T(8,128)}, u32[]{:S(2)}) copy-start(f32[2,128,128]{2,1,0:T(8,128)} %param.9) | copy-start | bytes 393220
  4.3 40.3 %collective-permute-start = (f32[3336,128]{1,0:T(8,128)S(1)}, f32[3336,128]{1,0:T(8,128)S(1)}, u32[]{:S(2)}, u32[]{:S(2)}) collective-permute-start(f32[3336,128]{1,0:T(8,128)S(1)} %get-tuple-element.51.sent1), channel_id=1, source_target_pairs={{1,5},{3,7},{4,0},{5,9},{6,2},{7,11},{8,4},{9,13},{10,6},{11,15},{... | collective-permute-start | bytes 5124104 | tf_op jit(solution)/shard_map/ppermute | solution.py:19
  5.6 43.3 %collective-permute-start.1 = (f32[3336,128]{1,0:T(8,128)S(1)}, f32[3336,128]{1,0:T(8,128)S(1)}, u32[]{:S(2)}, u32[]{:S(2)}) collective-permute-start(f32[3336,128]{1,0:T(8,128)S(1)} %get-tuple-element.52.sent0), channel_id=1, source_target_pairs={{0,4},{2,6},{4,8},{5,1},{6,10},{7,3},{8,12},{9,5},{10,14},{11,7},{... | collective-permute-start | bytes 5124104 | tf_op jit(solution)/shard_map/ppermute | solution.py:19
  11.3 5.3 %collective-permute-start.6 = (f32[2,128,128]{2,1,0:T(8,128)S(1)}, f32[2,128,128]{2,1,0:T(8,128)S(1)}, u32[]{:S(2)}, u32[]{:S(2)}) collective-permute-start(f32[2,128,128]{2,1,0:T(8,128)S(1)} %copy-done.1), channel_id=1, source_target_pairs={{0,1},{1,0},{2,3},{3,2},{4,5},{5,4},{6,7},{7,6},{8,9},{9,8},{10,11... | collective-permute-start | bytes 393224 | tf_op jit(solution)/shard_map/ppermute | solution.py:24
  11.3 6.4 %collective-permute-start.7 = (f32[2,128,128]{2,1,0:T(8,128)S(1)}, f32[2,128,128]{2,1,0:T(8,128)S(1)}, u32[]{:S(2)}, u32[]{:S(2)}) collective-permute-start(f32[2,128,128]{2,1,0:T(8,128)S(1)} %copy-done.1), channel_id=1, source_target_pairs={{0,2},{1,3},{2,0},{3,1},{4,6},{5,7},{6,4},{7,5},{8,10},{9,11},{10,... | collective-permute-start | bytes 393224 | tf_op jit(solution)/shard_map/ppermute | solution.py:24
  13.4 6.6 %collective-permute-start.8 = (f32[2,128,128]{2,1,0:T(8,128)S(1)}, f32[2,128,128]{2,1,0:T(8,128)S(1)}, u32[]{:S(2)}, u32[]{:S(2)}) collective-permute-start(f32[2,128,128]{2,1,0:T(8,128)S(1)} %copy-done.1), channel_id=1, source_target_pairs={{0,3},{1,2},{2,1},{3,0},{4,7},{5,6},{6,5},{7,4},{8,11},{9,10},{10,... | collective-permute-start | bytes 393224 | tf_op jit(solution)/shard_map/ppermute | solution.py:24
  20.0 58.4 %collective-permute-start.10 = (f32[3072,128]{1,0:T(8,128)S(1)}, f32[3072,128]{1,0:T(8,128)S(1)}, u32[]{:S(2)}, u32[]{:S(2)}) collective-permute-start(f32[3072,128]{1,0:T(8,128)S(1)} %get-tuple-element.60.sent1), channel_id=1, source_target_pairs={{1,5},{3,7},{4,0},{5,9},{6,2},{7,11},{8,4},{9,13},{10,6},{11,15},{... | collective-permute-start | bytes 4718600 | tf_op jit(solution)/shard_map/ppermute | solution.py:19
  21.3 59.5 %collective-permute-start.9 = (f32[3072,128]{1,0:T(8,128)S(1)}, f32[3072,128]{1,0:T(8,128)S(1)}, u32[]{:S(2)}, u32[]{:S(2)}) collective-permute-start(f32[3072,128]{1,0:T(8,128)S(1)} %get-tuple-element.59.sent0), channel_id=1, source_target_pairs={{0,4},{2,6},{4,8},{5,1},{6,10},{7,3},{8,12},{9,5},{10,14},{11,7},{... | collective-permute-start | bytes 4718600 | tf_op jit(solution)/shard_map/ppermute | solution.py:19
  48.9 14.6 %copy-start = (f32[2,128,128]{2,1,0:T(8,128)S(1)}, f32[2,128,128]{2,1,0:T(8,128)}, u32[]{:S(2)}) copy-start(f32[2,128,128]{2,1,0:T(8,128)} %onsite.1) | copy-start | bytes 393220
  49.0 3.0 %collective-permute-start.11 = (f32[2,2,128,128]{3,2,1,0:T(8,128)S(1)}, f32[2,2,128,128]{3,2,1,0:T(8,128)S(1)}, u32[]{:S(2)}, u32[]{:S(2)}) collective-permute-start(f32[2,2,128,128]{3,2,1,0:T(8,128)S(1)} %get-tuple-element.101), channel_id=1, source_target_pairs={{0,1},{1,0},{2,3},{3,2},{4,5},{5,4},{6,7},{7,6},{8,9},{9,8},{10,11... | collective-permute-start | bytes 786440 | tf_op jit(solution)/shard_map/ppermute | solution.py:24
  50.4 9.2 %collective-permute-start.12 = (f32[2,2,128,128]{3,2,1,0:T(8,128)S(1)}, f32[2,2,128,128]{3,2,1,0:T(8,128)S(1)}, u32[]{:S(2)}, u32[]{:S(2)}) collective-permute-start(f32[2,2,128,128]{3,2,1,0:T(8,128)S(1)} %get-tuple-element.101), channel_id=1, source_target_pairs={{0,2},{1,3},{2,0},{3,1},{4,6},{5,7},{6,4},{7,5},{8,10},{9,11},{10,... | collective-permute-start | bytes 786440 | tf_op jit(solution)/shard_map/ppermute | solution.py:24
  51.9 11.5 %collective-permute-start.13 = (f32[2,2,128,128]{3,2,1,0:T(8,128)S(1)}, f32[2,2,128,128]{3,2,1,0:T(8,128)S(1)}, u32[]{:S(2)}, u32[]{:S(2)}) collective-permute-start(f32[2,2,128,128]{3,2,1,0:T(8,128)S(1)} %get-tuple-element.101), channel_id=1, source_target_pairs={{0,3},{1,2},{2,1},{3,0},{4,7},{5,6},{6,5},{7,4},{8,11},{9,10},{10,... | collective-permute-start | bytes 786440 | tf_op jit(solution)/shard_map/ppermute | solution.py:24
  68.4 2.1 %collective-permute-start.14 = (f32[3,128,128]{2,1,0:T(8,128)S(1)}, f32[3,128,128]{2,1,0:T(8,128)S(1)}, u32[]{:S(2)}, u32[]{:S(2)}) collective-permute-start(f32[3,128,128]{2,1,0:T(8,128)S(1)} %get-tuple-element.65.part), channel_id=1, source_target_pairs={{0,1},{1,0},{2,3},{3,2},{4,5},{5,4},{6,7},{7,6},{8,9},{9,8},{10,11... | collective-permute-start | bytes 589832 | tf_op jit(solution)/shard_map/ppermute | solution.py:24
  70.5 7.2 %collective-permute-start.15 = (f32[3,128,128]{2,1,0:T(8,128)S(1)}, f32[3,128,128]{2,1,0:T(8,128)S(1)}, u32[]{:S(2)}, u32[]{:S(2)}) collective-permute-start(f32[3,128,128]{2,1,0:T(8,128)S(1)} %add.18), channel_id=1, source_target_pairs={{0,2},{1,3},{2,0},{3,1},{4,6},{5,7},{6,4},{7,5},{8,10},{9,11},{10,... | collective-permute-start | bytes 589832 | tf_op jit(solution)/shard_map/ppermute | solution.py:24
  72.1 26.2 %collective-permute-start.4 = (f32[1024,128]{1,0:T(8,128)S(1)}, f32[1024,128]{1,0:T(8,128)S(1)}, u32[]{:S(2)}, u32[]{:S(2)}) collective-permute-start(f32[1024,128]{1,0:T(8,128)S(1)} %get-tuple-element.55.sent0), channel_id=1, source_target_pairs={{0,4},{2,6},{4,8},{5,1},{6,10},{7,3},{8,12},{9,5},{10,14},{11,7},{... | collective-permute-start | bytes 1572872 | tf_op jit(solution)/shard_map/ppermute | solution.py:19
  76.1 22.2 %collective-permute-start.5 = (f32[1024,128]{1,0:T(8,128)S(1)}, f32[1024,128]{1,0:T(8,128)S(1)}, u32[]{:S(2)}, u32[]{:S(2)}) collective-permute-start(f32[1024,128]{1,0:T(8,128)S(1)} %get-tuple-element.56.sent1), channel_id=1, source_target_pairs={{1,5},{3,7},{4,0},{5,9},{6,2},{7,11},{8,4},{9,13},{10,6},{11,15},{... | collective-permute-start | bytes 1572872 | tf_op jit(solution)/shard_map/ppermute | solution.py:19
  83.9 6.0 %collective-permute-start.16 = (f32[3,128,128]{2,1,0:T(8,128)S(1)}, f32[3,128,128]{2,1,0:T(8,128)S(1)}, u32[]{:S(2)}, u32[]{:S(2)}) collective-permute-start(f32[3,128,128]{2,1,0:T(8,128)S(1)} %get-tuple-element.68.part), channel_id=1, source_target_pairs={{0,1},{1,0},{2,3},{3,2},{4,5},{5,4},{6,7},{7,6},{8,9},{9,8},{10,11... | collective-permute-start | bytes 589832 | tf_op jit(solution)/shard_map/ppermute | solution.py:24
  84.1 21.4 %collective-permute-start.2 = (f32[1024,128]{1,0:T(8,128)S(1)}, f32[1024,128]{1,0:T(8,128)S(1)}, u32[]{:S(2)}, u32[]{:S(2)}) collective-permute-start(f32[1024,128]{1,0:T(8,128)S(1)} %get-tuple-element.53.sent0), channel_id=1, source_target_pairs={{0,4},{2,6},{4,8},{5,1},{6,10},{7,3},{8,12},{9,5},{10,14},{11,7},{... | collective-permute-start | bytes 1572872 | tf_op jit(solution)/shard_map/ppermute | solution.py:19
  88.4 17.1 %collective-permute-start.3 = (f32[1024,128]{1,0:T(8,128)S(1)}, f32[1024,128]{1,0:T(8,128)S(1)}, u32[]{:S(2)}, u32[]{:S(2)}) collective-permute-start(f32[1024,128]{1,0:T(8,128)S(1)} %get-tuple-element.54.sent1), channel_id=1, source_target_pairs={{1,5},{3,7},{4,0},{5,9},{6,2},{7,11},{8,4},{9,13},{10,6},{11,15},{... | collective-permute-start | bytes 1572872 | tf_op jit(solution)/shard_map/ppermute | solution.py:19
  89.9 8.4 %collective-permute-start.17 = (f32[3,128,128]{2,1,0:T(8,128)S(1)}, f32[3,128,128]{2,1,0:T(8,128)S(1)}, u32[]{:S(2)}, u32[]{:S(2)}) collective-permute-start(f32[3,128,128]{2,1,0:T(8,128)S(1)} %add.20), channel_id=1, source_target_pairs={{0,2},{1,3},{2,0},{3,1},{4,6},{5,7},{6,4},{7,5},{8,10},{9,11},{10,... | collective-permute-start | bytes 589832 | tf_op jit(solution)/shard_map/ppermute | solution.py:24
  99.6 1.3 %collective-permute-start.18 = (f32[1,128,128]{2,1,0:T(8,128)S(1)}, f32[1,128,128]{2,1,0:T(8,128)S(1)}, u32[]{:S(2)}, u32[]{:S(2)}) collective-permute-start(f32[1,128,128]{2,1,0:T(8,128)S(1)} %get-tuple-element.78.part), channel_id=1, source_target_pairs={{0,1},{1,0},{2,3},{3,2},{4,5},{5,4},{6,7},{7,6},{8,9},{9,8},{10,11... | collective-permute-start | bytes 196616 | tf_op jit(solution)/shard_map/ppermute | solution.py:24
  100.9 4.5 %collective-permute-start.19 = (f32[1,128,128]{2,1,0:T(8,128)S(1)}, f32[1,128,128]{2,1,0:T(8,128)S(1)}, u32[]{:S(2)}, u32[]{:S(2)}) collective-permute-start(f32[1,128,128]{2,1,0:T(8,128)S(1)} %add.22), channel_id=1, source_target_pairs={{0,2},{1,3},{2,0},{3,1},{4,6},{5,7},{6,4},{7,5},{8,10},{9,11},{10,... | collective-permute-start | bytes 196616 | tf_op jit(solution)/shard_map/ppermute | solution.py:24
  106.7 3.4 %collective-permute-start.20 = (f32[1,128,128]{2,1,0:T(8,128)S(1)}, f32[1,128,128]{2,1,0:T(8,128)S(1)}, u32[]{:S(2)}, u32[]{:S(2)}) collective-permute-start(f32[1,128,128]{2,1,0:T(8,128)S(1)} %get-tuple-element.85.part0), channel_id=1, source_target_pairs={{0,1},{1,0},{2,3},{3,2},{4,5},{5,4},{6,7},{7,6},{8,9},{9,8},{10,11... | collective-permute-start | bytes 196616 | tf_op jit(solution)/shard_map/ppermute | solution.py:24
  106.8 4.6 %collective-permute-start.21 = (f32[1,128,128]{2,1,0:T(8,128)S(1)}, f32[1,128,128]{2,1,0:T(8,128)S(1)}, u32[]{:S(2)}, u32[]{:S(2)}) collective-permute-start(f32[1,128,128]{2,1,0:T(8,128)S(1)} %get-tuple-element.85.part0), channel_id=1, source_target_pairs={{0,2},{1,3},{2,0},{3,1},{4,6},{5,7},{6,4},{7,5},{8,10},{9,11},{10,... | collective-permute-start | bytes 196616 | tf_op jit(solution)/shard_map/ppermute | solution.py:24
  108.7 4.0 %collective-permute-start.22 = (f32[1,128,128]{2,1,0:T(8,128)S(1)}, f32[1,128,128]{2,1,0:T(8,128)S(1)}, u32[]{:S(2)}, u32[]{:S(2)}) collective-permute-start(f32[1,128,128]{2,1,0:T(8,128)S(1)} %get-tuple-element.85.part0), channel_id=1, source_target_pairs={{0,3},{1,2},{2,1},{3,0},{4,7},{5,6},{6,5},{7,4},{8,11},{9,10},{10,... | collective-permute-start | bytes 196616 | tf_op jit(solution)/shard_map/ppermute | solution.py:24
  114.0 1.9 %collective-permute-start.23 = (f32[1,8,128]{2,1,0:T(8,128)S(1)}, f32[1,8,128]{2,1,0:T(8,128)S(1)}, u32[]{:S(2)}, u32[]{:S(2)}) collective-permute-start(f32[1,8,128]{2,1,0:T(8,128)S(1)} %slice.50), channel_id=1, source_target_pairs={{0,1},{1,0},{2,3},{3,2},{4,5},{5,4},{6,7},{7,6},{8,9},{9,8},{10,11... | collective-permute-start | bytes 12296 | tf_op jit(solution)/shard_map/ppermute | solution.py:24
  114.3 3.6 %collective-permute-start.24 = (f32[1,8,128]{2,1,0:T(8,128)S(1)}, f32[1,8,128]{2,1,0:T(8,128)S(1)}, u32[]{:S(2)}, u32[]{:S(2)}) collective-permute-start(f32[1,8,128]{2,1,0:T(8,128)S(1)} %slice.50), channel_id=1, source_target_pairs={{0,2},{1,3},{2,0},{3,1},{4,6},{5,7},{6,4},{7,5},{8,10},{9,11},{10,... | collective-permute-start | bytes 12296 | tf_op jit(solution)/shard_map/ppermute | solution.py:24
  115.7 3.0 %collective-permute-start.25 = (f32[1,8,128]{2,1,0:T(8,128)S(1)}, f32[1,8,128]{2,1,0:T(8,128)S(1)}, u32[]{:S(2)}, u32[]{:S(2)}) collective-permute-start(f32[1,8,128]{2,1,0:T(8,128)S(1)} %slice.50), channel_id=1, source_target_pairs={{0,3},{1,2},{2,1},{3,0},{4,7},{5,6},{6,5},{7,4},{8,11},{9,10},{10,... | collective-permute-start | bytes 12296 | tf_op jit(solution)/shard_map/ppermute | solution.py:24

commit v6 on v5

--- a/solution.py
+++ b/solution.py
@@ -511,9 +511,10 @@
             resids.append(resid)
             stats.append(stat)
         if c < len(CHUNKS) - 1:
-            image = total_of(part)
+            beside = part + partner(part, 1)
+            image = beside + partner(beside, 2)
             held = (begin, width, image, part, env, mixed)
-            waits.append([image] + stats[-1:])
+            waits.append([beside if c == len(CHUNKS) - 2 else image] + stats[-1:])
 
     parts = [part] + [partner(part, mask) for mask in (1, 2, 3)]
     second, share = pl.pallas_call(

time: 120 us -> 118 us (0.983)
  starting transfers between devices: 41.1 us -> 39.2 us
    ppermute x18, starting transfers between devices: 17.1 us -> 15.1 us  [partner(): return lax.ppermute(block, 'sites', route)]
  transfers between devices with their start and end apart: 26 -> 26, of which waited for: 17 -> 16; matrix products, arithmetic and copies ran while one was open for 2% -> 2% of each run, Pallas kernels for 15% -> 16%
where the time goes in v6:
time: 118 us; the launch traced here: 117 us
  waiting for transfers between devices  48.3 us (41%)
  starting transfers between devices  39.2 us (33%)
  Pallas kernels  24.3 us (21%)
  between operations  3.11 us (3%)
  other arithmetic  1.73 us (1%)
    ppermute x18, waiting for transfers between devices, partner(): return lax.ppermute(block, 'sites', route)  25.8 us
    ppermute x8, starting transfers between devices, hand_over(): lax.ppermute(block, 'sites', [(i, j) for i, j in route if 0 <= j < count])  24.1 us
    ppermute x8, waiting for transfers between devices, hand_over(): lax.ppermute(block, 'sites', [(i, j) for i, j in route if 0 <= j < count])  22.5 us
    ppermute x18, starting transfers between devices, partner(): return lax.ppermute(block, 'sites', route)  15.1 us
    pallas_call x4, Pallas kernels, on_device(): pl.pallas_call(functools.partial(first_kernel, begin), in_specs=[vmem] *...  8.82 us
    pallas_call x3, Pallas kernels, early(): pl.pallas_call(functools.partial(early_kernel, begin), in_specs=[vmem] *...  5.27 us
    pallas_call x1, Pallas kernels, on_device(): pl.pallas_call(functools.partial(open_kernel, CHUNKS[:1], parts), in_spec...  3.62 us
    pallas_call x1, Pallas kernels, on_device(): pl.pallas_call(functools.partial(pick_kernel, CHUNKS[0], CHUNKS[1:]), in_...  3.15 us
  transfers between devices with their start and end apart: 26, of which 16 were waited for; matrix products, arithmetic and copies ran while one was open for 2% of the time, Pallas kernels for 16%

profile of v6, /device:TPU:0, one launch (start us, length us, event | category | flops | bytes accessed | tf_op | source)
XLA Modules:
  0.0 117.5 jit_solution(1463375378125975468)
XLA Ops:
  0.6 3.6 %open.1 = (s32[46]{0:T(128)S(1)}, f32[3336,128]{1,0:T(8,128)S(1)}, f32[3336,128]{1,0:T(8,128)S(1)}) custom-call(s32[1]{0:T(128)} %bitcast.place_hbm, s32[4,8]{1,0:T(4,128)} %sectors_hbm.1, s32[4,8]{1,0:T(4,128)} %flow_hbm.1, f32[8,8]{1,0:T(8,128)} %bond_hbm.1, f32[2,128,128]{2,1,0:T(8,128)} %left_tensor.1, f32[2,128,128]{2,1,0:T(8,128)} %right_tensor.1, ...), custom_call_target="tpu_custom_call" | custom-call | flops 1 | bytes 1 | tf_op jit(solution)/shard_map/open/pallas_call | solution.py:404
  4.3 1.3 %collective-permute-start = (f32[3336,128]{1,0:T(8,128)S(1)}, f32[3336,128]{1,0:T(8,128)S(1)}, u32[]{:S(2)}, u32[]{:S(2)}) collective-permute-start(f32[3336,128]{1,0:T(8,128)S(1)} %get-tuple-element.51.sent1), channel_id=1, source_target_pairs={{1,5},{3,7},{4,0},{5,9},{6,2},{7,11},{8,4},{9,13},{10,6},{11,15},{... | collective-permute-start | bytes 5124104 | tf_op jit(solution)/shard_map/ppermute | solution.py:19
  5.6 5.7 %collective-permute-start.1 = (f32[3336,128]{1,0:T(8,128)S(1)}, f32[3336,128]{1,0:T(8,128)S(1)}, u32[]{:S(2)}, u32[]{:S(2)}) collective-permute-start(f32[3336,128]{1,0:T(8,128)S(1)} %get-tuple-element.52.sent0), channel_id=1, source_target_pairs={{0,4},{2,6},{4,8},{5,1},{6,10},{7,3},{8,12},{9,5},{10,14},{11,7},{... | collective-permute-start | bytes 5124104 | tf_op jit(solution)/shard_map/ppermute | solution.py:19
  11.3 2.0 %collective-permute-start.7 = (f32[2,128,128]{2,1,0:T(8,128)S(1)}, f32[2,128,128]{2,1,0:T(8,128)S(1)}, u32[]{:S(2)}, u32[]{:S(2)}) collective-permute-start(f32[2,128,128]{2,1,0:T(8,128)S(1)} %copy-done.1), channel_id=1, source_target_pairs={{0,2},{1,3},{2,0},{3,1},{4,6},{5,7},{6,4},{7,5},{8,10},{9,11},{10,... | collective-permute-start | bytes 393224 | tf_op jit(solution)/shard_map/ppermute | solution.py:24
  13.4 3.1 %pick.1 = (f32[3072,128]{1,0:T(8,128)S(1)}, f32[3072,128]{1,0:T(8,128)S(1)}, f32[1024,128]{1,0:T(8,128)S(1)}, f32[1024,128]{1,0:T(8,128)S(1)}, f32[1024,128]{1,0:T(8,128)S(1)}, /*index=5*/f32[1024,128]{1,0:T(8,128)S(1)}) custom-call(s32[46]{0:T(128)S(1)} %get-tuple-element.50.table, f32[8,8,128,128]{3,2,1,0:T(8,128)} %left_env.3, f32[8,8,128,128]{3,2,1,0:T(8,128)} %right_env.3), custom_call_target="tpu_custom_call" | custom-call | flops 1 | bytes 1 | tf_op jit(solution)/shard_map/pick/pallas_call | solution.py:430
  17.8 2.2 %collective-permute-done.8 = f32[2,128,128]{2,1,0:T(8,128)S(1)} collective-permute-done((f32[2,128,128]{2,1,0:T(8,128)S(1)}, f32[2,128,128]{2,1,0:T(8,128)S(1)}, u32[]{:S(2)}, u32[]{:S(2)}) %collective-permute-start.8) | collective-permute-done | bytes 131104 | tf_op jit(solution)/shard_map/ppermute | solution.py:24
  21.3 4.6 %collective-permute-start.9 = (f32[3072,128]{1,0:T(8,128)S(1)}, f32[3072,128]{1,0:T(8,128)S(1)}, u32[]{:S(2)}, u32[]{:S(2)}) collective-permute-start(f32[3072,128]{1,0:T(8,128)S(1)} %get-tuple-element.59.sent0), channel_id=1, source_target_pairs={{0,4},{2,6},{4,8},{5,1},{6,10},{7,3},{8,12},{9,5},{10,14},{11,7},{... | collective-permute-start | bytes 4718600 | tf_op jit(solution)/shard_map/ppermute | solution.py:19
  29.8 14.8 %collective-permute-done.got1 = f32[3336,128]{1,0:T(8,128)S(1)} collective-permute-done((f32[3336,128]{1,0:T(8,128)S(1)}, f32[3336,128]{1,0:T(8,128)S(1)}, u32[]{:S(2)}, u32[]{:S(2)}) %collective-permute-start) | collective-permute-done | bytes 1708064 | tf_op jit(solution)/shard_map/ppermute | solution.py:19
  44.6 4.3 %collective-permute-done.1.got0 = f32[3336,128]{1,0:T(8,128)S(1)} collective-permute-done((f32[3336,128]{1,0:T(8,128)S(1)}, f32[3336,128]{1,0:T(8,128)S(1)}, u32[]{:S(2)}, u32[]{:S(2)}) %collective-permute-start.1) | collective-permute-done | bytes 1708064 | tf_op jit(solution)/shard_map/ppermute | solution.py:19
  49.0 1.4 %collective-permute-start.11 = (f32[2,2,128,128]{3,2,1,0:T(8,128)S(1)}, f32[2,2,128,128]{3,2,1,0:T(8,128)S(1)}, u32[]{:S(2)}, u32[]{:S(2)}) collective-permute-start(f32[2,2,128,128]{3,2,1,0:T(8,128)S(1)} %get-tuple-element.101), channel_id=1, source_target_pairs={{0,1},{1,0},{2,3},{3,2},{4,5},{5,4},{6,7},{7,6},{8,9},{9,8},{10,11... | collective-permute-start | bytes 786440 | tf_op jit(solution)/shard_map/ppermute | solution.py:24
  50.4 1.5 %collective-permute-start.12 = (f32[2,2,128,128]{3,2,1,0:T(8,128)S(1)}, f32[2,2,128,128]{3,2,1,0:T(8,128)S(1)}, u32[]{:S(2)}, u32[]{:S(2)}) collective-permute-start(f32[2,2,128,128]{3,2,1,0:T(8,128)S(1)} %get-tuple-element.101), channel_id=1, source_target_pairs={{0,2},{1,3},{2,0},{3,1},{4,6},{5,7},{6,4},{7,5},{8,10},{9,11},{10,... | collective-permute-start | bytes 786440 | tf_op jit(solution)/shard_map/ppermute | solution.py:24
  52.0 7.5 %collective-permute-done.12 = f32[2,2,128,128]{3,2,1,0:T(8,128)S(1)} collective-permute-done((f32[2,2,128,128]{3,2,1,0:T(8,128)S(1)}, f32[2,2,128,128]{3,2,1,0:T(8,128)S(1)}, u32[]{:S(2)}, u32[]{:S(2)}) %collective-permute-start.12) | collective-permute-done | bytes 262176 | tf_op jit(solution)/shard_map/ppermute | solution.py:24
  59.5 3.9 %collective-permute-done.13 = f32[2,2,128,128]{3,2,1,0:T(8,128)S(1)} collective-permute-done((f32[2,2,128,128]{3,2,1,0:T(8,128)S(1)}, f32[2,2,128,128]{3,2,1,0:T(8,128)S(1)}, u32[]{:S(2)}, u32[]{:S(2)}) %collective-permute-start.13) | collective-permute-done | bytes 262176 | tf_op jit(solution)/shard_map/ppermute | solution.py:24
  63.5 1.4 %prepare.1 = (f32[8,128,128]{2,1,0:T(8,128)S(1)}, bf16[8,256,256]{2,1,0:T(8,128)(2,1)S(1)}, f32[8,128,128]{2,1,0:T(8,128)S(1)}, bf16[8,128,256]{2,1,0:T(8,128)(2...) custom-call(s32[46]{0:T(128)S(1)} %get-tuple-element.50.table, ...), custom_call_target="tpu_custom_call" | custom-call | flops 1 | bytes 1 | tf_op jit(solution)/shard_map/prepare/pallas_call | solution.py:460
  65.1 3.3 %first_matvec0.1 = (bf16[3,1024,256]{2,1,0:T(8,128)(2,1)S(1)}, bf16[3,1024,256]{2,1,0:T(8,128)(2,1)S(1)}, f32[3,128,128]{2,1,0:T(8,128)S(1)}) custom-call(s32[7,8,128]{2,1,0:T(8,128)S(1)} %broadcast_in_dim.4.flags, f32[8,8,8,128]{3,2,1,0:T(8,128)S(1)} %broadcast_in_dim.5.bond, f32[3336,128]{1,0:T(8,128)S(1)} %collective-permute-done.1.got0, ...), custom_call_target="tpu_custom_call" | custom-call | flops 1 | bytes 1 | tf_op jit(solution)/shard_map/first_matvec0/pallas_call | solution.py:496
  70.5 1.6 %collective-permute-start.15 = (f32[3,128,128]{2,1,0:T(8,128)S(1)}, f32[3,128,128]{2,1,0:T(8,128)S(1)}, u32[]{:S(2)}, u32[]{:S(2)}) collective-permute-start(f32[3,128,128]{2,1,0:T(8,128)S(1)} %add.18), channel_id=1, source_target_pairs={{0,2},{1,3},{2,0},{3,1},{4,6},{5,7},{6,4},{7,5},{8,10},{9,11},{10,... | collective-permute-start | bytes 589832 | tf_op jit(solution)/shard_map/ppermute | solution.py:24
  72.1 4.0 %collective-permute-start.4 = (f32[1024,128]{1,0:T(8,128)S(1)}, f32[1024,128]{1,0:T(8,128)S(1)}, u32[]{:S(2)}, u32[]{:S(2)}) collective-permute-start(f32[1024,128]{1,0:T(8,128)S(1)} %get-tuple-element.55.sent0), channel_id=1, source_target_pairs={{0,4},{2,6},{4,8},{5,1},{6,10},{7,3},{8,12},{9,5},{10,14},{11,7},{... | collective-permute-start | bytes 1572872 | tf_op jit(solution)/shard_map/ppermute | solution.py:19
  78.3 4.5 %collective-permute-start.2 = (f32[1024,128]{1,0:T(8,128)S(1)}, f32[1024,128]{1,0:T(8,128)S(1)}, u32[]{:S(2)}, u32[]{:S(2)}) collective-permute-start(f32[1024,128]{1,0:T(8,128)S(1)} %get-tuple-element.53.sent0), channel_id=1, source_target_pairs={{0,4},{2,6},{4,8},{5,1},{6,10},{7,3},{8,12},{9,5},{10,14},{11,7},{... | collective-permute-start | bytes 1572872 | tf_op jit(solution)/shard_map/ppermute | solution.py:19
  82.8 1.5 %collective-permute-start.3 = (f32[1024,128]{1,0:T(8,128)S(1)}, f32[1024,128]{1,0:T(8,128)S(1)}, u32[]{:S(2)}, u32[]{:S(2)}) collective-permute-start(f32[1024,128]{1,0:T(8,128)S(1)} %get-tuple-element.54.sent1), channel_id=1, source_target_pairs={{1,5},{3,7},{4,0},{5,9},{6,2},{7,11},{8,4},{9,13},{10,6},{11,15},{... | collective-permute-start | bytes 1572872 | tf_op jit(solution)/shard_map/ppermute | solution.py:19
  84.3 3.1 %first_matvec1.1 = (bf16[3,1024,256]{2,1,0:T(8,128)(2,1)S(1)}, bf16[3,1024,256]{2,1,0:T(8,128)(2,1)S(1)}, f32[3,128,128]{2,1,0:T(8,128)S(1)}) custom-call(s32[7,8,128]{2,1,0:T(8,128)S(1)} %broadcast_in_dim.4.flags, f32[8,8,8,128]{3,2,1,0:T(8,128)S(1)} %broadcast_in_dim.5.bond, f32[3072,128]{1,0:T(8,128)S(1)} %collective-permute-done.9.got0, ...), custom_call_target="tpu_custom_call" | custom-call | flops 1 | bytes 1 | tf_op jit(solution)/shard_map/first_matvec1/pallas_call | solution.py:496
  87.5 1.4 %collective-permute-done.16 = f32[3,128,128]{2,1,0:T(8,128)S(1)} collective-permute-done((f32[3,128,128]{2,1,0:T(8,128)S(1)}, f32[3,128,128]{2,1,0:T(8,128)S(1)}, u32[]{:S(2)}, u32[]{:S(2)}) %collective-permute-start.16) | collective-permute-done | bytes 196640 | tf_op jit(solution)/shard_map/ppermute | solution.py:24
  89.0 1.6 %collective-permute-start.17 = (f32[3,128,128]{2,1,0:T(8,128)S(1)}, f32[3,128,128]{2,1,0:T(8,128)S(1)}, u32[]{:S(2)}, u32[]{:S(2)}) collective-permute-start(f32[3,128,128]{2,1,0:T(8,128)S(1)} %add.20), channel_id=1, source_target_pairs={{0,2},{1,3},{2,0},{3,1},{4,6},{5,7},{6,4},{7,5},{8,10},{9,11},{10,... | collective-permute-start | bytes 589832 | tf_op jit(solution)/shard_map/ppermute | solution.py:24
  90.6 2.0 %early_second_matvec.3 = (f32[3,128,128]{2,1,0:T(8,128)S(1)}, f32[8,8,128]{2,1,0:T(8,128)S(1)}) custom-call(f32[3,128,128]{2,1,0:T(8,128)S(1)} %add.19.image, f32[3,128,128]{2,1,0:T(8,128)S(1)} %get-tuple-element.65.part, f32[8,128,128]{2,1,0:T(8,128)S(1)} %get-tuple-element.62.vec, f32[8,128,128]{2,1,0:T(8,128)S(1)} %get-tuple-element.70.middle, ...), custom_call_target="tpu_custom_call" | custom-call | flops 1 | bytes 1 | tf_op jit(solution)/shard_map/early_second_matvec/pallas_call | solution.py:481
  92.6 3.4 %collective-permute-done.17 = f32[3,128,128]{2,1,0:T(8,128)S(1)} collective-permute-done((f32[3,128,128]{2,1,0:T(8,128)S(1)}, f32[3,128,128]{2,1,0:T(8,128)S(1)}, u32[]{:S(2)}, u32[]{:S(2)}) %collective-permute-start.17) | collective-permute-done | bytes 196640 | tf_op jit(solution)/shard_map/ppermute | solution.py:24
  97.4 2.0 %early_second_matvec.4 = (f32[3,128,128]{2,1,0:T(8,128)S(1)}, f32[8,8,128]{2,1,0:T(8,128)S(1)}) custom-call(f32[3,128,128]{2,1,0:T(8,128)S(1)} %add.21.image, f32[3,128,128]{2,1,0:T(8,128)S(1)} %get-tuple-element.68.part, f32[8,128,128]{2,1,0:T(8,128)S(1)} %get-tuple-element.62.vec, f32[8,128,128]{2,1,0:T(8,128)S(1)} %get-tuple-element.70.middle, ...), custom_call_target="tpu_custom_call" | custom-call | flops 1 | bytes 1 | tf_op jit(solution)/shard_map/early_second_matvec/pallas_call | solution.py:481
  99.4 1.6 %collective-permute-start.22 = (f32[1,128,128]{2,1,0:T(8,128)S(1)}, f32[1,128,128]{2,1,0:T(8,128)S(1)}, u32[]{:S(2)}, u32[]{:S(2)}) collective-permute-start(f32[1,128,128]{2,1,0:T(8,128)S(1)} %add.22), channel_id=1, source_target_pairs={{0,2},{1,3},{2,0},{3,1},{4,6},{5,7},{6,4},{7,5},{8,10},{9,11},{10,... | collective-permute-start | bytes 196616 | tf_op jit(solution)/shard_map/ppermute | solution.py:24
  102.0 1.6 %collective-permute-done.3.got1 = f32[1024,128]{1,0:T(8,128)S(1)} collective-permute-done((f32[1024,128]{1,0:T(8,128)S(1)}, f32[1024,128]{1,0:T(8,128)S(1)}, u32[]{:S(2)}, u32[]{:S(2)}) %collective-permute-start.3) | collective-permute-done | bytes 524320 | tf_op jit(solution)/shard_map/ppermute | solution.py:19
  104.8 2.0 %collective-permute-start.20 = (f32[1,128,128]{2,1,0:T(8,128)S(1)}, f32[1,128,128]{2,1,0:T(8,128)S(1)}, u32[]{:S(2)}, u32[]{:S(2)}) collective-permute-start(f32[1,128,128]{2,1,0:T(8,128)S(1)} %get-tuple-element.85.part0), channel_id=1, source_target_pairs={{0,2},{1,3},{2,0},{3,1},{4,6},{5,7},{6,4},{7,5},{8,10},{9,11},{10,... | collective-permute-start | bytes 196616 | tf_op jit(solution)/shard_map/ppermute | solution.py:24
  106.9 1.3 %early_second_matvec.5 = (f32[1,128,128]{2,1,0:T(8,128)S(1)}, f32[8,8,128]{2,1,0:T(8,128)S(1)}) custom-call(f32[1,128,128]{2,1,0:T(8,128)S(1)} %add.23.image, f32[1,128,128]{2,1,0:T(8,128)S(1)} %get-tuple-element.78.part, f32[8,128,128]{2,1,0:T(8,128)S(1)} %get-tuple-element.62.vec, f32[8,128,128]{2,1,0:T(8,128)S(1)} %get-tuple-element.70.middle, ...), custom_call_target="tpu_custom_call" | custom-call | flops 1 | bytes 1 | tf_op jit(solution)/shard_map/early_second_matvec/pallas_call | solution.py:481
  109.3 1.9 %collective-permute-done.21.part3 = f32[1,128,128]{2,1,0:T(8,128)S(1)} collective-permute-done((f32[1,128,128]{2,1,0:T(8,128)S(1)}, f32[1,128,128]{2,1,0:T(8,128)S(1)}, u32[]{:S(2)}, u32[]{:S(2)}) %collective-permute-start.21) | collective-permute-done | bytes 65568 | tf_op jit(solution)/shard_map/ppermute | solution.py:24
  111.2 1.3 %second_matvec.1 = (f32[2,128,128]{2,1,0:T(8,128)S(1)}, f32[3,8,128]{2,1,0:T(8,128)S(1)}) custom-call(s32[7,8,128]{2,1,0:T(8,128)S(1)} %broadcast_in_dim.4.flags, f32[1,128,128]{2,1,0:T(8,128)S(1)} %get-tuple-element.85.part0, f32[1,128,128]{2,1,0:T(8,128)S(1)} %collective-permute-done.19.part1, f32[1,128,128]{2,1,0:T(8,128)S(1)} %collective-permute-done.20.part2, ...), custom_call_target="tpu_custom_call" | custom-call | flops 1 | bytes 1 | tf_op jit(solution)/shard_map/second_matvec/pallas_call | solution.py:520
  114.5 1.8 %collective-permute-done.24.share2 = f32[1,8,128]{2,1,0:T(8,128)S(1)} collective-permute-done((f32[1,8,128]{2,1,0:T(8,128)S(1)}, f32[1,8,128]{2,1,0:T(8,128)S(1)}, u32[]{:S(2)}, u32[]{:S(2)}) %collective-permute-start.24) | collective-permute-done | bytes 4128 | tf_op jit(solution)/shard_map/ppermute | solution.py:24
  (56 shorter events, 17.3 us)
Async XLA Ops:
  0.6 10.6 %copy-start.1 = (f32[2,128,128]{2,1,0:T(8,128)S(1)}, f32[2,128,128]{2,1,0:T(8,128)}, u32[]{:S(2)}) copy-start(f32[2,128,128]{2,1,0:T(8,128)} %param.9) | copy-start | bytes 393220
  4.3 40.3 %collective-permute-start = (f32[3336,128]{1,0:T(8,128)S(1)}, f32[3336,128]{1,0:T(8,128)S(1)}, u32[]{:S(2)}, u32[]{:S(2)}) collective-permute-start(f32[3336,128]{1,0:T(8,128)S(1)} %get-tuple-element.51.sent1), channel_id=1, source_target_pairs={{1,5},{3,7},{4,0},{5,9},{6,2},{7,11},{8,4},{9,13},{10,6},{11,15},{... | collective-permute-start | bytes 5124104 | tf_op jit(solution)/shard_map/ppermute | solution.py:19
  5.6 43.3 %collective-permute-start.1 = (f32[3336,128]{1,0:T(8,128)S(1)}, f32[3336,128]{1,0:T(8,128)S(1)}, u32[]{:S(2)}, u32[]{:S(2)}) collective-permute-start(f32[3336,128]{1,0:T(8,128)S(1)} %get-tuple-element.52.sent0), channel_id=1, source_target_pairs={{0,4},{2,6},{4,8},{5,1},{6,10},{7,3},{8,12},{9,5},{10,14},{11,7},{... | collective-permute-start | bytes 5124104 | tf_op jit(solution)/shard_map/ppermute | solution.py:19
  11.3 5.3 %collective-permute-start.6 = (f32[2,128,128]{2,1,0:T(8,128)S(1)}, f32[2,128,128]{2,1,0:T(8,128)S(1)}, u32[]{:S(2)}, u32[]{:S(2)}) collective-permute-start(f32[2,128,128]{2,1,0:T(8,128)S(1)} %copy-done.1), channel_id=1, source_target_pairs={{0,1},{1,0},{2,3},{3,2},{4,5},{5,4},{6,7},{7,6},{8,9},{9,8},{10,11... | collective-permute-start | bytes 393224 | tf_op jit(solution)/shard_map/ppermute | solution.py:24
  11.3 6.4 %collective-permute-start.7 = (f32[2,128,128]{2,1,0:T(8,128)S(1)}, f32[2,128,128]{2,1,0:T(8,128)S(1)}, u32[]{:S(2)}, u32[]{:S(2)}) collective-permute-start(f32[2,128,128]{2,1,0:T(8,128)S(1)} %copy-done.1), channel_id=1, source_target_pairs={{0,2},{1,3},{2,0},{3,1},{4,6},{5,7},{6,4},{7,5},{8,10},{9,11},{10,... | collective-permute-start | bytes 393224 | tf_op jit(solution)/shard_map/ppermute | solution.py:24
  13.4 6.6 %collective-permute-start.8 = (f32[2,128,128]{2,1,0:T(8,128)S(1)}, f32[2,128,128]{2,1,0:T(8,128)S(1)}, u32[]{:S(2)}, u32[]{:S(2)}) collective-permute-start(f32[2,128,128]{2,1,0:T(8,128)S(1)} %copy-done.1), channel_id=1, source_target_pairs={{0,3},{1,2},{2,1},{3,0},{4,7},{5,6},{6,5},{7,4},{8,11},{9,10},{10,... | collective-permute-start | bytes 393224 | tf_op jit(solution)/shard_map/ppermute | solution.py:24
  20.0 58.4 %collective-permute-start.10 = (f32[3072,128]{1,0:T(8,128)S(1)}, f32[3072,128]{1,0:T(8,128)S(1)}, u32[]{:S(2)}, u32[]{:S(2)}) collective-permute-start(f32[3072,128]{1,0:T(8,128)S(1)} %get-tuple-element.60.sent1), channel_id=1, source_target_pairs={{1,5},{3,7},{4,0},{5,9},{6,2},{7,11},{8,4},{9,13},{10,6},{11,15},{... | collective-permute-start | bytes 4718600 | tf_op jit(solution)/shard_map/ppermute | solution.py:19
  21.3 63.1 %collective-permute-start.9 = (f32[3072,128]{1,0:T(8,128)S(1)}, f32[3072,128]{1,0:T(8,128)S(1)}, u32[]{:S(2)}, u32[]{:S(2)}) collective-permute-start(f32[3072,128]{1,0:T(8,128)S(1)} %get-tuple-element.59.sent0), channel_id=1, source_target_pairs={{0,4},{2,6},{4,8},{5,1},{6,10},{7,3},{8,12},{9,5},{10,14},{11,7},{... | collective-permute-start | bytes 4718600 | tf_op jit(solution)/shard_map/ppermute | solution.py:19
  48.9 14.6 %copy-start = (f32[2,128,128]{2,1,0:T(8,128)S(1)}, f32[2,128,128]{2,1,0:T(8,128)}, u32[]{:S(2)}) copy-start(f32[2,128,128]{2,1,0:T(8,128)} %onsite.1) | copy-start | bytes 393220
  49.0 3.0 %collective-permute-start.11 = (f32[2,2,128,128]{3,2,1,0:T(8,128)S(1)}, f32[2,2,128,128]{3,2,1,0:T(8,128)S(1)}, u32[]{:S(2)}, u32[]{:S(2)}) collective-permute-start(f32[2,2,128,128]{3,2,1,0:T(8,128)S(1)} %get-tuple-element.101), channel_id=1, source_target_pairs={{0,1},{1,0},{2,3},{3,2},{4,5},{5,4},{6,7},{7,6},{8,9},{9,8},{10,11... | collective-permute-start | bytes 786440 | tf_op jit(solution)/shard_map/ppermute | solution.py:24
  50.4 9.2 %collective-permute-start.12 = (f32[2,2,128,128]{3,2,1,0:T(8,128)S(1)}, f32[2,2,128,128]{3,2,1,0:T(8,128)S(1)}, u32[]{:S(2)}, u32[]{:S(2)}) collective-permute-start(f32[2,2,128,128]{3,2,1,0:T(8,128)S(1)} %get-tuple-element.101), channel_id=1, source_target_pairs={{0,2},{1,3},{2,0},{3,1},{4,6},{5,7},{6,4},{7,5},{8,10},{9,11},{10,... | collective-permute-start | bytes 786440 | tf_op jit(solution)/shard_map/ppermute | solution.py:24
  51.9 11.5 %collective-permute-start.13 = (f32[2,2,128,128]{3,2,1,0:T(8,128)S(1)}, f32[2,2,128,128]{3,2,1,0:T(8,128)S(1)}, u32[]{:S(2)}, u32[]{:S(2)}) collective-permute-start(f32[2,2,128,128]{3,2,1,0:T(8,128)S(1)} %get-tuple-element.101), channel_id=1, source_target_pairs={{0,3},{1,2},{2,1},{3,0},{4,7},{5,6},{6,5},{7,4},{8,11},{9,10},{10,... | collective-permute-start | bytes 786440 | tf_op jit(solution)/shard_map/ppermute | solution.py:24
  68.4 2.1 %collective-permute-start.14 = (f32[3,128,128]{2,1,0:T(8,128)S(1)}, f32[3,128,128]{2,1,0:T(8,128)S(1)}, u32[]{:S(2)}, u32[]{:S(2)}) collective-permute-start(f32[3,128,128]{2,1,0:T(8,128)S(1)} %get-tuple-element.65.part), channel_id=1, source_target_pairs={{0,1},{1,0},{2,3},{3,2},{4,5},{5,4},{6,7},{7,6},{8,9},{9,8},{10,11... | collective-permute-start | bytes 589832 | tf_op jit(solution)/shard_map/ppermute | solution.py:24
  70.5 12.3 %collective-permute-start.15 = (f32[3,128,128]{2,1,0:T(8,128)S(1)}, f32[3,128,128]{2,1,0:T(8,128)S(1)}, u32[]{:S(2)}, u32[]{:S(2)}) collective-permute-start(f32[3,128,128]{2,1,0:T(8,128)S(1)} %add.18), channel_id=1, source_target_pairs={{0,2},{1,3},{2,0},{3,1},{4,6},{5,7},{6,4},{7,5},{8,10},{9,11},{10,... | collective-permute-start | bytes 589832 | tf_op jit(solution)/shard_map/ppermute | solution.py:24
  72.1 23.9 %collective-permute-start.4 = (f32[1024,128]{1,0:T(8,128)S(1)}, f32[1024,128]{1,0:T(8,128)S(1)}, u32[]{:S(2)}, u32[]{:S(2)}) collective-permute-start(f32[1024,128]{1,0:T(8,128)S(1)} %get-tuple-element.55.sent0), channel_id=1, source_target_pairs={{0,4},{2,6},{4,8},{5,1},{6,10},{7,3},{8,12},{9,5},{10,14},{11,7},{... | collective-permute-start | bytes 1572872 | tf_op jit(solution)/shard_map/ppermute | solution.py:19
  76.1 20.0 %collective-permute-start.5 = (f32[1024,128]{1,0:T(8,128)S(1)}, f32[1024,128]{1,0:T(8,128)S(1)}, u32[]{:S(2)}, u32[]{:S(2)}) collective-permute-start(f32[1024,128]{1,0:T(8,128)S(1)} %get-tuple-element.56.sent1), channel_id=1, source_target_pairs={{1,5},{3,7},{4,0},{5,9},{6,2},{7,11},{8,4},{9,13},{10,6},{11,15},{... | collective-permute-start | bytes 1572872 | tf_op jit(solution)/shard_map/ppermute | solution.py:19
  78.3 23.6 %collective-permute-start.2 = (f32[1024,128]{1,0:T(8,128)S(1)}, f32[1024,128]{1,0:T(8,128)S(1)}, u32[]{:S(2)}, u32[]{:S(2)}) collective-permute-start(f32[1024,128]{1,0:T(8,128)S(1)} %get-tuple-element.53.sent0), channel_id=1, source_target_pairs={{0,4},{2,6},{4,8},{5,1},{6,10},{7,3},{8,12},{9,5},{10,14},{11,7},{... | collective-permute-start | bytes 1572872 | tf_op jit(solution)/shard_map/ppermute | solution.py:19
  82.8 20.7 %collective-permute-start.3 = (f32[1024,128]{1,0:T(8,128)S(1)}, f32[1024,128]{1,0:T(8,128)S(1)}, u32[]{:S(2)}, u32[]{:S(2)}) collective-permute-start(f32[1024,128]{1,0:T(8,128)S(1)} %get-tuple-element.54.sent1), channel_id=1, source_target_pairs={{1,5},{3,7},{4,0},{5,9},{6,2},{7,11},{8,4},{9,13},{10,6},{11,15},{... | collective-permute-start | bytes 1572872 | tf_op jit(solution)/shard_map/ppermute | solution.py:19
  87.5 1.5 %collective-permute-start.16 = (f32[3,128,128]{2,1,0:T(8,128)S(1)}, f32[3,128,128]{2,1,0:T(8,128)S(1)}, u32[]{:S(2)}, u32[]{:S(2)}) collective-permute-start(f32[3,128,128]{2,1,0:T(8,128)S(1)} %get-tuple-element.68.part), channel_id=1, source_target_pairs={{0,1},{1,0},{2,3},{3,2},{4,5},{5,4},{6,7},{7,6},{8,9},{9,8},{10,11... | collective-permute-start | bytes 589832 | tf_op jit(solution)/shard_map/ppermute | solution.py:24
  89.0 7.0 %collective-permute-start.17 = (f32[3,128,128]{2,1,0:T(8,128)S(1)}, f32[3,128,128]{2,1,0:T(8,128)S(1)}, u32[]{:S(2)}, u32[]{:S(2)}) collective-permute-start(f32[3,128,128]{2,1,0:T(8,128)S(1)} %add.20), channel_id=1, source_target_pairs={{0,2},{1,3},{2,0},{3,1},{4,6},{5,7},{6,4},{7,5},{8,10},{9,11},{10,... | collective-permute-start | bytes 589832 | tf_op jit(solution)/shard_map/ppermute | solution.py:24
  97.3 2.1 %collective-permute-start.18 = (f32[1,128,128]{2,1,0:T(8,128)S(1)}, f32[1,128,128]{2,1,0:T(8,128)S(1)}, u32[]{:S(2)}, u32[]{:S(2)}) collective-permute-start(f32[1,128,128]{2,1,0:T(8,128)S(1)} %get-tuple-element.78.part), channel_id=1, source_target_pairs={{0,1},{1,0},{2,3},{3,2},{4,5},{5,4},{6,7},{7,6},{8,9},{9,8},{10,11... | collective-permute-start | bytes 196616 | tf_op jit(solution)/shard_map/ppermute | solution.py:24
  99.4 7.5 %collective-permute-start.22 = (f32[1,128,128]{2,1,0:T(8,128)S(1)}, f32[1,128,128]{2,1,0:T(8,128)S(1)}, u32[]{:S(2)}, u32[]{:S(2)}) collective-permute-start(f32[1,128,128]{2,1,0:T(8,128)S(1)} %add.22), channel_id=1, source_target_pairs={{0,2},{1,3},{2,0},{3,1},{4,6},{5,7},{6,4},{7,5},{8,10},{9,11},{10,... | collective-permute-start | bytes 196616 | tf_op jit(solution)/shard_map/ppermute | solution.py:24
  104.7 3.5 %collective-permute-start.19 = (f32[1,128,128]{2,1,0:T(8,128)S(1)}, f32[1,128,128]{2,1,0:T(8,128)S(1)}, u32[]{:S(2)}, u32[]{:S(2)}) collective-permute-start(f32[1,128,128]{2,1,0:T(8,128)S(1)} %get-tuple-element.85.part0), channel_id=1, source_target_pairs={{0,1},{1,0},{2,3},{3,2},{4,5},{5,4},{6,7},{7,6},{8,9},{9,8},{10,11... | collective-permute-start | bytes 196616 | tf_op jit(solution)/shard_map/ppermute | solution.py:24
  104.8 4.5 %collective-permute-start.20 = (f32[1,128,128]{2,1,0:T(8,128)S(1)}, f32[1,128,128]{2,1,0:T(8,128)S(1)}, u32[]{:S(2)}, u32[]{:S(2)}) collective-permute-start(f32[1,128,128]{2,1,0:T(8,128)S(1)} %get-tuple-element.85.part0), channel_id=1, source_target_pairs={{0,2},{1,3},{2,0},{3,1},{4,6},{5,7},{6,4},{7,5},{8,10},{9,11},{10,... | collective-permute-start | bytes 196616 | tf_op jit(solution)/shard_map/ppermute | solution.py:24
  106.9 4.4 %collective-permute-start.21 = (f32[1,128,128]{2,1,0:T(8,128)S(1)}, f32[1,128,128]{2,1,0:T(8,128)S(1)}, u32[]{:S(2)}, u32[]{:S(2)}) collective-permute-start(f32[1,128,128]{2,1,0:T(8,128)S(1)} %get-tuple-element.85.part0), channel_id=1, source_target_pairs={{0,3},{1,2},{2,1},{3,0},{4,7},{5,6},{6,5},{7,4},{8,11},{9,10},{10,... | collective-permute-start | bytes 196616 | tf_op jit(solution)/shard_map/ppermute | solution.py:24
  112.6 1.9 %collective-permute-start.23 = (f32[1,8,128]{2,1,0:T(8,128)S(1)}, f32[1,8,128]{2,1,0:T(8,128)S(1)}, u32[]{:S(2)}, u32[]{:S(2)}) collective-permute-start(f32[1,8,128]{2,1,0:T(8,128)S(1)} %slice.50), channel_id=1, source_target_pairs={{0,1},{1,0},{2,3},{3,2},{4,5},{5,4},{6,7},{7,6},{8,9},{9,8},{10,11... | collective-permute-start | bytes 12296 | tf_op jit(solution)/shard_map/ppermute | solution.py:24
  112.7 3.6 %collective-permute-start.24 = (f32[1,8,128]{2,1,0:T(8,128)S(1)}, f32[1,8,128]{2,1,0:T(8,128)S(1)}, u32[]{:S(2)}, u32[]{:S(2)}) collective-permute-start(f32[1,8,128]{2,1,0:T(8,128)S(1)} %slice.50), channel_id=1, source_target_pairs={{0,2},{1,3},{2,0},{3,1},{4,6},{5,7},{6,4},{7,5},{8,10},{9,11},{10,... | collective-permute-start | bytes 12296 | tf_op jit(solution)/shard_map/ppermute | solution.py:24
  113.6 3.1 %collective-permute-start.25 = (f32[1,8,128]{2,1,0:T(8,128)S(1)}, f32[1,8,128]{2,1,0:T(8,128)S(1)}, u32[]{:S(2)}, u32[]{:S(2)}) collective-permute-start(f32[1,8,128]{2,1,0:T(8,128)S(1)} %slice.50), channel_id=1, source_target_pairs={{0,3},{1,2},{2,1},{3,0},{4,7},{5,6},{6,5},{7,4},{8,11},{9,10},{10,... | collective-permute-start | bytes 12296 | tf_op jit(solution)/shard_map/ppermute | solution.py:24

commit v7 on v6

--- a/solution.py
+++ b/solution.py
@@ -9,7 +9,7 @@
 from jax.sharding import PartitionSpec as P
 
 GROUP = 4
-CHUNKS = (3, 3, 1, 1)
+CHUNKS = (2, 3, 2, 1)
 MIB = 1024 * 1024
 
 
@@ -307,7 +307,7 @@
 
 
 def second_kernel(
-    own, widths, flags, part0, part1, part2, part3, vec, left, right, diagonal, env, mixed, *refs
+    own, widths, flags, part0, part1, vec, left, right, diagonal, env, mixed, *refs
 ):
     count = len(widths)
     resids, stats = refs[:count], refs[count : 2 * count]
@@ -318,7 +318,7 @@
     zero = jnp.zeros((size, size), jnp.float32)
     tile = lambda value: jnp.full((8, 128), value, jnp.float32)
 
-    images = [(part0[i] + part1[i]) + (part2[i] + part3[i]) for i in range(late)]
+    images = [part0[i] + part1[i] for i in range(late)]
     along = zero
     for i in range(late):
         along = along + vec[early + i] * images[i]
@@ -516,10 +516,11 @@
             held = (begin, width, image, part, env, mixed)
             waits.append([beside if c == len(CHUNKS) - 2 else image] + stats[-1:])
 
-    parts = [part] + [partner(part, mask) for mask in (1, 2, 3)]
+    beside = part + partner(part, 1)
+    parts = [beside, partner(beside, 2)]
     second, share = pl.pallas_call(
         functools.partial(second_kernel, own, CHUNKS[:-1]),
-        in_specs=[vmem] * (11 + 2 * (len(CHUNKS) - 1)),
+        in_specs=[vmem] * (9 + 2 * (len(CHUNKS) - 1)),
         out_specs=[vmem] * 2,
         out_shape=[shape((own, size, size), f32), shape((3, 8, 128), f32)],
         scratch_shapes=[pltpu.VMEM((total, size, size), f32)],

time: 118 us -> 118 us (level)
  starting transfers between devices: 39.2 us -> 41.5 us
  waiting for transfers between devices: 48.3 us -> 46 us
    ppermute x18 -> x17, starting transfers between devices: 15.1 us -> 18.7 us  [partner(): return lax.ppermute(block, 'sites', route)]
    ppermute x8, waiting for transfers between devices: 22.5 us -> 20.3 us  [hand_over(): lax.ppermute(block, 'sites', [(i, j) for i, j in route if 0 <= j < count])]
    ppermute x8, starting transfers between devices: 24.1 us -> 22.7 us  [hand_over(): lax.ppermute(block, 'sites', [(i, j) for i, j in route if 0 <= j < count])]
    ppermute x18 -> x17, waiting for transfers between devices: 25.8 us -> 25.7 us  [partner(): return lax.ppermute(block, 'sites', route)]
  transfers between devices with their start and end apart: 26 -> 25, of which waited for: 16 -> 15; matrix products, arithmetic and copies ran while one was open for 2% -> 2% of each run, Pallas kernels for 16% -> 16%
where the time goes in v7:
time: 118 us; the launch traced here: 117 us
  waiting for transfers between devices  46 us (39%)
  starting transfers between devices  41.5 us (35%)
  Pallas kernels  24.2 us (21%)
  between operations  3.06 us (3%)
  other arithmetic  1.74 us (1%)
    ppermute x17, waiting for transfers between devices, partner(): return lax.ppermute(block, 'sites', route)  25.7 us
    ppermute x8, starting transfers between devices, hand_over(): lax.ppermute(block, 'sites', [(i, j) for i, j in route if 0 <= j < count])  22.7 us
    ppermute x8, waiting for transfers between devices, hand_over(): lax.ppermute(block, 'sites', [(i, j) for i, j in route if 0 <= j < count])  20.3 us
    ppermute x17, starting transfers between devices, partner(): return lax.ppermute(block, 'sites', route)  18.7 us
    pallas_call x4, Pallas kernels, on_device(): pl.pallas_call(functools.partial(first_kernel, begin), in_specs=[vmem] *...  8.74 us
    pallas_call x3, Pallas kernels, early(): pl.pallas_call(functools.partial(early_kernel, begin), in_specs=[vmem] *...  5.25 us
    pallas_call x1, Pallas kernels, on_device(): pl.pallas_call(functools.partial(pick_kernel, CHUNKS[0], CHUNKS[1:]), in_...  3.46 us
    pallas_call x1, Pallas kernels, on_device(): pl.pallas_call(functools.partial(open_kernel, CHUNKS[:1], parts), in_spec...  3.31 us
  transfers between devices with their start and end apart: 25, of which 15 were waited for; matrix products, arithmetic and copies ran while one was open for 2% of the time, Pallas kernels for 16%

profile of v7, /device:TPU:0, one launch (start us, length us, event | category | flops | bytes accessed | tf_op | source)
XLA Modules:
  0.0 117.3 jit_solution(1512733053182408331)
XLA Ops:
  0.6 3.3 %open.1 = (s32[46]{0:T(128)S(1)}, f32[2312,128]{1,0:T(8,128)S(1)}, f32[2312,128]{1,0:T(8,128)S(1)}) custom-call(s32[1]{0:T(128)} %bitcast.place_hbm, s32[4,8]{1,0:T(4,128)} %sectors_hbm.1, s32[4,8]{1,0:T(4,128)} %flow_hbm.1, f32[8,8]{1,0:T(8,128)} %bond_hbm.1, f32[2,128,128]{2,1,0:T(8,128)} %left_tensor.1, f32[2,128,128]{2,1,0:T(8,128)} %right_tensor.1, ...), custom_call_target="tpu_custom_call" | custom-call | flops 1 | bytes 1 | tf_op jit(solution)/shard_map/open/pallas_call | solution.py:404
  5.3 5.6 %collective-permute-start.1 = (f32[2312,128]{1,0:T(8,128)S(1)}, f32[2312,128]{1,0:T(8,128)S(1)}, u32[]{:S(2)}, u32[]{:S(2)}) collective-permute-start(f32[2312,128]{1,0:T(8,128)S(1)} %get-tuple-element.52.sent0), channel_id=1, source_target_pairs={{0,4},{2,6},{4,8},{5,1},{6,10},{7,3},{8,12},{9,5},{10,14},{11,7},{... | collective-permute-start | bytes 3551240 | tf_op jit(solution)/shard_map/ppermute | solution.py:19
  11.0 2.0 %collective-permute-start.7 = (f32[2,128,128]{2,1,0:T(8,128)S(1)}, f32[2,128,128]{2,1,0:T(8,128)S(1)}, u32[]{:S(2)}, u32[]{:S(2)}) collective-permute-start(f32[2,128,128]{2,1,0:T(8,128)S(1)} %copy-done.1), channel_id=1, source_target_pairs={{0,2},{1,3},{2,0},{3,1},{4,6},{5,7},{6,4},{7,5},{8,10},{9,11},{10,... | collective-permute-start | bytes 393224 | tf_op jit(solution)/shard_map/ppermute | solution.py:24
  13.1 3.5 %pick.1 = (f32[3072,128]{1,0:T(8,128)S(1)}, f32[3072,128]{1,0:T(8,128)S(1)}, f32[2048,128]{1,0:T(8,128)S(1)}, f32[2048,128]{1,0:T(8,128)S(1)}, f32[1024,128]{1,0:T(8,128)S(1)}, /*index=5*/f32[1024,128]{1,0:T(8,128)S(1)}) custom-call(s32[46]{0:T(128)S(1)} %get-tuple-element.50.table, f32[8,8,128,128]{3,2,1,0:T(8,128)} %left_env.3, f32[8,8,128,128]{3,2,1,0:T(8,128)} %right_env.3), custom_call_target="tpu_custom_call" | custom-call | flops 1 | bytes 1 | tf_op jit(solution)/shard_map/pick/pallas_call | solution.py:430
  17.4 2.2 %collective-permute-done.8 = f32[2,128,128]{2,1,0:T(8,128)S(1)} collective-permute-done((f32[2,128,128]{2,1,0:T(8,128)S(1)}, f32[2,128,128]{2,1,0:T(8,128)S(1)}, u32[]{:S(2)}, u32[]{:S(2)}) %collective-permute-start.8) | collective-permute-done | bytes 131104 | tf_op jit(solution)/shard_map/ppermute | solution.py:24
  20.9 4.6 %collective-permute-start.9 = (f32[3072,128]{1,0:T(8,128)S(1)}, f32[3072,128]{1,0:T(8,128)S(1)}, u32[]{:S(2)}, u32[]{:S(2)}) collective-permute-start(f32[3072,128]{1,0:T(8,128)S(1)} %get-tuple-element.59.sent0), channel_id=1, source_target_pairs={{0,4},{2,6},{4,8},{5,1},{6,10},{7,3},{8,12},{9,5},{10,14},{11,7},{... | collective-permute-start | bytes 4718600 | tf_op jit(solution)/shard_map/ppermute | solution.py:19
  26.9 6.2 %collective-permute-done.got1 = f32[2312,128]{1,0:T(8,128)S(1)} collective-permute-done((f32[2312,128]{1,0:T(8,128)S(1)}, f32[2312,128]{1,0:T(8,128)S(1)}, u32[]{:S(2)}, u32[]{:S(2)}) %collective-permute-start) | collective-permute-done | bytes 1183776 | tf_op jit(solution)/shard_map/ppermute | solution.py:19
  33.1 4.2 %collective-permute-done.1.got0 = f32[2312,128]{1,0:T(8,128)S(1)} collective-permute-done((f32[2312,128]{1,0:T(8,128)S(1)}, f32[2312,128]{1,0:T(8,128)S(1)}, u32[]{:S(2)}, u32[]{:S(2)}) %collective-permute-start.1) | collective-permute-done | bytes 1183776 | tf_op jit(solution)/shard_map/ppermute | solution.py:19
  38.8 1.5 %collective-permute-start.12 = (f32[2,2,128,128]{3,2,1,0:T(8,128)S(1)}, f32[2,2,128,128]{3,2,1,0:T(8,128)S(1)}, u32[]{:S(2)}, u32[]{:S(2)}) collective-permute-start(f32[2,2,128,128]{3,2,1,0:T(8,128)S(1)} %get-tuple-element.101), channel_id=1, source_target_pairs={{0,2},{1,3},{2,0},{3,1},{4,6},{5,7},{6,4},{7,5},{8,10},{9,11},{10,... | collective-permute-start | bytes 786440 | tf_op jit(solution)/shard_map/ppermute | solution.py:24
  40.3 3.7 %collective-permute-start.4 = (f32[2048,128]{1,0:T(8,128)S(1)}, f32[2048,128]{1,0:T(8,128)S(1)}, u32[]{:S(2)}, u32[]{:S(2)}) collective-permute-start(f32[2048,128]{1,0:T(8,128)S(1)} %get-tuple-element.55.sent0), channel_id=1, source_target_pairs={{0,4},{2,6},{4,8},{5,1},{6,10},{7,3},{8,12},{9,5},{10,14},{11,7},{... | collective-permute-start | bytes 3145736 | tf_op jit(solution)/shard_map/ppermute | solution.py:19
  48.5 7.5 %collective-permute-done.13 = f32[2,2,128,128]{3,2,1,0:T(8,128)S(1)} collective-permute-done((f32[2,2,128,128]{3,2,1,0:T(8,128)S(1)}, f32[2,2,128,128]{3,2,1,0:T(8,128)S(1)}, u32[]{:S(2)}, u32[]{:S(2)}) %collective-permute-start.13) | collective-permute-done | bytes 262176 | tf_op jit(solution)/shard_map/ppermute | solution.py:24
  56.0 1.4 %prepare.1 = (f32[8,128,128]{2,1,0:T(8,128)S(1)}, bf16[8,256,256]{2,1,0:T(8,128)(2,1)S(1)}, f32[8,128,128]{2,1,0:T(8,128)S(1)}, bf16[8,128,256]{2,1,0:T(8,128)(2...) custom-call(s32[46]{0:T(128)S(1)} %get-tuple-element.50.table, ...), custom_call_target="tpu_custom_call" | custom-call | flops 1 | bytes 1 | tf_op jit(solution)/shard_map/prepare/pallas_call | solution.py:460
  57.6 2.3 %first_matvec0.1 = (bf16[2,1024,256]{2,1,0:T(8,128)(2,1)S(1)}, bf16[2,1024,256]{2,1,0:T(8,128)(2,1)S(1)}, f32[2,128,128]{2,1,0:T(8,128)S(1)}) custom-call(s32[7,8,128]{2,1,0:T(8,128)S(1)} %broadcast_in_dim.4.flags, f32[8,8,8,128]{3,2,1,0:T(8,128)S(1)} %broadcast_in_dim.5.bond, f32[2312,128]{1,0:T(8,128)S(1)} %collective-permute-done.1.got0, ...), custom_call_target="tpu_custom_call" | custom-call | flops 1 | bytes 1 | tf_op jit(solution)/shard_map/first_matvec0/pallas_call | solution.py:496
  62.4 5.1 %collective-permute-done.15 = f32[2,128,128]{2,1,0:T(8,128)S(1)} collective-permute-done((f32[2,128,128]{2,1,0:T(8,128)S(1)}, f32[2,128,128]{2,1,0:T(8,128)S(1)}, u32[]{:S(2)}, u32[]{:S(2)}) %collective-permute-start.15) | collective-permute-done | bytes 131104 | tf_op jit(solution)/shard_map/ppermute | solution.py:24
  67.6 3.4 %collective-permute-done.9.got0 = f32[3072,128]{1,0:T(8,128)S(1)} collective-permute-done((f32[3072,128]{1,0:T(8,128)S(1)}, f32[3072,128]{1,0:T(8,128)S(1)}, u32[]{:S(2)}, u32[]{:S(2)}) %collective-permute-start.9) | collective-permute-done | bytes 1572896 | tf_op jit(solution)/shard_map/ppermute | solution.py:19
  71.0 3.1 %first_matvec1.1 = (bf16[3,1024,256]{2,1,0:T(8,128)(2,1)S(1)}, bf16[3,1024,256]{2,1,0:T(8,128)(2,1)S(1)}, f32[3,128,128]{2,1,0:T(8,128)S(1)}) custom-call(s32[7,8,128]{2,1,0:T(8,128)S(1)} %broadcast_in_dim.4.flags, f32[8,8,8,128]{3,2,1,0:T(8,128)S(1)} %broadcast_in_dim.5.bond, f32[3072,128]{1,0:T(8,128)S(1)} %collective-permute-done.9.got0, ...), custom_call_target="tpu_custom_call" | custom-call | flops 1 | bytes 1 | tf_op jit(solution)/shard_map/first_matvec1/pallas_call | solution.py:496
  74.2 1.4 %collective-permute-start.16 = (f32[3,128,128]{2,1,0:T(8,128)S(1)}, f32[3,128,128]{2,1,0:T(8,128)S(1)}, u32[]{:S(2)}, u32[]{:S(2)}) collective-permute-start(f32[3,128,128]{2,1,0:T(8,128)S(1)} %get-tuple-element.68.part), channel_id=1, source_target_pairs={{0,1},{1,0},{2,3},{3,2},{4,5},{5,4},{6,7},{7,6},{8,9},{9,8},{10,11... | collective-permute-start | bytes 589832 | tf_op jit(solution)/shard_map/ppermute | solution.py:24
  75.5 3.4 %collective-permute-start.2 = (f32[1024,128]{1,0:T(8,128)S(1)}, f32[1024,128]{1,0:T(8,128)S(1)}, u32[]{:S(2)}, u32[]{:S(2)}) collective-permute-start(f32[1024,128]{1,0:T(8,128)S(1)} %get-tuple-element.53.sent0), channel_id=1, source_target_pairs={{0,4},{2,6},{4,8},{5,1},{6,10},{7,3},{8,12},{9,5},{10,14},{11,7},{... | collective-permute-start | bytes 1572872 | tf_op jit(solution)/shard_map/ppermute | solution.py:19
  78.9 1.5 %collective-permute-start.3 = (f32[1024,128]{1,0:T(8,128)S(1)}, f32[1024,128]{1,0:T(8,128)S(1)}, u32[]{:S(2)}, u32[]{:S(2)}) collective-permute-start(f32[1024,128]{1,0:T(8,128)S(1)} %get-tuple-element.54.sent1), channel_id=1, source_target_pairs={{1,5},{3,7},{4,0},{5,9},{6,2},{7,11},{8,4},{9,13},{10,6},{11,15},{... | collective-permute-start | bytes 1572872 | tf_op jit(solution)/shard_map/ppermute | solution.py:19
  80.5 1.7 %collective-permute-start.17 = (f32[3,128,128]{2,1,0:T(8,128)S(1)}, f32[3,128,128]{2,1,0:T(8,128)S(1)}, u32[]{:S(2)}, u32[]{:S(2)}) collective-permute-start(f32[3,128,128]{2,1,0:T(8,128)S(1)} %add.23), channel_id=1, source_target_pairs={{0,2},{1,3},{2,0},{3,1},{4,6},{5,7},{6,4},{7,5},{8,10},{9,11},{10,... | collective-permute-start | bytes 589832 | tf_op jit(solution)/shard_map/ppermute | solution.py:24
  82.2 1.6 %early_second_matvec.3 = (f32[2,128,128]{2,1,0:T(8,128)S(1)}, f32[8,8,128]{2,1,0:T(8,128)S(1)}) custom-call(f32[2,128,128]{2,1,0:T(8,128)S(1)} %add.22.image, f32[2,128,128]{2,1,0:T(8,128)S(1)} %get-tuple-element.65.part, f32[8,128,128]{2,1,0:T(8,128)S(1)} %get-tuple-element.62.vec, f32[8,128,128]{2,1,0:T(8,128)S(1)} %get-tuple-element.70.middle, ...), custom_call_target="tpu_custom_call" | custom-call | flops 1 | bytes 1 | tf_op jit(solution)/shard_map/early_second_matvec/pallas_call | solution.py:481
  83.9 4.3 %collective-permute-done.17 = f32[3,128,128]{2,1,0:T(8,128)S(1)} collective-permute-done((f32[3,128,128]{2,1,0:T(8,128)S(1)}, f32[3,128,128]{2,1,0:T(8,128)S(1)}, u32[]{:S(2)}, u32[]{:S(2)}) %collective-permute-start.17) | collective-permute-done | bytes 196640 | tf_op jit(solution)/shard_map/ppermute | solution.py:24
  88.1 5.4 %collective-permute-done.4.got0 = f32[2048,128]{1,0:T(8,128)S(1)} collective-permute-done((f32[2048,128]{1,0:T(8,128)S(1)}, f32[2048,128]{1,0:T(8,128)S(1)}, u32[]{:S(2)}, u32[]{:S(2)}) %collective-permute-start.4) | collective-permute-done | bytes 1048608 | tf_op jit(solution)/shard_map/ppermute | solution.py:19
  93.5 2.1 %first_matvec2.1 = (bf16[2,1024,256]{2,1,0:T(8,128)(2,1)S(1)}, bf16[2,1024,256]{2,1,0:T(8,128)(2,1)S(1)}, f32[2,128,128]{2,1,0:T(8,128)S(1)}) custom-call(s32[7,8,128]{2,1,0:T(8,128)S(1)} %broadcast_in_dim.4.flags, f32[8,8,8,128]{3,2,1,0:T(8,128)S(1)} %broadcast_in_dim.5.bond, f32[2048,128]{1,0:T(8,128)S(1)} %collective-permute-done.4.got0, ...), custom_call_target="tpu_custom_call" | custom-call | flops 1 | bytes 1 | tf_op jit(solution)/shard_map/first_matvec2/pallas_call | solution.py:496
  95.7 1.3 %collective-permute-start.18 = (f32[2,128,128]{2,1,0:T(8,128)S(1)}, f32[2,128,128]{2,1,0:T(8,128)S(1)}, u32[]{:S(2)}, u32[]{:S(2)}) collective-permute-start(f32[2,128,128]{2,1,0:T(8,128)S(1)} %get-tuple-element.78.part), channel_id=1, source_target_pairs={{0,1},{1,0},{2,3},{3,2},{4,5},{5,4},{6,7},{7,6},{8,9},{9,8},{10,11... | collective-permute-start | bytes 393224 | tf_op jit(solution)/shard_map/ppermute | solution.py:24
  97.0 2.0 %early_second_matvec.4 = (f32[3,128,128]{2,1,0:T(8,128)S(1)}, f32[8,8,128]{2,1,0:T(8,128)S(1)}) custom-call(f32[3,128,128]{2,1,0:T(8,128)S(1)} %add.24.image, f32[3,128,128]{2,1,0:T(8,128)S(1)} %get-tuple-element.68.part, f32[8,128,128]{2,1,0:T(8,128)S(1)} %get-tuple-element.62.vec, f32[8,128,128]{2,1,0:T(8,128)S(1)} %get-tuple-element.70.middle, ...), custom_call_target="tpu_custom_call" | custom-call | flops 1 | bytes 1 | tf_op jit(solution)/shard_map/early_second_matvec/pallas_call | solution.py:481
  99.0 1.6 %collective-permute-start.21 = (f32[2,128,128]{2,1,0:T(8,128)S(1)}, f32[2,128,128]{2,1,0:T(8,128)S(1)}, u32[]{:S(2)}, u32[]{:S(2)}) collective-permute-start(f32[2,128,128]{2,1,0:T(8,128)S(1)} %add.25), channel_id=1, source_target_pairs={{0,2},{1,3},{2,0},{3,1},{4,6},{5,7},{6,4},{7,5},{8,10},{9,11},{10,... | collective-permute-start | bytes 393224 | tf_op jit(solution)/shard_map/ppermute | solution.py:24
  102.9 1.7 %collective-permute-start.19 = (f32[1,128,128]{2,1,0:T(8,128)S(1)}, f32[1,128,128]{2,1,0:T(8,128)S(1)}, u32[]{:S(2)}, u32[]{:S(2)}) collective-permute-start(f32[1,128,128]{2,1,0:T(8,128)S(1)} %get-tuple-element.85), channel_id=1, source_target_pairs={{0,1},{1,0},{2,3},{3,2},{4,5},{5,4},{6,7},{7,6},{8,9},{9,8},{10,11... | collective-permute-start | bytes 196616 | tf_op jit(solution)/shard_map/ppermute | solution.py:24
  105.5 2.0 %collective-permute-start.20 = (f32[1,128,128]{2,1,0:T(8,128)S(1)}, f32[1,128,128]{2,1,0:T(8,128)S(1)}, u32[]{:S(2)}, u32[]{:S(2)}) collective-permute-start(f32[1,128,128]{2,1,0:T(8,128)S(1)} %add.26.part0), channel_id=1, source_target_pairs={{0,2},{1,3},{2,0},{3,1},{4,6},{5,7},{6,4},{7,5},{8,10},{9,11},{10,... | collective-permute-start | bytes 196616 | tf_op jit(solution)/shard_map/ppermute | solution.py:24
  107.6 1.6 %early_second_matvec.5 = (f32[2,128,128]{2,1,0:T(8,128)S(1)}, f32[8,8,128]{2,1,0:T(8,128)S(1)}) custom-call(f32[2,128,128]{2,1,0:T(8,128)S(1)} %add.27.image, f32[2,128,128]{2,1,0:T(8,128)S(1)} %get-tuple-element.78.part, f32[8,128,128]{2,1,0:T(8,128)S(1)} %get-tuple-element.62.vec, f32[8,128,128]{2,1,0:T(8,128)S(1)} %get-tuple-element.70.middle, ...), custom_call_target="tpu_custom_call" | custom-call | flops 1 | bytes 1 | tf_op jit(solution)/shard_map/early_second_matvec/pallas_call | solution.py:481
  111.6 1.8 %collective-permute-start.23 = (f32[1,8,128]{2,1,0:T(8,128)S(1)}, f32[1,8,128]{2,1,0:T(8,128)S(1)}, u32[]{:S(2)}, u32[]{:S(2)}) collective-permute-start(f32[1,8,128]{2,1,0:T(8,128)S(1)} %slice.50), channel_id=1, source_target_pairs={{0,2},{1,3},{2,0},{3,1},{4,6},{5,7},{6,4},{7,5},{8,10},{9,11},{10,... | collective-permute-start | bytes 12296 | tf_op jit(solution)/shard_map/ppermute | solution.py:24
  113.5 1.8 %collective-permute-done.23.share2 = f32[1,8,128]{2,1,0:T(8,128)S(1)} collective-permute-done((f32[1,8,128]{2,1,0:T(8,128)S(1)}, f32[1,8,128]{2,1,0:T(8,128)S(1)}, u32[]{:S(2)}, u32[]{:S(2)}) %collective-permute-start.23) | collective-permute-done | bytes 4128 | tf_op jit(solution)/shard_map/ppermute | solution.py:24
  (55 shorter events, 19.3 us)
Async XLA Ops:
  0.6 10.3 %copy-start.1 = (f32[2,128,128]{2,1,0:T(8,128)S(1)}, f32[2,128,128]{2,1,0:T(8,128)}, u32[]{:S(2)}) copy-start(f32[2,128,128]{2,1,0:T(8,128)} %param.9) | copy-start | bytes 393220
  4.0 29.1 %collective-permute-start = (f32[2312,128]{1,0:T(8,128)S(1)}, f32[2312,128]{1,0:T(8,128)S(1)}, u32[]{:S(2)}, u32[]{:S(2)}) collective-permute-start(f32[2312,128]{1,0:T(8,128)S(1)} %get-tuple-element.51.sent1), channel_id=1, source_target_pairs={{1,5},{3,7},{4,0},{5,9},{6,2},{7,11},{8,4},{9,13},{10,6},{11,15},{... | collective-permute-start | bytes 3551240 | tf_op jit(solution)/shard_map/ppermute | solution.py:19
  5.3 32.1 %collective-permute-start.1 = (f32[2312,128]{1,0:T(8,128)S(1)}, f32[2312,128]{1,0:T(8,128)S(1)}, u32[]{:S(2)}, u32[]{:S(2)}) collective-permute-start(f32[2312,128]{1,0:T(8,128)S(1)} %get-tuple-element.52.sent0), channel_id=1, source_target_pairs={{0,4},{2,6},{4,8},{5,1},{6,10},{7,3},{8,12},{9,5},{10,14},{11,7},{... | collective-permute-start | bytes 3551240 | tf_op jit(solution)/shard_map/ppermute | solution.py:19
  10.9 5.6 %collective-permute-start.6 = (f32[2,128,128]{2,1,0:T(8,128)S(1)}, f32[2,128,128]{2,1,0:T(8,128)S(1)}, u32[]{:S(2)}, u32[]{:S(2)}) collective-permute-start(f32[2,128,128]{2,1,0:T(8,128)S(1)} %copy-done.1), channel_id=1, source_target_pairs={{0,1},{1,0},{2,3},{3,2},{4,5},{5,4},{6,7},{7,6},{8,9},{9,8},{10,11... | collective-permute-start | bytes 393224 | tf_op jit(solution)/shard_map/ppermute | solution.py:24
  11.0 6.4 %collective-permute-start.7 = (f32[2,128,128]{2,1,0:T(8,128)S(1)}, f32[2,128,128]{2,1,0:T(8,128)S(1)}, u32[]{:S(2)}, u32[]{:S(2)}) collective-permute-start(f32[2,128,128]{2,1,0:T(8,128)S(1)} %copy-done.1), channel_id=1, source_target_pairs={{0,2},{1,3},{2,0},{3,1},{4,6},{5,7},{6,4},{7,5},{8,10},{9,11},{10,... | collective-permute-start | bytes 393224 | tf_op jit(solution)/shard_map/ppermute | solution.py:24
  13.0 6.6 %collective-permute-start.8 = (f32[2,128,128]{2,1,0:T(8,128)S(1)}, f32[2,128,128]{2,1,0:T(8,128)S(1)}, u32[]{:S(2)}, u32[]{:S(2)}) collective-permute-start(f32[2,128,128]{2,1,0:T(8,128)S(1)} %copy-done.1), channel_id=1, source_target_pairs={{0,3},{1,2},{2,1},{3,0},{4,7},{5,6},{6,5},{7,4},{8,11},{9,10},{10,... | collective-permute-start | bytes 393224 | tf_op jit(solution)/shard_map/ppermute | solution.py:24
  19.6 47.9 %collective-permute-start.10 = (f32[3072,128]{1,0:T(8,128)S(1)}, f32[3072,128]{1,0:T(8,128)S(1)}, u32[]{:S(2)}, u32[]{:S(2)}) collective-permute-start(f32[3072,128]{1,0:T(8,128)S(1)} %get-tuple-element.60.sent1), channel_id=1, source_target_pairs={{1,5},{3,7},{4,0},{5,9},{6,2},{7,11},{8,4},{9,13},{10,6},{11,15},{... | collective-permute-start | bytes 4718600 | tf_op jit(solution)/shard_map/ppermute | solution.py:19
  20.9 50.1 %collective-permute-start.9 = (f32[3072,128]{1,0:T(8,128)S(1)}, f32[3072,128]{1,0:T(8,128)S(1)}, u32[]{:S(2)}, u32[]{:S(2)}) collective-permute-start(f32[3072,128]{1,0:T(8,128)S(1)} %get-tuple-element.59.sent0), channel_id=1, source_target_pairs={{0,4},{2,6},{4,8},{5,1},{6,10},{7,3},{8,12},{9,5},{10,14},{11,7},{... | collective-permute-start | bytes 4718600 | tf_op jit(solution)/shard_map/ppermute | solution.py:19
  37.4 18.7 %copy-start = (f32[2,128,128]{2,1,0:T(8,128)S(1)}, f32[2,128,128]{2,1,0:T(8,128)}, u32[]{:S(2)}) copy-start(f32[2,128,128]{2,1,0:T(8,128)} %onsite.1) | copy-start | bytes 393220
  37.4 9.2 %collective-permute-start.11 = (f32[2,2,128,128]{3,2,1,0:T(8,128)S(1)}, f32[2,2,128,128]{3,2,1,0:T(8,128)S(1)}, u32[]{:S(2)}, u32[]{:S(2)}) collective-permute-start(f32[2,2,128,128]{3,2,1,0:T(8,128)S(1)} %get-tuple-element.101), channel_id=1, source_target_pairs={{0,1},{1,0},{2,3},{3,2},{4,5},{5,4},{6,7},{7,6},{8,9},{9,8},{10,11... | collective-permute-start | bytes 786440 | tf_op jit(solution)/shard_map/ppermute | solution.py:24
  38.8 9.1 %collective-permute-start.12 = (f32[2,2,128,128]{3,2,1,0:T(8,128)S(1)}, f32[2,2,128,128]{3,2,1,0:T(8,128)S(1)}, u32[]{:S(2)}, u32[]{:S(2)}) collective-permute-start(f32[2,2,128,128]{3,2,1,0:T(8,128)S(1)} %get-tuple-element.101), channel_id=1, source_target_pairs={{0,2},{1,3},{2,0},{3,1},{4,6},{5,7},{6,4},{7,5},{8,10},{9,11},{10,... | collective-permute-start | bytes 786440 | tf_op jit(solution)/shard_map/ppermute | solution.py:24
  40.3 53.2 %collective-permute-start.4 = (f32[2048,128]{1,0:T(8,128)S(1)}, f32[2048,128]{1,0:T(8,128)S(1)}, u32[]{:S(2)}, u32[]{:S(2)}) collective-permute-start(f32[2048,128]{1,0:T(8,128)S(1)} %get-tuple-element.55.sent0), channel_id=1, source_target_pairs={{0,4},{2,6},{4,8},{5,1},{6,10},{7,3},{8,12},{9,5},{10,14},{11,7},{... | collective-permute-start | bytes 3145736 | tf_op jit(solution)/shard_map/ppermute | solution.py:19
  46.6 46.9 %collective-permute-start.5 = (f32[2048,128]{1,0:T(8,128)S(1)}, f32[2048,128]{1,0:T(8,128)S(1)}, u32[]{:S(2)}, u32[]{:S(2)}) collective-permute-start(f32[2048,128]{1,0:T(8,128)S(1)} %get-tuple-element.56.sent1), channel_id=1, source_target_pairs={{1,5},{3,7},{4,0},{5,9},{6,2},{7,11},{8,4},{9,13},{10,6},{11,15},{... | collective-permute-start | bytes 3145736 | tf_op jit(solution)/shard_map/ppermute | solution.py:19
  47.9 8.0 %collective-permute-start.13 = (f32[2,2,128,128]{3,2,1,0:T(8,128)S(1)}, f32[2,2,128,128]{3,2,1,0:T(8,128)S(1)}, u32[]{:S(2)}, u32[]{:S(2)}) collective-permute-start(f32[2,2,128,128]{3,2,1,0:T(8,128)S(1)} %get-tuple-element.101), channel_id=1, source_target_pairs={{0,3},{1,2},{2,1},{3,0},{4,7},{5,6},{6,5},{7,4},{8,11},{9,10},{10,... | collective-permute-start | bytes 786440 | tf_op jit(solution)/shard_map/ppermute | solution.py:24
  59.9 1.8 %collective-permute-start.14 = (f32[2,128,128]{2,1,0:T(8,128)S(1)}, f32[2,128,128]{2,1,0:T(8,128)S(1)}, u32[]{:S(2)}, u32[]{:S(2)}) collective-permute-start(f32[2,128,128]{2,1,0:T(8,128)S(1)} %get-tuple-element.65.part), channel_id=1, source_target_pairs={{0,1},{1,0},{2,3},{3,2},{4,5},{5,4},{6,7},{7,6},{8,9},{9,8},{10,11... | collective-permute-start | bytes 393224 | tf_op jit(solution)/shard_map/ppermute | solution.py:24
  61.7 5.8 %collective-permute-start.15 = (f32[2,128,128]{2,1,0:T(8,128)S(1)}, f32[2,128,128]{2,1,0:T(8,128)S(1)}, u32[]{:S(2)}, u32[]{:S(2)}) collective-permute-start(f32[2,128,128]{2,1,0:T(8,128)S(1)} %add.21), channel_id=1, source_target_pairs={{0,2},{1,3},{2,0},{3,1},{4,6},{5,7},{6,4},{7,5},{8,10},{9,11},{10,... | collective-permute-start | bytes 393224 | tf_op jit(solution)/shard_map/ppermute | solution.py:24
  74.2 6.3 %collective-permute-start.16 = (f32[3,128,128]{2,1,0:T(8,128)S(1)}, f32[3,128,128]{2,1,0:T(8,128)S(1)}, u32[]{:S(2)}, u32[]{:S(2)}) collective-permute-start(f32[3,128,128]{2,1,0:T(8,128)S(1)} %get-tuple-element.68.part), channel_id=1, source_target_pairs={{0,1},{1,0},{2,3},{3,2},{4,5},{5,4},{6,7},{7,6},{8,9},{9,8},{10,11... | collective-permute-start | bytes 589832 | tf_op jit(solution)/shard_map/ppermute | solution.py:24
  75.5 26.1 %collective-permute-start.2 = (f32[1024,128]{1,0:T(8,128)S(1)}, f32[1024,128]{1,0:T(8,128)S(1)}, u32[]{:S(2)}, u32[]{:S(2)}) collective-permute-start(f32[1024,128]{1,0:T(8,128)S(1)} %get-tuple-element.53.sent0), channel_id=1, source_target_pairs={{0,4},{2,6},{4,8},{5,1},{6,10},{7,3},{8,12},{9,5},{10,14},{11,7},{... | collective-permute-start | bytes 1572872 | tf_op jit(solution)/shard_map/ppermute | solution.py:19
  78.9 22.7 %collective-permute-start.3 = (f32[1024,128]{1,0:T(8,128)S(1)}, f32[1024,128]{1,0:T(8,128)S(1)}, u32[]{:S(2)}, u32[]{:S(2)}) collective-permute-start(f32[1024,128]{1,0:T(8,128)S(1)} %get-tuple-element.54.sent1), channel_id=1, source_target_pairs={{1,5},{3,7},{4,0},{5,9},{6,2},{7,11},{8,4},{9,13},{10,6},{11,15},{... | collective-permute-start | bytes 1572872 | tf_op jit(solution)/shard_map/ppermute | solution.py:19
  80.5 7.6 %collective-permute-start.17 = (f32[3,128,128]{2,1,0:T(8,128)S(1)}, f32[3,128,128]{2,1,0:T(8,128)S(1)}, u32[]{:S(2)}, u32[]{:S(2)}) collective-permute-start(f32[3,128,128]{2,1,0:T(8,128)S(1)} %add.23), channel_id=1, source_target_pairs={{0,2},{1,3},{2,0},{3,1},{4,6},{5,7},{6,4},{7,5},{8,10},{9,11},{10,... | collective-permute-start | bytes 589832 | tf_op jit(solution)/shard_map/ppermute | solution.py:24
  95.7 3.3 %collective-permute-start.18 = (f32[2,128,128]{2,1,0:T(8,128)S(1)}, f32[2,128,128]{2,1,0:T(8,128)S(1)}, u32[]{:S(2)}, u32[]{:S(2)}) collective-permute-start(f32[2,128,128]{2,1,0:T(8,128)S(1)} %get-tuple-element.78.part), channel_id=1, source_target_pairs={{0,1},{1,0},{2,3},{3,2},{4,5},{5,4},{6,7},{7,6},{8,9},{9,8},{10,11... | collective-permute-start | bytes 393224 | tf_op jit(solution)/shard_map/ppermute | solution.py:24
  99.0 8.6 %collective-permute-start.21 = (f32[2,128,128]{2,1,0:T(8,128)S(1)}, f32[2,128,128]{2,1,0:T(8,128)S(1)}, u32[]{:S(2)}, u32[]{:S(2)}) collective-permute-start(f32[2,128,128]{2,1,0:T(8,128)S(1)} %add.25), channel_id=1, source_target_pairs={{0,2},{1,3},{2,0},{3,1},{4,6},{5,7},{6,4},{7,5},{8,10},{9,11},{10,... | collective-permute-start | bytes 393224 | tf_op jit(solution)/shard_map/ppermute | solution.py:24
  102.9 2.6 %collective-permute-start.19 = (f32[1,128,128]{2,1,0:T(8,128)S(1)}, f32[1,128,128]{2,1,0:T(8,128)S(1)}, u32[]{:S(2)}, u32[]{:S(2)}) collective-permute-start(f32[1,128,128]{2,1,0:T(8,128)S(1)} %get-tuple-element.85), channel_id=1, source_target_pairs={{0,1},{1,0},{2,3},{3,2},{4,5},{5,4},{6,7},{7,6},{8,9},{9,8},{10,11... | collective-permute-start | bytes 196616 | tf_op jit(solution)/shard_map/ppermute | solution.py:24
  105.5 4.6 %collective-permute-start.20 = (f32[1,128,128]{2,1,0:T(8,128)S(1)}, f32[1,128,128]{2,1,0:T(8,128)S(1)}, u32[]{:S(2)}, u32[]{:S(2)}) collective-permute-start(f32[1,128,128]{2,1,0:T(8,128)S(1)} %add.26.part0), channel_id=1, source_target_pairs={{0,2},{1,3},{2,0},{3,1},{4,6},{5,7},{6,4},{7,5},{8,10},{9,11},{10,... | collective-permute-start | bytes 196616 | tf_op jit(solution)/shard_map/ppermute | solution.py:24
  111.5 2.0 %collective-permute-start.22 = (f32[1,8,128]{2,1,0:T(8,128)S(1)}, f32[1,8,128]{2,1,0:T(8,128)S(1)}, u32[]{:S(2)}, u32[]{:S(2)}) collective-permute-start(f32[1,8,128]{2,1,0:T(8,128)S(1)} %slice.50), channel_id=1, source_target_pairs={{0,1},{1,0},{2,3},{3,2},{4,5},{5,4},{6,7},{7,6},{8,9},{9,8},{10,11... | collective-permute-start | bytes 12296 | tf_op jit(solution)/shard_map/ppermute | solution.py:24
  111.6 3.7 %collective-permute-start.23 = (f32[1,8,128]{2,1,0:T(8,128)S(1)}, f32[1,8,128]{2,1,0:T(8,128)S(1)}, u32[]{:S(2)}, u32[]{:S(2)}) collective-permute-start(f32[1,8,128]{2,1,0:T(8,128)S(1)} %slice.50), channel_id=1, source_target_pairs={{0,2},{1,3},{2,0},{3,1},{4,6},{5,7},{6,4},{7,5},{8,10},{9,11},{10,... | collective-permute-start | bytes 12296 | tf_op jit(solution)/shard_map/ppermute | solution.py:24
  113.4 3.0 %collective-permute-start.24 = (f32[1,8,128]{2,1,0:T(8,128)S(1)}, f32[1,8,128]{2,1,0:T(8,128)S(1)}, u32[]{:S(2)}, u32[]{:S(2)}) collective-permute-start(f32[1,8,128]{2,1,0:T(8,128)S(1)} %slice.50), channel_id=1, source_target_pairs={{0,3},{1,2},{2,1},{3,0},{4,7},{5,6},{6,5},{7,4},{8,11},{9,10},{10,... | collective-permute-start | bytes 12296 | tf_op jit(solution)/shard_map/ppermute | solution.py:24

commit v8 on v7

--- a/solution.py
+++ b/solution.py
@@ -92,97 +92,144 @@
     return pltpu.make_async_copy(env.at[:, index], target, sem)
 
 
-def pick(table, left_env, right_env, outs, sems, begin, chunks):
+def ends(parts):
+    position = lax.axis_index("sites")
+    partition = position // GROUP
+    return partition, partition == 0, partition == parts - 1, position % 2 == 1
+
+
+def open_kernel(
+    width, parts, bond_hbm, left_tensor, right_tensor, left_env, right_env, out0, out1,
+    bond, sems, more, some,
+):
+    own, size = left_tensor.shape[0], left_tensor.shape[1]
+    terms = left_env.shape[0]
+    base = width * terms * size
+    _, first, last, swap = ends(parts)
+    load = pltpu.make_async_copy(bond_hbm, bond, some.at[0])
+    ahead, behind = jnp.logical_not(last), first
+    copies = []
+
+    def start(flag, one, other):
+        pl.when(flag)(one.start)
+        pl.when(jnp.logical_not(flag))(other.start)
+        copies.append(one)
+
+    for side, out in enumerate((out0, out1)):
+        crossed = swap if side == 0 else jnp.logical_not(swap)
+        from_left = jnp.logical_or(
+            jnp.logical_and(jnp.logical_not(crossed), ahead), jnp.logical_and(crossed, behind)
+        )
+        for i in range(width):
+            place = (i, out, i * terms * size, sems.at[side, i])
+            start(from_left, sector_copy(left_env, *place), sector_copy(right_env, *place))
+        for i in range(own):
+            target = out.at[pl.ds(base + i * size, size)]
+            start(
+                jnp.logical_not(crossed),
+                pltpu.make_async_copy(left_tensor.at[i], target, more.at[side, i]),
+                pltpu.make_async_copy(right_tensor.at[i], target, more.at[side, i]),
+            )
+    load.start()
+    load.wait()
+    for out in (out0, out1):
+        rows = slice(base + own * size, base + own * size + terms)
+        out[rows] = jnp.zeros((terms, size), jnp.float32)
+        out[rows, : bond.shape[1]] = bond[...]
+    for copy in copies:
+        copy.wait()
+
+
+def pick_kernel(
+    chunks, parts, sectors_hbm, flow_hbm, left_env, right_env, table, *refs
+):
+    outs, (sectors, flow, turned, lists, sems, some) = refs[:-6], refs[-6:]
     terms, total, size = left_env.shape[:3]
+    width = chunks[0]
+    paired = width + chunks[1]
+    partition, first, last, swap = ends(parts)
+    loads = [
+        pltpu.make_async_copy(sectors_hbm, sectors, some.at[0]),
+        pltpu.make_async_copy(flow_hbm, flow, some.at[1]),
+    ]
+    for copy in loads:
+        copy.start()
+    for copy in loads:
+        copy.wait()
+    as_int = lambda flag: flag.astype(jnp.int32)
+    table[0] = as_int(first)
+    table[1] = as_int(last)
+    table[2] = lax.axis_index("sites") % GROUP
+    table[3] = as_int(swap)
+    step = total + 1
+
+    def orders(which, index):
+        index = jnp.clip(index, 0, parts - 1)
+        base = which * 7 * step
+        before, after = jnp.maximum(index - 1, 0), jnp.minimum(index + 1, parts - 1)
+        for j in range(total):
+            turned[flow[before, j]] = j
+            turned[total + flow[after, j]] = j
+        lefts, rights = [], []
+        for t in range(total):
+            joined = sectors[index, t]
+            lefts.append(jnp.where(index == 0, t, turned[t]))
+            rights.append(jnp.where(index == parts - 1, joined, turned[total + joined]))
+        count = jnp.int32(0)
+        known = [jnp.logical_or(a < width, b < width) for a, b in zip(lefts, rights)]
+        for wanted in (True, False):
+            for t in range(total):
+                lists[base + count] = lefts[t]
+                lists[base + step + count] = rights[t]
+                lists[base + 2 * step + count] = t
+                count = count + as_int(known[t] if wanted else jnp.logical_not(known[t]))
+        for side in range(2):
+            count = jnp.int32(width)
+            for i in range(width):
+                lists[base + (3 + side) * step + i] = i
+            for i in range(paired):
+                source = lists[base + side * step + i]
+                lists[base + (3 + side) * step + count] = source
+                late = source >= width
+                lists[base + (5 + side) * step + i] = jnp.where(late, count, source)
+                count = count + as_int(late)
+            for i in range(paired, total):
+                lists[base + (3 + side) * step + i] = lists[base + side * step + i]
+        return base
+
+    behind_base = orders(0, partition - 1)
+    here = orders(1, partition)
+    ahead_base = orders(2, partition + 1)
+    for i in range(total):
+        for row, source in ((0, 0), (1, 1), (2, 2), (5, 5), (6, 6)):
+            table[HEAD + row * total + i] = lists[here + source * step + i]
+        ahead = jnp.where(last, lists[here + 4 * step + i], lists[ahead_base + 3 * step + i])
+        behind = jnp.where(first, lists[here + 3 * step + i], lists[behind_base + 4 * step + i])
+        table[HEAD + 3 * total + i] = jnp.where(swap, behind, ahead)
+        table[HEAD + 4 * total + i] = jnp.where(swap, ahead, behind)
+    ahead, behind = last.astype(jnp.int32), 1 - first.astype(jnp.int32)
     copies = []
-    for c, width in enumerate(chunks):
+    begin = width
+    for c, count in enumerate(chunks[1:]):
         for side in range(2):
-            base = HEAD + (3 + side) * total
-            from_left = table[HEAD + 5 * total + side] == 0
-            for s in range(width):
+            kinds = (ahead, behind) if side == 0 else (behind, ahead)
+            from_left = jnp.where(swap, kinds[1], kinds[0]) == 0
+            for i in range(count):
                 place = (
-                    table[base + begin + s], outs[2 * c + side], s * terms * size,
-                    sems.at[side, begin + s],
+                    table[HEAD + (3 + side) * total + begin + i], outs[2 * c + side],
+                    i * terms * size, sems.at[side, begin + i],
                 )
                 left, right = sector_copy(left_env, *place), sector_copy(right_env, *place)
                 pl.when(from_left)(left.start)
                 pl.when(jnp.logical_not(from_left))(right.start)
                 copies.append(left)
-        begin += width
-    return copies
-
-
-def open_kernel(
-    chunks, parts, place_hbm, sectors_hbm, flow_hbm, bond_hbm, left_tensor, right_tensor,
-    left_env, right_env, table, *refs,
-):
-    outs, refs = refs[: 2 * len(chunks)], refs[2 * len(chunks) :]
-    place, sectors, flow, order, bond, small, sems, more, some = refs
-    own, size = left_tensor.shape[0], left_tensor.shape[1]
-    terms, total = left_env.shape[0], left_env.shape[1]
-    base = chunks[0] * terms * size
-    inputs = ((place_hbm, place), (sectors_hbm, sectors), (flow_hbm, flow), (bond_hbm, bond))
-    loads = [pltpu.make_async_copy(a, b, some.at[i]) for i, (a, b) in enumerate(inputs)]
-    for copy in loads:
-        copy.start()
-    for copy in loads:
-        copy.wait()
-    partition = place[0] // GROUP
-    before = jnp.maximum(partition - 1, 0)
-    after = jnp.minimum(partition + 1, parts - 1)
-    first, last = partition == 0, partition == parts - 1
-    swap = place[0] % 2 == 1
-    table[0] = first.astype(jnp.int32)
-    table[1] = last.astype(jnp.int32)
-    table[2] = place[0] % GROUP
-    table[3] = swap.astype(jnp.int32)
-    for j in range(total):
-        order[flow[before, j]] = j
-        order[total + flow[partition, j]] = j
-        order[2 * total + flow[after, j]] = j
-    for j in range(total):
-        joined = sectors[partition, j]
-        table[HEAD + j] = order[j]
-        table[HEAD + total + j] = order[2 * total + joined]
-        table[HEAD + 2 * total + j] = joined
-        ahead = jnp.where(last, joined, order[total + j])
-        behind = jnp.where(first, j, order[total + sectors[before, j]])
-        table[HEAD + 3 * total + j] = jnp.where(swap, behind, ahead)
-        table[HEAD + 4 * total + j] = jnp.where(swap, ahead, behind)
-    ahead, behind = last.astype(jnp.int32), 1 - first.astype(jnp.int32)
-    table[HEAD + 5 * total] = jnp.where(swap, behind, ahead)
-    table[HEAD + 5 * total + 1] = jnp.where(swap, ahead, behind)
-    copies = pick(table, left_env, right_env, outs, sems, 0, chunks)
-    small[...] = jnp.zeros_like(small)
-    small[:, : bond.shape[1]] = bond[...]
-    for side in range(2):
-        for i in range(own):
-            target = outs[side].at[pl.ds(base + i * size, size)]
-            straight = pltpu.make_async_copy(
-                (left_tensor, right_tensor)[side].at[i], target, more.at[side, i]
-            )
-            crossed = pltpu.make_async_copy(
-                (right_tensor, left_tensor)[side].at[i], target, more.at[side, i]
-            )
-            pl.when(jnp.logical_not(swap))(straight.start)
-            pl.when(swap)(crossed.start)
-            copies.append(straight)
-        copy = pltpu.make_async_copy(
-            small, outs[side].at[pl.ds(base + own * size, terms)], more.at[side, own]
-        )
-        copy.start()
-        copies.append(copy)
+        begin += count
     for copy in copies:
         copy.wait()
 
 
-def pick_kernel(begin, chunks, table, left_env, right_env, *refs):
-    for copy in pick(table, left_env, right_env, refs[:-1], refs[-1], begin, chunks):
-        copy.wait()
-
-
 def prepare_kernel(
-    own, table, states, pieces, onsite, vec_out, middle_out, plain_out, left_out, right_out,
+    own, table, states, pieces, onsite, vec_out, plain_out, left_out, right_out,
     back_out, diagonal_out, mine_out,
 ):
     total, size = vec_out.shape[0], vec_out.shape[1]
@@ -201,9 +248,9 @@
     norm = jnp.sqrt(jnp.full((8, size), jnp.sum(square), jnp.float32))[0:1]
 
     for j in range(total):
-        vec = states[(j // own) ^ member, j % own] / norm
-        vec_out[j] = vec
-        diagonal_out[j] = jnp.where(j // own == member, onsite[j % own], 0.0)
+        target = table[HEAD + 2 * total + j]
+        vec_out[j] = states[(target // own) ^ member, target % own] / norm
+        diagonal_out[j] = jnp.where(target // own == member, onsite[target % own], 0.0)
         left = jnp.where(table[0] == 1, eye, block(table[HEAD + j], 0))
         right = jnp.where(table[1] == 1, eye, block(table[HEAD + total + j], 1))
         left_out[j] = split_left(left)
@@ -213,49 +260,93 @@
     for i in range(own):
         mine_out[i] = states[0, i] / norm
     for j in range(total):
-        middle = inward(vec_out[j], left_out[j], right_out[j])
-        middle_out[j] = split_right(middle)
-        plain_out[j] = middle
-
-
-def first_kernel(
-    begin, flags, bond, got0, got1, sent0, sent1, middle, vec, back, diagonal,
-    env_out, mixed_out, part_out,
-):
-    size = vec.shape[-1]
-    terms = bond.shape[0]
+        plain_out[j] = inward(vec_out[j], left_out[j], right_out[j])
+
+
+def chooser(flags, got0, got1, sent0, sent1, terms, size):
     flag = lambda k: jnp.broadcast_to(flags[k, 0:1] != 0, (size, size))
     first, last, swap = flag(0), flag(1), flag(2)
-    rows = lambda s, m: slice((s * terms + m) * size, (s * terms + m + 1) * size)
-
-    def chosen(at, end, sent_a, sent_b, got_a, got_b):
+
+    def chosen(s, m, end, sent_a, sent_b, got_a, got_b):
+        at = slice((s * terms + m) * size, (s * terms + m + 1) * size)
         there = jnp.where(swap, got_b[at], got_a[at])
         return jnp.where(end, jnp.where(swap, sent_b[at], sent_a[at]), there)
+
+    left_of = lambda s, m: chosen(s, m, first, sent1, sent0, got0, got1)
+    right_of = lambda s, m: chosen(s, m, last, sent0, sent1, got1, got0)
+    return left_of, right_of
+
+
+def spread(s, slot, bond, env_out, mixed_out, left_of, right_of):
+    terms, size = bond.shape[0], bond.shape[-1]
 
     def weighted(m, k, block):
         tiles = block.reshape(size // 8, 8, size)
         return (tiles * bond[m, k][None]).reshape(size, size)
 
+    rows = lambda m: slice(m * size, (m + 1) * size)
+    for m in range(terms):
+        env_out[slot, rows(m)] = split_left(left_of(s, m))
+    blocks = [right_of(s, m) for m in range(terms)]
+    for m in range(terms):
+        total = weighted(m, 0, blocks[0])
+        for k in range(1, terms):
+            total = total + weighted(m, k, blocks[k])
+        mixed_out[slot, rows(m)] = split_left(total)
+
+
+def image_of(j, env, mixed, terms, plain, vec, back, diagonal):
+    core = core_of(env, mixed, split_right(plain[j]), terms)
+    return product(product(back[j, 0], core), back[j, 1]) + diagonal[j] * vec[j]
+
+
+def either(before, after, slot):
+    count = before.shape[0]
+    late = slot >= count
+    return jnp.where(
+        late, after[jnp.maximum(slot - count, 0)], before[jnp.minimum(slot, count - 1)]
+    )
+
+
+def split_kernel(flags, bond, got0, got1, sent0, sent1, env_out, mixed_out):
+    terms, size = bond.shape[0], bond.shape[-1]
+    left_of, right_of = chooser(flags, got0, got1, sent0, sent1, terms, size)
+    for s in range(env_out.shape[0]):
+        spread(s, s, bond, env_out, mixed_out, left_of, right_of)
+
+
+def first_kernel(
+    begin, flags, bond, got0, got1, sent0, sent1, plain, vec, back, diagonal,
+    env_out, mixed_out, part_out,
+):
+    terms, size = bond.shape[0], bond.shape[-1]
+    left_of, right_of = chooser(flags, got0, got1, sent0, sent1, terms, size)
     for s in range(part_out.shape[0]):
-        for m in range(terms):
-            block = chosen(rows(s, m), first, sent1, sent0, got0, got1)
-            env_out[s, rows(0, m)] = split_left(block)
-        blocks = [chosen(rows(s, m), last, sent0, sent1, got1, got0) for m in range(terms)]
-        for m in range(terms):
-            total = weighted(m, 0, blocks[0])
-            for k in range(1, terms):
-                total = total + weighted(m, k, blocks[k])
-            mixed_out[s, rows(0, m)] = split_left(total)
-        j = begin + s
-        core = core_of(env_out[s], mixed_out[s], middle[j], terms)
-        part = product(product(back[j, 0], core), back[j, 1])
-        part_out[s] = part + diagonal[j] * vec[j]
+        spread(s, s, bond, env_out, mixed_out, left_of, right_of)
+        part_out[s] = image_of(
+            begin + s, env_out[s], mixed_out[s], terms, plain, vec, back, diagonal
+        )
+
+
+def paired_kernel(
+    slots, flags, bond, got0, got1, sent0, sent1, env_before, mixed_before,
+    plain, vec, back, diagonal, env_out, mixed_out, part_out,
+):
+    terms, size = bond.shape[0], bond.shape[-1]
+    total = vec.shape[0]
+    left_of, right_of = chooser(flags, got0, got1, sent0, sent1, terms, size)
+    for s in range(env_out.shape[0]):
+        spread(s, s, bond, env_out, mixed_out, left_of, right_of)
+    for j in range(part_out.shape[0]):
+        env = either(env_before, env_out, slots[j])
+        mixed = either(mixed_before, mixed_out, slots[total + j])
+        part_out[j] = image_of(j, env, mixed, terms, plain, vec, back, diagonal)
 
 
 def early_kernel(
-    begin, image, part, vec, middle, left, right, diagonal, env, mixed,
-    resid_out, stat_out, moved, cores,
-):
+    begin, slots, image, part, vec, middle, left, right, diagonal, env, mixed, *refs
+):
+    before, (resid_out, stat_out, moved, cores) = refs[:-4], refs[-4:]
     width, size = image.shape[0], image.shape[1]
     terms = mixed.shape[1] // size
     zero = jnp.zeros((size, size), jnp.float32)
@@ -287,7 +378,14 @@
         resid_out[i] = resid
         moved[i] = inward(resid, left[begin + i], right[begin + i])
     for i in range(width):
-        cores[i] = core_of(env[i], mixed[i], split_right(moved[i]), terms)
+        if slots is None:
+            sides = env[i], mixed[i]
+        else:
+            sides = (
+                either(before[0], env, slots[i]),
+                either(before[1], mixed, slots[vec.shape[0] + i]),
+            )
+        cores[i] = core_of(*sides, split_right(moved[i]), terms)
     shares = lambda i: diagonal[begin + i]
     both = zero
     for i in range(width):
@@ -357,9 +455,9 @@
     share_out[1] = alpha1
     share_out[2] = beta
     for i in range(own):
-        mine = work[i]
-        for g in range(1, total // own):
-            mine = jnp.where(flags[3 + g, 0:1] != 0, work[g * own + i], mine)
+        mine = work[0]
+        for j in range(1, total):
+            mine = jnp.where(flags[3 + i * total + j, 0:1] != 0, work[j], mine)
         second_out[i] = mine
 
 
@@ -379,7 +477,6 @@
 def on_device(
     state, left_tensor, right_tensor, onsite, left_env, right_env, mpo_bond, sectors, flow
 ):
-    position = lax.axis_index("sites")
     parts = lax.axis_size("sites") // GROUP
     own, size = state.shape[0], state.shape[1]
     terms, total = left_env.shape[0], left_env.shape[1]
@@ -401,42 +498,40 @@
     in_hbm = lambda *values: [
         pltpu.with_memory_space_constraint(value, pltpu.HBM) for value in values
     ]
-    table, *opened = pl.pallas_call(
-        functools.partial(open_kernel, CHUNKS[:1], parts),
-        in_specs=[hbm] * 8,
-        out_specs=[smem] + [vmem] * 2,
-        out_shape=[shape((HEAD + 5 * total + 2,), jnp.int32)] + chunks([0]),
+    opened = pl.pallas_call(
+        functools.partial(open_kernel, CHUNKS[0], parts),
+        in_specs=[hbm] * 5,
+        out_specs=[vmem] * 2,
+        out_shape=chunks([0]),
         scratch_shapes=[
-            pltpu.SMEM((1,), jnp.int32),
+            pltpu.VMEM(mpo_bond.shape, f32),
+            dma((2, CHUNKS[0])),
+            dma((2, own)),
+            dma((1,)),
+        ],
+        cost_estimate=small_cost,
+        compiler_params=params(4),
+        name="open",
+    )(*in_hbm(mpo_bond, left_tensor, right_tensor, left_env, right_env))
+    later = range(1, len(CHUNKS))
+    table, *picked = pl.pallas_call(
+        functools.partial(pick_kernel, CHUNKS, parts),
+        in_specs=[hbm] * 4,
+        out_specs=[smem] + [vmem] * (2 * len(later)),
+        out_shape=[shape((HEAD + 7 * total,), jnp.int32)] + chunks(later),
+        scratch_shapes=[
             pltpu.SMEM(sectors.shape, jnp.int32),
             pltpu.SMEM(flow.shape, jnp.int32),
-            pltpu.SMEM((3 * total,), jnp.int32),
-            pltpu.VMEM(mpo_bond.shape, f32),
-            pltpu.VMEM((terms, size), f32),
+            pltpu.SMEM((2 * total,), jnp.int32),
+            pltpu.SMEM((3 * 7 * (total + 1),), jnp.int32),
             dma((2, total)),
-            dma((2, own + 1)),
-            dma((4,)),
+            dma((2,)),
         ],
         cost_estimate=small_cost,
-        compiler_params=params(16),
-        name="open",
-    )(
-        *in_hbm(
-            jnp.reshape(position, (1,)).astype(jnp.int32), sectors, flow, mpo_bond,
-            left_tensor, right_tensor, left_env, right_env,
-        )
-    )
-    later = range(1, len(CHUNKS))
-    opened += pl.pallas_call(
-        functools.partial(pick_kernel, CHUNKS[0], CHUNKS[1:]),
-        in_specs=[smem] + [hbm] * 2,
-        out_specs=[vmem] * (2 * len(later)),
-        out_shape=chunks(later),
-        scratch_shapes=[dma((2, total))],
-        cost_estimate=small_cost,
-        compiler_params=params(16),
+        compiler_params=params(4),
         name="pick",
-    )(table, *in_hbm(left_env, right_env))
+    )(*in_hbm(sectors, flow, left_env, right_env))
+    opened = list(opened) + picked
     sent = [tuple(opened[2 * c : 2 * c + 2]) for c in range(len(CHUNKS))]
     states = gather(state)
     sent[1], _ = lax.optimization_barrier((sent[1], states))
@@ -451,19 +546,25 @@
     bond = jnp.sum(bond_left[:, None, :] * bond_right[None, :, :], axis=2)
     bond = jnp.broadcast_to(bond[:, :, None, None], (terms, terms, 8, size))
     flags = jnp.concatenate(
-        [table[0:2], table[3:4], (table[2] == jnp.arange(GROUP)).astype(jnp.int32)]
+        [
+            table[0:2],
+            table[3:4],
+            (
+                table[HEAD + 2 * total : HEAD + 3 * total][None, :]
+                == table[2] * own + jnp.arange(own, dtype=jnp.int32)[:, None]
+            ).astype(jnp.int32).reshape(-1),
+        ]
     )
-    flags = jnp.broadcast_to(flags[:, None, None], (3 + GROUP, 8, size))
+    flags = jnp.broadcast_to(flags[:, None, None], (3 + own * total, 8, size))
     tensors = lambda block: block[: own * size].reshape(own, size, size)
     pieces = gather(jnp.stack([tensors(from_left), tensors(from_right)], 1))
 
-    vec, middle, plain, left, right, back, diagonal, mine = pl.pallas_call(
+    vec, plain, left, right, back, diagonal, mine = pl.pallas_call(
         functools.partial(prepare_kernel, own),
         in_specs=[smem] + [vmem] * 3,
-        out_specs=[vmem] * 8,
+        out_specs=[vmem] * 7,
         out_shape=[
             shape((total, size, size), f32),
-            shape((total, 2 * size, 2 * size), bf16),
             shape((total, size, size), f32),
             shape((total, size, 2 * size), bf16),
             shape((total, 2 * size, 2 * size), bf16),
@@ -479,48 +580,67 @@
     def early(begin, width, image, part, env, mixed, after):
         image, _ = lax.optimization_barrier((image, after))
         return pl.pallas_call(
-            functools.partial(early_kernel, begin),
-            in_specs=[vmem] * 9,
+            functools.partial(early_kernel, begin) if begin == 0 else functools.partial(
+                early_kernel, begin, None
+            ),
+            in_specs=([smem] + [vmem] * 2 if begin == 0 else []) + [vmem] * 9,
             out_specs=[vmem] * 2,
             out_shape=[shape((width, size, size), f32), shape((8, 8, 128), f32)],
             scratch_shapes=[pltpu.VMEM((width, size, size), f32)] * 2,
             cost_estimate=small_cost,
             compiler_params=params(12),
             name="early_second_matvec",
-        )(image, part, vec, plain, left, right, diagonal, env, mixed)
+        )(*([slots] if begin == 0 else []), image, part, vec, plain, left, right, diagonal, env, mixed, *(before if begin == 0 else []))
 
     resids, stats, waits, held = [], [], [], None
-    for c, (begin, width) in enumerate(zip(begins, CHUNKS)):
+    slots = table[HEAD + 5 * total : HEAD + 7 * total]
+    groups = (CHUNKS[0] + CHUNKS[1],) + CHUNKS[2:]
+    for c, (begin, width) in enumerate(zip([0] + begins[2:], groups)):
         if c > 0:
-            got[c], _ = lax.optimization_barrier((got[c], waits[c - 1]))
+            got[c + 1], _ = lax.optimization_barrier((got[c + 1], waits[c - 1]))
+            kernel, ahead = functools.partial(first_kernel, begin), [vmem] * 6
+            operands = (flags, bond, *got[c + 1], *sent[c + 1])
+        else:
+            split = shape((CHUNKS[0], rows(1), 2 * size), bf16)
+            kernel, ahead = paired_kernel, [smem] + [vmem] * 8
+            before = pl.pallas_call(
+                split_kernel,
+                in_specs=[vmem] * 6,
+                out_specs=[vmem] * 2,
+                out_shape=[split, split],
+                cost_estimate=small_cost,
+                compiler_params=params(12),
+                name="split",
+            )(flags, bond, *got[0], *sent[0])
+            operands = (slots, flags, bond, *got[1], *sent[1], *before)
         env, mixed, part = pl.pallas_call(
-            functools.partial(first_kernel, begin),
-            in_specs=[vmem] * 10,
+            kernel,
+            in_specs=ahead + [vmem] * 4,
             out_specs=[vmem] * 3,
             out_shape=[
-                shape((width, rows(1), 2 * size), bf16),
-                shape((width, rows(1), 2 * size), bf16),
+                shape((CHUNKS[c + 1], rows(1), 2 * size), bf16),
+                shape((CHUNKS[c + 1], rows(1), 2 * size), bf16),
                 shape((width, size, size), f32),
             ],
             cost_estimate=small_cost,
-        compiler_params=params(12),
+            compiler_params=params(12),
             name=f"first_matvec{c}",
-        )(flags, bond, *got[c], *sent[c], middle, vec, back, diagonal)
+        )(*operands, plain, vec, back, diagonal)
         if held is not None:
             resid, stat = early(*held, after=part)
             resids.append(resid)
             stats.append(stat)
-        if c < len(CHUNKS) - 1:
+        if c < len(groups) - 1:
             beside = part + partner(part, 1)
             image = beside + partner(beside, 2)
             held = (begin, width, image, part, env, mixed)
-            waits.append([beside if c == len(CHUNKS) - 2 else image] + stats[-1:])
+            waits.append([beside if c == len(groups) - 2 else image] + stats[-1:])
 
     beside = part + partner(part, 1)
     parts = [beside, partner(beside, 2)]
     second, share = pl.pallas_call(
-        functools.partial(second_kernel, own, CHUNKS[:-1]),
-        in_specs=[vmem] * (9 + 2 * (len(CHUNKS) - 1)),
+        functools.partial(second_kernel, own, groups[:-1]),
+        in_specs=[vmem] * (9 + 2 * (len(groups) - 1)),
         out_specs=[vmem] * 2,
         out_shape=[shape((own, size, size), f32), shape((3, 8, 128), f32)],
         scratch_shapes=[pltpu.VMEM((total, size, size), f32)],

time: 118 us -> 116 us (0.983)
  waiting for transfers between devices: 46 us -> 31.9 us
  local copies, waits for them, and re-layouts: 0.87 us -> 9.84 us
  starting transfers between devices: 41.5 us -> 36.8 us
  Pallas kernels: 24.2 us -> 28.8 us
  other arithmetic: 1.74 us -> 4.32 us
    unnamed x4 -> x32, local copies, waits for them, and re-layouts: 0.01 us -> 8.22 us
    ppermute x8, waiting for transfers between devices: 20.3 us -> 12.2 us  [hand_over(): lax.ppermute(block, 'sites', [(i, j) for i, j in route if 0 <= j < count])]
    ppermute x17 -> x15, waiting for transfers between devices: 25.7 us -> 19.7 us  [partner(): return lax.ppermute(block, 'sites', route)]
    ppermute x17 -> x15, starting transfers between devices: 18.7 us -> 13.3 us  [partner(): return lax.ppermute(block, 'sites', route)]
    pallas_call x10 -> x9, Pallas kernels: 22.1 us -> 26.8 us  [the longest x3 12.1 us: on_device(): pl.pallas_call(kernel, in_specs=ahead + [vmem] * 4, out_specs=[vmem] * 3,...]
    another operation x3, other arithmetic: 0.17 us -> 1.9 us  [gather(): return jnp.stack(pieces, 0)]
  transfers between devices with their start and end apart: 25 -> 23, of which waited for: 15 -> 11; matrix products, arithmetic and copies ran while one was open for 2% -> 5% of each run, Pallas kernels for 16% -> 22%
where the time goes in v8:
time: 116 us; the launch traced here: 115 us
  starting transfers between devices  36.8 us (32%)
  waiting for transfers between devices  31.9 us (28%)
  Pallas kernels  28.8 us (25%)
  local copies, waits for them, and re-layouts  9.84 us (8%)
  other arithmetic  4.32 us (4%)
  between operations  3.79 us (3%)
    ppermute x8, starting transfers between devices, hand_over(): lax.ppermute(block, 'sites', [(i, j) for i, j in route if 0 <= j < count])  23.5 us
    ppermute x15, waiting for transfers between devices, partner(): return lax.ppermute(block, 'sites', route)  19.7 us
    ppermute x15, starting transfers between devices, partner(): return lax.ppermute(block, 'sites', route)  13.3 us
    ppermute x8, waiting for transfers between devices, hand_over(): lax.ppermute(block, 'sites', [(i, j) for i, j in route if 0 <= j < count])  12.2 us
    pallas_call x3, Pallas kernels, on_device(): pl.pallas_call(kernel, in_specs=ahead + [vmem] * 4, out_specs=[vmem] * 3,...  12.1 us
    unnamed x32, local copies, waits for them, and re-layouts  8.22 us
    pallas_call x1, Pallas kernels, on_device(): pl.pallas_call(functools.partial(pick_kernel, CHUNKS, parts), in_specs=[h...  5.67 us
    pallas_call x2, Pallas kernels, early(): pl.pallas_call(functools.partial(early_kernel, begin) if begin == 0 else...  4.8 us
  transfers between devices with their start and end apart: 23, of which 11 were waited for; matrix products, arithmetic and copies ran while one was open for 5% of the time, Pallas kernels for 22%

profile of v8, /device:TPU:0, one launch (start us, length us, event | category | flops | bytes accessed | tf_op | source)
XLA Modules:
  0.0 115.4 jit_solution(15271304281379954403)
XLA Ops:
  0.6 1.7 %open.1 = (f32[2312,128]{1,0:T(8,128)S(1)}, f32[2312,128]{1,0:T(8,128)S(1)}) custom-call(f32[8,8]{1,0:T(8,128)} %bond_hbm.1, f32[2,128,128]{2,1,0:T(8,128)} %left_tensor.1, f32[2,128,128]{2,1,0:T(8,128)} %right_tensor.1, f32[8,8,128,128]{3,2,1,0:T(8,128)} %left_env.3, f32[8,8,128,128]{3,2,1,0:T(8,128)} %right_env.3), custom_call_target="tpu_custom_call" | custom-call | flops 1 | bytes 1 | tf_op jit(solution)/shard_map/open/pallas_call | solution.py:501
  2.4 1.3 %collective-permute-start = (f32[2312,128]{1,0:T(8,128)S(1)}, f32[2312,128]{1,0:T(8,128)S(1)}, u32[]{:S(2)}, u32[]{:S(2)}) collective-permute-start(f32[2312,128]{1,0:T(8,128)S(1)} %get-tuple-element.44.sent1), channel_id=1, source_target_pairs={{1,5},{3,7},{4,0},{5,9},{6,2},{7,11},{8,4},{9,13},{10,6},{11,15},{... | collective-permute-start | bytes 3551240 | tf_op jit(solution)/shard_map/ppermute | solution.py:19
  3.7 5.6 %collective-permute-start.1 = (f32[2312,128]{1,0:T(8,128)S(1)}, f32[2312,128]{1,0:T(8,128)S(1)}, u32[]{:S(2)}, u32[]{:S(2)}) collective-permute-start(f32[2312,128]{1,0:T(8,128)S(1)} %get-tuple-element.45.sent0), channel_id=1, source_target_pairs={{0,4},{2,6},{4,8},{5,1},{6,10},{7,3},{8,12},{9,5},{10,14},{11,7},{... | collective-permute-start | bytes 3551240 | tf_op jit(solution)/shard_map/ppermute | solution.py:19
  9.4 2.0 %collective-permute-start.7 = (f32[2,128,128]{2,1,0:T(8,128)S(1)}, f32[2,128,128]{2,1,0:T(8,128)S(1)}, u32[]{:S(2)}, u32[]{:S(2)}) collective-permute-start(f32[2,128,128]{2,1,0:T(8,128)S(1)} %copy-done.15), channel_id=1, source_target_pairs={{0,2},{1,3},{2,0},{3,1},{4,6},{5,7},{6,4},{7,5},{8,10},{9,11},{10,... | collective-permute-start | bytes 393224 | tf_op jit(solution)/shard_map/ppermute | solution.py:24
  11.5 5.7 %pick.1 = (s32[60]{0:T(128)S(1)}, f32[3072,128]{1,0:T(8,128)S(1)}, f32[3072,128]{1,0:T(8,128)}, f32[2048,128]{1,0:T(8,128)}, f32[2048,128]{1,0:T(8,128)S(1)}, /*...) custom-call(s32[4,8]{1,0:T(4,128)} %sectors_hbm.1, s32[4,8]{1,0:T(4,128)} %flow_hbm.1, f32[8,8,128,128]{3,2,1,0:T(8,128)} %left_env.3, ...), custom_call_target="tpu_custom_call" | custom-call | flops 1 | bytes 1 | tf_op jit(solution)/shard_map/pick/pallas_call | solution.py:517
  19.8 1.3 %collective-permute-start.10 = (f32[3072,128]{1,0:T(8,128)}, f32[3072,128]{1,0:T(8,128)}, u32[]{:S(2)}, u32[]{:S(2)}) collective-permute-start(f32[3072,128]{1,0:T(8,128)} %get-tuple-element.53.sent1), channel_id=1, source_target_pairs={{1,5},{3,7},{4,0},{5,9},{6,2},{7,11},{8,4},{9,13},{10,6},{11,15},{... | collective-permute-start | bytes 4718600 | tf_op jit(solution)/shard_map/ppermute | solution.py:19
  21.1 5.7 %collective-permute-start.9 = (f32[3072,128]{1,0:T(8,128)S(1)}, f32[3072,128]{1,0:T(8,128)}, u32[]{:S(2)}, u32[]{:S(2)}) collective-permute-start(f32[3072,128]{1,0:T(8,128)S(1)} %get-tuple-element.52.sent0), channel_id=1, source_target_pairs={{0,4},{2,6},{4,8},{5,1},{6,10},{7,3},{8,12},{9,5},{10,14},{11,7},{... | collective-permute-start | bytes 4718600 | tf_op jit(solution)/shard_map/ppermute | solution.py:19
  26.8 3.3 %collective-permute-start.4 = (f32[2048,128]{1,0:T(8,128)}, f32[2048,128]{1,0:T(8,128)}, u32[]{:S(2)}, u32[]{:S(2)}) collective-permute-start(f32[2048,128]{1,0:T(8,128)} %get-tuple-element.48.sent0), channel_id=1, source_target_pairs={{0,4},{2,6},{4,8},{5,1},{6,10},{7,3},{8,12},{9,5},{10,14},{11,7},{... | collective-permute-start | bytes 3145736 | tf_op jit(solution)/shard_map/ppermute | solution.py:19
  33.6 2.1 %collective-permute-done.1.got0 = f32[2312,128]{1,0:T(8,128)S(1)} collective-permute-done((f32[2312,128]{1,0:T(8,128)S(1)}, f32[2312,128]{1,0:T(8,128)S(1)}, u32[]{:S(2)}, u32[]{:S(2)}) %collective-permute-start.1) | collective-permute-done | bytes 1183776 | tf_op jit(solution)/shard_map/ppermute | solution.py:19
  38.3 1.3 %collective-permute-start.11 = (f32[2,2,128,128]{3,2,1,0:T(8,128)}, f32[2,2,128,128]{3,2,1,0:T(8,128)}, u32[]{:S(2)}, u32[]{:S(2)}) collective-permute-start(f32[2,2,128,128]{3,2,1,0:T(8,128)} %get-tuple-element.87), channel_id=1, source_target_pairs={{0,1},{1,0},{2,3},{3,2},{4,5},{5,4},{6,7},{7,6},{8,9},{9,8},{10,11... | collective-permute-start | bytes 786440 | tf_op jit(solution)/shard_map/ppermute | solution.py:24
  39.7 1.5 %collective-permute-start.12 = (f32[2,2,128,128]{3,2,1,0:T(8,128)}, f32[2,2,128,128]{3,2,1,0:T(8,128)}, u32[]{:S(2)}, u32[]{:S(2)}) collective-permute-start(f32[2,2,128,128]{3,2,1,0:T(8,128)} %get-tuple-element.87), channel_id=1, source_target_pairs={{0,2},{1,3},{2,0},{3,1},{4,6},{5,7},{6,4},{7,5},{8,10},{9,11},{10,... | collective-permute-start | bytes 786440 | tf_op jit(solution)/shard_map/ppermute | solution.py:24
  41.8 1.4 %pad_add_fusion = s32[19]{0:T(128)S(1)} fusion(s32[16]{0:T(128)} %reshape.28, s32[1]{0:T(128)} %get-tuple-element.91, s32[2]{0:T(128)S(1)} %bitcast.16), kind=kLoop, calls=%fused_computation.10 | loop fusion | flops 38 | bytes 152 | tf_op jit(solution)/shard_map/concatenate | solution.py:548
  43.2 1.3 %collective-permute-start.5 = (f32[2048,128]{1,0:T(8,128)}, f32[2048,128]{1,0:T(8,128)S(1)}, u32[]{:S(2)}, u32[]{:S(2)}) collective-permute-start(f32[2048,128]{1,0:T(8,128)} %copy-done.6), channel_id=1, source_target_pairs={{1,5},{3,7},{4,0},{5,9},{6,2},{7,11},{8,4},{9,13},{10,6},{11,15},{... | collective-permute-start | bytes 3145736 | tf_op jit(solution)/shard_map/ppermute | solution.py:19
  44.5 3.6 %collective-permute-done.12 = f32[2,2,128,128]{3,2,1,0:T(8,128)} collective-permute-done((f32[2,2,128,128]{3,2,1,0:T(8,128)}, f32[2,2,128,128]{3,2,1,0:T(8,128)}, u32[]{:S(2)}, u32[]{:S(2)}) %collective-permute-start.12) | collective-permute-done | bytes 262176 | tf_op jit(solution)/shard_map/ppermute | solution.py:24
  50.7 1.3 %copy-done.3 = f32[2312,128]{1,0:T(8,128)S(1)} copy-done((f32[2312,128]{1,0:T(8,128)S(1)}, f32[2312,128]{1,0:T(8,128)}, u32[]{:S(2)}) %copy-start.3) | copy-done | bytes 1183768
  52.0 1.3 %copy-done.5 = f32[2312,128]{1,0:T(8,128)S(1)} copy-done((f32[2312,128]{1,0:T(8,128)S(1)}, f32[2312,128]{1,0:T(8,128)}, u32[]{:S(2)}) %copy-start.5) | copy-done | bytes 1183768
  54.5 2.4 %collective-permute-done.13 = f32[2,2,128,128]{3,2,1,0:T(8,128)S(1)} collective-permute-done((f32[2,2,128,128]{3,2,1,0:T(8,128)}, f32[2,2,128,128]{3,2,1,0:T(8,128)S(1)}, u32[]{:S(2)}, u32[]{:S(2)}) %collective-permute-start.13) | collective-permute-done | bytes 262176 | tf_op jit(solution)/shard_map/ppermute | solution.py:24
  58.1 1.3 %prepare.1 = (f32[8,128,128]{2,1,0:T(8,128)S(1)}, f32[8,128,128]{2,1,0:T(8,128)S(1)}, bf16[8,128,256]{2,1,0:T(8,128)(2,1)S(1)}, bf16[8,256,256]{2,1,0:T(8,128)(2...) custom-call(s32[60]{0:T(128)S(1)} %get-tuple-element.43.table, ...), custom_call_target="tpu_custom_call" | custom-call | flops 1 | bytes 1 | tf_op jit(solution)/shard_map/prepare/pallas_call | solution.py:562
  59.4 5.9 %collective-permute-done.10.got1 = f32[3072,128]{1,0:T(8,128)} collective-permute-done((f32[3072,128]{1,0:T(8,128)}, f32[3072,128]{1,0:T(8,128)}, u32[]{:S(2)}, u32[]{:S(2)}) %collective-permute-start.10) | collective-permute-done | bytes 1572896 | tf_op jit(solution)/shard_map/ppermute | solution.py:19
  65.3 4.1 %collective-permute-done.9.got0 = f32[3072,128]{1,0:T(8,128)} collective-permute-done((f32[3072,128]{1,0:T(8,128)S(1)}, f32[3072,128]{1,0:T(8,128)}, u32[]{:S(2)}, u32[]{:S(2)}) %collective-permute-start.9) | collective-permute-done | bytes 1572896 | tf_op jit(solution)/shard_map/ppermute | solution.py:19
  69.4 7.4 %first_matvec0.1 = (bf16[3,1024,256]{2,1,0:T(8,128)(2,1)S(1)}, bf16[3,1024,256]{2,1,0:T(8,128)(2,1)S(1)}, f32[5,128,128]{2,1,0:T(8,128)S(1)}) custom-call(s32[16]{0:T(128)S(1)} %slice.55.slots, s32[19,8,128]{2,1,0:T(8,128)S(1)} %broadcast_in_dim.4.flags, f32[8,8,8,128]{3,2,1,0:T(8,128)S(1)} %broadcast_in_dim.5.bond, ...), custom_call_target="tpu_custom_call" | custom-call | flops 1 | bytes 1 | tf_op jit(solution)/shard_map/first_matvec0/pallas_call | solution.py:616
  76.8 1.3 %collective-permute-start.14 = (f32[5,128,128]{2,1,0:T(8,128)S(1)}, f32[5,128,128]{2,1,0:T(8,128)S(1)}, u32[]{:S(2)}, u32[]{:S(2)}) collective-permute-start(f32[5,128,128]{2,1,0:T(8,128)S(1)} %get-tuple-element.60.part), channel_id=1, source_target_pairs={{0,1},{1,0},{2,3},{3,2},{4,5},{5,4},{6,7},{7,6},{8,9},{9,8},{10,11... | collective-permute-start | bytes 983048 | tf_op jit(solution)/shard_map/ppermute | solution.py:24
  78.1 3.5 %collective-permute-start.2 = (f32[1024,128]{1,0:T(8,128)S(1)}, f32[1024,128]{1,0:T(8,128)S(1)}, u32[]{:S(2)}, u32[]{:S(2)}) collective-permute-start(f32[1024,128]{1,0:T(8,128)S(1)} %copy-done.9), channel_id=1, source_target_pairs={{0,4},{2,6},{4,8},{5,1},{6,10},{7,3},{8,12},{9,5},{10,14},{11,7},{... | collective-permute-start | bytes 1572872 | tf_op jit(solution)/shard_map/ppermute | solution.py:19
  81.7 1.5 %collective-permute-start.3 = (f32[1024,128]{1,0:T(8,128)S(1)}, f32[1024,128]{1,0:T(8,128)S(1)}, u32[]{:S(2)}, u32[]{:S(2)}) collective-permute-start(f32[1024,128]{1,0:T(8,128)S(1)} %copy-done.11), channel_id=1, source_target_pairs={{1,5},{3,7},{4,0},{5,9},{6,2},{7,11},{8,4},{9,13},{10,6},{11,15},{... | collective-permute-start | bytes 1572872 | tf_op jit(solution)/shard_map/ppermute | solution.py:19
  83.2 1.9 %collective-permute-start.15 = (f32[5,128,128]{2,1,0:T(8,128)S(1)}, f32[5,128,128]{2,1,0:T(8,128)S(1)}, u32[]{:S(2)}, u32[]{:S(2)}) collective-permute-start(f32[5,128,128]{2,1,0:T(8,128)S(1)} %add.28), channel_id=1, source_target_pairs={{0,2},{1,3},{2,0},{3,1},{4,6},{5,7},{6,4},{7,5},{8,10},{9,11},{10,... | collective-permute-start | bytes 983048 | tf_op jit(solution)/shard_map/ppermute | solution.py:24
  85.2 8.6 %collective-permute-done.15 = f32[5,128,128]{2,1,0:T(8,128)S(1)} collective-permute-done((f32[5,128,128]{2,1,0:T(8,128)S(1)}, f32[5,128,128]{2,1,0:T(8,128)S(1)}, u32[]{:S(2)}, u32[]{:S(2)}) %collective-permute-start.15) | collective-permute-done | bytes 327712 | tf_op jit(solution)/shard_map/ppermute | solution.py:24
  93.8 3.6 %first_matvec1.1 = (bf16[2,1024,256]{2,1,0:T(8,128)(2,1)S(1)}, bf16[2,1024,256]{2,1,0:T(8,128)(2,1)S(1)}, f32[2,128,128]{2,1,0:T(8,128)S(1)}) custom-call(s32[19,8,128]{2,1,0:T(8,128)S(1)} %broadcast_in_dim.4.flags, f32[8,8,8,128]{3,2,1,0:T(8,128)S(1)} %broadcast_in_dim.5.bond, f32[2048,128]{1,0:T(8,128)} %collective-permute-done.4.got0, ...), custom_call_target="tpu_custom_call" | custom-call | flops 1 | bytes 1 | tf_op jit(solution)/shard_map/first_matvec1/pallas_call | solution.py:616
  97.5 3.2 %early_second_matvec.2 = (f32[5,128,128]{2,1,0:T(8,128)S(1)}, f32[8,8,128]{2,1,0:T(8,128)S(1)}) custom-call(s32[16]{0:T(128)S(1)} %slice.55.slots, f32[5,128,128]{2,1,0:T(8,128)S(1)} %add.29.image, f32[5,128,128]{2,1,0:T(8,128)S(1)} %get-tuple-element.60.part, f32[8,128,128]{2,1,0:T(8,128)S(1)} %get-tuple-element.57.vec, ...), custom_call_target="tpu_custom_call" | custom-call | flops 1 | bytes 1 | tf_op jit(solution)/shard_map/early_second_matvec/pallas_call | solution.py:582
  100.7 1.8 %collective-permute-start.19 = (f32[2,128,128]{2,1,0:T(8,128)S(1)}, f32[2,128,128]{2,1,0:T(8,128)S(1)}, u32[]{:S(2)}, u32[]{:S(2)}) collective-permute-start(f32[2,128,128]{2,1,0:T(8,128)S(1)} %add.30), channel_id=1, source_target_pairs={{0,2},{1,3},{2,0},{3,1},{4,6},{5,7},{6,4},{7,5},{8,10},{9,11},{10,... | collective-permute-start | bytes 393224 | tf_op jit(solution)/shard_map/ppermute | solution.py:24
  106.7 1.6 %early_second_matvec.3 = (f32[2,128,128]{2,1,0:T(8,128)S(1)}, f32[8,8,128]{2,1,0:T(8,128)S(1)}) custom-call(f32[2,128,128]{2,1,0:T(8,128)S(1)} %add.32.image, f32[2,128,128]{2,1,0:T(8,128)S(1)} %get-tuple-element.63.part, f32[8,128,128]{2,1,0:T(8,128)S(1)} %get-tuple-element.57.vec, f32[8,128,128]{2,1,0:T(8,128)S(1)} %get-tuple-element.56.plain.middle, ...), custom_call_target="tpu_custom_call" | custom-call | flops 1 | bytes 1 | tf_op jit(solution)/shard_map/early_second_matvec/pallas_call | solution.py:582
  109.3 1.3 %second_matvec.1 = (f32[2,128,128]{2,1,0:T(8,128)S(1)}, f32[3,8,128]{2,1,0:T(8,128)S(1)}) custom-call(s32[19,8,128]{2,1,0:T(8,128)S(1)} %broadcast_in_dim.4.flags, f32[1,128,128]{2,1,0:T(8,128)S(1)} %add.31.part0, f32[1,128,128]{2,1,0:T(8,128)S(1)} %collective-permute-done.18.part1, f32[8,128,128]{2,1,0:T(8,128)S(1)} %get-tuple-element.57.vec, ...), custom_call_target="tpu_custom_call" | custom-call | flops 1 | bytes 1 | tf_op jit(solution)/shard_map/second_matvec/pallas_call | solution.py:641
  112.6 1.8 %collective-permute-done.21.share2 = f32[1,8,128]{2,1,0:T(8,128)S(1)} collective-permute-done((f32[1,8,128]{2,1,0:T(8,128)S(1)}, f32[1,8,128]{2,1,0:T(8,128)S(1)}, u32[]{:S(2)}, u32[]{:S(2)}) %collective-permute-start.21) | collective-permute-done | bytes 4128 | tf_op jit(solution)/shard_map/ppermute | solution.py:24
  (80 shorter events, 19.9 us)
Async XLA Ops:
  0.6 8.7 %copy-start.15 = (f32[2,128,128]{2,1,0:T(8,128)S(1)}, f32[2,128,128]{2,1,0:T(8,128)}, u32[]{:S(2)}) copy-start(f32[2,128,128]{2,1,0:T(8,128)} %param.9) | copy-start | bytes 393220
  2.4 14.8 %copy-start.2 = (f32[2312,128]{1,0:T(8,128)}, f32[2312,128]{1,0:T(8,128)S(1)}, u32[]{:S(2)}) copy-start(f32[2312,128]{1,0:T(8,128)S(1)} %get-tuple-element.45.sent0) | copy-start | bytes 3551236
  2.4 14.8 %copy-start.4 = (f32[2312,128]{1,0:T(8,128)}, f32[2312,128]{1,0:T(8,128)S(1)}, u32[]{:S(2)}) copy-start(f32[2312,128]{1,0:T(8,128)S(1)} %get-tuple-element.44.sent1) | copy-start | bytes 3551236
  2.4 31.2 %collective-permute-start = (f32[2312,128]{1,0:T(8,128)S(1)}, f32[2312,128]{1,0:T(8,128)S(1)}, u32[]{:S(2)}, u32[]{:S(2)}) collective-permute-start(f32[2312,128]{1,0:T(8,128)S(1)} %get-tuple-element.44.sent1), channel_id=1, source_target_pairs={{1,5},{3,7},{4,0},{5,9},{6,2},{7,11},{8,4},{9,13},{10,6},{11,15},{... | collective-permute-start | bytes 3551240 | tf_op jit(solution)/shard_map/ppermute | solution.py:19
  3.7 32.0 %collective-permute-start.1 = (f32[2312,128]{1,0:T(8,128)S(1)}, f32[2312,128]{1,0:T(8,128)S(1)}, u32[]{:S(2)}, u32[]{:S(2)}) collective-permute-start(f32[2312,128]{1,0:T(8,128)S(1)} %get-tuple-element.45.sent0), channel_id=1, source_target_pairs={{0,4},{2,6},{4,8},{5,1},{6,10},{7,3},{8,12},{9,5},{10,14},{11,7},{... | collective-permute-start | bytes 3551240 | tf_op jit(solution)/shard_map/ppermute | solution.py:19
  9.3 10.5 %collective-permute-start.6 = (f32[2,128,128]{2,1,0:T(8,128)S(1)}, f32[2,128,128]{2,1,0:T(8,128)S(1)}, u32[]{:S(2)}, u32[]{:S(2)}) collective-permute-start(f32[2,128,128]{2,1,0:T(8,128)S(1)} %copy-done.15), channel_id=1, source_target_pairs={{0,1},{1,0},{2,3},{3,2},{4,5},{5,4},{6,7},{7,6},{8,9},{9,8},{10,11... | collective-permute-start | bytes 393224 | tf_op jit(solution)/shard_map/ppermute | solution.py:24
  9.4 10.4 %collective-permute-start.7 = (f32[2,128,128]{2,1,0:T(8,128)S(1)}, f32[2,128,128]{2,1,0:T(8,128)S(1)}, u32[]{:S(2)}, u32[]{:S(2)}) collective-permute-start(f32[2,128,128]{2,1,0:T(8,128)S(1)} %copy-done.15), channel_id=1, source_target_pairs={{0,2},{1,3},{2,0},{3,1},{4,6},{5,7},{6,4},{7,5},{8,10},{9,11},{10,... | collective-permute-start | bytes 393224 | tf_op jit(solution)/shard_map/ppermute | solution.py:24
  11.4 8.4 %collective-permute-start.8 = (f32[2,128,128]{2,1,0:T(8,128)S(1)}, f32[2,128,128]{2,1,0:T(8,128)S(1)}, u32[]{:S(2)}, u32[]{:S(2)}) collective-permute-start(f32[2,128,128]{2,1,0:T(8,128)S(1)} %copy-done.15), channel_id=1, source_target_pairs={{0,3},{1,2},{2,1},{3,0},{4,7},{5,6},{6,5},{7,4},{8,11},{9,10},{10,... | collective-permute-start | bytes 393224 | tf_op jit(solution)/shard_map/ppermute | solution.py:24
  19.8 45.5 %collective-permute-start.10 = (f32[3072,128]{1,0:T(8,128)}, f32[3072,128]{1,0:T(8,128)}, u32[]{:S(2)}, u32[]{:S(2)}) collective-permute-start(f32[3072,128]{1,0:T(8,128)} %get-tuple-element.53.sent1), channel_id=1, source_target_pairs={{1,5},{3,7},{4,0},{5,9},{6,2},{7,11},{8,4},{9,13},{10,6},{11,15},{... | collective-permute-start | bytes 4718600 | tf_op jit(solution)/shard_map/ppermute | solution.py:19
  21.1 48.3 %collective-permute-start.9 = (f32[3072,128]{1,0:T(8,128)S(1)}, f32[3072,128]{1,0:T(8,128)}, u32[]{:S(2)}, u32[]{:S(2)}) collective-permute-start(f32[3072,128]{1,0:T(8,128)S(1)} %get-tuple-element.52.sent0), channel_id=1, source_target_pairs={{0,4},{2,6},{4,8},{5,1},{6,10},{7,3},{8,12},{9,5},{10,14},{11,7},{... | collective-permute-start | bytes 4718600 | tf_op jit(solution)/shard_map/ppermute | solution.py:19
  26.8 66.9 %collective-permute-start.4 = (f32[2048,128]{1,0:T(8,128)}, f32[2048,128]{1,0:T(8,128)}, u32[]{:S(2)}, u32[]{:S(2)}) collective-permute-start(f32[2048,128]{1,0:T(8,128)} %get-tuple-element.48.sent0), channel_id=1, source_target_pairs={{0,4},{2,6},{4,8},{5,1},{6,10},{7,3},{8,12},{9,5},{10,14},{11,7},{... | collective-permute-start | bytes 3145736 | tf_op jit(solution)/shard_map/ppermute | solution.py:19
  38.3 4.9 %collective-permute-start.11 = (f32[2,2,128,128]{3,2,1,0:T(8,128)}, f32[2,2,128,128]{3,2,1,0:T(8,128)}, u32[]{:S(2)}, u32[]{:S(2)}) collective-permute-start(f32[2,2,128,128]{3,2,1,0:T(8,128)} %get-tuple-element.87), channel_id=1, source_target_pairs={{0,1},{1,0},{2,3},{3,2},{4,5},{5,4},{6,7},{7,6},{8,9},{9,8},{10,11... | collective-permute-start | bytes 786440 | tf_op jit(solution)/shard_map/ppermute | solution.py:24
  39.7 8.5 %collective-permute-start.12 = (f32[2,2,128,128]{3,2,1,0:T(8,128)}, f32[2,2,128,128]{3,2,1,0:T(8,128)}, u32[]{:S(2)}, u32[]{:S(2)}) collective-permute-start(f32[2,2,128,128]{3,2,1,0:T(8,128)} %get-tuple-element.87), channel_id=1, source_target_pairs={{0,2},{1,3},{2,0},{3,1},{4,6},{5,7},{6,4},{7,5},{8,10},{9,11},{10,... | collective-permute-start | bytes 786440 | tf_op jit(solution)/shard_map/ppermute | solution.py:24
  43.2 50.6 %collective-permute-start.5 = (f32[2048,128]{1,0:T(8,128)}, f32[2048,128]{1,0:T(8,128)S(1)}, u32[]{:S(2)}, u32[]{:S(2)}) collective-permute-start(f32[2048,128]{1,0:T(8,128)} %copy-done.6), channel_id=1, source_target_pairs={{1,5},{3,7},{4,0},{5,9},{6,2},{7,11},{8,4},{9,13},{10,6},{11,15},{... | collective-permute-start | bytes 3145736 | tf_op jit(solution)/shard_map/ppermute | solution.py:19
  48.2 8.7 %collective-permute-start.13 = (f32[2,2,128,128]{3,2,1,0:T(8,128)}, f32[2,2,128,128]{3,2,1,0:T(8,128)S(1)}, u32[]{:S(2)}, u32[]{:S(2)}) collective-permute-start(f32[2,2,128,128]{3,2,1,0:T(8,128)} %get-tuple-element.87), channel_id=1, source_target_pairs={{0,3},{1,2},{2,1},{3,0},{4,7},{5,6},{6,5},{7,4},{8,11},{9,10},{10,... | collective-permute-start | bytes 786440 | tf_op jit(solution)/shard_map/ppermute | solution.py:24
  49.5 1.3 %copy-start.1 = (f32[2312,128]{1,0:T(8,128)S(1)}, f32[2312,128]{1,0:T(8,128)}, u32[]{:S(2)}) copy-start(f32[2312,128]{1,0:T(8,128)} %copy-done) | copy-start | bytes 3551236
  52.0 1.3 %copy-start.5 = (f32[2312,128]{1,0:T(8,128)S(1)}, f32[2312,128]{1,0:T(8,128)}, u32[]{:S(2)}) copy-start(f32[2312,128]{1,0:T(8,128)} %copy-done.4) | copy-start | bytes 3551236
  54.5 3.6 %copy-start.12 = (f32[2,128,128]{2,1,0:T(8,128)S(1)}, f32[2,128,128]{2,1,0:T(8,128)}, u32[]{:S(2)}) copy-start(f32[2,128,128]{2,1,0:T(8,128)} %onsite.1) | copy-start | bytes 393220
  69.4 8.7 %copy-start.9 = (f32[1024,128]{1,0:T(8,128)S(1)}, f32[1024,128]{1,0:T(8,128)}, u32[]{:S(2)}) copy-start(f32[1024,128]{1,0:T(8,128)} %copy-done.8) | copy-start | bytes 1572868
  69.4 12.3 %copy-start.11 = (f32[1024,128]{1,0:T(8,128)S(1)}, f32[1024,128]{1,0:T(8,128)}, u32[]{:S(2)}) copy-start(f32[1024,128]{1,0:T(8,128)} %copy-done.10) | copy-start | bytes 1572868
  76.8 17.0 %copy-start.7 = (f32[2048,128]{1,0:T(8,128)S(1)}, f32[2048,128]{1,0:T(8,128)}, u32[]{:S(2)}) copy-start(f32[2048,128]{1,0:T(8,128)} %copy-done.6) | copy-start | bytes 3145732
  76.8 6.3 %collective-permute-start.14 = (f32[5,128,128]{2,1,0:T(8,128)S(1)}, f32[5,128,128]{2,1,0:T(8,128)S(1)}, u32[]{:S(2)}, u32[]{:S(2)}) collective-permute-start(f32[5,128,128]{2,1,0:T(8,128)S(1)} %get-tuple-element.60.part), channel_id=1, source_target_pairs={{0,1},{1,0},{2,3},{3,2},{4,5},{5,4},{6,7},{7,6},{8,9},{9,8},{10,11... | collective-permute-start | bytes 983048 | tf_op jit(solution)/shard_map/ppermute | solution.py:24
  78.1 24.3 %collective-permute-start.2 = (f32[1024,128]{1,0:T(8,128)S(1)}, f32[1024,128]{1,0:T(8,128)S(1)}, u32[]{:S(2)}, u32[]{:S(2)}) collective-permute-start(f32[1024,128]{1,0:T(8,128)S(1)} %copy-done.9), channel_id=1, source_target_pairs={{0,4},{2,6},{4,8},{5,1},{6,10},{7,3},{8,12},{9,5},{10,14},{11,7},{... | collective-permute-start | bytes 1572872 | tf_op jit(solution)/shard_map/ppermute | solution.py:19
  81.7 20.8 %collective-permute-start.3 = (f32[1024,128]{1,0:T(8,128)S(1)}, f32[1024,128]{1,0:T(8,128)S(1)}, u32[]{:S(2)}, u32[]{:S(2)}) collective-permute-start(f32[1024,128]{1,0:T(8,128)S(1)} %copy-done.11), channel_id=1, source_target_pairs={{1,5},{3,7},{4,0},{5,9},{6,2},{7,11},{8,4},{9,13},{10,6},{11,15},{... | collective-permute-start | bytes 1572872 | tf_op jit(solution)/shard_map/ppermute | solution.py:19
  83.2 10.5 %collective-permute-start.15 = (f32[5,128,128]{2,1,0:T(8,128)S(1)}, f32[5,128,128]{2,1,0:T(8,128)S(1)}, u32[]{:S(2)}, u32[]{:S(2)}) collective-permute-start(f32[5,128,128]{2,1,0:T(8,128)S(1)} %add.28), channel_id=1, source_target_pairs={{0,2},{1,3},{2,0},{3,1},{4,6},{5,7},{6,4},{7,5},{8,10},{9,11},{10,... | collective-permute-start | bytes 983048 | tf_op jit(solution)/shard_map/ppermute | solution.py:24
  97.4 3.2 %collective-permute-start.16 = (f32[2,128,128]{2,1,0:T(8,128)S(1)}, f32[2,128,128]{2,1,0:T(8,128)S(1)}, u32[]{:S(2)}, u32[]{:S(2)}) collective-permute-start(f32[2,128,128]{2,1,0:T(8,128)S(1)} %get-tuple-element.63.part), channel_id=1, source_target_pairs={{0,1},{1,0},{2,3},{3,2},{4,5},{5,4},{6,7},{7,6},{8,9},{9,8},{10,11... | collective-permute-start | bytes 393224 | tf_op jit(solution)/shard_map/ppermute | solution.py:24
  100.7 6.0 %collective-permute-start.19 = (f32[2,128,128]{2,1,0:T(8,128)S(1)}, f32[2,128,128]{2,1,0:T(8,128)S(1)}, u32[]{:S(2)}, u32[]{:S(2)}) collective-permute-start(f32[2,128,128]{2,1,0:T(8,128)S(1)} %add.30), channel_id=1, source_target_pairs={{0,2},{1,3},{2,0},{3,1},{4,6},{5,7},{6,4},{7,5},{8,10},{9,11},{10,... | collective-permute-start | bytes 393224 | tf_op jit(solution)/shard_map/ppermute | solution.py:24
  103.7 1.3 %collective-permute-start.17 = (f32[1,128,128]{2,1,0:T(8,128)S(1)}, f32[1,128,128]{2,1,0:T(8,128)S(1)}, u32[]{:S(2)}, u32[]{:S(2)}) collective-permute-start(f32[1,128,128]{2,1,0:T(8,128)S(1)} %get-tuple-element.72), channel_id=1, source_target_pairs={{0,1},{1,0},{2,3},{3,2},{4,5},{5,4},{6,7},{7,6},{8,9},{9,8},{10,11... | collective-permute-start | bytes 196616 | tf_op jit(solution)/shard_map/ppermute | solution.py:24
  105.0 4.3 %collective-permute-start.18 = (f32[1,128,128]{2,1,0:T(8,128)S(1)}, f32[1,128,128]{2,1,0:T(8,128)S(1)}, u32[]{:S(2)}, u32[]{:S(2)}) collective-permute-start(f32[1,128,128]{2,1,0:T(8,128)S(1)} %add.31.part0), channel_id=1, source_target_pairs={{0,2},{1,3},{2,0},{3,1},{4,6},{5,7},{6,4},{7,5},{8,10},{9,11},{10,... | collective-permute-start | bytes 196616 | tf_op jit(solution)/shard_map/ppermute | solution.py:24
  110.7 1.9 %collective-permute-start.20 = (f32[1,8,128]{2,1,0:T(8,128)S(1)}, f32[1,8,128]{2,1,0:T(8,128)S(1)}, u32[]{:S(2)}, u32[]{:S(2)}) collective-permute-start(f32[1,8,128]{2,1,0:T(8,128)S(1)} %slice.58), channel_id=1, source_target_pairs={{0,1},{1,0},{2,3},{3,2},{4,5},{5,4},{6,7},{7,6},{8,9},{9,8},{10,11... | collective-permute-start | bytes 12296 | tf_op jit(solution)/shard_map/ppermute | solution.py:24
  110.7 3.7 %collective-permute-start.21 = (f32[1,8,128]{2,1,0:T(8,128)S(1)}, f32[1,8,128]{2,1,0:T(8,128)S(1)}, u32[]{:S(2)}, u32[]{:S(2)}) collective-permute-start(f32[1,8,128]{2,1,0:T(8,128)S(1)} %slice.58), channel_id=1, source_target_pairs={{0,2},{1,3},{2,0},{3,1},{4,6},{5,7},{6,4},{7,5},{8,10},{9,11},{10,... | collective-permute-start | bytes 12296 | tf_op jit(solution)/shard_map/ppermute | solution.py:24
  111.5 3.0 %collective-permute-start.22 = (f32[1,8,128]{2,1,0:T(8,128)S(1)}, f32[1,8,128]{2,1,0:T(8,128)S(1)}, u32[]{:S(2)}, u32[]{:S(2)}) collective-permute-start(f32[1,8,128]{2,1,0:T(8,128)S(1)} %slice.58), channel_id=1, source_target_pairs={{0,3},{1,2},{2,1},{3,0},{4,7},{5,6},{6,5},{7,4},{8,11},{9,10},{10,... | collective-permute-start | bytes 12296 | tf_op jit(solution)/shard_map/ppermute | solution.py:24
  (7 other events, 6.4 us)

commit v9 on v8

--- a/solution.py
+++ b/solution.py
@@ -534,7 +534,6 @@
     opened = list(opened) + picked
     sent = [tuple(opened[2 * c : 2 * c + 2]) for c in range(len(CHUNKS))]
     states = gather(state)
-    sent[1], _ = lax.optimization_barrier((sent[1], states))
     got = [tuple(hand_over(block, side) for side, block in enumerate(pair)) for pair in sent]
 
     tail = [block[rows(CHUNKS[0]) :] for block in got[0]]

time: 116 us -> 116 us (level)
  waiting for transfers between devices: 31.9 us -> 27.7 us
  starting transfers between devices: 36.8 us -> 40.2 us
  Pallas kernels: 28.8 us -> 26.2 us
  local copies, waits for them, and re-layouts: 9.84 us -> 12 us
    ppermute x15, waiting for transfers between devices: 19.7 us -> 14.3 us  [partner(): return lax.ppermute(block, 'sites', route)]
    ppermute x15, starting transfers between devices: 13.3 us -> 16.9 us  [partner(): return lax.ppermute(block, 'sites', route)]
    unnamed x32 -> x40, local copies, waits for them, and re-layouts: 8.22 us -> 10.4 us
    pallas_call x3, Pallas kernels: 12.1 us -> 10.3 us  [on_device(): pl.pallas_call(kernel, in_specs=ahead + [vmem] * 4, out_specs=[vmem] * 3,...]
    ppermute x8, waiting for transfers between devices: 12.2 us -> 13.4 us  [hand_over(): lax.ppermute(block, 'sites', [(i, j) for i, j in route if 0 <= j < count])]
  transfers between devices with their start and end apart: 23 -> 23, of which waited for: 11 -> 9; matrix products, arithmetic and copies ran while one was open for 5% -> 6% of each run, Pallas kernels for 22% -> 19%
where the time goes in v9:
time: 116 us; the launch traced here: 115 us
  starting transfers between devices  40.2 us (35%)
  waiting for transfers between devices  27.7 us (24%)
  Pallas kernels  26.2 us (23%)
  local copies, waits for them, and re-layouts  12 us (10%)
  other arithmetic  5.42 us (5%)
  between operations  3.84 us (3%)
    ppermute x8, starting transfers between devices, hand_over(): lax.ppermute(block, 'sites', [(i, j) for i, j in route if 0 <= j < count])  23.4 us
    ppermute x15, starting transfers between devices, partner(): return lax.ppermute(block, 'sites', route)  16.9 us
    ppermute x15, waiting for transfers between devices, partner(): return lax.ppermute(block, 'sites', route)  14.3 us
    ppermute x8, waiting for transfers between devices, hand_over(): lax.ppermute(block, 'sites', [(i, j) for i, j in route if 0 <= j < count])  13.4 us
    unnamed x40, local copies, waits for them, and re-layouts  10.4 us
    pallas_call x3, Pallas kernels, on_device(): pl.pallas_call(kernel, in_specs=ahead + [vmem] * 4, out_specs=[vmem] * 3,...  10.3 us
    pallas_call x2, Pallas kernels, early(): pl.pallas_call(functools.partial(early_kernel, begin) if begin == 0 else...  4.86 us
    pallas_call x1, Pallas kernels, on_device(): pl.pallas_call(functools.partial(pick_kernel, CHUNKS, parts), in_specs=[h...  4.81 us
  transfers between devices with their start and end apart: 23, of which 9 were waited for; matrix products, arithmetic and copies ran while one was open for 6% of the time, Pallas kernels for 19%

profile of v9, /device:TPU:0, one launch (start us, length us, event | category | flops | bytes accessed | tf_op | source)
XLA Modules:
  0.0 115.4 jit_solution(15859497883668479815)
XLA Ops:
  0.6 1.7 %open.1 = (f32[2312,128]{1,0:T(8,128)S(1)}, f32[2312,128]{1,0:T(8,128)S(1)}) custom-call(f32[8,8]{1,0:T(8,128)} %bond_hbm.1, f32[2,128,128]{2,1,0:T(8,128)} %left_tensor.1, f32[2,128,128]{2,1,0:T(8,128)} %right_tensor.1, f32[8,8,128,128]{3,2,1,0:T(8,128)} %left_env.3, f32[8,8,128,128]{3,2,1,0:T(8,128)} %right_env.3), custom_call_target="tpu_custom_call" | custom-call | flops 1 | bytes 1 | tf_op jit(solution)/shard_map/open/pallas_call | solution.py:501
  2.4 1.3 %collective-permute-start = (f32[2312,128]{1,0:T(8,128)S(1)}, f32[2312,128]{1,0:T(8,128)S(1)}, u32[]{:S(2)}, u32[]{:S(2)}) collective-permute-start(f32[2312,128]{1,0:T(8,128)S(1)} %get-tuple-element.42.sent1), channel_id=1, source_target_pairs={{1,5},{3,7},{4,0},{5,9},{6,2},{7,11},{8,4},{9,13},{10,6},{11,15},{... | collective-permute-start | bytes 3551240 | tf_op jit(solution)/shard_map/ppermute | solution.py:19
  3.7 5.6 %collective-permute-start.1 = (f32[2312,128]{1,0:T(8,128)S(1)}, f32[2312,128]{1,0:T(8,128)S(1)}, u32[]{:S(2)}, u32[]{:S(2)}) collective-permute-start(f32[2312,128]{1,0:T(8,128)S(1)} %get-tuple-element.43.sent0), channel_id=1, source_target_pairs={{0,4},{2,6},{4,8},{5,1},{6,10},{7,3},{8,12},{9,5},{10,14},{11,7},{... | collective-permute-start | bytes 3551240 | tf_op jit(solution)/shard_map/ppermute | solution.py:19
  9.3 4.8 %pick.1 = (s32[60]{0:T(128)S(1)}, f32[3072,128]{1,0:T(8,128)S(1)}, f32[3072,128]{1,0:T(8,128)S(1)}, f32[2048,128]{1,0:T(8,128)S(1)}, f32[2048,128]{1,0:T(8,128)S...) custom-call(s32[4,8]{1,0:T(4,128)} %sectors_hbm.1, s32[4,8]{1,0:T(4,128)} %flow_hbm.1, ...), custom_call_target="tpu_custom_call" | custom-call | flops 1 | bytes 1 | tf_op jit(solution)/shard_map/pick/pallas_call | solution.py:517
  17.8 4.9 %collective-permute-start.6 = (f32[3072,128]{1,0:T(8,128)S(1)}, f32[3072,128]{1,0:T(8,128)}, u32[]{:S(2)}, u32[]{:S(2)}) collective-permute-start(f32[3072,128]{1,0:T(8,128)S(1)} %get-tuple-element.48.sent0), channel_id=1, source_target_pairs={{0,4},{2,6},{4,8},{5,1},{6,10},{7,3},{8,12},{9,5},{10,14},{11,7},{... | collective-permute-start | bytes 4718600 | tf_op jit(solution)/shard_map/ppermute | solution.py:19
  22.7 1.3 %collective-permute-start.7 = (f32[3072,128]{1,0:T(8,128)S(1)}, f32[3072,128]{1,0:T(8,128)}, u32[]{:S(2)}, u32[]{:S(2)}) collective-permute-start(f32[3072,128]{1,0:T(8,128)S(1)} %get-tuple-element.49.sent1), channel_id=1, source_target_pairs={{1,5},{3,7},{4,0},{5,9},{6,2},{7,11},{8,4},{9,13},{10,6},{11,15},{... | collective-permute-start | bytes 4718600 | tf_op jit(solution)/shard_map/ppermute | solution.py:19
  26.1 5.4 %collective-permute-done.got1 = f32[2312,128]{1,0:T(8,128)S(1)} collective-permute-done((f32[2312,128]{1,0:T(8,128)S(1)}, f32[2312,128]{1,0:T(8,128)S(1)}, u32[]{:S(2)}, u32[]{:S(2)}) %collective-permute-start) | collective-permute-done | bytes 1183776 | tf_op jit(solution)/shard_map/ppermute | solution.py:19
  31.5 2.5 %collective-permute-start.9 = (f32[2,128,128]{2,1,0:T(8,128)}, f32[2,128,128]{2,1,0:T(8,128)S(1)}, u32[]{:S(2)}, u32[]{:S(2)}) collective-permute-start(f32[2,128,128]{2,1,0:T(8,128)} %param.9), channel_id=1, source_target_pairs={{0,2},{1,3},{2,0},{3,1},{4,6},{5,7},{6,4},{7,5},{8,10},{9,11},{10,... | collective-permute-start | bytes 393224 | tf_op jit(solution)/shard_map/ppermute | solution.py:24
  34.0 1.7 %collective-permute-done.1.got0 = f32[2312,128]{1,0:T(8,128)S(1)} collective-permute-done((f32[2312,128]{1,0:T(8,128)S(1)}, f32[2312,128]{1,0:T(8,128)S(1)}, u32[]{:S(2)}, u32[]{:S(2)}) %collective-permute-start.1) | collective-permute-done | bytes 1183776 | tf_op jit(solution)/shard_map/ppermute | solution.py:19
  35.7 2.5 %collective-permute-start.10 = (f32[2,128,128]{2,1,0:T(8,128)}, f32[2,128,128]{2,1,0:T(8,128)}, u32[]{:S(2)}, u32[]{:S(2)}) collective-permute-start(f32[2,128,128]{2,1,0:T(8,128)} %param.9), channel_id=1, source_target_pairs={{0,3},{1,2},{2,1},{3,0},{4,7},{5,6},{6,5},{7,4},{8,11},{9,10},{10,... | collective-permute-start | bytes 393224 | tf_op jit(solution)/shard_map/ppermute | solution.py:24
  44.5 1.4 %pad_add_fusion = s32[19]{0:T(128)S(1)} fusion(s32[16]{0:T(128)} %reshape.28, s32[1]{0:T(128)} %get-tuple-element.87, s32[2]{0:T(128)S(1)} %bitcast.16), kind=kLoop, calls=%fused_computation.10 | loop fusion | flops 38 | bytes 152 | tf_op jit(solution)/shard_map/concatenate | solution.py:547
  45.9 4.0 %collective-permute-start.4 = (f32[2048,128]{1,0:T(8,128)}, f32[2048,128]{1,0:T(8,128)S(1)}, u32[]{:S(2)}, u32[]{:S(2)}) collective-permute-start(f32[2048,128]{1,0:T(8,128)} %copy-done.8), channel_id=1, source_target_pairs={{0,4},{2,6},{4,8},{5,1},{6,10},{7,3},{8,12},{9,5},{10,14},{11,7},{... | collective-permute-start | bytes 3145736 | tf_op jit(solution)/shard_map/ppermute | solution.py:19
  51.1 1.3 %collective-permute-start.5 = (f32[2048,128]{1,0:T(8,128)}, f32[2048,128]{1,0:T(8,128)S(1)}, u32[]{:S(2)}, u32[]{:S(2)}) collective-permute-start(f32[2048,128]{1,0:T(8,128)} %copy-done.10), channel_id=1, source_target_pairs={{1,5},{3,7},{4,0},{5,9},{6,2},{7,11},{8,4},{9,13},{10,6},{11,15},{... | collective-permute-start | bytes 3145736 | tf_op jit(solution)/shard_map/ppermute | solution.py:19
  52.4 1.3 %collective-permute-start.13 = (f32[2,2,128,128]{3,2,1,0:T(8,128)}, f32[2,2,128,128]{3,2,1,0:T(8,128)S(1)}, u32[]{:S(2)}, u32[]{:S(2)}) collective-permute-start(f32[2,2,128,128]{3,2,1,0:T(8,128)} %get-tuple-element.83), channel_id=1, source_target_pairs={{0,3},{1,2},{2,1},{3,0},{4,7},{5,6},{6,5},{7,4},{8,11},{9,10},{10,... | collective-permute-start | bytes 786440 | tf_op jit(solution)/shard_map/ppermute | solution.py:24
  56.0 1.3 %copy-done.5 = f32[2312,128]{1,0:T(8,128)S(1)} copy-done((f32[2312,128]{1,0:T(8,128)S(1)}, f32[2312,128]{1,0:T(8,128)}, u32[]{:S(2)}) %copy-start.5) | copy-done | bytes 1183768
  57.3 1.3 %copy-done.7 = f32[2312,128]{1,0:T(8,128)S(1)} copy-done((f32[2312,128]{1,0:T(8,128)S(1)}, f32[2312,128]{1,0:T(8,128)}, u32[]{:S(2)}) %copy-start.7) | copy-done | bytes 1183768
  61.8 1.3 %prepare.1 = (f32[8,128,128]{2,1,0:T(8,128)S(1)}, f32[8,128,128]{2,1,0:T(8,128)S(1)}, bf16[8,128,256]{2,1,0:T(8,128)(2,1)S(1)}, bf16[8,256,256]{2,1,0:T(8,128)(2...) custom-call(s32[60]{0:T(128)S(1)} %get-tuple-element.41.table, ...), custom_call_target="tpu_custom_call" | custom-call | flops 1 | bytes 1 | tf_op jit(solution)/shard_map/prepare/pallas_call | solution.py:561
  63.2 6.2 %collective-permute-done.6.got0 = f32[3072,128]{1,0:T(8,128)} collective-permute-done((f32[3072,128]{1,0:T(8,128)S(1)}, f32[3072,128]{1,0:T(8,128)}, u32[]{:S(2)}, u32[]{:S(2)}) %collective-permute-start.6) | collective-permute-done | bytes 1572896 | tf_op jit(solution)/shard_map/ppermute | solution.py:19
  69.4 6.9 %first_matvec0.1 = (bf16[3,1024,256]{2,1,0:T(8,128)(2,1)S(1)}, bf16[3,1024,256]{2,1,0:T(8,128)(2,1)S(1)}, f32[5,128,128]{2,1,0:T(8,128)S(1)}) custom-call(s32[16]{0:T(128)S(1)} %slice.55.slots, s32[19,8,128]{2,1,0:T(8,128)S(1)} %broadcast_in_dim.4.flags, f32[8,8,8,128]{3,2,1,0:T(8,128)S(1)} %broadcast_in_dim.5.bond, ...), custom_call_target="tpu_custom_call" | custom-call | flops 1 | bytes 1 | tf_op jit(solution)/shard_map/first_matvec0/pallas_call | solution.py:615
  76.3 1.3 %collective-permute-start.14 = (f32[5,128,128]{2,1,0:T(8,128)S(1)}, f32[5,128,128]{2,1,0:T(8,128)S(1)}, u32[]{:S(2)}, u32[]{:S(2)}) collective-permute-start(f32[5,128,128]{2,1,0:T(8,128)S(1)} %get-tuple-element.56.part), channel_id=1, source_target_pairs={{0,1},{1,0},{2,3},{3,2},{4,5},{5,4},{6,7},{7,6},{8,9},{9,8},{10,11... | collective-permute-start | bytes 983048 | tf_op jit(solution)/shard_map/ppermute | solution.py:24
  77.6 3.6 %collective-permute-start.2 = (f32[1024,128]{1,0:T(8,128)S(1)}, f32[1024,128]{1,0:T(8,128)S(1)}, u32[]{:S(2)}, u32[]{:S(2)}) collective-permute-start(f32[1024,128]{1,0:T(8,128)S(1)} %copy-done.13), channel_id=1, source_target_pairs={{0,4},{2,6},{4,8},{5,1},{6,10},{7,3},{8,12},{9,5},{10,14},{11,7},{... | collective-permute-start | bytes 1572872 | tf_op jit(solution)/shard_map/ppermute | solution.py:19
  81.2 1.5 %collective-permute-start.3 = (f32[1024,128]{1,0:T(8,128)S(1)}, f32[1024,128]{1,0:T(8,128)S(1)}, u32[]{:S(2)}, u32[]{:S(2)}) collective-permute-start(f32[1024,128]{1,0:T(8,128)S(1)} %copy-done.15), channel_id=1, source_target_pairs={{1,5},{3,7},{4,0},{5,9},{6,2},{7,11},{8,4},{9,13},{10,6},{11,15},{... | collective-permute-start | bytes 1572872 | tf_op jit(solution)/shard_map/ppermute | solution.py:19
  82.8 1.9 %collective-permute-start.15 = (f32[5,128,128]{2,1,0:T(8,128)S(1)}, f32[5,128,128]{2,1,0:T(8,128)S(1)}, u32[]{:S(2)}, u32[]{:S(2)}) collective-permute-start(f32[5,128,128]{2,1,0:T(8,128)S(1)} %add.28), channel_id=1, source_target_pairs={{0,2},{1,3},{2,0},{3,1},{4,6},{5,7},{6,4},{7,5},{8,10},{9,11},{10,... | collective-permute-start | bytes 983048 | tf_op jit(solution)/shard_map/ppermute | solution.py:24
  84.7 8.6 %collective-permute-done.15 = f32[5,128,128]{2,1,0:T(8,128)S(1)} collective-permute-done((f32[5,128,128]{2,1,0:T(8,128)S(1)}, f32[5,128,128]{2,1,0:T(8,128)S(1)}, u32[]{:S(2)}, u32[]{:S(2)}) %collective-permute-start.15) | collective-permute-done | bytes 327712 | tf_op jit(solution)/shard_map/ppermute | solution.py:24
  93.4 2.1 %first_matvec1.1 = (bf16[2,1024,256]{2,1,0:T(8,128)(2,1)S(1)}, bf16[2,1024,256]{2,1,0:T(8,128)(2,1)S(1)}, f32[2,128,128]{2,1,0:T(8,128)S(1)}) custom-call(s32[19,8,128]{2,1,0:T(8,128)S(1)} %broadcast_in_dim.4.flags, f32[8,8,8,128]{3,2,1,0:T(8,128)S(1)} %broadcast_in_dim.5.bond, f32[2048,128]{1,0:T(8,128)S(1)} %collective-permute-done.4.got0, ...), custom_call_target="tpu_custom_call" | custom-call | flops 1 | bytes 1 | tf_op jit(solution)/shard_map/first_matvec1/pallas_call | solution.py:615
  95.6 3.2 %early_second_matvec.2 = (f32[5,128,128]{2,1,0:T(8,128)S(1)}, f32[8,8,128]{2,1,0:T(8,128)S(1)}) custom-call(s32[16]{0:T(128)S(1)} %slice.55.slots, f32[5,128,128]{2,1,0:T(8,128)S(1)} %add.29.image, f32[5,128,128]{2,1,0:T(8,128)S(1)} %get-tuple-element.56.part, f32[8,128,128]{2,1,0:T(8,128)S(1)} %get-tuple-element.53.vec, ...), custom_call_target="tpu_custom_call" | custom-call | flops 1 | bytes 1 | tf_op jit(solution)/shard_map/early_second_matvec/pallas_call | solution.py:581
  98.8 1.8 %collective-permute-start.19 = (f32[2,128,128]{2,1,0:T(8,128)S(1)}, f32[2,128,128]{2,1,0:T(8,128)S(1)}, u32[]{:S(2)}, u32[]{:S(2)}) collective-permute-start(f32[2,128,128]{2,1,0:T(8,128)S(1)} %add.30), channel_id=1, source_target_pairs={{0,2},{1,3},{2,0},{3,1},{4,6},{5,7},{6,4},{7,5},{8,10},{9,11},{10,... | collective-permute-start | bytes 393224 | tf_op jit(solution)/shard_map/ppermute | solution.py:24
  103.6 2.1 %collective-permute-start.18 = (f32[1,128,128]{2,1,0:T(8,128)S(1)}, f32[1,128,128]{2,1,0:T(8,128)S(1)}, u32[]{:S(2)}, u32[]{:S(2)}) collective-permute-start(f32[1,128,128]{2,1,0:T(8,128)S(1)} %add.31.part0), channel_id=1, source_target_pairs={{0,2},{1,3},{2,0},{3,1},{4,6},{5,7},{6,4},{7,5},{8,10},{9,11},{10,... | collective-permute-start | bytes 196616 | tf_op jit(solution)/shard_map/ppermute | solution.py:24
  105.7 1.6 %early_second_matvec.3 = (f32[2,128,128]{2,1,0:T(8,128)S(1)}, f32[8,8,128]{2,1,0:T(8,128)S(1)}) custom-call(f32[2,128,128]{2,1,0:T(8,128)S(1)} %add.32.image, f32[2,128,128]{2,1,0:T(8,128)S(1)} %get-tuple-element.59.part, f32[8,128,128]{2,1,0:T(8,128)S(1)} %get-tuple-element.53.vec, f32[8,128,128]{2,1,0:T(8,128)S(1)} %get-tuple-element.52.plain.middle, ...), custom_call_target="tpu_custom_call" | custom-call | flops 1 | bytes 1 | tf_op jit(solution)/shard_map/early_second_matvec/pallas_call | solution.py:581
  108.3 1.3 %second_matvec.1 = (f32[2,128,128]{2,1,0:T(8,128)S(1)}, f32[3,8,128]{2,1,0:T(8,128)S(1)}) custom-call(s32[19,8,128]{2,1,0:T(8,128)S(1)} %broadcast_in_dim.4.flags, f32[1,128,128]{2,1,0:T(8,128)S(1)} %add.31.part0, f32[1,128,128]{2,1,0:T(8,128)S(1)} %collective-permute-done.18.part1, f32[8,128,128]{2,1,0:T(8,128)S(1)} %get-tuple-element.53.vec, ...), custom_call_target="tpu_custom_call" | custom-call | flops 1 | bytes 1 | tf_op jit(solution)/shard_map/second_matvec/pallas_call | solution.py:640
  109.7 1.8 %collective-permute-start.21 = (f32[1,8,128]{2,1,0:T(8,128)S(1)}, f32[1,8,128]{2,1,0:T(8,128)S(1)}, u32[]{:S(2)}, u32[]{:S(2)}) collective-permute-start(f32[1,8,128]{2,1,0:T(8,128)S(1)} %slice.58), channel_id=1, source_target_pairs={{0,2},{1,3},{2,0},{3,1},{4,6},{5,7},{6,4},{7,5},{8,10},{9,11},{10,... | collective-permute-start | bytes 12296 | tf_op jit(solution)/shard_map/ppermute | solution.py:24
  111.6 1.8 %collective-permute-done.21.share2 = f32[1,8,128]{2,1,0:T(8,128)S(1)} collective-permute-done((f32[1,8,128]{2,1,0:T(8,128)S(1)}, f32[1,8,128]{2,1,0:T(8,128)S(1)}, u32[]{:S(2)}, u32[]{:S(2)}) %collective-permute-start.21) | collective-permute-done | bytes 4128 | tf_op jit(solution)/shard_map/ppermute | solution.py:24
  (88 shorter events, 22.2 us)
Async XLA Ops:
  2.3 11.7 %copy-start.4 = (f32[2312,128]{1,0:T(8,128)}, f32[2312,128]{1,0:T(8,128)S(1)}, u32[]{:S(2)}) copy-start(f32[2312,128]{1,0:T(8,128)S(1)} %get-tuple-element.43.sent0) | copy-start | bytes 3551236
  2.4 11.7 %copy-start.6 = (f32[2312,128]{1,0:T(8,128)}, f32[2312,128]{1,0:T(8,128)S(1)}, u32[]{:S(2)}) copy-start(f32[2312,128]{1,0:T(8,128)S(1)} %get-tuple-element.42.sent1) | copy-start | bytes 3551236
  2.4 29.1 %collective-permute-start = (f32[2312,128]{1,0:T(8,128)S(1)}, f32[2312,128]{1,0:T(8,128)S(1)}, u32[]{:S(2)}, u32[]{:S(2)}) collective-permute-start(f32[2312,128]{1,0:T(8,128)S(1)} %get-tuple-element.42.sent1), channel_id=1, source_target_pairs={{1,5},{3,7},{4,0},{5,9},{6,2},{7,11},{8,4},{9,13},{10,6},{11,15},{... | collective-permute-start | bytes 3551240 | tf_op jit(solution)/shard_map/ppermute | solution.py:19
  3.7 32.0 %collective-permute-start.1 = (f32[2312,128]{1,0:T(8,128)S(1)}, f32[2312,128]{1,0:T(8,128)S(1)}, u32[]{:S(2)}, u32[]{:S(2)}) collective-permute-start(f32[2312,128]{1,0:T(8,128)S(1)} %get-tuple-element.43.sent0), channel_id=1, source_target_pairs={{0,4},{2,6},{4,8},{5,1},{6,10},{7,3},{8,12},{9,5},{10,14},{11,7},{... | collective-permute-start | bytes 3551240 | tf_op jit(solution)/shard_map/ppermute | solution.py:19
  17.8 51.6 %collective-permute-start.6 = (f32[3072,128]{1,0:T(8,128)S(1)}, f32[3072,128]{1,0:T(8,128)}, u32[]{:S(2)}, u32[]{:S(2)}) collective-permute-start(f32[3072,128]{1,0:T(8,128)S(1)} %get-tuple-element.48.sent0), channel_id=1, source_target_pairs={{0,4},{2,6},{4,8},{5,1},{6,10},{7,3},{8,12},{9,5},{10,14},{11,7},{... | collective-permute-start | bytes 4718600 | tf_op jit(solution)/shard_map/ppermute | solution.py:19
  22.7 46.7 %collective-permute-start.7 = (f32[3072,128]{1,0:T(8,128)S(1)}, f32[3072,128]{1,0:T(8,128)}, u32[]{:S(2)}, u32[]{:S(2)}) collective-permute-start(f32[3072,128]{1,0:T(8,128)S(1)} %get-tuple-element.49.sent1), channel_id=1, source_target_pairs={{1,5},{3,7},{4,0},{5,9},{6,2},{7,11},{8,4},{9,13},{10,6},{11,15},{... | collective-permute-start | bytes 4718600 | tf_op jit(solution)/shard_map/ppermute | solution.py:19
  23.9 17.8 %collective-permute-start.8 = (f32[2,128,128]{2,1,0:T(8,128)}, f32[2,128,128]{2,1,0:T(8,128)S(1)}, u32[]{:S(2)}, u32[]{:S(2)}) collective-permute-start(f32[2,128,128]{2,1,0:T(8,128)} %param.9), channel_id=1, source_target_pairs={{0,1},{1,0},{2,3},{3,2},{4,5},{5,4},{6,7},{7,6},{8,9},{9,8},{10,11... | collective-permute-start | bytes 393224 | tf_op jit(solution)/shard_map/ppermute | solution.py:24
  31.5 10.2 %collective-permute-start.9 = (f32[2,128,128]{2,1,0:T(8,128)}, f32[2,128,128]{2,1,0:T(8,128)S(1)}, u32[]{:S(2)}, u32[]{:S(2)}) collective-permute-start(f32[2,128,128]{2,1,0:T(8,128)} %param.9), channel_id=1, source_target_pairs={{0,2},{1,3},{2,0},{3,1},{4,6},{5,7},{6,4},{7,5},{8,10},{9,11},{10,... | collective-permute-start | bytes 393224 | tf_op jit(solution)/shard_map/ppermute | solution.py:24
  35.7 10.2 %collective-permute-start.10 = (f32[2,128,128]{2,1,0:T(8,128)}, f32[2,128,128]{2,1,0:T(8,128)}, u32[]{:S(2)}, u32[]{:S(2)}) collective-permute-start(f32[2,128,128]{2,1,0:T(8,128)} %param.9), channel_id=1, source_target_pairs={{0,3},{1,2},{2,1},{3,0},{4,7},{5,6},{6,5},{7,4},{8,11},{9,10},{10,... | collective-permute-start | bytes 393224 | tf_op jit(solution)/shard_map/ppermute | solution.py:24
  41.7 9.4 %collective-permute-start.11 = (f32[2,2,128,128]{3,2,1,0:T(8,128)}, f32[2,2,128,128]{3,2,1,0:T(8,128)}, u32[]{:S(2)}, u32[]{:S(2)}) collective-permute-start(f32[2,2,128,128]{3,2,1,0:T(8,128)} %get-tuple-element.83), channel_id=1, source_target_pairs={{0,1},{1,0},{2,3},{3,2},{4,5},{5,4},{6,7},{7,6},{8,9},{9,8},{10,11... | collective-permute-start | bytes 786440 | tf_op jit(solution)/shard_map/ppermute | solution.py:24
  41.7 10.6 %collective-permute-start.12 = (f32[2,2,128,128]{3,2,1,0:T(8,128)}, f32[2,2,128,128]{3,2,1,0:T(8,128)}, u32[]{:S(2)}, u32[]{:S(2)}) collective-permute-start(f32[2,2,128,128]{3,2,1,0:T(8,128)} %get-tuple-element.83), channel_id=1, source_target_pairs={{0,2},{1,3},{2,0},{3,1},{4,6},{5,7},{6,4},{7,5},{8,10},{9,11},{10,... | collective-permute-start | bytes 786440 | tf_op jit(solution)/shard_map/ppermute | solution.py:24
  44.4 10.3 %copy-start.1 = (f32[2312,128]{1,0:T(8,128)S(1)}, f32[2312,128]{1,0:T(8,128)}, u32[]{:S(2)}) copy-start(f32[2312,128]{1,0:T(8,128)} %copy-done) | copy-start | bytes 3551236
  45.9 47.4 %collective-permute-start.4 = (f32[2048,128]{1,0:T(8,128)}, f32[2048,128]{1,0:T(8,128)S(1)}, u32[]{:S(2)}, u32[]{:S(2)}) collective-permute-start(f32[2048,128]{1,0:T(8,128)} %copy-done.8), channel_id=1, source_target_pairs={{0,4},{2,6},{4,8},{5,1},{6,10},{7,3},{8,12},{9,5},{10,14},{11,7},{... | collective-permute-start | bytes 3145736 | tf_op jit(solution)/shard_map/ppermute | solution.py:19
  51.1 42.2 %collective-permute-start.5 = (f32[2048,128]{1,0:T(8,128)}, f32[2048,128]{1,0:T(8,128)S(1)}, u32[]{:S(2)}, u32[]{:S(2)}) collective-permute-start(f32[2048,128]{1,0:T(8,128)} %copy-done.10), channel_id=1, source_target_pairs={{1,5},{3,7},{4,0},{5,9},{6,2},{7,11},{8,4},{9,13},{10,6},{11,15},{... | collective-permute-start | bytes 3145736 | tf_op jit(solution)/shard_map/ppermute | solution.py:19
  52.4 8.3 %collective-permute-start.13 = (f32[2,2,128,128]{3,2,1,0:T(8,128)}, f32[2,2,128,128]{3,2,1,0:T(8,128)S(1)}, u32[]{:S(2)}, u32[]{:S(2)}) collective-permute-start(f32[2,2,128,128]{3,2,1,0:T(8,128)} %get-tuple-element.83), channel_id=1, source_target_pairs={{0,3},{1,2},{2,1},{3,0},{4,7},{5,6},{6,5},{7,4},{8,11},{9,10},{10,... | collective-permute-start | bytes 786440 | tf_op jit(solution)/shard_map/ppermute | solution.py:24
  54.7 1.3 %copy-start.3 = (f32[2312,128]{1,0:T(8,128)S(1)}, f32[2312,128]{1,0:T(8,128)}, u32[]{:S(2)}) copy-start(f32[2312,128]{1,0:T(8,128)} %copy-done.2) | copy-start | bytes 3551236
  59.8 2.0 %copy-start.16 = (f32[2,128,128]{2,1,0:T(8,128)S(1)}, f32[2,128,128]{2,1,0:T(8,128)}, u32[]{:S(2)}) copy-start(f32[2,128,128]{2,1,0:T(8,128)} %onsite.1) | copy-start | bytes 393220
  69.4 8.2 %copy-start.13 = (f32[1024,128]{1,0:T(8,128)S(1)}, f32[1024,128]{1,0:T(8,128)}, u32[]{:S(2)}) copy-start(f32[1024,128]{1,0:T(8,128)} %copy-done.12) | copy-start | bytes 1572868
  69.4 11.8 %copy-start.15 = (f32[1024,128]{1,0:T(8,128)S(1)}, f32[1024,128]{1,0:T(8,128)}, u32[]{:S(2)}) copy-start(f32[1024,128]{1,0:T(8,128)} %copy-done.14) | copy-start | bytes 1572868
  69.4 23.9 %copy-start.11 = (f32[2048,128]{1,0:T(8,128)S(1)}, f32[2048,128]{1,0:T(8,128)}, u32[]{:S(2)}) copy-start(f32[2048,128]{1,0:T(8,128)} %copy-done.10) | copy-start | bytes 3145732
  76.3 17.0 %copy-start.9 = (f32[2048,128]{1,0:T(8,128)S(1)}, f32[2048,128]{1,0:T(8,128)}, u32[]{:S(2)}) copy-start(f32[2048,128]{1,0:T(8,128)} %copy-done.8) | copy-start | bytes 3145732
  76.3 6.4 %collective-permute-start.14 = (f32[5,128,128]{2,1,0:T(8,128)S(1)}, f32[5,128,128]{2,1,0:T(8,128)S(1)}, u32[]{:S(2)}, u32[]{:S(2)}) collective-permute-start(f32[5,128,128]{2,1,0:T(8,128)S(1)} %get-tuple-element.56.part), channel_id=1, source_target_pairs={{0,1},{1,0},{2,3},{3,2},{4,5},{5,4},{6,7},{7,6},{8,9},{9,8},{10,11... | collective-permute-start | bytes 983048 | tf_op jit(solution)/shard_map/ppermute | solution.py:24
  77.6 23.0 %collective-permute-start.2 = (f32[1024,128]{1,0:T(8,128)S(1)}, f32[1024,128]{1,0:T(8,128)S(1)}, u32[]{:S(2)}, u32[]{:S(2)}) collective-permute-start(f32[1024,128]{1,0:T(8,128)S(1)} %copy-done.13), channel_id=1, source_target_pairs={{0,4},{2,6},{4,8},{5,1},{6,10},{7,3},{8,12},{9,5},{10,14},{11,7},{... | collective-permute-start | bytes 1572872 | tf_op jit(solution)/shard_map/ppermute | solution.py:19
  81.2 19.4 %collective-permute-start.3 = (f32[1024,128]{1,0:T(8,128)S(1)}, f32[1024,128]{1,0:T(8,128)S(1)}, u32[]{:S(2)}, u32[]{:S(2)}) collective-permute-start(f32[1024,128]{1,0:T(8,128)S(1)} %copy-done.15), channel_id=1, source_target_pairs={{1,5},{3,7},{4,0},{5,9},{6,2},{7,11},{8,4},{9,13},{10,6},{11,15},{... | collective-permute-start | bytes 1572872 | tf_op jit(solution)/shard_map/ppermute | solution.py:19
  82.8 10.5 %collective-permute-start.15 = (f32[5,128,128]{2,1,0:T(8,128)S(1)}, f32[5,128,128]{2,1,0:T(8,128)S(1)}, u32[]{:S(2)}, u32[]{:S(2)}) collective-permute-start(f32[5,128,128]{2,1,0:T(8,128)S(1)} %add.28), channel_id=1, source_target_pairs={{0,2},{1,3},{2,0},{3,1},{4,6},{5,7},{6,4},{7,5},{8,10},{9,11},{10,... | collective-permute-start | bytes 983048 | tf_op jit(solution)/shard_map/ppermute | solution.py:24
  95.5 3.3 %collective-permute-start.16 = (f32[2,128,128]{2,1,0:T(8,128)S(1)}, f32[2,128,128]{2,1,0:T(8,128)S(1)}, u32[]{:S(2)}, u32[]{:S(2)}) collective-permute-start(f32[2,128,128]{2,1,0:T(8,128)S(1)} %get-tuple-element.59.part), channel_id=1, source_target_pairs={{0,1},{1,0},{2,3},{3,2},{4,5},{5,4},{6,7},{7,6},{8,9},{9,8},{10,11... | collective-permute-start | bytes 393224 | tf_op jit(solution)/shard_map/ppermute | solution.py:24
  98.8 6.8 %collective-permute-start.19 = (f32[2,128,128]{2,1,0:T(8,128)S(1)}, f32[2,128,128]{2,1,0:T(8,128)S(1)}, u32[]{:S(2)}, u32[]{:S(2)}) collective-permute-start(f32[2,128,128]{2,1,0:T(8,128)S(1)} %add.30), channel_id=1, source_target_pairs={{0,2},{1,3},{2,0},{3,1},{4,6},{5,7},{6,4},{7,5},{8,10},{9,11},{10,... | collective-permute-start | bytes 393224 | tf_op jit(solution)/shard_map/ppermute | solution.py:24
  101.9 1.7 %collective-permute-start.17 = (f32[1,128,128]{2,1,0:T(8,128)S(1)}, f32[1,128,128]{2,1,0:T(8,128)S(1)}, u32[]{:S(2)}, u32[]{:S(2)}) collective-permute-start(f32[1,128,128]{2,1,0:T(8,128)S(1)} %get-tuple-element.68), channel_id=1, source_target_pairs={{0,1},{1,0},{2,3},{3,2},{4,5},{5,4},{6,7},{7,6},{8,9},{9,8},{10,11... | collective-permute-start | bytes 196616 | tf_op jit(solution)/shard_map/ppermute | solution.py:24
  103.6 4.7 %collective-permute-start.18 = (f32[1,128,128]{2,1,0:T(8,128)S(1)}, f32[1,128,128]{2,1,0:T(8,128)S(1)}, u32[]{:S(2)}, u32[]{:S(2)}) collective-permute-start(f32[1,128,128]{2,1,0:T(8,128)S(1)} %add.31.part0), channel_id=1, source_target_pairs={{0,2},{1,3},{2,0},{3,1},{4,6},{5,7},{6,4},{7,5},{8,10},{9,11},{10,... | collective-permute-start | bytes 196616 | tf_op jit(solution)/shard_map/ppermute | solution.py:24
  109.6 2.0 %collective-permute-start.20 = (f32[1,8,128]{2,1,0:T(8,128)S(1)}, f32[1,8,128]{2,1,0:T(8,128)S(1)}, u32[]{:S(2)}, u32[]{:S(2)}) collective-permute-start(f32[1,8,128]{2,1,0:T(8,128)S(1)} %slice.58), channel_id=1, source_target_pairs={{0,1},{1,0},{2,3},{3,2},{4,5},{5,4},{6,7},{7,6},{8,9},{9,8},{10,11... | collective-permute-start | bytes 12296 | tf_op jit(solution)/shard_map/ppermute | solution.py:24
  109.7 3.7 %collective-permute-start.21 = (f32[1,8,128]{2,1,0:T(8,128)S(1)}, f32[1,8,128]{2,1,0:T(8,128)S(1)}, u32[]{:S(2)}, u32[]{:S(2)}) collective-permute-start(f32[1,8,128]{2,1,0:T(8,128)S(1)} %slice.58), channel_id=1, source_target_pairs={{0,2},{1,3},{2,0},{3,1},{4,6},{5,7},{6,4},{7,5},{8,10},{9,11},{10,... | collective-permute-start | bytes 12296 | tf_op jit(solution)/shard_map/ppermute | solution.py:24
  111.5 3.0 %collective-permute-start.22 = (f32[1,8,128]{2,1,0:T(8,128)S(1)}, f32[1,8,128]{2,1,0:T(8,128)S(1)}, u32[]{:S(2)}, u32[]{:S(2)}) collective-permute-start(f32[1,8,128]{2,1,0:T(8,128)S(1)} %slice.58), channel_id=1, source_target_pairs={{0,3},{1,2},{2,1},{3,0},{4,7},{5,6},{6,5},{7,4},{8,11},{9,10},{10,... | collective-permute-start | bytes 12296 | tf_op jit(solution)/shard_map/ppermute | solution.py:24
  (11 other events, 10.4 us)

commit v10 on v9

--- a/solution.py
+++ b/solution.py
@@ -630,8 +630,9 @@
             resids.append(resid)
             stats.append(stat)
         if c < len(groups) - 1:
-            beside = part + partner(part, 1)
-            image = beside + partner(beside, 2)
+            near, far = (2, 1) if c == 0 else (1, 2)
+            beside = part + partner(part, near)
+            image = beside + partner(beside, far)
             held = (begin, width, image, part, env, mixed)
             waits.append([beside if c == len(groups) - 2 else image] + stats[-1:])
 

time: 116 us -> 116 us (level)
  starting transfers between devices: 40.2 us -> 41.9 us
  waiting for transfers between devices: 27.7 us -> 26.1 us
    ppermute x15, waiting for transfers between devices: 14.3 us -> 9.29 us  [partner(): return lax.ppermute(block, 'sites', route)]
    ppermute x8, waiting for transfers between devices: 13.4 us -> 16.8 us  [hand_over(): lax.ppermute(block, 'sites', [(i, j) for i, j in route if 0 <= j < count])]
  transfers between devices with their start and end apart: 23 -> 23, of which waited for: 9 -> 11; matrix products, arithmetic and copies ran while one was open for 6% -> 6% of each run, Pallas kernels for 19% -> 19%
where the time goes in v10:
time: 116 us; the launch traced here: 115 us
  starting transfers between devices  41.9 us (36%)
  Pallas kernels  26.2 us (23%)
  waiting for transfers between devices  26.1 us (22%)
  local copies, waits for them, and re-layouts  12 us (10%)
  other arithmetic  5.41 us (5%)
  between operations  3.8 us (3%)
    ppermute x8, starting transfers between devices, hand_over(): lax.ppermute(block, 'sites', [(i, j) for i, j in route if 0 <= j < count])  24.4 us
    ppermute x15, starting transfers between devices, partner(): return lax.ppermute(block, 'sites', route)  17.5 us
    ppermute x8, waiting for transfers between devices, hand_over(): lax.ppermute(block, 'sites', [(i, j) for i, j in route if 0 <= j < count])  16.8 us
    unnamed x40, local copies, waits for them, and re-layouts  10.4 us
    pallas_call x3, Pallas kernels, on_device(): pl.pallas_call(kernel, in_specs=ahead + [vmem] * 4, out_specs=[vmem] * 3,...  10.3 us
    ppermute x15, waiting for transfers between devices, partner(): return lax.ppermute(block, 'sites', route)  9.29 us
    pallas_call x2, Pallas kernels, early(): pl.pallas_call(functools.partial(early_kernel, begin) if begin == 0 else...  4.85 us
    pallas_call x1, Pallas kernels, on_device(): pl.pallas_call(functools.partial(pick_kernel, CHUNKS, parts), in_specs=[h...  4.77 us
  transfers between devices with their start and end apart: 23, of which 11 were waited for; matrix products, arithmetic and copies ran while one was open for 6% of the time, Pallas kernels for 19%

profile of v10, /device:TPU:0, one launch (start us, length us, event | category | flops | bytes accessed | tf_op | source)
XLA Modules:
  0.0 115.4 jit_solution(16332818568283799652)
XLA Ops:
  0.6 1.7 %open.1 = (f32[2312,128]{1,0:T(8,128)S(1)}, f32[2312,128]{1,0:T(8,128)S(1)}) custom-call(f32[8,8]{1,0:T(8,128)} %bond_hbm.1, f32[2,128,128]{2,1,0:T(8,128)} %left_tensor.1, f32[2,128,128]{2,1,0:T(8,128)} %right_tensor.1, f32[8,8,128,128]{3,2,1,0:T(8,128)} %left_env.3, f32[8,8,128,128]{3,2,1,0:T(8,128)} %right_env.3), custom_call_target="tpu_custom_call" | custom-call | flops 1 | bytes 1 | tf_op jit(solution)/shard_map/open/pallas_call | solution.py:501
  2.4 1.3 %collective-permute-start = (f32[2312,128]{1,0:T(8,128)S(1)}, f32[2312,128]{1,0:T(8,128)S(1)}, u32[]{:S(2)}, u32[]{:S(2)}) collective-permute-start(f32[2312,128]{1,0:T(8,128)S(1)} %get-tuple-element.42.sent1), channel_id=1, source_target_pairs={{1,5},{3,7},{4,0},{5,9},{6,2},{7,11},{8,4},{9,13},{10,6},{11,15},{... | collective-permute-start | bytes 3551240 | tf_op jit(solution)/shard_map/ppermute | solution.py:19
  3.7 5.6 %collective-permute-start.1 = (f32[2312,128]{1,0:T(8,128)S(1)}, f32[2312,128]{1,0:T(8,128)S(1)}, u32[]{:S(2)}, u32[]{:S(2)}) collective-permute-start(f32[2312,128]{1,0:T(8,128)S(1)} %get-tuple-element.43.sent0), channel_id=1, source_target_pairs={{0,4},{2,6},{4,8},{5,1},{6,10},{7,3},{8,12},{9,5},{10,14},{11,7},{... | collective-permute-start | bytes 3551240 | tf_op jit(solution)/shard_map/ppermute | solution.py:19
  9.3 4.8 %pick.1 = (s32[60]{0:T(128)S(1)}, f32[3072,128]{1,0:T(8,128)S(1)}, f32[3072,128]{1,0:T(8,128)S(1)}, f32[2048,128]{1,0:T(8,128)S(1)}, f32[2048,128]{1,0:T(8,128)S...) custom-call(s32[4,8]{1,0:T(4,128)} %sectors_hbm.1, s32[4,8]{1,0:T(4,128)} %flow_hbm.1, ...), custom_call_target="tpu_custom_call" | custom-call | flops 1 | bytes 1 | tf_op jit(solution)/shard_map/pick/pallas_call | solution.py:517
  17.8 4.9 %collective-permute-start.6 = (f32[3072,128]{1,0:T(8,128)S(1)}, f32[3072,128]{1,0:T(8,128)}, u32[]{:S(2)}, u32[]{:S(2)}) collective-permute-start(f32[3072,128]{1,0:T(8,128)S(1)} %get-tuple-element.48.sent0), channel_id=1, source_target_pairs={{0,4},{2,6},{4,8},{5,1},{6,10},{7,3},{8,12},{9,5},{10,14},{11,7},{... | collective-permute-start | bytes 4718600 | tf_op jit(solution)/shard_map/ppermute | solution.py:19
  22.7 1.3 %collective-permute-start.7 = (f32[3072,128]{1,0:T(8,128)S(1)}, f32[3072,128]{1,0:T(8,128)}, u32[]{:S(2)}, u32[]{:S(2)}) collective-permute-start(f32[3072,128]{1,0:T(8,128)S(1)} %get-tuple-element.49.sent1), channel_id=1, source_target_pairs={{1,5},{3,7},{4,0},{5,9},{6,2},{7,11},{8,4},{9,13},{10,6},{11,15},{... | collective-permute-start | bytes 4718600 | tf_op jit(solution)/shard_map/ppermute | solution.py:19
  26.1 5.4 %collective-permute-done.got1 = f32[2312,128]{1,0:T(8,128)S(1)} collective-permute-done((f32[2312,128]{1,0:T(8,128)S(1)}, f32[2312,128]{1,0:T(8,128)S(1)}, u32[]{:S(2)}, u32[]{:S(2)}) %collective-permute-start) | collective-permute-done | bytes 1183776 | tf_op jit(solution)/shard_map/ppermute | solution.py:19
  31.5 2.5 %collective-permute-start.9 = (f32[2,128,128]{2,1,0:T(8,128)}, f32[2,128,128]{2,1,0:T(8,128)S(1)}, u32[]{:S(2)}, u32[]{:S(2)}) collective-permute-start(f32[2,128,128]{2,1,0:T(8,128)} %param.9), channel_id=1, source_target_pairs={{0,2},{1,3},{2,0},{3,1},{4,6},{5,7},{6,4},{7,5},{8,10},{9,11},{10,... | collective-permute-start | bytes 393224 | tf_op jit(solution)/shard_map/ppermute | solution.py:24
  34.0 1.7 %collective-permute-done.1.got0 = f32[2312,128]{1,0:T(8,128)S(1)} collective-permute-done((f32[2312,128]{1,0:T(8,128)S(1)}, f32[2312,128]{1,0:T(8,128)S(1)}, u32[]{:S(2)}, u32[]{:S(2)}) %collective-permute-start.1) | collective-permute-done | bytes 1183776 | tf_op jit(solution)/shard_map/ppermute | solution.py:19
  35.7 2.5 %collective-permute-start.10 = (f32[2,128,128]{2,1,0:T(8,128)}, f32[2,128,128]{2,1,0:T(8,128)}, u32[]{:S(2)}, u32[]{:S(2)}) collective-permute-start(f32[2,128,128]{2,1,0:T(8,128)} %param.9), channel_id=1, source_target_pairs={{0,3},{1,2},{2,1},{3,0},{4,7},{5,6},{6,5},{7,4},{8,11},{9,10},{10,... | collective-permute-start | bytes 393224 | tf_op jit(solution)/shard_map/ppermute | solution.py:24
  44.5 1.4 %pad_add_fusion = s32[19]{0:T(128)S(1)} fusion(s32[16]{0:T(128)} %reshape.28, s32[1]{0:T(128)} %get-tuple-element.87, s32[2]{0:T(128)S(1)} %bitcast.16), kind=kLoop, calls=%fused_computation.10 | loop fusion | flops 38 | bytes 152 | tf_op jit(solution)/shard_map/concatenate | solution.py:547
  45.9 4.0 %collective-permute-start.4 = (f32[2048,128]{1,0:T(8,128)}, f32[2048,128]{1,0:T(8,128)S(1)}, u32[]{:S(2)}, u32[]{:S(2)}) collective-permute-start(f32[2048,128]{1,0:T(8,128)} %copy-done.8), channel_id=1, source_target_pairs={{0,4},{2,6},{4,8},{5,1},{6,10},{7,3},{8,12},{9,5},{10,14},{11,7},{... | collective-permute-start | bytes 3145736 | tf_op jit(solution)/shard_map/ppermute | solution.py:19
  51.1 1.3 %collective-permute-start.5 = (f32[2048,128]{1,0:T(8,128)}, f32[2048,128]{1,0:T(8,128)S(1)}, u32[]{:S(2)}, u32[]{:S(2)}) collective-permute-start(f32[2048,128]{1,0:T(8,128)} %copy-done.10), channel_id=1, source_target_pairs={{1,5},{3,7},{4,0},{5,9},{6,2},{7,11},{8,4},{9,13},{10,6},{11,15},{... | collective-permute-start | bytes 3145736 | tf_op jit(solution)/shard_map/ppermute | solution.py:19
  52.4 1.3 %collective-permute-start.13 = (f32[2,2,128,128]{3,2,1,0:T(8,128)}, f32[2,2,128,128]{3,2,1,0:T(8,128)S(1)}, u32[]{:S(2)}, u32[]{:S(2)}) collective-permute-start(f32[2,2,128,128]{3,2,1,0:T(8,128)} %get-tuple-element.83), channel_id=1, source_target_pairs={{0,3},{1,2},{2,1},{3,0},{4,7},{5,6},{6,5},{7,4},{8,11},{9,10},{10,... | collective-permute-start | bytes 786440 | tf_op jit(solution)/shard_map/ppermute | solution.py:24
  56.0 1.3 %copy-done.5 = f32[2312,128]{1,0:T(8,128)S(1)} copy-done((f32[2312,128]{1,0:T(8,128)S(1)}, f32[2312,128]{1,0:T(8,128)}, u32[]{:S(2)}) %copy-start.5) | copy-done | bytes 1183768
  61.8 1.3 %prepare.1 = (f32[8,128,128]{2,1,0:T(8,128)S(1)}, f32[8,128,128]{2,1,0:T(8,128)S(1)}, bf16[8,128,256]{2,1,0:T(8,128)(2,1)S(1)}, bf16[8,256,256]{2,1,0:T(8,128)(2...) custom-call(s32[60]{0:T(128)S(1)} %get-tuple-element.41.table, ...), custom_call_target="tpu_custom_call" | custom-call | flops 1 | bytes 1 | tf_op jit(solution)/shard_map/prepare/pallas_call | solution.py:561
  63.2 6.2 %collective-permute-done.6.got0 = f32[3072,128]{1,0:T(8,128)} collective-permute-done((f32[3072,128]{1,0:T(8,128)S(1)}, f32[3072,128]{1,0:T(8,128)}, u32[]{:S(2)}, u32[]{:S(2)}) %collective-permute-start.6) | collective-permute-done | bytes 1572896 | tf_op jit(solution)/shard_map/ppermute | solution.py:19
  69.4 6.9 %first_matvec0.1 = (bf16[3,1024,256]{2,1,0:T(8,128)(2,1)S(1)}, bf16[3,1024,256]{2,1,0:T(8,128)(2,1)S(1)}, f32[5,128,128]{2,1,0:T(8,128)S(1)}) custom-call(s32[16]{0:T(128)S(1)} %slice.55.slots, s32[19,8,128]{2,1,0:T(8,128)S(1)} %broadcast_in_dim.4.flags, f32[8,8,8,128]{3,2,1,0:T(8,128)S(1)} %broadcast_in_dim.5.bond, ...), custom_call_target="tpu_custom_call" | custom-call | flops 1 | bytes 1 | tf_op jit(solution)/shard_map/first_matvec0/pallas_call | solution.py:615
  76.3 2.1 %collective-permute-start.14 = (f32[5,128,128]{2,1,0:T(8,128)S(1)}, f32[5,128,128]{2,1,0:T(8,128)S(1)}, u32[]{:S(2)}, u32[]{:S(2)}) collective-permute-start(f32[5,128,128]{2,1,0:T(8,128)S(1)} %get-tuple-element.56.part), channel_id=1, source_target_pairs={{0,2},{1,3},{2,0},{3,1},{4,6},{5,7},{6,4},{7,5},{8,10},{9,11},{10,... | collective-permute-start | bytes 983048 | tf_op jit(solution)/shard_map/ppermute | solution.py:24
  78.4 4.5 %collective-permute-start.2 = (f32[1024,128]{1,0:T(8,128)S(1)}, f32[1024,128]{1,0:T(8,128)S(1)}, u32[]{:S(2)}, u32[]{:S(2)}) collective-permute-start(f32[1024,128]{1,0:T(8,128)S(1)} %copy-done.13), channel_id=1, source_target_pairs={{0,4},{2,6},{4,8},{5,1},{6,10},{7,3},{8,12},{9,5},{10,14},{11,7},{... | collective-permute-start | bytes 1572872 | tf_op jit(solution)/shard_map/ppermute | solution.py:19
  82.9 1.5 %collective-permute-start.3 = (f32[1024,128]{1,0:T(8,128)S(1)}, f32[1024,128]{1,0:T(8,128)S(1)}, u32[]{:S(2)}, u32[]{:S(2)}) collective-permute-start(f32[1024,128]{1,0:T(8,128)S(1)} %copy-done.15), channel_id=1, source_target_pairs={{1,5},{3,7},{4,0},{5,9},{6,2},{7,11},{8,4},{9,13},{10,6},{11,15},{... | collective-permute-start | bytes 1572872 | tf_op jit(solution)/shard_map/ppermute | solution.py:19
  84.4 2.3 %collective-permute-done.14 = f32[5,128,128]{2,1,0:T(8,128)S(1)} collective-permute-done((f32[5,128,128]{2,1,0:T(8,128)S(1)}, f32[5,128,128]{2,1,0:T(8,128)S(1)}, u32[]{:S(2)}, u32[]{:S(2)}) %collective-permute-start.14) | collective-permute-done | bytes 327712 | tf_op jit(solution)/shard_map/ppermute | solution.py:24
  88.5 3.4 %collective-permute-done.4.got0 = f32[2048,128]{1,0:T(8,128)S(1)} collective-permute-done((f32[2048,128]{1,0:T(8,128)}, f32[2048,128]{1,0:T(8,128)S(1)}, u32[]{:S(2)}, u32[]{:S(2)}) %collective-permute-start.4) | collective-permute-done | bytes 1048608 | tf_op jit(solution)/shard_map/ppermute | solution.py:19
  92.0 2.1 %first_matvec1.1 = (bf16[2,1024,256]{2,1,0:T(8,128)(2,1)S(1)}, bf16[2,1024,256]{2,1,0:T(8,128)(2,1)S(1)}, f32[2,128,128]{2,1,0:T(8,128)S(1)}) custom-call(s32[19,8,128]{2,1,0:T(8,128)S(1)} %broadcast_in_dim.4.flags, f32[8,8,8,128]{3,2,1,0:T(8,128)S(1)} %broadcast_in_dim.5.bond, f32[2048,128]{1,0:T(8,128)S(1)} %collective-permute-done.4.got0, ...), custom_call_target="tpu_custom_call" | custom-call | flops 1 | bytes 1 | tf_op jit(solution)/shard_map/first_matvec1/pallas_call | solution.py:615
  94.5 3.2 %early_second_matvec.2 = (f32[5,128,128]{2,1,0:T(8,128)S(1)}, f32[8,8,128]{2,1,0:T(8,128)S(1)}) custom-call(s32[16]{0:T(128)S(1)} %slice.55.slots, f32[5,128,128]{2,1,0:T(8,128)S(1)} %add.29.image, f32[5,128,128]{2,1,0:T(8,128)S(1)} %get-tuple-element.56.part, f32[8,128,128]{2,1,0:T(8,128)S(1)} %get-tuple-element.53.vec, ...), custom_call_target="tpu_custom_call" | custom-call | flops 1 | bytes 1 | tf_op jit(solution)/shard_map/early_second_matvec/pallas_call | solution.py:581
  97.8 2.4 %collective-permute-start.19 = (f32[2,128,128]{2,1,0:T(8,128)S(1)}, f32[2,128,128]{2,1,0:T(8,128)S(1)}, u32[]{:S(2)}, u32[]{:S(2)}) collective-permute-start(f32[2,128,128]{2,1,0:T(8,128)S(1)} %add.30), channel_id=1, source_target_pairs={{0,2},{1,3},{2,0},{3,1},{4,6},{5,7},{6,4},{7,5},{8,10},{9,11},{10,... | collective-permute-start | bytes 393224 | tf_op jit(solution)/shard_map/ppermute | solution.py:24
  101.4 1.3 %collective-permute-start.17 = (f32[1,128,128]{2,1,0:T(8,128)S(1)}, f32[1,128,128]{2,1,0:T(8,128)S(1)}, u32[]{:S(2)}, u32[]{:S(2)}) collective-permute-start(f32[1,128,128]{2,1,0:T(8,128)S(1)} %get-tuple-element.68), channel_id=1, source_target_pairs={{0,1},{1,0},{2,3},{3,2},{4,5},{5,4},{6,7},{7,6},{8,9},{9,8},{10,11... | collective-permute-start | bytes 196616 | tf_op jit(solution)/shard_map/ppermute | solution.py:24
  103.6 2.1 %collective-permute-start.18 = (f32[1,128,128]{2,1,0:T(8,128)S(1)}, f32[1,128,128]{2,1,0:T(8,128)S(1)}, u32[]{:S(2)}, u32[]{:S(2)}) collective-permute-start(f32[1,128,128]{2,1,0:T(8,128)S(1)} %add.31.part0), channel_id=1, source_target_pairs={{0,2},{1,3},{2,0},{3,1},{4,6},{5,7},{6,4},{7,5},{8,10},{9,11},{10,... | collective-permute-start | bytes 196616 | tf_op jit(solution)/shard_map/ppermute | solution.py:24
  105.7 1.6 %early_second_matvec.3 = (f32[2,128,128]{2,1,0:T(8,128)S(1)}, f32[8,8,128]{2,1,0:T(8,128)S(1)}) custom-call(f32[2,128,128]{2,1,0:T(8,128)S(1)} %add.32.image, f32[2,128,128]{2,1,0:T(8,128)S(1)} %get-tuple-element.59.part, f32[8,128,128]{2,1,0:T(8,128)S(1)} %get-tuple-element.53.vec, f32[8,128,128]{2,1,0:T(8,128)S(1)} %get-tuple-element.52.plain.middle, ...), custom_call_target="tpu_custom_call" | custom-call | flops 1 | bytes 1 | tf_op jit(solution)/shard_map/early_second_matvec/pallas_call | solution.py:581
  108.3 1.3 %second_matvec.1 = (f32[2,128,128]{2,1,0:T(8,128)S(1)}, f32[3,8,128]{2,1,0:T(8,128)S(1)}) custom-call(s32[19,8,128]{2,1,0:T(8,128)S(1)} %broadcast_in_dim.4.flags, f32[1,128,128]{2,1,0:T(8,128)S(1)} %add.31.part0, f32[1,128,128]{2,1,0:T(8,128)S(1)} %collective-permute-done.18.part1, f32[8,128,128]{2,1,0:T(8,128)S(1)} %get-tuple-element.53.vec, ...), custom_call_target="tpu_custom_call" | custom-call | flops 1 | bytes 1 | tf_op jit(solution)/shard_map/second_matvec/pallas_call | solution.py:641
  109.7 1.8 %collective-permute-start.21 = (f32[1,8,128]{2,1,0:T(8,128)S(1)}, f32[1,8,128]{2,1,0:T(8,128)S(1)}, u32[]{:S(2)}, u32[]{:S(2)}) collective-permute-start(f32[1,8,128]{2,1,0:T(8,128)S(1)} %slice.58), channel_id=1, source_target_pairs={{0,2},{1,3},{2,0},{3,1},{4,6},{5,7},{6,4},{7,5},{8,10},{9,11},{10,... | collective-permute-start | bytes 12296 | tf_op jit(solution)/shard_map/ppermute | solution.py:24
  111.6 1.8 %collective-permute-done.21.share2 = f32[1,8,128]{2,1,0:T(8,128)S(1)} collective-permute-done((f32[1,8,128]{2,1,0:T(8,128)S(1)}, f32[1,8,128]{2,1,0:T(8,128)S(1)}, u32[]{:S(2)}, u32[]{:S(2)}) %collective-permute-start.21) | collective-permute-done | bytes 4128 | tf_op jit(solution)/shard_map/ppermute | solution.py:24
  (88 shorter events, 24.7 us)
Async XLA Ops:
  2.3 11.7 %copy-start.4 = (f32[2312,128]{1,0:T(8,128)}, f32[2312,128]{1,0:T(8,128)S(1)}, u32[]{:S(2)}) copy-start(f32[2312,128]{1,0:T(8,128)S(1)} %get-tuple-element.43.sent0) | copy-start | bytes 3551236
  2.4 11.7 %copy-start.6 = (f32[2312,128]{1,0:T(8,128)}, f32[2312,128]{1,0:T(8,128)S(1)}, u32[]{:S(2)}) copy-start(f32[2312,128]{1,0:T(8,128)S(1)} %get-tuple-element.42.sent1) | copy-start | bytes 3551236
  2.4 29.1 %collective-permute-start = (f32[2312,128]{1,0:T(8,128)S(1)}, f32[2312,128]{1,0:T(8,128)S(1)}, u32[]{:S(2)}, u32[]{:S(2)}) collective-permute-start(f32[2312,128]{1,0:T(8,128)S(1)} %get-tuple-element.42.sent1), channel_id=1, source_target_pairs={{1,5},{3,7},{4,0},{5,9},{6,2},{7,11},{8,4},{9,13},{10,6},{11,15},{... | collective-permute-start | bytes 3551240 | tf_op jit(solution)/shard_map/ppermute | solution.py:19
  3.7 32.0 %collective-permute-start.1 = (f32[2312,128]{1,0:T(8,128)S(1)}, f32[2312,128]{1,0:T(8,128)S(1)}, u32[]{:S(2)}, u32[]{:S(2)}) collective-permute-start(f32[2312,128]{1,0:T(8,128)S(1)} %get-tuple-element.43.sent0), channel_id=1, source_target_pairs={{0,4},{2,6},{4,8},{5,1},{6,10},{7,3},{8,12},{9,5},{10,14},{11,7},{... | collective-permute-start | bytes 3551240 | tf_op jit(solution)/shard_map/ppermute | solution.py:19
  17.8 51.6 %collective-permute-start.6 = (f32[3072,128]{1,0:T(8,128)S(1)}, f32[3072,128]{1,0:T(8,128)}, u32[]{:S(2)}, u32[]{:S(2)}) collective-permute-start(f32[3072,128]{1,0:T(8,128)S(1)} %get-tuple-element.48.sent0), channel_id=1, source_target_pairs={{0,4},{2,6},{4,8},{5,1},{6,10},{7,3},{8,12},{9,5},{10,14},{11,7},{... | collective-permute-start | bytes 4718600 | tf_op jit(solution)/shard_map/ppermute | solution.py:19
  22.7 46.7 %collective-permute-start.7 = (f32[3072,128]{1,0:T(8,128)S(1)}, f32[3072,128]{1,0:T(8,128)}, u32[]{:S(2)}, u32[]{:S(2)}) collective-permute-start(f32[3072,128]{1,0:T(8,128)S(1)} %get-tuple-element.49.sent1), channel_id=1, source_target_pairs={{1,5},{3,7},{4,0},{5,9},{6,2},{7,11},{8,4},{9,13},{10,6},{11,15},{... | collective-permute-start | bytes 4718600 | tf_op jit(solution)/shard_map/ppermute | solution.py:19
  23.9 17.8 %collective-permute-start.8 = (f32[2,128,128]{2,1,0:T(8,128)}, f32[2,128,128]{2,1,0:T(8,128)S(1)}, u32[]{:S(2)}, u32[]{:S(2)}) collective-permute-start(f32[2,128,128]{2,1,0:T(8,128)} %param.9), channel_id=1, source_target_pairs={{0,1},{1,0},{2,3},{3,2},{4,5},{5,4},{6,7},{7,6},{8,9},{9,8},{10,11... | collective-permute-start | bytes 393224 | tf_op jit(solution)/shard_map/ppermute | solution.py:24
  31.5 10.2 %collective-permute-start.9 = (f32[2,128,128]{2,1,0:T(8,128)}, f32[2,128,128]{2,1,0:T(8,128)S(1)}, u32[]{:S(2)}, u32[]{:S(2)}) collective-permute-start(f32[2,128,128]{2,1,0:T(8,128)} %param.9), channel_id=1, source_target_pairs={{0,2},{1,3},{2,0},{3,1},{4,6},{5,7},{6,4},{7,5},{8,10},{9,11},{10,... | collective-permute-start | bytes 393224 | tf_op jit(solution)/shard_map/ppermute | solution.py:24
  35.7 10.2 %collective-permute-start.10 = (f32[2,128,128]{2,1,0:T(8,128)}, f32[2,128,128]{2,1,0:T(8,128)}, u32[]{:S(2)}, u32[]{:S(2)}) collective-permute-start(f32[2,128,128]{2,1,0:T(8,128)} %param.9), channel_id=1, source_target_pairs={{0,3},{1,2},{2,1},{3,0},{4,7},{5,6},{6,5},{7,4},{8,11},{9,10},{10,... | collective-permute-start | bytes 393224 | tf_op jit(solution)/shard_map/ppermute | solution.py:24
  41.7 9.4 %collective-permute-start.11 = (f32[2,2,128,128]{3,2,1,0:T(8,128)}, f32[2,2,128,128]{3,2,1,0:T(8,128)}, u32[]{:S(2)}, u32[]{:S(2)}) collective-permute-start(f32[2,2,128,128]{3,2,1,0:T(8,128)} %get-tuple-element.83), channel_id=1, source_target_pairs={{0,1},{1,0},{2,3},{3,2},{4,5},{5,4},{6,7},{7,6},{8,9},{9,8},{10,11... | collective-permute-start | bytes 786440 | tf_op jit(solution)/shard_map/ppermute | solution.py:24
  41.7 10.6 %collective-permute-start.12 = (f32[2,2,128,128]{3,2,1,0:T(8,128)}, f32[2,2,128,128]{3,2,1,0:T(8,128)}, u32[]{:S(2)}, u32[]{:S(2)}) collective-permute-start(f32[2,2,128,128]{3,2,1,0:T(8,128)} %get-tuple-element.83), channel_id=1, source_target_pairs={{0,2},{1,3},{2,0},{3,1},{4,6},{5,7},{6,4},{7,5},{8,10},{9,11},{10,... | collective-permute-start | bytes 786440 | tf_op jit(solution)/shard_map/ppermute | solution.py:24
  44.4 10.3 %copy-start.1 = (f32[2312,128]{1,0:T(8,128)S(1)}, f32[2312,128]{1,0:T(8,128)}, u32[]{:S(2)}) copy-start(f32[2312,128]{1,0:T(8,128)} %copy-done) | copy-start | bytes 3551236
  45.9 46.1 %collective-permute-start.4 = (f32[2048,128]{1,0:T(8,128)}, f32[2048,128]{1,0:T(8,128)S(1)}, u32[]{:S(2)}, u32[]{:S(2)}) collective-permute-start(f32[2048,128]{1,0:T(8,128)} %copy-done.8), channel_id=1, source_target_pairs={{0,4},{2,6},{4,8},{5,1},{6,10},{7,3},{8,12},{9,5},{10,14},{11,7},{... | collective-permute-start | bytes 3145736 | tf_op jit(solution)/shard_map/ppermute | solution.py:19
  51.1 40.9 %collective-permute-start.5 = (f32[2048,128]{1,0:T(8,128)}, f32[2048,128]{1,0:T(8,128)S(1)}, u32[]{:S(2)}, u32[]{:S(2)}) collective-permute-start(f32[2048,128]{1,0:T(8,128)} %copy-done.10), channel_id=1, source_target_pairs={{1,5},{3,7},{4,0},{5,9},{6,2},{7,11},{8,4},{9,13},{10,6},{11,15},{... | collective-permute-start | bytes 3145736 | tf_op jit(solution)/shard_map/ppermute | solution.py:19
  52.4 8.3 %collective-permute-start.13 = (f32[2,2,128,128]{3,2,1,0:T(8,128)}, f32[2,2,128,128]{3,2,1,0:T(8,128)S(1)}, u32[]{:S(2)}, u32[]{:S(2)}) collective-permute-start(f32[2,2,128,128]{3,2,1,0:T(8,128)} %get-tuple-element.83), channel_id=1, source_target_pairs={{0,3},{1,2},{2,1},{3,0},{4,7},{5,6},{6,5},{7,4},{8,11},{9,10},{10,... | collective-permute-start | bytes 786440 | tf_op jit(solution)/shard_map/ppermute | solution.py:24
  54.7 1.3 %copy-start.3 = (f32[2312,128]{1,0:T(8,128)S(1)}, f32[2312,128]{1,0:T(8,128)}, u32[]{:S(2)}) copy-start(f32[2312,128]{1,0:T(8,128)} %copy-done.2) | copy-start | bytes 3551236
  59.8 2.0 %copy-start.16 = (f32[2,128,128]{2,1,0:T(8,128)S(1)}, f32[2,128,128]{2,1,0:T(8,128)}, u32[]{:S(2)}) copy-start(f32[2,128,128]{2,1,0:T(8,128)} %onsite.1) | copy-start | bytes 393220
  69.4 9.0 %copy-start.13 = (f32[1024,128]{1,0:T(8,128)S(1)}, f32[1024,128]{1,0:T(8,128)}, u32[]{:S(2)}) copy-start(f32[1024,128]{1,0:T(8,128)} %copy-done.12) | copy-start | bytes 1572868
  69.4 13.5 %copy-start.15 = (f32[1024,128]{1,0:T(8,128)S(1)}, f32[1024,128]{1,0:T(8,128)}, u32[]{:S(2)}) copy-start(f32[1024,128]{1,0:T(8,128)} %copy-done.14) | copy-start | bytes 1572868
  69.4 22.6 %copy-start.11 = (f32[2048,128]{1,0:T(8,128)S(1)}, f32[2048,128]{1,0:T(8,128)}, u32[]{:S(2)}) copy-start(f32[2048,128]{1,0:T(8,128)} %copy-done.10) | copy-start | bytes 3145732
  76.3 15.7 %copy-start.9 = (f32[2048,128]{1,0:T(8,128)S(1)}, f32[2048,128]{1,0:T(8,128)}, u32[]{:S(2)}) copy-start(f32[2048,128]{1,0:T(8,128)} %copy-done.8) | copy-start | bytes 3145732
  76.3 10.4 %collective-permute-start.14 = (f32[5,128,128]{2,1,0:T(8,128)S(1)}, f32[5,128,128]{2,1,0:T(8,128)S(1)}, u32[]{:S(2)}, u32[]{:S(2)}) collective-permute-start(f32[5,128,128]{2,1,0:T(8,128)S(1)} %get-tuple-element.56.part), channel_id=1, source_target_pairs={{0,2},{1,3},{2,0},{3,1},{4,6},{5,7},{6,4},{7,5},{8,10},{9,11},{10,... | collective-permute-start | bytes 983048 | tf_op jit(solution)/shard_map/ppermute | solution.py:24
  78.4 21.8 %collective-permute-start.2 = (f32[1024,128]{1,0:T(8,128)S(1)}, f32[1024,128]{1,0:T(8,128)S(1)}, u32[]{:S(2)}, u32[]{:S(2)}) collective-permute-start(f32[1024,128]{1,0:T(8,128)S(1)} %copy-done.13), channel_id=1, source_target_pairs={{0,4},{2,6},{4,8},{5,1},{6,10},{7,3},{8,12},{9,5},{10,14},{11,7},{... | collective-permute-start | bytes 1572872 | tf_op jit(solution)/shard_map/ppermute | solution.py:19
  82.9 17.2 %collective-permute-start.3 = (f32[1024,128]{1,0:T(8,128)S(1)}, f32[1024,128]{1,0:T(8,128)S(1)}, u32[]{:S(2)}, u32[]{:S(2)}) collective-permute-start(f32[1024,128]{1,0:T(8,128)S(1)} %copy-done.15), channel_id=1, source_target_pairs={{1,5},{3,7},{4,0},{5,9},{6,2},{7,11},{8,4},{9,13},{10,6},{11,15},{... | collective-permute-start | bytes 1572872 | tf_op jit(solution)/shard_map/ppermute | solution.py:19
  86.7 1.7 %collective-permute-start.15 = (f32[5,128,128]{2,1,0:T(8,128)S(1)}, f32[5,128,128]{2,1,0:T(8,128)S(1)}, u32[]{:S(2)}, u32[]{:S(2)}) collective-permute-start(f32[5,128,128]{2,1,0:T(8,128)S(1)} %add.28), channel_id=1, source_target_pairs={{0,1},{1,0},{2,3},{3,2},{4,5},{5,4},{6,7},{7,6},{8,9},{9,8},{10,11... | collective-permute-start | bytes 983048 | tf_op jit(solution)/shard_map/ppermute | solution.py:24
  94.1 3.7 %collective-permute-start.16 = (f32[2,128,128]{2,1,0:T(8,128)S(1)}, f32[2,128,128]{2,1,0:T(8,128)S(1)}, u32[]{:S(2)}, u32[]{:S(2)}) collective-permute-start(f32[2,128,128]{2,1,0:T(8,128)S(1)} %get-tuple-element.59.part), channel_id=1, source_target_pairs={{0,1},{1,0},{2,3},{3,2},{4,5},{5,4},{6,7},{7,6},{8,9},{9,8},{10,11... | collective-permute-start | bytes 393224 | tf_op jit(solution)/shard_map/ppermute | solution.py:24
  97.8 7.9 %collective-permute-start.19 = (f32[2,128,128]{2,1,0:T(8,128)S(1)}, f32[2,128,128]{2,1,0:T(8,128)S(1)}, u32[]{:S(2)}, u32[]{:S(2)}) collective-permute-start(f32[2,128,128]{2,1,0:T(8,128)S(1)} %add.30), channel_id=1, source_target_pairs={{0,2},{1,3},{2,0},{3,1},{4,6},{5,7},{6,4},{7,5},{8,10},{9,11},{10,... | collective-permute-start | bytes 393224 | tf_op jit(solution)/shard_map/ppermute | solution.py:24
  101.4 2.2 %collective-permute-start.17 = (f32[1,128,128]{2,1,0:T(8,128)S(1)}, f32[1,128,128]{2,1,0:T(8,128)S(1)}, u32[]{:S(2)}, u32[]{:S(2)}) collective-permute-start(f32[1,128,128]{2,1,0:T(8,128)S(1)} %get-tuple-element.68), channel_id=1, source_target_pairs={{0,1},{1,0},{2,3},{3,2},{4,5},{5,4},{6,7},{7,6},{8,9},{9,8},{10,11... | collective-permute-start | bytes 196616 | tf_op jit(solution)/shard_map/ppermute | solution.py:24
  103.6 4.7 %collective-permute-start.18 = (f32[1,128,128]{2,1,0:T(8,128)S(1)}, f32[1,128,128]{2,1,0:T(8,128)S(1)}, u32[]{:S(2)}, u32[]{:S(2)}) collective-permute-start(f32[1,128,128]{2,1,0:T(8,128)S(1)} %add.31.part0), channel_id=1, source_target_pairs={{0,2},{1,3},{2,0},{3,1},{4,6},{5,7},{6,4},{7,5},{8,10},{9,11},{10,... | collective-permute-start | bytes 196616 | tf_op jit(solution)/shard_map/ppermute | solution.py:24
  109.6 2.0 %collective-permute-start.20 = (f32[1,8,128]{2,1,0:T(8,128)S(1)}, f32[1,8,128]{2,1,0:T(8,128)S(1)}, u32[]{:S(2)}, u32[]{:S(2)}) collective-permute-start(f32[1,8,128]{2,1,0:T(8,128)S(1)} %slice.58), channel_id=1, source_target_pairs={{0,1},{1,0},{2,3},{3,2},{4,5},{5,4},{6,7},{7,6},{8,9},{9,8},{10,11... | collective-permute-start | bytes 12296 | tf_op jit(solution)/shard_map/ppermute | solution.py:24
  109.7 3.7 %collective-permute-start.21 = (f32[1,8,128]{2,1,0:T(8,128)S(1)}, f32[1,8,128]{2,1,0:T(8,128)S(1)}, u32[]{:S(2)}, u32[]{:S(2)}) collective-permute-start(f32[1,8,128]{2,1,0:T(8,128)S(1)} %slice.58), channel_id=1, source_target_pairs={{0,2},{1,3},{2,0},{3,1},{4,6},{5,7},{6,4},{7,5},{8,10},{9,11},{10,... | collective-permute-start | bytes 12296 | tf_op jit(solution)/shard_map/ppermute | solution.py:24
  111.5 3.0 %collective-permute-start.22 = (f32[1,8,128]{2,1,0:T(8,128)S(1)}, f32[1,8,128]{2,1,0:T(8,128)S(1)}, u32[]{:S(2)}, u32[]{:S(2)}) collective-permute-start(f32[1,8,128]{2,1,0:T(8,128)S(1)} %slice.58), channel_id=1, source_target_pairs={{0,3},{1,2},{2,1},{3,0},{4,7},{5,6},{6,5},{7,4},{8,11},{9,10},{10,... | collective-permute-start | bytes 12296 | tf_op jit(solution)/shard_map/ppermute | solution.py:24
  (11 other events, 10.4 us)
